TPU v7x, 128 devices: a whole 4x4x4 slice. The times are simulated.
128 devices in a mesh: grp: 2 (over z_lo), dp: 4 (over y), mp: 16 (over x, z_hi, core).
Axes of the slice: x: 4, y: 4, z: 4 (z_hi: 2, z_lo: 2; z = z_hi * 2 + z_lo), core: 2. Of those that a mesh axis runs over, the one named last changes fastest.
Arguments:
- queries: bfloat16 [4, 2048, 4096], P('dp', None, 'mp'), may hold values from -5 to 5
- keys: bfloat16 [4, 2048, 512], P('dp'), may hold values from -5 to 5
- values: bfloat16 [4, 2048, 512], P('dp'), may hold values from -6 to 6
- out_weight: bfloat16 [4096, 5120], P('mp'), may hold values from -0.09375 to 0.09375
- residual: bfloat16 [4, 2048, 5120], P('dp', 'mp'), may hold values from -24 to 24
- student_hidden: bfloat16 [4, 2048, 2560], P('dp', 'mp'), may hold values from -6 to 6
- norm_gain: float32 [2560], replicated, may hold values from 0.5 to 1.5
- projection: bfloat16 [2560, 5120], P(None, ('grp', 'dp')), may hold values from -0.125 to 0.125
- lengths: int32 [4], replicated, may hold values from 512 to 2048, as said below
Outputs:
- teacher_out: bfloat16 [4, 2048, 5120], P('dp', 'mp', 'grp')
- distill_loss: float32 [], replicated
- grad_proj: float32 [2560, 5120], P('mp', ('grp', 'dp'))
- grad_gain: float32 [2560], P('grp')
- grad_hidden: float32 [4, 2048, 2560], P('dp', 'mp', 'grp')
Inputs may be any that keep to these rules, and one draw needn't show every extreme that they name: `lengths`: at least one sequence is live throughout.
All inputs are finite; a program needn't handle non-finite values.
Results may differ from a plain program's by a relative error of at most 0.018.
Values may be sent and summed in bfloat16 or wider, within the bound.
No kernel may reach another device: no remote copies, remote signals or barrier semaphores. Data moves between devices by JAX's collectives and lax.ppermute only.
A program may use at most 128 MiB of HBM per device.

v0:
```python
import jax
import jax.numpy as jnp
from jax import lax
from jax.sharding import PartitionSpec as P

D_T = 5120
D_S = 2560
HD = 128
HQ = 32
KVH = 4


def passed_along(array, axis, by):
    length = lax.axis_size(axis)
    pairs = [(i, i + by) for i in range(length) if 0 <= i + by < length]
    return lax.ppermute(array, axis, pairs)


def attend(query_rows, positions, key_rows, value_rows):
    total_rows = query_rows.shape[0]
    block_rows = min(512, total_rows)
    head_count = query_rows.shape[1] // HD
    key_positions = jnp.arange(key_rows.shape[0], dtype=jnp.int32)
    score_scale = HD ** (-0.5)

    def one_block(inputs):
        row_block, row_positions = inputs
        query_heads = row_block.reshape(block_rows, head_count, HD)
        scores = (
            jnp.einsum("bhd,kd->hbk", query_heads, key_rows, preferred_element_type=jnp.float32)
            * score_scale
        )
        allowed = row_positions[None, :, None] >= key_positions[None, None, :]
        scores = jnp.where(allowed, scores, -1e30)
        row_max = jnp.max(scores, axis=-1, keepdims=True)
        exponent = jnp.exp(scores - row_max)
        weights = (exponent / jnp.sum(exponent, axis=-1, keepdims=True)).astype(jnp.bfloat16)
        context_rows = jnp.einsum(
            "hbk,kd->bhd", weights, value_rows, preferred_element_type=jnp.float32
        )
        return context_rows.reshape(block_rows, head_count * HD).astype(jnp.bfloat16)

    blocks = total_rows // block_rows
    result = lax.map(
        one_block,
        (query_rows.reshape(blocks, block_rows, -1), positions.reshape(blocks, block_rows)),
    )
    return result.reshape(total_rows, head_count * HD)


def body(
    queries, keys, values, out_weight, residual, student_hidden, norm_gain, projection, lengths
):
    seq_len = queries.shape[1]
    tok_rows = residual.shape[1]
    half_cols = residual.shape[2] // 2
    grp_index = lax.axis_index("grp")
    mp_index = lax.axis_index("mp")
    local_heads = queries.shape[2] // HD
    kv_head = mp_index * local_heads // (HQ // KVH)
    key_rows = lax.dynamic_slice_in_dim(keys[0], kv_head * HD, HD, 1)
    value_rows = lax.dynamic_slice_in_dim(values[0], kv_head * HD, HD, 1)
    context_width = queries.shape[2]
    out_cols = out_weight.shape[1]
    positions = jnp.arange(seq_len, dtype=jnp.int32)
    context = lax.cond(
        grp_index == 0,
        lambda: attend(queries[0], positions, key_rows, value_rows),
        lambda: jnp.zeros((seq_len, context_width), jnp.bfloat16),
    )
    attn_rows = lax.psum_scatter(
        lax.cond(
            grp_index == 0,
            lambda: jnp.dot(context, out_weight, preferred_element_type=jnp.float32),
            lambda: jnp.zeros((tok_rows * lax.axis_size("mp"), out_cols), jnp.float32),
        ).astype(jnp.bfloat16),
        "mp",
        scatter_dimension=0,
        tiled=True,
    ).astype(jnp.float32)
    full_rows = (residual[0].astype(jnp.float32) + attn_rows).astype(jnp.bfloat16)
    shifted = passed_along(full_rows[:, half_cols:], "grp", 1)
    own_target = jnp.where(grp_index == 0, full_rows[:, :half_cols], shifted)
    hidden = student_hidden[0].astype(jnp.float32)
    inverse_rms = lax.rsqrt(jnp.mean(hidden * hidden, axis=-1, keepdims=True) + 1e-06)
    unit_rows = hidden * inverse_rms
    normed = (unit_rows * norm_gain).astype(jnp.bfloat16)
    normed_all = lax.all_gather(normed, "dp", axis=0, tiled=True)
    targets = lax.all_to_all(own_target, "dp", split_axis=1, concat_axis=0, tiled=True)
    predicted = jnp.dot(normed_all, projection, preferred_element_type=jnp.float32)
    row_ids = jnp.arange(normed_all.shape[0], dtype=jnp.int32)
    seq_ids = row_ids // tok_rows
    row_positions = mp_index * tok_rows + row_ids % tok_rows
    limits = jnp.sum(
        jnp.where(
            seq_ids[:, None] == jnp.arange(lengths.shape[0], dtype=jnp.int32)[None, :],
            lengths[None, :],
            0,
        ),
        axis=1,
    )
    live_rows = (row_positions < limits)[:, None]
    difference = jnp.where(live_rows, predicted - targets.astype(jnp.float32), 0.0)
    live_count = jnp.sum(lengths).astype(jnp.float32)
    squared = lax.psum(jnp.sum(difference * difference), ("grp", "dp", "mp"))
    distill_loss = squared / (live_count * D_T)
    grad_pred = difference.astype(jnp.bfloat16)
    grad_proj = (
        lax.psum_scatter(
            lax.dot_general(
                normed_all, grad_pred, (((0,), (0,)), ((), ())), preferred_element_type=jnp.float32
            ).astype(jnp.bfloat16),
            "mp",
            scatter_dimension=0,
            tiled=True,
        ).astype(jnp.float32)
        / live_count
    )
    partial_grad = lax.psum_scatter(
        lax.dot_general(
            grad_pred, projection, (((1,), (1,)), ((), ())), preferred_element_type=jnp.float32
        ).astype(jnp.bfloat16),
        "dp",
        scatter_dimension=0,
        tiled=True,
    )
    width_half = norm_gain.shape[0] // 2
    gain_half = lax.dynamic_slice_in_dim(norm_gain, grp_index * width_half, width_half, 0)
    unit_half = lax.dynamic_slice_in_dim(unit_rows, grp_index * width_half, width_half, 1)
    grad_normed = lax.psum(partial_grad, "grp").astype(jnp.float32)
    inner_sum = jnp.sum(grad_normed * norm_gain * unit_rows, axis=-1, keepdims=True)
    grad_half = lax.dynamic_slice_in_dim(grad_normed, grp_index * width_half, width_half, 1)
    mean_term = inner_sum / D_S
    grad_hidden = inverse_rms * (grad_half * gain_half - unit_half * mean_term)
    grad_gain = lax.psum(jnp.sum(grad_half * unit_half, axis=0), ("dp", "mp")) / live_count
    return (own_target[None], distill_loss, grad_proj, grad_gain, grad_hidden[None])


def solution(mesh):
    in_specs = (
        P("dp", None, "mp"),
        P("dp", None, None),
        P("dp", None, None),
        P("mp", None),
        P("dp", "mp", None),
        P("dp", "mp", None),
        P(),
        P(None, ("grp", "dp")),
        P(),
    )
    out_specs = (P("dp", "mp", "grp"), P(), P("mp", ("grp", "dp")), P("grp"), P("dp", "mp", "grp"))
    return jax.shard_map(body, mesh=mesh, in_specs=in_specs, out_specs=out_specs, check_vma=False)
```

profile of v0, /device:TPU:0, one launch (start us, length us, event | category | flops | bytes accessed | tf_op | source)
XLA Modules:
  0.0 655.8 jit_solution(2401725420533888465)
XLA Ops:
  8.1 85.0 %conditional.2 = (bf16[2048,256]{1,0:T(8,128)(2,1)}) conditional(s32[]{:T(128)} %convert_element_type.76, () %tuple.25, (bf16[1,2048,256]{2,1,0:T(8,128)(2,1)}, s32[2048]{0:T(1024)S(1)}, bf16[1,2048,512]{2,1,0:T(8,128)(2,1)}, bf16[1,2048,512]{2,1,0:T(8,128)(2,1)}, s32[]{:T(128)}) %tuple.41), branch_computations={%region_0.1_spmd, %region_1.6_spmd.clone.clone} | conditional | flops 1087506432 | bytes 28867236 | solution.py:66
  8.1 4.1 copy.41
  16.5 76.7 %while.12 = (s32[]{:T(128)}, bf16[4,512,256]{2,1,0:T(8,128)(2,1)}, s32[4,512]{1,0:T(4,128)S(1)}, bf16[4,512,256]{2,1,0:T(8,128)(2,1)}, bf16[2048,128]{1,0:T(8,128)(2,1)}, /*index=5*/bf16[2048,128]{0,1:T(8,128)(2,1)}, s32[]{:T(128)}) while((s32[]{:T(128)}, bf16[4,512,256]{2,1,0:T(8,128)(2,1)}, s32[4,512]{1,0:T(4,128)S(1)}, ...), condition=%wide.region_5.5_spmd.clone, body=%wide.region_2.4_spmd.clone.sunk | while | flops 1087506432 | bytes 22559316 | solution.py:44
  20.0 8.1 %fusion.60 = (f32[2,512]{1,0:T(2,128)S(1)}, f32[2,512,2048]{2,1,0:T(8,128)}) fusion(pred[512,2048]{1,0:T(8,128)(4,1)} %iota_compare_fusion.3, bf16[512,2,128]{0,2,1:T(8,128)(2,1)} %bitcast.87, bf16[2048,128]{1,0:T(8,128)(2,1)} %get-tuple-element.239), kind=kOutput, calls=%fused_computation.62.clone.1 | convolution fusion | flops 545261568 | bytes 10227712 | tf_op jit(solution)/shard_map/cond/branch_1_fun/while/body/eval_jaxpr/sub | solution.py:36
  28.1 5.7 fusion.61
  39.2 8.1 %fusion.60 = (f32[2,512]{1,0:T(2,128)S(1)}, f32[2,512,2048]{2,1,0:T(8,128)}) fusion(pred[512,2048]{1,0:T(8,128)(4,1)} %iota_compare_fusion.3, bf16[512,2,128]{0,2,1:T(8,128)(2,1)} %bitcast.87, bf16[2048,128]{1,0:T(8,128)(2,1)} %get-tuple-element.239), kind=kOutput, calls=%fused_computation.62.clone.1 | convolution fusion | flops 545261568 | bytes 10227712 | tf_op jit(solution)/shard_map/cond/branch_1_fun/while/body/eval_jaxpr/sub | solution.py:36
  47.3 5.7 fusion.61
  58.3 8.1 %fusion.60 = (f32[2,512]{1,0:T(2,128)S(1)}, f32[2,512,2048]{2,1,0:T(8,128)}) fusion(pred[512,2048]{1,0:T(8,128)(4,1)} %iota_compare_fusion.3, bf16[512,2,128]{0,2,1:T(8,128)(2,1)} %bitcast.87, bf16[2048,128]{1,0:T(8,128)(2,1)} %get-tuple-element.239), kind=kOutput, calls=%fused_computation.62.clone.1 | convolution fusion | flops 545261568 | bytes 10227712 | tf_op jit(solution)/shard_map/cond/branch_1_fun/while/body/eval_jaxpr/sub | solution.py:36
  66.4 5.7 fusion.61
  77.5 8.1 %fusion.60 = (f32[2,512]{1,0:T(2,128)S(1)}, f32[2,512,2048]{2,1,0:T(8,128)}) fusion(pred[512,2048]{1,0:T(8,128)(4,1)} %iota_compare_fusion.3, bf16[512,2,128]{0,2,1:T(8,128)(2,1)} %bitcast.87, bf16[2048,128]{1,0:T(8,128)(2,1)} %get-tuple-element.239), kind=kOutput, calls=%fused_computation.62.clone.1 | convolution fusion | flops 545261568 | bytes 10227712 | tf_op jit(solution)/shard_map/cond/branch_1_fun/while/body/eval_jaxpr/sub | solution.py:36
  85.6 5.7 fusion.61
  93.1 11.6 %conditional.3 = (bf16[2048,5120]{1,0:T(8,128)(2,1)}) conditional(s32[]{:T(128)} %convert_element_type.76, () %tuple.24, (bf16[2048,256]{1,0:T(8,128)(2,1)}, bf16[256,5120]{1,0:T(8,128)(2,1)}) %tuple.27), branch_computations={%region_6.7_spmd, %region_7.8_spmd} | conditional | flops 5368709120 | bytes 24641544 | solution.py:72
  93.1 11.6 %fusion.41 = bf16[2048,5120]{1,0:T(8,128)(2,1)} fusion(bf16[2048,256]{1,0:T(8,128)(2,1)} %get-tuple-element.59, bf16[256,5120]{1,0:T(8,128)(2,1)} %get-tuple-element.81), kind=kOutput, calls=%fused_computation.63 | convolution fusion | flops 5368709120 | bytes 24641536 | tf_op jit(solution)/shard_map/cond/branch_1_fun/dot_general | solution.py:74
  108.4 167.5 %reduce-scatter.4.cloned.1.call-done = bf16[128,5120]{1,0:T(8,128)(2,1)} async-done(((bf16[2048,5120]{1,0:T(8,128)(2,1)}), bf16[128,5120]{1,0:T(8,128)(2,1)}) %reduce-scatter.4.cloned.1.call-update) | async-done | bytes 1310736 | tf_op jit(solution)/shard_map/reduce_scatter | solution.py:71
  280.6 13.4 %collective-permute-done = bf16[128,2560]{1,0:T(8,128)(2,1)S(1)} collective-permute-done((bf16[128,2560]{1,0:T(8,128)(2,1)S(1)}, bf16[128,2560]{1,0:T(8,128)(2,1)S(1)}, u32[]{:S(2)}, u32[]{:S(2)}) %collective-permute-start) | collective-permute-done | bytes 655392 | tf_op jit(solution)/shard_map/ppermute | solution.py:16
  295.8 4.3 all-to-all-start
  300.3 9.4 %all-to-all-done = bf16[128,4,640]{2,0,1:T(8,128)(2,1)} async-done(((bf16[128,4,640]{2,0,1:T(8,128)(2,1)}), bf16[128,4,640]{2,0,1:T(8,128)(2,1)}, u32[]{:S(2)}, u32[]{:S(2)}) %all-to-all-start) | async-done | bytes 655392 | tf_op jit(solution)/shard_map/all_to_all | solution.py:89
  311.9 5.0 multiply_reduce_fusion.1
  321.6 5.8 convolution_convert_fusion
  327.5 25.8 %reduce-scatter.8.cloned.1.call-done = bf16[128,2560]{1,0:T(8,128)(2,1)} async-done(((bf16[512,2560]{1,0:T(8,128)(2,1)}), bf16[128,2560]{1,0:T(8,128)(2,1)}) %reduce-scatter.8.cloned.1.call-update) | async-done | bytes 655376 | tf_op jit(solution)/shard_map/reduce_scatter | solution.py:119
  354.6 65.6 %psum.21 = f32[]{:T(128)} all-reduce(f32[]{:T(128)} %get-tuple-element.176), channel_id=1, replica_groups=mesh['grp'=2,'dp'=4,'mp'=16] {'grp','dp','mp'}, use_global_device_ids=true, to_apply=%region_12.13 | all-reduce | flops 1 | bytes 8 | tf_op jit(solution)/shard_map/psum | solution.py:105
  420.9 12.4 %reduce-scatter.6.cloned.1.call-done = bf16[160,640]{1,0:T(8,128)(2,1)} async-done(((bf16[2560,640]{1,0:T(8,128)(2,1)}), bf16[160,640]{1,0:T(8,128)(2,1)}) %reduce-scatter.6.cloned.1.call-update) | async-done | bytes 204816 | tf_op jit(solution)/shard_map/reduce_scatter | solution.py:109
  435.0 37.5 %all-reduce.2.cloned.1.call-done = bf16[128,2560]{1,0:T(8,128)(2,1)} async-done(((bf16[128,2560]{1,0:T(8,128)(2,1)}), bf16[128,2560]{1,0:T(8,128)(2,1)}) %all-reduce.2.cloned.1.call-update) | async-done | bytes 655376 | tf_op jit(solution)/shard_map/psum | solution.py:130
  475.4 171.0 %psum.23 = f32[1280]{0:T(1024)S(1)} all-reduce(f32[1280]{0:T(1024)S(1)} %get-tuple-element.173), channel_id=1, replica_groups=mesh['grp'=2,'dp'=4,'mp'=16] {'dp','mp'}, use_global_device_ids=true, to_apply=%region_18.19 | all-reduce | flops 1280 | bytes 10240 | tf_op jit(solution)/shard_map/psum | solution.py:135
  (73 shorter events, 48.9 us)
Async XLA Ops:
  8.0 303.9 %copy-start = (bf16[2560,640]{1,0:T(8,128)(2,1)S(1)}, bf16[2560,640]{1,0:T(8,128)(2,1)}, u32[]{:S(2)}) copy-start(bf16[2560,640]{1,0:T(8,128)(2,1)} %param.22) | copy-start | bytes 9830404
  8.0 267.9 %reduce-scatter.4.cloned.1.call-start = ((), (), s32[]{:S(2)}) async-start(), calls=%async_computation.4 | async-start | bytes 22282240 | tf_op jit(solution)/shard_map/reduce_scatter | solution.py:71
  104.8 1.4 copy-start.3
  104.8 207.1 %all-gather.2.cloned.1.call-start = ((), (), s32[]{:S(2)}) async-start(), calls=%async_computation.5 | async-start | bytes 3276800 | tf_op jit(solution)/shard_map/all_gather | solution.py:88
  278.0 22.2 %copy-start.4 = (s32[4]{0:T(128)S(1)}, s32[4]{0:T(128)}, u32[]{:S(2)}) copy-start(s32[4]{0:T(128)} %param.23) | copy-start | bytes 52
  278.0 16.0 %collective-permute-start = (bf16[128,2560]{1,0:T(8,128)(2,1)S(1)}, bf16[128,2560]{1,0:T(8,128)(2,1)S(1)}, u32[]{:S(2)}, u32[]{:S(2)}) collective-permute-start(bf16[128,2560]{1,0:T(8,128)(2,1)S(1)} %slice.9), channel_id=1, source_target_pairs={{0,64},{1,65},{2,66},{3,67},{4,68},{5,69},{6,70},{7,71},{8,72},{9,... | collective-permute-start | bytes 1966088 | tf_op jit(solution)/shard_map/ppermute | solution.py:16
  294.1 0.8 copy-start.1
  295.8 13.9 %all-to-all-start = ((bf16[128,4,640]{2,0,1:T(8,128)(2,1)}), bf16[128,4,640]{2,0,1:T(8,128)(2,1)}, u32[]{:S(2)}, u32[]{:S(2)}) async-start(bf16[128,4,640]{2,0,1:T(8,128)(2,1)} %bitcast.92), calls=%async_computation.1 | async-start | bytes 1310720 | tf_op jit(solution)/shard_map/all_to_all | solution.py:89
  300.1 53.2 %reduce-scatter.8.cloned.1.call-start = ((), (), s32[]{:S(2)}) async-start(), calls=%async_computation.7 | async-start | bytes 3276800 | tf_op jit(solution)/shard_map/reduce_scatter | solution.py:119
  316.9 0.8 copy-start.5
  321.5 111.8 %reduce-scatter.6.cloned.1.call-start = ((), (), s32[]{:S(2)}) async-start(), calls=%async_computation.6 | async-start | bytes 3481600 | tf_op jit(solution)/shard_map/reduce_scatter | solution.py:109
  327.4 145.1 %all-reduce.2.cloned.1.call-start = ((), (), s32[]{:S(2)}) async-start(), calls=%async_computation.8 | async-start | bytes 1310720 | tf_op jit(solution)/shard_map/psum | solution.py:130
  472.5 1.8 copy-start.2
Sparse Core Ops, SparseCore 0:
  104.9 170.9 reduce-scatter.3
Sparse Core Ops, SparseCore 1:
  108.5 37.3 all-gather.1
  321.6 31.6 reduce-scatter.7
  357.7 75.6 reduce-scatter.5
  435.8 36.7 all-reduce.1
where the time goes:
time: 657 us; the launch traced here: 656 us
  waiting for transfers between devices  266 us (40%)
  blocking collectives  237 us (36%)
  matrix products  81.4 us (12%)
  local copies, waits for them, and re-layouts  25.6 us (4%)
  other arithmetic  20.7 us (3%)
  between operations  18.3 us (3%)
  starting transfers between devices  7.15 us (1%)
    psum x1, blocking collectives, body(): lax.psum(jnp.sum(grad_half * unit_half, axis=0), ('dp', 'mp')) / live_count  171 us
    reduce_scatter x1, waiting for transfers between devices, body(): lax.psum_scatter(lax.cond(grp_index == 0, lambda: jnp.dot(context, out_we...  167 us
    psum x1, blocking collectives, body(): squared = lax.psum(jnp.sum(difference * difference), ('grp', 'dp', 'mp'))  65.6 us
    psum x1, waiting for transfers between devices, body(): grad_normed = lax.psum(partial_grad, 'grp').astype(jnp.float32)  37.5 us
    sub x4, matrix products, one_block(): exponent = jnp.exp(scores - row_max)  32.3 us
    reduce_scatter x1, waiting for transfers between devices, body(): lax.psum_scatter(lax.dot_general(grad_pred, projection, (((1,), (1,)), ((...  25.8 us
    dot_general x4, matrix products, one_block(): jnp.einsum('hbk,kd->bhd', weights, value_rows, preferred_element_type=jnp...  22.9 us
    ppermute x1, waiting for transfers between devices, passed_along(): return lax.ppermute(array, axis, pairs)  13.4 us
  transfers between devices with their start and end apart: 7, of which 6 were waited for; matrix products, arithmetic and copies ran while one was open for 3% of the time, Pallas kernels for 0%

commit v1 on v0

v1 whole, which is shorter than its diff:
```python
import functools
import math

import jax
import jax.numpy as jnp
from jax import lax
from jax.experimental import pallas as pl
from jax.experimental.pallas import tpu as pltpu
from jax.sharding import Mesh
from jax.sharding import PartitionSpec as P

D_T = 5120
D_S = 2560
HD = 128
HQ = 32
KVH = 4

BF = jnp.bfloat16
F32 = jnp.float32
NX = 4
NZ = 4
MP = ("x", "zh", "core")


def ring(n, k):
    return [(i, (i + k) % n) for i in range(n)]


WRAP = [(g * 2 + z, (1 - g) * 2 + (1 - z)) for g in range(2) for z in range(2)]
WRAP_CORE = [
    (g * 4 + z * 2 + c, (1 - g) * 4 + (1 - z) * 2 + (1 - c))
    for g in range(2)
    for z in range(2)
    for c in range(2)
]


def attend_kernel(scalars, q0_ref, q1_ref, k_ref, v_ref, out_ref, vext):
    first = scalars[1] * 128
    vext[:, :HD] = v_ref[...]
    vext[:, HD:] = jnp.ones((v_ref.shape[0], HD), BF)
    scale = HD ** (-0.5) * math.log2(math.e)
    rows = lax.broadcasted_iota(jnp.int32, (256, 512), 0) % 128
    cols = lax.broadcasted_iota(jnp.int32, (256, 512), 1)
    allowed = cols <= rows + first
    for part in range(NX):
        length = 512 * (part + 1)
        for pair, q_ref in enumerate((q0_ref, q1_ref)):
            q = jnp.concatenate([q_ref[part, :, :HD], q_ref[part, :, HD:]], axis=0)
            scores = lax.dot_general(
                q, k_ref[:length, :], (((1,), (1,)), ((), ())), preferred_element_type=F32
            )
            last = jnp.where(allowed, scores[:, length - 512 :], -1e30)
            if part:
                scores = jnp.concatenate([scores[:, : length - 512], last], axis=1)
            else:
                scores = last
            top = jnp.max(scores, axis=-1, keepdims=True)
            probs = jnp.exp2((scores - top) * scale).astype(BF)
            mixed = jnp.dot(probs, vext[:length, :], preferred_element_type=F32)
            mixed = (mixed[:, :HD] / mixed[:, HD:]).astype(BF)
            for head in range(2):
                at = (pair * 2 + head) * HD
                out_ref[part * 128 : part * 128 + 128, at : at + HD] = mixed[
                    head * 128 : head * 128 + 128
                ]


def attend(scalars, q0, q1, keys, values):
    seq_len = keys.shape[0]
    return pl.pallas_call(
        attend_kernel,
        out_shape=jax.ShapeDtypeStruct((NX * 128, 4 * HD), BF),
        grid_spec=pltpu.PrefetchScalarGridSpec(
            num_scalar_prefetch=1,
            grid=(1,),
            in_specs=[
                pl.BlockSpec((NX, 128, 256), lambda i, s: (0, 0, 0)),
                pl.BlockSpec((NX, 128, 256), lambda i, s: (0, 0, 0)),
                pl.BlockSpec((seq_len, HD), lambda i, s: (0, s[0])),
                pl.BlockSpec((seq_len, HD), lambda i, s: (0, s[0])),
            ],
            out_specs=pl.BlockSpec((NX * 128, 4 * HD), lambda i, s: (0, 0)),
            scratch_shapes=[pltpu.VMEM((seq_len, 2 * HD), BF)],
        ),
        compiler_params=pltpu.CompilerParams(vmem_limit_bytes=40 * 1024 * 1024),
        cost_estimate=pl.CostEstimate(
            flops=4 * 512 * 4 * 1280 * HD * 2, bytes_accessed=2 * 1024 * 1024, transcendentals=2621440
        ),
        name="attend",
    )(scalars, q0, q1, keys, values)


def body(
    queries, keys, values, out_weight, residual, student_hidden, norm_gain, projection, lengths
):
    g, d = lax.axis_index("grp"), lax.axis_index("dp")
    x, zh, c = lax.axis_index("x"), lax.axis_index("zh"), lax.axis_index("core")
    zc = zh * 2 + c
    m = x * 4 + zc
    half = D_T // 2
    blk = D_T // 8

    q4 = queries[0].reshape(NX, 512, 256)

    def q_for(block):
        return lax.dynamic_slice_in_dim(q4, block * 128, 128, 1)

    q_own = q_for(zc)
    q_core = lax.ppermute(q_for(zh * 2 + 1 - c), "core", ring(2, 1))
    q_z0 = lax.ppermute(q_for((1 - zh) * 2 + c), ("grp", "zh"), WRAP)
    q_z1 = lax.ppermute(q_for((1 - zh) * 2 + 1 - c), ("grp", "zh", "core"), WRAP_CORE)

    w_own = lax.dynamic_slice_in_dim(out_weight, g * half, half, 1)
    w_sent = lax.dynamic_slice_in_dim(out_weight, (1 - g) * half, half, 1)
    w_core = lax.ppermute(w_own, "core", ring(2, 1))
    w_z0 = lax.ppermute(w_sent, ("grp", "zh"), WRAP)
    w_z1 = lax.ppermute(w_z0, "core", ring(2, 1))

    hidden = student_hidden[0].astype(F32)
    inverse_rms = lax.rsqrt(jnp.mean(hidden * hidden, axis=-1, keepdims=True) + 1e-06)
    unit_rows = hidden * inverse_rms
    scaled_rows = unit_rows * norm_gain
    normed = scaled_rows.astype(BF)
    normed_all = lax.all_gather(normed, "dp", axis=0, tiled=True)
    predicted = jnp.dot(normed_all, projection, preferred_element_type=F32)

    scalars = jnp.stack([x, zc]).astype(jnp.int32)
    ctx_a = attend(scalars, q_own, q_core, keys[0], values[0])
    ctx_b = attend(scalars, q_z0, q_z1, keys[0], values[0])
    weight = jnp.concatenate([w_own, w_core, w_z0, w_z1], axis=0)
    ctx = jnp.concatenate([ctx_a, ctx_b], axis=1)

    live_count = jnp.sum(lengths).astype(F32)
    positions = m * 128 + jnp.arange(128, dtype=jnp.int32)
    squared = jnp.zeros((), F32)
    gain_part = jnp.zeros((D_S,), F32)
    summed = jnp.zeros((128, D_S), F32)
    target = jnp.zeros((128, half), BF)
    grad_pred = jnp.zeros((512, blk), BF)
    for k in (2, 1, 3, 0):
        at = ((d + k) % 4) * blk
        part = jnp.dot(
            ctx, lax.dynamic_slice_in_dim(weight, at, blk, 1), preferred_element_type=F32
        ).astype(BF).reshape(NX, 128, blk)
        rows = lax.dynamic_index_in_dim(part, x, 0, keepdims=False).astype(F32)
        for j in (2, 1, 3):
            piece = lax.dynamic_index_in_dim(part, (x + j) % NX, 0, keepdims=False)
            rows = rows + lax.ppermute(piece, "x", ring(NX, j)).astype(F32)
        res = lax.dynamic_slice_in_dim(residual[0], g * half + at, blk, 1)
        done = (res.astype(F32) + rows).astype(BF)
        target = lax.dynamic_update_slice_in_dim(target, done, at, 1)
        got = done if k == 0 else lax.ppermute(done, "dp", ring(4, k))
        seq = (d + 4 - k) % 4
        live = (positions < lax.dynamic_index_in_dim(lengths, seq, 0, keepdims=False))[:, None]
        pred = lax.dynamic_slice_in_dim(predicted, seq * 128, 128, 0)
        diff = jnp.where(live, pred - got.astype(F32), 0.0)
        squared = squared + jnp.sum(diff * diff)
        gp = diff.astype(BF)
        grad_pred = lax.dynamic_update_slice_in_dim(grad_pred, gp, seq * 128, 0)
        back = lax.dot_general(
            gp, projection, (((1,), (1,)), ((), ())), preferred_element_type=F32
        )
        normed_seq = lax.dynamic_slice_in_dim(normed_all, seq * 128, 128, 0)
        gain_part = gain_part + jnp.sum(back * normed_seq.astype(F32), axis=0)
        if k == 0:
            summed = summed + back
        else:
            summed = summed + lax.ppermute(back.astype(BF), "dp", ring(4, 4 - k)).astype(F32)

    small = jnp.concatenate([gain_part / norm_gain, jnp.full((128,), squared)])
    small = small.reshape(-1, 128)
    small = small + lax.ppermute(small, "core", ring(2, 1))
    for axis, n in (("x", 4), ("dp", 4), (("grp", "zh"), 4)):
        small = sum([lax.ppermute(small, axis, ring(n, j)) for j in range(1, n)], small)
    small = small.reshape(-1)
    distill_loss = small[D_S] / (live_count * D_T)
    grad_gain = lax.dynamic_slice_in_dim(small, g * (D_S // 2), D_S // 2, 0) / live_count

    gproj = lax.dot_general(
        normed_all, grad_pred, (((0,), (0,)), ((), ())), preferred_element_type=F32
    ).astype(BF).reshape(NX, 2, 2, D_S // 16, blk)
    take = functools.partial(lax.dynamic_index_in_dim, keepdims=False)
    gproj = (
        take(gproj, c, 2).astype(F32)
        + lax.ppermute(take(gproj, 1 - c, 2), "core", ring(2, 1)).astype(F32)
    ).astype(BF)
    acc = take(gproj, x, 0).astype(F32)
    for j in (2, 1, 3):
        acc = acc + lax.ppermute(take(gproj, (x + j) % NX, 0), "x", ring(NX, j)).astype(F32)
    acc16 = acc.astype(BF)
    grad_proj = (
        take(acc, zh, 0) + lax.ppermute(take(acc16, 1 - zh, 0), "zh", ring(2, 1)).astype(F32)
    ) / live_count

    width = D_S // 2
    inner = jnp.sum(summed * scaled_rows, axis=-1)
    inner = inner + lax.ppermute(inner, "grp", ring(2, 1))
    sent = lax.dynamic_slice_in_dim(summed, (1 - g) * width, width, 1).astype(BF)
    kept = lax.dynamic_slice_in_dim(summed, g * width, width, 1)
    grad_half = kept + lax.ppermute(sent, "grp", ring(2, 1)).astype(F32)
    gain_half = lax.dynamic_slice_in_dim(norm_gain, g * width, width, 0)
    unit_half = lax.dynamic_slice_in_dim(unit_rows, g * width, width, 1)
    mean_term = (inner / D_S)[:, None]
    grad_hidden = inverse_rms * (grad_half * gain_half - unit_half * mean_term)
    return (target[None], distill_loss, grad_proj, grad_gain, grad_hidden[None])


def solution(mesh):
    fine = Mesh(mesh.devices.reshape(2, 4, 4, 2, 2), ("grp", "dp", "x", "zh", "core"))
    in_specs = (
        P("dp", None, MP),
        P("dp", None, None),
        P("dp", None, None),
        P(MP, None),
        P("dp", MP, None),
        P("dp", MP, None),
        P(),
        P(None, ("grp", "dp")),
        P(),
    )
    out_specs = (P("dp", MP, "grp"), P(), P(MP, ("grp", "dp")), P("grp"), P("dp", MP, "grp"))
    return jax.shard_map(body, mesh=fine, in_specs=in_specs, out_specs=out_specs, check_vma=False)
```

time: 657 us -> 231 us (0.35)
  blocking collectives: 237 us -> 0 us
  waiting for transfers between devices: 266 us -> 71.4 us
  matrix products: 81.4 us -> 24.4 us
  starting transfers between devices: 7.15 us -> 54 us
  Pallas kernels: 0 us -> 11.9 us
    psum x2 -> x0, blocking collectives: 237 us -> none  [the longest x1 171 us: body(): lax.psum(jnp.sum(grad_half * unit_half, axis=0), ('dp', 'mp')) / live_count]
    reduce_scatter x3 -> x0, waiting for transfers between devices: 206 us -> none  [the longest x1 167 us: body(): lax.psum_scatter(lax.cond(grp_index == 0, lambda: jnp.dot(context, out_we...]
    ppermute x1 -> x41, waiting for transfers between devices: 13.4 us -> 71.4 us  [the longest x1 27.1 us: body(): w_z0 = lax.ppermute(w_sent, ('grp', 'zh'), WRAP)]
    ppermute x1 -> x41, starting transfers between devices: 2.59 us -> 54 us  [the longest x12 15.9 us: body(): rows = rows + lax.ppermute(piece, 'x', ring(NX, j)).astype(F32)]
    psum x1 -> x0, waiting for transfers between devices: 37.5 us -> none  [body(): grad_normed = lax.psum(partial_grad, 'grp').astype(jnp.float32)]
    sub x4 -> x0, matrix products: 32.3 us -> none  [one_block(): exponent = jnp.exp(scores - row_max)]
    dot_general x7 -> x9, matrix products: 43.3 us -> 22.1 us  [the longest x4 14.2 us: body(): lax.dot_general(gp, projection, (((1,), (1,)), ((), ())), preferred_eleme...]
    pallas_call x0 -> x2, Pallas kernels: none -> 11.9 us  [attend(): pl.pallas_call(attend_kernel, out_shape=jax.ShapeDtypeStruct((NX * 128, 4...]
  transfers between devices with their start and end apart: 7 -> 42, of which waited for: 6 -> 16; matrix products, arithmetic and copies ran while one was open for 3% -> 27% of each run, Pallas kernels for 0% -> 5%
where the time goes in v1:
time: 231 us; the launch traced here: 228 us
  waiting for transfers between devices  71.4 us (31%)
  starting transfers between devices  54 us (23%)
  other arithmetic  26.7 us (12%)
  matrix products  24.4 us (11%)
  between operations  20 us (9%)
  local copies, waits for them, and re-layouts  19.8 us (9%)
  Pallas kernels  11.9 us (5%)
    ppermute x1, waiting for transfers between devices, body(): w_z0 = lax.ppermute(w_sent, ('grp', 'zh'), WRAP)  27.1 us
    ppermute x12, starting transfers between devices, body(): rows = rows + lax.ppermute(piece, 'x', ring(NX, j)).astype(F32)  15.9 us
    dot_general x4, matrix products, body(): lax.dot_general(gp, projection, (((1,), (1,)), ((), ())), preferred_eleme...  14.2 us
    ppermute x3, waiting for transfers between devices, body(): lax.ppermute(take(gproj, (x + j) % NX, 0), 'x', ring(NX, j)).astype(F32)  13.2 us
    ppermute x9, starting transfers between devices, body(): lax.ppermute(small, axis, ring(n, j))  12.2 us
    pallas_call x2, Pallas kernels, attend(): pl.pallas_call(attend_kernel, out_shape=jax.ShapeDtypeStruct((NX * 128, 4...  11.9 us
    ppermute x3, waiting for transfers between devices, body(): lax.ppermute(back.astype(BF), 'dp', ring(4, 4 - k)).astype(F32)  7.6 us
    ppermute x9, waiting for transfers between devices, body(): lax.ppermute(small, axis, ring(n, j))  7.28 us
  transfers between devices with their start and end apart: 42, of which 16 were waited for; matrix products, arithmetic and copies ran while one was open for 27% of the time, Pallas kernels for 5%

profile of v1, /device:TPU:0, one launch (start us, length us, event | category | flops | bytes accessed | tf_op | source)
XLA Modules:
  0.0 228.3 jit_solution(8810606637312745744)
XLA Ops:
  7.3 3.6 %constant_dynamic-slice_fusion.1 = (bf16[256,2560]{1,0:T(8,128)(2,1)}, bf16[256,2560]{1,0:T(8,128)(2,1)}) fusion(bf16[256,5120]{1,0:T(8,128)(2,1)} %param.12, s32[]{:T(128)S(6)} %select_n.219, s32[]{:T(128)S(6)} %select_n.220), kind=kLoop, calls=%fused_computation.93 | loop fusion | bytes 5242888 | tf_op jit(solution)/shard_map/dynamic_slice | solution.py:114
  10.8 4.1 %collective-permute-start.4 = (bf16[256,2560]{1,0:T(8,128)(2,1)}, bf16[256,2560]{1,0:T(8,128)(2,1)}, u32[]{:S(2)}, u32[]{:S(2)}) collective-permute-start(bf16[256,2560]{1,0:T(8,128)(2,1)} %get-tuple-element.31), channel_id=1, source_target_pairs={{0,66},{2,64},{64,2},{66,0},{1,67},{3,65},{65,3},{67,1},{4,70},{6,... | collective-permute-start | bytes 3932168 | tf_op jit(solution)/shard_map/ppermute | solution.py:117
  17.0 27.1 %collective-permute-done.4 = bf16[256,2560]{1,0:T(8,128)(2,1)} collective-permute-done((bf16[256,2560]{1,0:T(8,128)(2,1)}, bf16[256,2560]{1,0:T(8,128)(2,1)}, u32[]{:S(2)}, u32[]{:S(2)}) %collective-permute-start.4) | collective-permute-done | bytes 1310752 | tf_op jit(solution)/shard_map/ppermute | solution.py:117
  46.1 3.0 %collective-permute-start.1 = (bf16[4,128,256]{2,1,0:T(8,128)(2,1)}, bf16[4,128,256]{2,1,0:T(8,128)(2,1)}, u32[]{:S(2)}, u32[]{:S(2)}) collective-permute-start(bf16[4,128,256]{2,1,0:T(8,128)(2,1)} %get-tuple-element.41), channel_id=1, source_target_pairs={{0,66},{2,64},{64,2},{66,0},{1,67},{3,65},{65,3},{67,1},{4,70},{6,... | collective-permute-start | bytes 786440 | tf_op jit(solution)/shard_map/ppermute | solution.py:111
  54.1 2.7 %collective-permute-done.1.q0_ref = bf16[4,128,256]{2,1,0:T(8,128)(2,1)} collective-permute-done((bf16[4,128,256]{2,1,0:T(8,128)(2,1)}, bf16[4,128,256]{2,1,0:T(8,128)(2,1)}, u32[]{:S(2)}, u32[]{:S(2)}) %collective-permute-start.1) | collective-permute-done | bytes 262176 | tf_op jit(solution)/shard_map/ppermute | solution.py:111
  56.8 4.9 %collective-permute-done.2.q1_ref = bf16[4,128,256]{2,1,0:T(8,128)(2,1)} collective-permute-done((bf16[4,128,256]{2,1,0:T(8,128)(2,1)}, bf16[4,128,256]{2,1,0:T(8,128)(2,1)}, u32[]{:S(2)}, u32[]{:S(2)}) %collective-permute-start.2) | collective-permute-done | bytes 262176 | tf_op jit(solution)/shard_map/ppermute | solution.py:112
  64.8 6.1 %attend.3 = bf16[512,512]{1,0:T(8,128)(2,1)S(1)} custom-call(s32[2]{0:T(128)S(1)} %pad_add_fusion.scalars, bf16[4,128,256]{2,1,0:T(8,128)(2,1)} %collective-permute-done.1.q0_ref, bf16[4,128,256]{2,1,0:T(8,128)(2,1)} %collective-permute-done.2.q1_ref, bf16[2048,512]{1,0:T(8,128)(2,1)S(1)} %bitcast.127, bf16[2048,512]{1,0:T(8,128)(2,1)S(1)} %bitcast.129), custom_call_target="tpu_custom_call" | custom-call | flops 2684354560 | bytes 2097152 | tf_op jit(solution)/shard_map/attend/pallas_call | solution.py:71
  71.0 5.8 %attend.2 = bf16[512,512]{1,0:T(8,128)(2,1)S(1)} custom-call(s32[2]{0:T(128)S(1)} %pad_add_fusion.scalars, bf16[4,128,256]{2,1,0:T(8,128)(2,1)S(1)} %get-tuple-element.42.q0_ref, bf16[4,128,256]{2,1,0:T(8,128)(2,1)} %collective-permute-done.q1_ref, bf16[2048,512]{1,0:T(8,128)(2,1)S(1)} %bitcast.128, bf16[2048,512]{1,0:T(8,128)(2,1)S(1)} %bitcast.130), custom_call_target="tpu_custom_call" | custom-call | flops 2684354560 | bytes 2097152 | tf_op jit(solution)/shard_map/attend/pallas_call | solution.py:71
  76.9 3.1 %pad_maximum_fusion = bf16[1024,2560]{1,0:T(8,128)(2,1)S(1)} fusion(bf16[256,2560]{1,0:T(8,128)(2,1)} %collective-permute-done.5, bf16[256,2560]{1,0:T(8,128)(2,1)} %collective-permute-done.4, bf16[256,2560]{1,0:T(8,128)(2,1)} %collective-permute-done.3, bf16[256,2560]{1,0:T(8,128)(2,1)S(1)} %copy-done.7), kind=kLoop, calls=%fused_computation | loop fusion | flops 20971520 | bytes 10485760 | tf_op jit(solution)/shard_map/concatenate | solution.py:131
  81.1 2.8 %collective-permute-start.8 = (bf16[128,640]{1,0:T(8,128)(2,1)S(1)}, bf16[128,640]{1,0:T(8,128)(2,1)S(1)}, u32[]{:S(2)}, u32[]{:S(2)}) collective-permute-start(bf16[128,640]{1,0:T(8,128)(2,1)S(1)} %get-tuple-element.54), channel_id=1, source_target_pairs={{0,12},{4,0},{8,4},{12,8},{1,13},{5,1},{9,5},{13,9},{2,14},{6,2},{... | collective-permute-start | bytes 491528 | tf_op jit(solution)/shard_map/ppermute | solution.py:149
  109.4 3.2 %collective-permute-start.18 = (bf16[128,640]{1,0:T(8,128)(2,1)}, bf16[128,640]{1,0:T(8,128)(2,1)S(1)}, u32[]{:S(2)}, u32[]{:S(2)}) collective-permute-start(bf16[128,640]{1,0:T(8,128)(2,1)} %get-tuple-element.29), channel_id=1, source_target_pairs={{0,32},{16,48},{32,0},{48,16},{1,33},{17,49},{33,1},{49,17},{2,34}... | collective-permute-start | bytes 491528 | tf_op jit(solution)/shard_map/ppermute | solution.py:153
  115.1 4.0 %fusion.50 = f32[512,640]{1,0:T(8,128)S(1)} fusion(bf16[512,2560]{1,0:T(8,128)(2,1)} %all-gather.2.cloned.1.call-done, bf16[2560,640]{1,0:T(8,128)(2,1)S(1)} %copy-done), kind=kOutput, calls=%fused_computation.116 | convolution fusion | flops 1677721600 | bytes 7208960 | tf_op jit(solution)/shard_map/dot_general | solution.py:126
  119.1 2.6 %collective-permute-start.20 = (bf16[128,640]{1,0:T(8,128)(2,1)S(1)}, bf16[128,640]{1,0:T(8,128)(2,1)S(1)}, u32[]{:S(2)}, u32[]{:S(2)}) collective-permute-start(bf16[128,640]{1,0:T(8,128)(2,1)S(1)} %copy-done.16), channel_id=1, source_target_pairs={{0,48},{16,0},{32,16},{48,32},{1,49},{17,1},{33,17},{49,33},{2,50}... | collective-permute-start | bytes 491528 | tf_op jit(solution)/shard_map/ppermute | solution.py:153
  127.1 2.5 %fusion.48 = (bf16[128,2560]{1,0:T(8,128)(2,1)}, f32[128,2560]{1,0:T(8,128)}) fusion(bf16[128,640]{1,0:T(8,128)(2,1)S(1)} %get-tuple-element.21, bf16[2560,640]{1,0:T(8,128)(2,1)S(1)} %copy-done), kind=kOutput, calls=%fused_computation.114 | convolution fusion | flops 419758080 | bytes 5406720 | tf_op jit(solution)/shard_map/dot_general | solution.py:161
  129.7 3.7 %collective-permute-start.37 = (bf16[128,2560]{1,0:T(8,128)(2,1)}, bf16[128,2560]{1,0:T(8,128)(2,1)}, u32[]{:S(2)}, u32[]{:S(2)}) collective-permute-start(bf16[128,2560]{1,0:T(8,128)(2,1)} %get-tuple-element.62), channel_id=1, source_target_pairs={{0,48},{16,0},{32,16},{48,32},{1,49},{17,1},{33,17},{49,33},{2,50}... | collective-permute-start | bytes 1966088 | tf_op jit(solution)/shard_map/ppermute | solution.py:169
  133.4 2.5 %fusion.49 = (bf16[128,2560]{1,0:T(8,128)(2,1)}, f32[128,2560]{1,0:T(8,128)}) fusion(bf16[128,640]{1,0:T(8,128)(2,1)S(1)} %get-tuple-element.23, bf16[2560,640]{1,0:T(8,128)(2,1)S(1)} %copy-done), kind=kOutput, calls=%fused_computation.115 | convolution fusion | flops 419758080 | bytes 5406720 | tf_op jit(solution)/shard_map/dot_general | solution.py:161
  148.7 7.6 %collective-permute-done.37 = bf16[128,2560]{1,0:T(8,128)(2,1)} collective-permute-done((bf16[128,2560]{1,0:T(8,128)(2,1)}, bf16[128,2560]{1,0:T(8,128)(2,1)}, u32[]{:S(2)}, u32[]{:S(2)}) %collective-permute-start.37) | collective-permute-done | bytes 655392 | tf_op jit(solution)/shard_map/ppermute | solution.py:169
  156.3 6.7 %multiply_reduce_fusion = (f32[128]{0:T(128)S(1)}, f32[128,2560]{1,0:T(8,128)}, f32[2560]{0:T(1024)S(1)}, f32[2560]{0:T(1024)S(1)}, f32[2560]{0:T(1024)S(1)}, /*index=5*/f32[2560]{0:T(1024)S(1)}, f32[128,2560]{1,0:T(8,128)}) fusion(f32[2560]{0:T(1024)S(1)} %copy-done.15, f32[128]{0:T(128)S(1)} %copy-done.20, bf16[1,128,2560]{2,1,0:T(8,128)(2,1)} %param.14, ...), kind=kOutput, calls=%fused_computation.12 | convolution fusion | flops 426956672 | bytes 15289360 | tf_op jit(solution)/shard_map/dot_general | solution.py:161
  168.4 3.0 %collective-permute-done.23 = f32[21,128]{1,0:T(8,128)S(1)} collective-permute-done((f32[21,128]{1,0:T(8,128)S(1)}, f32[21,128]{1,0:T(8,128)S(1)}, u32[]{:S(2)}, u32[]{:S(2)}) %collective-permute-start.23) | collective-permute-done | bytes 10784 | tf_op jit(solution)/shard_map/ppermute | solution.py:175
  172.0 3.7 %collective-permute-start.27 = (f32[21,128]{1,0:T(8,128)S(1)}, f32[21,128]{1,0:T(8,128)S(1)}, u32[]{:S(2)}, u32[]{:S(2)}) collective-permute-start(f32[21,128]{1,0:T(8,128)S(1)} %add_add_fusion.2), channel_id=1, source_target_pairs={{0,48},{16,0},{32,16},{48,32},{1,49},{17,1},{33,17},{49,33},{2,50}... | collective-permute-start | bytes 32264 | tf_op jit(solution)/shard_map/ppermute | solution.py:175
  182.0 3.0 %collective-permute-start.30 = (f32[21,128]{1,0:T(8,128)S(1)}, f32[21,128]{1,0:T(8,128)S(1)}, u32[]{:S(2)}, u32[]{:S(2)}) collective-permute-start(f32[21,128]{1,0:T(8,128)S(1)} %add_add_fusion.1), channel_id=1, source_target_pairs={{0,66},{2,0},{64,2},{66,64},{1,67},{3,1},{65,3},{67,65},{4,70},{6,... | collective-permute-start | bytes 32264 | tf_op jit(solution)/shard_map/ppermute | solution.py:175
  196.9 6.8 %collective-permute-done.34 = bf16[2,160,640]{2,1,0:T(8,128)(2,1)} collective-permute-done((bf16[2,160,640]{2,1,0:T(8,128)(2,1)}, bf16[2,160,640]{2,1,0:T(8,128)(2,1)}, u32[]{:S(2)}, u32[]{:S(2)}) %collective-permute-start.34) | collective-permute-done | bytes 409632 | tf_op jit(solution)/shard_map/ppermute | solution.py:190
  203.8 6.4 %collective-permute-done.33 = bf16[2,160,640]{2,1,0:T(8,128)(2,1)} collective-permute-done((bf16[2,160,640]{2,1,0:T(8,128)(2,1)}, bf16[2,160,640]{2,1,0:T(8,128)(2,1)}, u32[]{:S(2)}, u32[]{:S(2)}) %collective-permute-start.33) | collective-permute-done | bytes 409632 | tf_op jit(solution)/shard_map/ppermute | solution.py:190
  216.1 3.0 %collective-permute-done.35 = bf16[160,640]{1,0:T(8,128)(2,1)S(1)} collective-permute-done((bf16[160,640]{1,0:T(8,128)(2,1)S(1)}, bf16[160,640]{1,0:T(8,128)(2,1)S(1)}, u32[]{:S(2)}, u32[]{:S(2)}) %collective-permute-start.35) | collective-permute-done | bytes 204832 | tf_op jit(solution)/shard_map/ppermute | solution.py:193
  (167 shorter events, 86.4 us)
Async XLA Ops:
  7.2 107.9 %all-gather.2.cloned.1.call-start = ((), (), s32[]{:S(2)}) async-start(), calls=%async_computation | async-start | bytes 3276800 | tf_op jit(solution)/shard_map/all_gather | solution.py:125
  10.8 33.2 %collective-permute-start.4 = (bf16[256,2560]{1,0:T(8,128)(2,1)}, bf16[256,2560]{1,0:T(8,128)(2,1)}, u32[]{:S(2)}, u32[]{:S(2)}) collective-permute-start(bf16[256,2560]{1,0:T(8,128)(2,1)} %get-tuple-element.31), channel_id=1, source_target_pairs={{0,66},{2,64},{64,2},{66,0},{1,67},{3,65},{65,3},{67,1},{4,70},{6,... | collective-permute-start | bytes 3932168 | tf_op jit(solution)/shard_map/ppermute | solution.py:117
  16.9 60.0 %collective-permute-start.3 = (bf16[256,2560]{1,0:T(8,128)(2,1)}, bf16[256,2560]{1,0:T(8,128)(2,1)}, u32[]{:S(2)}, u32[]{:S(2)}) collective-permute-start(bf16[256,2560]{1,0:T(8,128)(2,1)} %get-tuple-element.30), channel_id=1, source_target_pairs={{0,1},{1,0},{2,3},{3,2},{4,5},{5,4},{6,7},{7,6},{8,9},{9,8},{10,11... | collective-permute-start | bytes 3932168 | tf_op jit(solution)/shard_map/ppermute | solution.py:116
  44.0 32.8 %collective-permute-start.5 = (bf16[256,2560]{1,0:T(8,128)(2,1)}, bf16[256,2560]{1,0:T(8,128)(2,1)}, u32[]{:S(2)}, u32[]{:S(2)}) collective-permute-start(bf16[256,2560]{1,0:T(8,128)(2,1)} %collective-permute-done.4), channel_id=1, source_target_pairs={{0,1},{1,0},{2,3},{3,2},{4,5},{5,4},{6,7},{7,6},{8,9},{9,8},{10,11... | collective-permute-start | bytes 3932168 | tf_op jit(solution)/shard_map/ppermute | solution.py:118
  49.1 12.6 %collective-permute-start.2 = (bf16[4,128,256]{2,1,0:T(8,128)(2,1)}, bf16[4,128,256]{2,1,0:T(8,128)(2,1)}, u32[]{:S(2)}, u32[]{:S(2)}) collective-permute-start(bf16[4,128,256]{2,1,0:T(8,128)(2,1)} %get-tuple-element.40), channel_id=1, source_target_pairs={{0,67},{1,66},{2,65},{3,64},{64,3},{65,2},{66,1},{67,0},{4,71},{5,... | collective-permute-start | bytes 786440 | tf_op jit(solution)/shard_map/ppermute | solution.py:112
  49.3 21.7 %collective-permute-start = (bf16[4,128,256]{2,1,0:T(8,128)(2,1)}, bf16[4,128,256]{2,1,0:T(8,128)(2,1)}, u32[]{:S(2)}, u32[]{:S(2)}) collective-permute-start(bf16[4,128,256]{2,1,0:T(8,128)(2,1)} %get-tuple-element.39), channel_id=1, source_target_pairs={{0,1},{1,0},{2,3},{3,2},{4,5},{5,4},{6,7},{7,6},{8,9},{9,8},{10,11... | collective-permute-start | bytes 786440 | tf_op jit(solution)/shard_map/ppermute | solution.py:110
  83.9 11.5 %collective-permute-start.7 = (bf16[128,640]{1,0:T(8,128)(2,1)S(1)}, bf16[128,640]{1,0:T(8,128)(2,1)S(1)}, u32[]{:S(2)}, u32[]{:S(2)}) collective-permute-start(bf16[128,640]{1,0:T(8,128)(2,1)S(1)} %get-tuple-element.55), channel_id=1, source_target_pairs={{0,4},{4,8},{8,12},{12,0},{1,5},{5,9},{9,13},{13,1},{2,6},{6,10},{... | collective-permute-start | bytes 491528 | tf_op jit(solution)/shard_map/ppermute | solution.py:149
  83.9 13.1 %collective-permute-start.6 = (bf16[128,640]{1,0:T(8,128)(2,1)S(1)}, bf16[128,640]{1,0:T(8,128)(2,1)S(1)}, u32[]{:S(2)}, u32[]{:S(2)}) collective-permute-start(bf16[128,640]{1,0:T(8,128)(2,1)S(1)} %get-tuple-element.53), channel_id=1, source_target_pairs={{0,8},{4,12},{8,0},{12,4},{1,9},{5,13},{9,1},{13,5},{2,10},{6,14},... | collective-permute-start | bytes 491528 | tf_op jit(solution)/shard_map/ppermute | solution.py:149
  87.2 12.8 %collective-permute-start.11 = (bf16[128,640]{1,0:T(8,128)(2,1)S(1)}, bf16[128,640]{1,0:T(8,128)(2,1)S(1)}, u32[]{:S(2)}, u32[]{:S(2)}) collective-permute-start(bf16[128,640]{1,0:T(8,128)(2,1)S(1)} %get-tuple-element.51), channel_id=1, source_target_pairs={{0,12},{4,0},{8,4},{12,8},{1,13},{5,1},{9,5},{13,9},{2,14},{6,2},{... | collective-permute-start | bytes 491528 | tf_op jit(solution)/shard_map/ppermute | solution.py:149
  88.4 14.0 %collective-permute-start.10 = (bf16[128,640]{1,0:T(8,128)(2,1)S(1)}, bf16[128,640]{1,0:T(8,128)(2,1)S(1)}, u32[]{:S(2)}, u32[]{:S(2)}) collective-permute-start(bf16[128,640]{1,0:T(8,128)(2,1)S(1)} %get-tuple-element.52), channel_id=1, source_target_pairs={{0,4},{4,8},{8,12},{12,0},{1,5},{5,9},{9,13},{13,1},{2,6},{6,10},{... | collective-permute-start | bytes 491528 | tf_op jit(solution)/shard_map/ppermute | solution.py:149
  97.0 12.4 %collective-permute-start.13 = (bf16[128,640]{1,0:T(8,128)(2,1)S(1)}, bf16[128,640]{1,0:T(8,128)(2,1)S(1)}, u32[]{:S(2)}, u32[]{:S(2)}) collective-permute-start(bf16[128,640]{1,0:T(8,128)(2,1)S(1)} %get-tuple-element.49), channel_id=1, source_target_pairs={{0,4},{4,8},{8,12},{12,0},{1,5},{5,9},{9,13},{13,1},{2,6},{6,10},{... | collective-permute-start | bytes 491528 | tf_op jit(solution)/shard_map/ppermute | solution.py:149
  100.1 12.6 %collective-permute-start.12 = (bf16[128,640]{1,0:T(8,128)(2,1)S(1)}, bf16[128,640]{1,0:T(8,128)(2,1)S(1)}, u32[]{:S(2)}, u32[]{:S(2)}) collective-permute-start(bf16[128,640]{1,0:T(8,128)(2,1)S(1)} %get-tuple-element.47), channel_id=1, source_target_pairs={{0,8},{4,12},{8,0},{12,4},{1,9},{5,13},{9,1},{13,5},{2,10},{6,14},... | collective-permute-start | bytes 491528 | tf_op jit(solution)/shard_map/ppermute | solution.py:149
  102.4 33.5 %collective-permute-start.17 = (bf16[128,640]{1,0:T(8,128)(2,1)}, bf16[128,640]{1,0:T(8,128)(2,1)}, u32[]{:S(2)}, u32[]{:S(2)}) collective-permute-start(bf16[128,640]{1,0:T(8,128)(2,1)} %get-tuple-element.45), channel_id=1, source_target_pairs={{0,12},{4,0},{8,4},{12,8},{1,13},{5,1},{9,5},{13,9},{2,14},{6,2},{... | collective-permute-start | bytes 491528 | tf_op jit(solution)/shard_map/ppermute | solution.py:149
  103.1 34.4 %collective-permute-start.16 = (bf16[128,640]{1,0:T(8,128)(2,1)}, bf16[128,640]{1,0:T(8,128)(2,1)}, u32[]{:S(2)}, u32[]{:S(2)}) collective-permute-start(bf16[128,640]{1,0:T(8,128)(2,1)} %get-tuple-element.46), channel_id=1, source_target_pairs={{0,4},{4,8},{8,12},{12,0},{1,5},{5,9},{9,13},{13,1},{2,6},{6,10},{... | collective-permute-start | bytes 491528 | tf_op jit(solution)/shard_map/ppermute | solution.py:149
  106.2 31.4 %collective-permute-start.15 = (bf16[128,640]{1,0:T(8,128)(2,1)}, bf16[128,640]{1,0:T(8,128)(2,1)}, u32[]{:S(2)}, u32[]{:S(2)}) collective-permute-start(bf16[128,640]{1,0:T(8,128)(2,1)} %get-tuple-element.44), channel_id=1, source_target_pairs={{0,8},{4,12},{8,0},{12,4},{1,9},{5,13},{9,1},{13,5},{2,10},{6,14},... | collective-permute-start | bytes 491528 | tf_op jit(solution)/shard_map/ppermute | solution.py:149
  127.1 21.6 %collective-permute-start.38 = (bf16[128,2560]{1,0:T(8,128)(2,1)}, bf16[128,2560]{1,0:T(8,128)(2,1)}, u32[]{:S(2)}, u32[]{:S(2)}) collective-permute-start(bf16[128,2560]{1,0:T(8,128)(2,1)} %get-tuple-element.60), channel_id=1, source_target_pairs={{0,16},{16,32},{32,48},{48,0},{1,17},{17,33},{33,49},{49,1},{2,18}... | collective-permute-start | bytes 1966088 | tf_op jit(solution)/shard_map/ppermute | solution.py:169
  129.7 26.6 %collective-permute-start.37 = (bf16[128,2560]{1,0:T(8,128)(2,1)}, bf16[128,2560]{1,0:T(8,128)(2,1)}, u32[]{:S(2)}, u32[]{:S(2)}) collective-permute-start(bf16[128,2560]{1,0:T(8,128)(2,1)} %get-tuple-element.62), channel_id=1, source_target_pairs={{0,48},{16,0},{32,16},{48,32},{1,49},{17,1},{33,17},{49,33},{2,50}... | collective-permute-start | bytes 1966088 | tf_op jit(solution)/shard_map/ppermute | solution.py:169
  135.9 20.4 %collective-permute-start.36 = (bf16[128,2560]{1,0:T(8,128)(2,1)}, bf16[128,2560]{1,0:T(8,128)(2,1)}, u32[]{:S(2)}, u32[]{:S(2)}) collective-permute-start(bf16[128,2560]{1,0:T(8,128)(2,1)} %get-tuple-element.64), channel_id=1, source_target_pairs={{0,32},{16,48},{32,0},{48,16},{1,33},{17,49},{33,1},{49,17},{2,34}... | collective-permute-start | bytes 1966088 | tf_op jit(solution)/shard_map/ppermute | solution.py:169
  144.2 42.4 %collective-permute-start.31 = (bf16[4,2,160,640]{3,2,1,0:T(8,128)(2,1)}, bf16[4,2,160,640]{3,2,1,0:T(8,128)(2,1)}, u32[]{:S(2)}, u32[]{:S(2)}) collective-permute-start(bf16[4,2,160,640]{3,2,1,0:T(8,128)(2,1)} %dynamic-slice_bitcast_fusion), channel_id=1, source_target_pairs={{0,1},{1,0},{2,3},{3,2},{4,5},{5,4},{6,7},{7,6},{8,9},{9,8},{10,11... | collective-permute-start | bytes 4915208 | tf_op jit(solution)/shard_map/ppermute | solution.py:186
  167.8 24.3 %collective-permute-start.40 = (f32[128]{0:T(128)S(1)}, f32[128]{0:T(128)S(1)}, u32[]{:S(2)}, u32[]{:S(2)}) collective-permute-start(f32[128]{0:T(128)S(1)} %get-tuple-element.13), channel_id=1, source_target_pairs={{0,64},{64,0},{1,65},{65,1},{2,66},{66,2},{3,67},{67,3},{4,68},{68... | collective-permute-start | bytes 1544 | tf_op jit(solution)/shard_map/ppermute | solution.py:198
  191.2 12.6 %collective-permute-start.34 = (bf16[2,160,640]{2,1,0:T(8,128)(2,1)}, bf16[2,160,640]{2,1,0:T(8,128)(2,1)}, u32[]{:S(2)}, u32[]{:S(2)}) collective-permute-start(bf16[2,160,640]{2,1,0:T(8,128)(2,1)} %get-tuple-element.33), channel_id=1, source_target_pairs={{0,12},{4,0},{8,4},{12,8},{1,13},{5,1},{9,5},{13,9},{2,14},{6,2},{... | collective-permute-start | bytes 1228808 | tf_op jit(solution)/shard_map/ppermute | solution.py:190
  192.1 18.0 %collective-permute-start.33 = (bf16[2,160,640]{2,1,0:T(8,128)(2,1)}, bf16[2,160,640]{2,1,0:T(8,128)(2,1)}, u32[]{:S(2)}, u32[]{:S(2)}) collective-permute-start(bf16[2,160,640]{2,1,0:T(8,128)(2,1)} %get-tuple-element.34), channel_id=1, source_target_pairs={{0,4},{4,8},{8,12},{12,0},{1,5},{5,9},{9,13},{13,1},{2,6},{6,10},{... | collective-permute-start | bytes 1228808 | tf_op jit(solution)/shard_map/ppermute | solution.py:190
  193.2 16.9 %collective-permute-start.32 = (bf16[2,160,640]{2,1,0:T(8,128)(2,1)}, bf16[2,160,640]{2,1,0:T(8,128)(2,1)}, u32[]{:S(2)}, u32[]{:S(2)}) collective-permute-start(bf16[2,160,640]{2,1,0:T(8,128)(2,1)} %get-tuple-element.32), channel_id=1, source_target_pairs={{0,8},{4,12},{8,0},{12,4},{1,9},{5,13},{9,1},{13,5},{2,10},{6,14},... | collective-permute-start | bytes 1228808 | tf_op jit(solution)/shard_map/ppermute | solution.py:190
  194.6 19.5 %collective-permute-start.39 = (bf16[128,1280]{1,0:T(8,128)(2,1)}, bf16[128,1280]{1,0:T(8,128)(2,1)}, u32[]{:S(2)}, u32[]{:S(2)}) collective-permute-start(bf16[128,1280]{1,0:T(8,128)(2,1)} %dynamic-slice_convert_fusion), channel_id=1, source_target_pairs={{0,64},{64,0},{1,65},{65,1},{2,66},{66,2},{3,67},{67,3},{4,68},{68... | collective-permute-start | bytes 983048 | tf_op jit(solution)/shard_map/ppermute | solution.py:201
  (43 other events, 427.9 us)
Sparse Core Ops, SparseCore 0:
  17.0 34.1 all-gather.1

commit v2 on v1

v2 whole, which is shorter than its diff:
```python
import math

import jax
import jax.numpy as jnp
from jax import lax
from jax.experimental import pallas as pl
from jax.experimental.pallas import tpu as pltpu
from jax.sharding import Mesh
from jax.sharding import PartitionSpec as P

D_T = 5120
D_S = 2560
HD = 128
HQ = 32
KVH = 4

BF = jnp.bfloat16
F32 = jnp.float32
NX = 4
NZ = 4
MP = ("x", "zh", "core")


def ring(n, k):
    return [(i, (i + k) % n) for i in range(n)]


WRAP = [(g * 2 + z, (1 - g) * 2 + (1 - z)) for g in range(2) for z in range(2)]
WRAP_CORE = [
    (g * 4 + z * 2 + c, (1 - g) * 4 + (1 - z) * 2 + (1 - c))
    for g in range(2)
    for z in range(2)
    for c in range(2)
]


MIB = 32
COST = 1
STEPS = (0, 10, 1, 11)
STAGES = ((2, 1), (3, 0))
ORDER = sum(STAGES, ())


def whole(shape):
    return pl.BlockSpec(shape, lambda i, s: (0,) * len(shape))


def call(kernel, scalars, ins, outs, name, scratch=(), mib=MIB):
    outs = pl.pallas_call(
        kernel,
        out_shape=[jax.ShapeDtypeStruct(shape, t) for shape, t in outs],
        grid_spec=pltpu.PrefetchScalarGridSpec(
            num_scalar_prefetch=1,
            grid=(1,),
            in_specs=[spec for _, spec in ins],
            out_specs=[whole(shape) for shape, _ in outs],
            scratch_shapes=list(scratch),
        ),
        compiler_params=pltpu.CompilerParams(vmem_limit_bytes=mib * 1024 * 1024),
        cost_estimate=pl.CostEstimate(flops=COST, bytes_accessed=COST, transcendentals=0),
        name=name,
    )(scalars.value, *[a for a, _ in ins])
    scalars.after(outs[0])
    return outs


class Ordered:
    def __init__(self, value):
        self.value = value

    def after(self, array):
        self.value, _ = lax.optimization_barrier((self.value, array))


X, ZC, G, D, ZH, C, FIRST, LENGTHS = range(8)


def pick_kernel(s, q1, q2, q3, *refs):
    o1, o2, o3 = refs[4:7]
    o1[...] = q1[:, 0]
    o2[...] = q2[:, 0]
    o3[...] = q3[:, 0]
    pieces = list(refs[:4])
    for ks, out in zip(STAGES, refs[7:]):
        for i in range(len(ks)):
            out[:, i * 640 : i * 640 + 640] = pieces.pop(0)[...]


def attend_kernel(scalars, q0_ref, q1_ref, k_ref, v_ref, out_ref, vext):
    first = scalars[ZC] * 128
    vext[:, :HD] = v_ref[...]
    vext[:, HD:] = jnp.ones((v_ref.shape[0], HD), BF)
    scale = HD ** (-0.5) * math.log2(math.e)
    rows = lax.broadcasted_iota(jnp.int32, (256, 512), 0) % 128
    cols = lax.broadcasted_iota(jnp.int32, (256, 512), 1)
    allowed = cols <= rows + first
    for part in range(NX):
        length = 512 * (part + 1)
        for pair, q_ref in enumerate((q0_ref, q1_ref)):
            q = q_ref[part] if len(q_ref.shape) == 3 else q_ref[part, 0]
            q = jnp.concatenate([q[:, :HD], q[:, HD:]], axis=0)
            scores = lax.dot_general(
                q, k_ref[:length, :], (((1,), (1,)), ((), ())), preferred_element_type=F32
            )
            last = jnp.where(allowed, scores[:, length - 512 :], -1e30)
            if part:
                scores = jnp.concatenate([scores[:, : length - 512], last], axis=1)
            else:
                scores = last
            top = jnp.max(scores, axis=-1, keepdims=True)
            probs = jnp.exp2((scores - top) * scale).astype(BF)
            mixed = jnp.dot(probs, vext[:length, :], preferred_element_type=F32)
            mixed = (mixed[:, :HD] / mixed[:, HD:]).astype(BF)
            for head in range(2):
                at = (pair * 2 + head) * HD
                out_ref[part * 128 : part * 128 + 128, at : at + HD] = mixed[
                    head * 128 : head * 128 + 128
                ]


def project_kernel(s, ctx_a, ctx_b, w2, w3, *refs):
    own, o1, o2, o3, total = refs[-5:]
    n = len(refs[:-5]) // 2

    def dot(a, b):
        return jnp.dot(a, b, preferred_element_type=F32)

    for part, (w0, w1) in enumerate(zip(refs[:n], refs[n : 2 * n])):
        cols = slice(part * 640, part * 640 + 640)
        total[:, cols] = (
            dot(ctx_a[:, :256], w0[...])
            + dot(ctx_a[:, 256:], w1[...])
            + dot(ctx_b[:, :256], w2[:, cols])
            + dot(ctx_b[:, 256:], w3[:, cols])
        )
    for j, out in enumerate((own, o1, o2, o3)):
        at = pl.multiple_of(((s[X] + j) % NX) * 128, 128)
        out[...] = total[pl.ds(at, 128), :].astype(out.dtype)


def finish_kernel(s, own, r1, r2, r3, *refs):
    n = own.shape[1] // 640
    rows = own[...] + r1[...].astype(F32) + r2[...].astype(F32) + r3[...].astype(F32)
    olds, target = [], None
    if len(refs) > 2 * n:
        olds, target = refs[n : -n - 1], refs[-1]
    news = refs[-n - 1 : -1] if olds else refs[-n:]
    for i in range(n):
        news[i][...] = (refs[i][...].astype(F32) + rows[:, i * 640 : i * 640 + 640]).astype(BF)
    for k, done in zip(ORDER, (*olds, *news) if olds else ()):
        at = pl.multiple_of(((s[D] + k) % 4) * 640, 128)
        target[:, pl.ds(at, 640)] = done[...]


def compare_kernel(ks, s, pred, normed, proj, *refs):
    n = len(ks)
    gots, gps, backs, (gain, loss, both) = refs[:n], refs[n : 2 * n], refs[2 * n : 3 * n], refs[3 * n :]
    square = jnp.zeros((1, 640), F32)
    starts = []
    for i, (k, got, gp) in enumerate(zip(ks, gots, gps)):
        seq = (s[D] + 4 - k) % 4
        at = pl.multiple_of(seq * 128, 128)
        starts.append(at)
        live = lax.broadcasted_iota(jnp.int32, (128, 640), 0) < s[LENGTHS + seq] - s[FIRST]
        diff = jnp.where(live, pred[pl.ds(at, 128), :] - got[...].astype(F32), 0.0)
        square = square + jnp.sum(diff * diff, axis=0, keepdims=True)
        rounded = diff.astype(BF)
        gp[...] = rounded
        both[i * 128 : i * 128 + 128] = rounded
    loss[...] = square
    for part in range(4):
        cols = slice(part * 640, part * 640 + 640)
        grad = lax.dot_general(
            both[...], proj[cols, :], (((1,), (1,)), ((), ())), preferred_element_type=F32
        )
        total = jnp.zeros((128, 640), F32)
        for i, (at, back) in enumerate(zip(starts, backs)):
            rows = grad[i * 128 : i * 128 + 128]
            back[:, cols] = rows.astype(back.dtype)
            total = total + rows * normed[pl.ds(at, 128), cols].astype(F32)
        gain[:, cols] = jnp.sum(total, axis=0, keepdims=True)


def combine_kernel(s, own, r1, r2, r3, scaled, sent, kept, inner):
    total = own[...] + r1[...].astype(F32) + r2[...].astype(F32) + r3[...].astype(F32)
    inner[...] = jnp.sum(total * scaled[...], axis=-1, keepdims=True)
    width = D_S // 2
    first = s[G] == 0
    kept[...] = jnp.where(first, total[:, :width], total[:, width:])
    sent[...] = jnp.where(first, total[:, width:], total[:, :width]).astype(BF)


def gproj_kernel(s, normed, gp2, gp1, gp3, gp0, sent, kept, gp):
    for k, part in zip((2, 1, 3, 0), (gp2, gp1, gp3, gp0)):
        at = pl.multiple_of(((s[D] + 4 - k) % 4) * 128, 128)
        gp[pl.ds(at, 128), :] = part[...]
    first = s[C] == 0
    for part in range(NX):
        total = lax.dot_general(
            normed[:, part * 640 : part * 640 + 640],
            gp[...],
            (((0,), (0,)), ((), ())),
            preferred_element_type=F32,
        )
        for z in range(2):
            low = total[z * 320 : z * 320 + 160]
            high = total[z * 320 + 160 : z * 320 + 320]
            sent[part, z] = jnp.where(first, high, low).astype(BF)
            kept[part, z] = jnp.where(first, low, high)


def gproj_add_kernel(s, kept, recv, own, o1, o2, o3):
    for j, out in enumerate((own, o1, o2, o3)):
        at = (s[X] + j) % NX
        out[...] = (kept[at] + recv[at].astype(F32)).astype(out.dtype)


def gproj_sum_kernel(s, own, r1, r2, r3, sent, kept):
    z = s[ZH]

    def total(at):
        return own[at] + r1[at].astype(F32) + r2[at].astype(F32) + r3[at].astype(F32)

    sent[...] = total(1 - z).astype(BF)
    kept[...] = total(z)


def body(
    queries, keys, values, out_weight, residual, student_hidden, norm_gain, projection, lengths
):
    g, d = lax.axis_index("grp"), lax.axis_index("dp")
    x, zh, c = lax.axis_index("x"), lax.axis_index("zh"), lax.axis_index("core")
    zc = zh * 2 + c
    m = x * 4 + zc
    half = D_T // 2
    blk = D_T // 8
    rows = D_S // 16
    barrier = lax.optimization_barrier
    scalars = Ordered(
        jnp.concatenate([jnp.stack([x, zc, g, d, zh, c, m * 128]).astype(jnp.int32), lengths])
    )
    swap = ring(2, 1)

    q5 = queries.reshape(NX, 4, 128, 256)

    def q_spec(flip_z, flip_c):
        def index(i, s):
            z = 1 - s[ZH] if flip_z else s[ZH]
            core = 1 - s[C] if flip_c else s[C]
            return (0, z * 2 + core, 0, 0)

        return pl.BlockSpec((NX, 1, 128, 256), index)

    def w_spec(k, other):
        return pl.BlockSpec(
            (256, blk), lambda i, s: (0, (1 - s[G] if other else s[G]) * 4 + (s[D] + k) % 4)
        )

    q_shape = ((NX, 128, 256), BF)
    w_shapes = [((256, len(ks) * blk), BF) for ks in STAGES]
    p_core, p_z0, p_z1, *w_sent = call(
        pick_kernel,
        scalars,
        [
            (q5, q_spec(False, True)),
            (q5, q_spec(True, False)),
            (q5, q_spec(True, True)),
            *[(out_weight, w_spec(k, True)) for ks in STAGES for k in ks],
        ],
        [q_shape, q_shape, q_shape, *w_shapes],
        "pick",
    )
    q_core = lax.ppermute(p_core, "core", swap)
    q_z0 = lax.ppermute(p_z0, ("grp", "zh"), WRAP)
    q_z1 = lax.ppermute(p_z1, ("grp", "zh", "core"), WRAP_CORE)
    w_half = jnp.where(g == 0, out_weight[:, :half], out_weight[:, half:])
    w_core = lax.ppermute(w_half, "core", swap)

    hidden, _ = barrier((student_hidden[0], p_core))
    hidden = hidden.astype(F32)
    inverse_rms = lax.rsqrt(jnp.mean(hidden * hidden, axis=-1, keepdims=True) + 1e-06)
    unit_rows = hidden * inverse_rms
    scaled_rows = unit_rows * norm_gain
    normed = scaled_rows.astype(BF)
    scalars.after(normed)
    normed = lax.all_gather(normed, "dp", axis=0, tiled=True)

    def attend(q0, spec0, q1, name):
        return call(
            attend_kernel,
            scalars,
            [
                (q0, spec0),
                (q1, whole((NX, 128, 256))),
                (keys[0], pl.BlockSpec((2048, HD), lambda i, s: (0, s[X]))),
                (values[0], pl.BlockSpec((2048, HD), lambda i, s: (0, s[X]))),
            ],
            [((512, 512), BF)],
            name,
            scratch=[pltpu.VMEM((2048, 2 * HD), BF)],
            mib=40,
        )[0]

    ctx_a = attend(q5, q_spec(False, False), q_core, "attend_chip")
    w_z = [lax.ppermute(w, ("grp", "zh"), WRAP) for w in w_sent]
    ctx_b = attend(q_z0, whole((NX, 128, 256)), q_z1, "attend_next")
    piece = ((128, blk), BF)
    projected = []
    for stage, ks in enumerate(STAGES):
        n = len(ks)
        w_mine, _ = barrier((w_z[stage], scalars.value))
        if stage:
            w_mine, _ = barrier((w_mine, projected[-1][1][1]))
        w_zc = lax.ppermute(w_mine, "core", swap)
        own, *outs = call(
            project_kernel,
            scalars,
            [
                (ctx_a, whole((512, 512))),
                (ctx_b, whole((512, 512))),
                (w_mine, whole((256, n * blk))),
                (w_zc, whole((256, n * blk))),
                *[(out_weight, w_spec(k, False)) for k in ks],
                *[
                    (w_core, pl.BlockSpec((256, blk), lambda i, s, k=k: (0, (s[D] + k) % 4)))
                    for k in ks
                ],
            ],
            [((128, n * blk), F32)] + [((128, n * blk), BF)] * 3,
            f"project_{stage}",
            scratch=[pltpu.VMEM((512, n * blk), F32)],
        )
        projected.append((own, {j: lax.ppermute(outs[j - 1], "x", ring(NX, j)) for j in (2, 1, 3)}))

    normed, _ = barrier((normed, own))
    predicted = jnp.dot(normed, projection, preferred_element_type=F32)
    scalars.after(predicted)

    done_of, there_of = {}, {}
    gp_of, back_of = {}, {}
    gain_part = jnp.zeros((1, D_S), F32)
    squared = jnp.zeros((), F32)

    def finish(stage):
        ks = STAGES[stage]
        n = len(ks)
        own, got = projected[stage]
        sums = [
            (own, whole((128, n * blk))),
            *[(got[j], whole((128, n * blk))) for j in (1, 2, 3)],
            *[
                (
                    residual[0],
                    pl.BlockSpec((128, blk), lambda i, s, k=k: (0, s[G] * 4 + (s[D] + k) % 4)),
                )
                for k in ks
            ],
        ]
        outs = [piece] * n
        if stage == len(STAGES) - 1:
            sums += [(done_of[k], whole((128, blk))) for k in ORDER[:-n]]
            outs = outs + [((128, half), BF)]
        done = call(finish_kernel, scalars, sums, outs, f"finish_{stage}")
        for k, a in zip(ks, done):
            done_of[k] = a
            there_of[k] = a if k == 0 else lax.ppermute(a, "dp", ring(4, k))
        return done[-1]

    def compare(stage):
        ks = STAGES[stage]
        n = len(ks)

        def kernel(*refs):
            compare_kernel(ks, *refs)

        outs = call(
            kernel,
            scalars,
            [
                (predicted, whole((512, blk))),
                (normed, whole((512, D_S))),
                (projection, whole((D_S, blk))),
                *[(there_of[k], whole((128, blk))) for k in ks],
            ],
            [piece] * n
            + [((128, D_S), F32 if k == 0 else BF) for k in ks]
            + [((1, D_S), F32), ((1, blk), F32)],
            f"compare_{stage}",
            scratch=[pltpu.VMEM((n * 128, blk), BF)],
        )
        for k, gp, back in zip(ks, outs[:n], outs[n:]):
            gp_of[k] = gp
            back_of[k] = back if k == 0 else lax.ppermute(back, "dp", ring(4, 4 - k))
        return outs[-2], outs[-1]

    for step in STEPS:
        if step < 10:
            target = finish(step)
        else:
            gain, loss = compare(step - 10)
            gain_part = gain_part + gain
            squared = squared + jnp.sum(loss)

    live_count = jnp.sum(lengths).astype(F32)
    part = (NX, 2, rows, blk)
    sent, kept = call(
        gproj_kernel,
        scalars,
        [(normed, whole((512, D_S)))] + [(gp_of[k], whole((128, blk))) for k in (2, 1, 3, 0)],
        [(part, BF), (part, F32)],
        "gproj",
        scratch=[pltpu.VMEM((512, blk), BF)],
    )
    small = jnp.concatenate([gain_part[0] / norm_gain, jnp.full((128,), squared)]).reshape(-1, 128)
    recv = lax.ppermute(sent, "core", swap)
    small, _ = barrier((small, sent))
    small = small + lax.ppermute(small, "core", swap)
    own, *outs = call(
        gproj_add_kernel,
        scalars,
        [(kept, whole(part)), (recv, whole(part))],
        [(part[1:], F32)] + [(part[1:], BF)] * 3,
        "gproj_add",
    )
    got = {j: lax.ppermute(outs[j - 1], "x", ring(NX, j)) for j in (2, 1, 3)}
    small, _ = barrier((small, own))
    small = sum([lax.ppermute(small, ("grp", "zh"), ring(NZ, j)) for j in range(1, 4)], small)

    scalars.after(got[1])
    width = D_S // 2
    sent, kept, inner = call(
        combine_kernel,
        scalars,
        [(back_of[k], whole((128, D_S))) for k in range(4)]
        + [(scaled_rows, whole((128, D_S)))],
        [((128, width), BF), ((128, width), F32), ((128, 1), F32)],
        "combine",
    )
    inner = inner.reshape(1, 128)
    inner_recv = lax.ppermute(inner, "grp", swap)
    half_recv = lax.ppermute(sent, "grp", swap)
    small, _ = barrier((small, sent))
    small = sum([lax.ppermute(small, "dp", ring(4, j)) for j in range(1, 4)], small)
    scalars.after(small)

    gsent, gkept = call(
        gproj_sum_kernel,
        scalars,
        [(own, whole(part[1:]))] + [(got[j], whole(part[1:])) for j in (1, 2, 3)],
        [((rows, blk), BF), ((rows, blk), F32)],
        "gproj_sum",
    )
    small, _ = barrier((small, gsent))
    gsent = lax.ppermute(gsent, "zh", swap)
    small = sum([lax.ppermute(small, "x", ring(NX, j)) for j in range(1, 4)], small)
    small = small.reshape(-1)
    gkept, kept = barrier((gkept, kept))
    inner = (inner + inner_recv).reshape(128, 1)
    grad_half = kept + half_recv.astype(F32)
    gain_half = lax.dynamic_slice_in_dim(norm_gain, g * width, width, 0)
    unit_half = jnp.where(g == 0, unit_rows[:, :width], unit_rows[:, width:])
    grad_hidden = inverse_rms * (grad_half * gain_half - unit_half * (inner / D_S))
    grad_proj = (gkept + gsent.astype(F32)) / live_count
    distill_loss = small[D_S] / (live_count * D_T)
    grad_gain = lax.dynamic_slice_in_dim(small, g * (D_S // 2), D_S // 2, 0) / live_count
    return (target[None], distill_loss, grad_proj, grad_gain, grad_hidden[None])


def solution(mesh):
    fine = Mesh(mesh.devices.reshape(2, 4, 4, 2, 2), ("grp", "dp", "x", "zh", "core"))
    in_specs = (
        P("dp", None, MP),
        P("dp", None, None),
        P("dp", None, None),
        P(MP, None),
        P("dp", MP, None),
        P("dp", MP, None),
        P(),
        P(None, ("grp", "dp")),
        P(),
    )
    out_specs = (P("dp", MP, "grp"), P(), P(MP, ("grp", "dp")), P("grp"), P("dp", MP, "grp"))
    return jax.shard_map(body, mesh=fine, in_specs=in_specs, out_specs=out_specs, check_vma=False)
```

time: 231 us -> 190 us (0.82)
  Pallas kernels: 11.9 us -> 37.4 us
  matrix products: 24.4 us -> 5.05 us
  other arithmetic: 26.7 us -> 8.05 us
  waiting for transfers between devices: 71.4 us -> 59 us
  local copies, waits for them, and re-layouts: 19.8 us -> 10.4 us
  starting transfers between devices: 54 us -> 50.2 us
    pallas_call x2 -> x13, Pallas kernels: 11.9 us -> 37.4 us  [call(): pl.pallas_call(kernel, out_shape=[jax.ShapeDtypeStruct(shape, t) for shap...]
    dot_general x10 -> x1, matrix products: 24.4 us -> 5.05 us  [body(): predicted = jnp.dot(normed, projection, preferred_element_type=F32)]
    ppermute x41 -> x37, waiting for transfers between devices: 71.4 us -> 59 us  [the longest x3 11.3 us: finish(): there_of[k] = a if k == 0 else lax.ppermute(a, 'dp', ring(4, k))]
    dynamic_update_slice x7 -> x0, other arithmetic: 8.63 us -> none  [the longest x3 5.27 us: body(): target = lax.dynamic_update_slice_in_dim(target, done, at, 1)]
    dynamic_slice x3 -> x0, local copies, waits for them, and re-layouts: 6.32 us -> none  [the longest x1 3.58 us: body(): w_own = lax.dynamic_slice_in_dim(out_weight, g * half, half, 1)]
    ppermute x41 -> x37, starting transfers between devices: 54 us -> 50.2 us  [the longest x6 9.92 us: body(): lax.ppermute(outs[j - 1], 'x', ring(NX, j))]
    lt x2 -> x0, other arithmetic: 3.66 us -> none  [body(): positions < lax.dynamic_index_in_dim(lengths, seq, 0, keepdims=False)]
    squeeze x7 -> x0, local copies, waits for them, and re-layouts: 3.56 us -> none  [the longest x1 1.37 us: body(): take(gproj, 1 - c, 2)]
  transfers between devices with their start and end apart: 42 -> 38, of which waited for: 16 -> 19; matrix products, arithmetic and copies ran while one was open for 27% -> 5% of each run, Pallas kernels for 5% -> 15%
where the time goes in v2:
time: 190 us; the launch traced here: 188 us
  waiting for transfers between devices  59 us (31%)
  starting transfers between devices  50.2 us (26%)
  Pallas kernels  37.4 us (20%)
  between operations  18.1 us (10%)
  local copies, waits for them, and re-layouts  10.4 us (5%)
  other arithmetic  8.05 us (4%)
  matrix products  5.05 us (3%)
    pallas_call x13, Pallas kernels, call(): pl.pallas_call(kernel, out_shape=[jax.ShapeDtypeStruct(shape, t) for shap...  37.4 us
    ppermute x3, waiting for transfers between devices, finish(): there_of[k] = a if k == 0 else lax.ppermute(a, 'dp', ring(4, k))  11.3 us
    ppermute x1, waiting for transfers between devices, body(): q_z0 = lax.ppermute(p_z0, ('grp', 'zh'), WRAP)  10.7 us
    ppermute x2, waiting for transfers between devices, body(): w_z = [lax.ppermute(w, ('grp', 'zh'), WRAP) for w in w_sent]  10.3 us
    ppermute x6, starting transfers between devices, body(): lax.ppermute(outs[j - 1], 'x', ring(NX, j))  9.92 us
    unnamed x64, local copies, waits for them, and re-layouts  9.1 us
    ppermute x3, waiting for transfers between devices, body(): lax.ppermute(small, ('grp', 'zh'), ring(NZ, j))  8.48 us
    ppermute x2, starting transfers between devices, body(): w_z = [lax.ppermute(w, ('grp', 'zh'), WRAP) for w in w_sent]  7.14 us
  transfers between devices with their start and end apart: 38, of which 19 were waited for; matrix products, arithmetic and copies ran while one was open for 5% of the time, Pallas kernels for 15%

profile of v2, /device:TPU:0, one launch (start us, length us, event | category | flops | bytes accessed | tf_op | source)
XLA Modules:
  0.0 188.3 jit_solution(7325616779124134965)
XLA Ops:
  14.8 4.2 %collective-permute-start.3 = (bf16[256,1280]{1,0:T(8,128)(2,1)}, bf16[256,1280]{1,0:T(8,128)(2,1)S(1)}, u32[]{:S(2)}, u32[]{:S(2)}) collective-permute-start(bf16[256,1280]{1,0:T(8,128)(2,1)} %copy-done.18), channel_id=1, source_target_pairs={{0,66},{2,64},{64,2},{66,0},{1,67},{3,65},{65,3},{67,1},{4,70},{6,... | collective-permute-start | bytes 1966088 | tf_op jit(solution)/shard_map/ppermute | solution.py:305
  24.7 5.0 %attend_chip.1.ctx_a = bf16[512,512]{1,0:T(8,128)(2,1)S(1)} custom-call(s32[11]{0:T(128)S(1)} %concatenate.6.s.scalars.refs_0_, bf16[4,4,128,256]{3,2,1,0:T(8,128)(2,1)S(1)} %bitcast.33, bf16[4,128,256]{2,1,0:T(8,128)(2,1)S(1)} %collective-permute-done.q1_ref, bf16[2048,512]{1,0:T(8,128)(2,1)S(1)} %bitcast.34, bf16[2048,512]{1,0:T(8,128)(2,1)S(1)} %bitcast.36), custom_call_target="tpu_custom_call" | custom-call | flops 1 | bytes 1 | tf_op jit(solution)/shard_map/attend_chip/pallas_call | solution.py:49
  29.7 10.7 %collective-permute-done.1.q0_ref = bf16[4,128,256]{2,1,0:T(8,128)(2,1)S(1)} collective-permute-done((bf16[4,128,256]{2,1,0:T(8,128)(2,1)S(1)}, bf16[4,128,256]{2,1,0:T(8,128)(2,1)S(1)}, u32[]{:S(2)}, u32[]{:S(2)}) %collective-permute-start.1) | collective-permute-done | bytes 262176 | tf_op jit(solution)/shard_map/ppermute | solution.py:274
  40.4 4.0 %collective-permute-done.2.q1_ref = bf16[4,128,256]{2,1,0:T(8,128)(2,1)S(1)} collective-permute-done((bf16[4,128,256]{2,1,0:T(8,128)(2,1)S(1)}, bf16[4,128,256]{2,1,0:T(8,128)(2,1)S(1)}, u32[]{:S(2)}, u32[]{:S(2)}) %collective-permute-start.2) | collective-permute-done | bytes 262176 | tf_op jit(solution)/shard_map/ppermute | solution.py:275
  44.4 5.0 %attend_next.1.ctx_b = bf16[512,512]{1,0:T(8,128)(2,1)S(1)} custom-call(s32[11]{0:T(128)S(1)} %concatenate.6.s.scalars.refs_0_, bf16[4,128,256]{2,1,0:T(8,128)(2,1)S(1)} %collective-permute-done.1.q0_ref, bf16[4,128,256]{2,1,0:T(8,128)(2,1)S(1)} %collective-permute-done.2.q1_ref, bf16[2048,512]{1,0:T(8,128)(2,1)S(1)} %bitcast.35, bf16[2048,512]{1,0:T(8,128)(2,1)S(1)} %bitcast.37), custom_call_target="tpu_custom_call" | custom-call | flops 1 | bytes 1 | tf_op jit(solution)/shard_map/attend_next/pallas_call | solution.py:49
  50.5 2.9 %collective-permute-start.6 = (bf16[256,1280]{1,0:T(8,128)(2,1)S(1)}, bf16[256,1280]{1,0:T(8,128)(2,1)S(1)}, u32[]{:S(2)}, u32[]{:S(2)}) collective-permute-start(bf16[256,1280]{1,0:T(8,128)(2,1)S(1)} %copy-done.17), channel_id=1, source_target_pairs={{0,66},{2,64},{64,2},{66,0},{1,67},{3,65},{65,3},{67,1},{4,70},{6,... | collective-permute-start | bytes 1966088 | tf_op jit(solution)/shard_map/ppermute | solution.py:305
  53.5 3.4 %project_0.1 = (f32[128,1280]{1,0:T(8,128)S(1)}, bf16[128,1280]{1,0:T(8,128)(2,1)S(1)}, bf16[128,1280]{1,0:T(8,128)(2,1)}, bf16[128,1280]{1,0:T(8,128)(2,1)}) custom-call(s32[11]{0:T(128)S(1)} %concatenate.6.s.scalars.refs_0_, bf16[512,512]{1,0:T(8,128)(2,1)S(1)} %attend_chip.1.ctx_a, bf16[512,512]{1,0:T(8,128)(2,1)S(1)} %attend_next.1.ctx_b, ...), custom_call_target="tpu_custom_call" | custom-call | flops 1 | bytes 1 | tf_op jit(solution)/shard_map/project_0/pallas_call | solution.py:49
  58.4 10.3 %collective-permute-done.6.w2 = bf16[256,1280]{1,0:T(8,128)(2,1)S(1)} collective-permute-done((bf16[256,1280]{1,0:T(8,128)(2,1)S(1)}, bf16[256,1280]{1,0:T(8,128)(2,1)S(1)}, u32[]{:S(2)}, u32[]{:S(2)}) %collective-permute-start.6) | collective-permute-done | bytes 655392 | tf_op jit(solution)/shard_map/ppermute | solution.py:305
  68.7 3.1 %collective-permute-start.9 = (bf16[128,1280]{1,0:T(8,128)(2,1)}, bf16[128,1280]{1,0:T(8,128)(2,1)}, u32[]{:S(2)}, u32[]{:S(2)}) collective-permute-start(bf16[128,1280]{1,0:T(8,128)(2,1)} %get-tuple-element.93), channel_id=1, source_target_pairs={{0,8},{4,12},{8,0},{12,4},{1,9},{5,13},{9,1},{13,5},{2,10},{6,14},... | collective-permute-start | bytes 983048 | tf_op jit(solution)/shard_map/ppermute | solution.py:333
  72.9 3.4 %project_1.1 = (f32[128,1280]{1,0:T(8,128)S(1)}, bf16[128,1280]{1,0:T(8,128)(2,1)}, bf16[128,1280]{1,0:T(8,128)(2,1)}, bf16[128,1280]{1,0:T(8,128)(2,1)}) custom-call(s32[11]{0:T(128)S(1)} %concatenate.6.s.scalars.refs_0_, bf16[512,512]{1,0:T(8,128)(2,1)S(1)} %attend_chip.1.ctx_a, bf16[512,512]{1,0:T(8,128)(2,1)S(1)} %attend_next.1.ctx_b, ...), custom_call_target="tpu_custom_call" | custom-call | flops 1 | bytes 1 | tf_op jit(solution)/shard_map/project_1/pallas_call | solution.py:49
  80.5 5.1 %fusion.6.refs_1_ = f32[512,640]{1,0:T(8,128)S(1)} fusion(bf16[512,2560]{1,0:T(8,128)(2,1)} %all-gather.2.cloned.1.call-done.refs_2_.normed, bf16[2560,640]{1,0:T(8,128)(2,1)} %refs_3_.5), kind=kOutput, calls=%fused_computation.20 | convolution fusion | flops 1677721600 | bytes 7208960 | tf_op jit(solution)/shard_map/dot_general | solution.py:336
  90.3 2.9 %collective-permute-start.11 = (bf16[128,640]{1,0:T(8,128)(2,1)S(1)}, bf16[128,640]{1,0:T(8,128)(2,1)S(1)}, u32[]{:S(2)}, u32[]{:S(2)}) collective-permute-start(bf16[128,640]{1,0:T(8,128)(2,1)S(1)} %get-tuple-element.95.refs_2_), channel_id=1, source_target_pairs={{0,32},{16,48},{32,0},{48,16},{1,33},{17,49},{33,1},{49,17},{2,34}... | collective-permute-start | bytes 491528 | tf_op jit(solution)/shard_map/ppermute | solution.py:366
  94.3 4.8 %collective-permute-done.11.refs_4_ = bf16[128,640]{1,0:T(8,128)(2,1)S(1)} collective-permute-done((bf16[128,640]{1,0:T(8,128)(2,1)S(1)}, bf16[128,640]{1,0:T(8,128)(2,1)S(1)}, u32[]{:S(2)}, u32[]{:S(2)}) %collective-permute-start.11) | collective-permute-done | bytes 163872 | tf_op jit(solution)/shard_map/ppermute | solution.py:366
  101.0 3.2 %compare_0.1 = (bf16[128,640]{1,0:T(8,128)(2,1)S(1)}, bf16[128,640]{1,0:T(8,128)(2,1)S(1)}, bf16[128,2560]{1,0:T(8,128)(2,1)}, bf16[128,2560]{1,0:T(8,128)(2,1)}...) custom-call(s32[11]{0:T(128)S(1)} %concatenate.6.s.scalars.refs_0_, f32[512,640]{1,0:T(8,128)S(1)} %fusion.6.refs_1_, ...), custom_call_target="tpu_custom_call" | custom-call | flops 1 | bytes 1 | tf_op jit(solution)/shard_map/compare_0/pallas_call | solution.py:49
  107.6 4.6 %collective-permute-done.16.refs_4_ = bf16[128,640]{1,0:T(8,128)(2,1)S(1)} collective-permute-done((bf16[128,640]{1,0:T(8,128)(2,1)S(1)}, bf16[128,640]{1,0:T(8,128)(2,1)S(1)}, u32[]{:S(2)}, u32[]{:S(2)}) %collective-permute-start.16) | collective-permute-done | bytes 163872 | tf_op jit(solution)/shard_map/ppermute | solution.py:366
  112.2 2.9 %compare_1.1 = (bf16[128,640]{1,0:T(8,128)(2,1)S(1)}, bf16[128,640]{1,0:T(8,128)(2,1)S(1)}, bf16[128,2560]{1,0:T(8,128)(2,1)}, f32[128,2560]{1,0:T(8,128)S(1)}, ...) custom-call(s32[11]{0:T(128)S(1)} %concatenate.6.s.scalars.refs_0_, f32[512,640]{1,0:T(8,128)S(1)} %fusion.6.refs_1_, ...), custom_call_target="tpu_custom_call" | custom-call | flops 1 | bytes 1 | tf_op jit(solution)/shard_map/compare_1/pallas_call | solution.py:49
  115.1 2.8 %gproj.1 = (bf16[4,2,160,640]{3,2,1,0:T(8,128)(2,1)S(1)}, f32[4,2,160,640]{3,2,1,0:T(8,128)S(1)}) custom-call(s32[11]{0:T(128)S(1)} %concatenate.6.s.scalars.refs_0_, bf16[512,2560]{1,0:T(8,128)(2,1)S(1)} %copy-done.2, bf16[128,640]{1,0:T(8,128)(2,1)S(1)} %get-tuple-element.98.gp2, bf16[128,640]{1,0:T(8,128)(2,1)S(1)} %get-tuple-element.113.gp1, ...), custom_call_target="tpu_custom_call" | custom-call | flops 1 | bytes 1 | tf_op jit(solution)/shard_map/gproj/pallas_call | solution.py:49
  131.3 2.9 %collective-permute-start.21 = (f32[21,128]{1,0:T(8,128)S(1)}, f32[21,128]{1,0:T(8,128)S(1)}, u32[]{:S(2)}, u32[]{:S(2)}) collective-permute-start(f32[21,128]{1,0:T(8,128)S(1)} %add.76), channel_id=1, source_target_pairs={{0,66},{2,0},{64,2},{66,64},{1,67},{3,1},{65,3},{67,65},{4,70},{6,... | collective-permute-start | bytes 32264 | tf_op jit(solution)/shard_map/ppermute | solution.py:427
  136.8 3.4 %collective-permute-done.20 = f32[21,128]{1,0:T(8,128)S(1)} collective-permute-done((f32[21,128]{1,0:T(8,128)S(1)}, f32[21,128]{1,0:T(8,128)S(1)}, u32[]{:S(2)}, u32[]{:S(2)}) %collective-permute-start.20) | collective-permute-done | bytes 10784 | tf_op jit(solution)/shard_map/ppermute | solution.py:427
  142.3 2.8 %collective-permute-done.19 = f32[21,128]{1,0:T(8,128)S(1)} collective-permute-done((f32[21,128]{1,0:T(8,128)S(1)}, f32[21,128]{1,0:T(8,128)S(1)}, u32[]{:S(2)}, u32[]{:S(2)}) %collective-permute-start.19) | collective-permute-done | bytes 10784 | tf_op jit(solution)/shard_map/ppermute | solution.py:427
  145.1 2.7 %collective-permute-start.29 = (bf16[2,160,640]{2,1,0:T(8,128)(2,1)}, bf16[2,160,640]{2,1,0:T(8,128)(2,1)}, u32[]{:S(2)}, u32[]{:S(2)}) collective-permute-start(bf16[2,160,640]{2,1,0:T(8,128)(2,1)} %copy-done.20), channel_id=1, source_target_pairs={{0,8},{4,12},{8,0},{12,4},{1,9},{5,13},{9,1},{13,5},{2,10},{6,14},... | collective-permute-start | bytes 1228808 | tf_op jit(solution)/shard_map/ppermute | solution.py:425
  149.5 3.7 %collective-permute-done.25.r3 = bf16[128,2560]{1,0:T(8,128)(2,1)} collective-permute-done((bf16[128,2560]{1,0:T(8,128)(2,1)}, bf16[128,2560]{1,0:T(8,128)(2,1)}, u32[]{:S(2)}, u32[]{:S(2)}) %collective-permute-start.25) | collective-permute-done | bytes 655392 | tf_op jit(solution)/shard_map/ppermute | solution.py:393
  165.6 3.3 %collective-permute-start.33 = (f32[21,128]{1,0:T(8,128)S(1)}, f32[21,128]{1,0:T(8,128)S(1)}, u32[]{:S(2)}, u32[]{:S(2)}) collective-permute-start(f32[21,128]{1,0:T(8,128)S(1)} %add_add_fusion), channel_id=1, source_target_pairs={{0,12},{4,0},{8,4},{12,8},{1,13},{5,1},{9,5},{13,9},{2,14},{6,2},{... | collective-permute-start | bytes 32264 | tf_op jit(solution)/shard_map/ppermute | solution.py:455
  170.2 3.3 %collective-permute-start.34 = (bf16[160,640]{1,0:T(8,128)(2,1)S(1)}, bf16[160,640]{1,0:T(8,128)(2,1)S(1)}, u32[]{:S(2)}, u32[]{:S(2)}) collective-permute-start(bf16[160,640]{1,0:T(8,128)(2,1)S(1)} %get-tuple-element.134), channel_id=1, source_target_pairs={{0,2},{2,0},{1,3},{3,1},{4,6},{6,4},{5,7},{7,5},{8,10},{10,8},{9,1... | collective-permute-start | bytes 614408 | tf_op jit(solution)/shard_map/ppermute | solution.py:454
  (153 shorter events, 69.6 us)
Async XLA Ops:
  7.2 73.3 %all-gather.2.cloned.1.call-start = ((), (), s32[]{:S(2)}) async-start(), calls=%async_computation | async-start | bytes 3276800 | tf_op jit(solution)/shard_map/all_gather | solution.py:286
  14.8 34.7 %collective-permute-start.3 = (bf16[256,1280]{1,0:T(8,128)(2,1)}, bf16[256,1280]{1,0:T(8,128)(2,1)S(1)}, u32[]{:S(2)}, u32[]{:S(2)}) collective-permute-start(bf16[256,1280]{1,0:T(8,128)(2,1)} %copy-done.18), channel_id=1, source_target_pairs={{0,66},{2,64},{64,2},{66,0},{1,67},{3,65},{65,3},{67,1},{4,70},{6,... | collective-permute-start | bytes 1966088 | tf_op jit(solution)/shard_map/ppermute | solution.py:305
  19.2 34.3 %collective-permute-start.5 = (bf16[256,2560]{1,0:T(8,128)(2,1)S(1)}, bf16[256,2560]{1,0:T(8,128)(2,1)S(1)}, u32[]{:S(2)}, u32[]{:S(2)}) collective-permute-start(bf16[256,2560]{1,0:T(8,128)(2,1)S(1)} %slice_select_fusion), channel_id=1, source_target_pairs={{0,1},{1,0},{2,3},{3,2},{4,5},{5,4},{6,7},{7,6},{8,9},{9,8},{10,11... | collective-permute-start | bytes 3932168 | tf_op jit(solution)/shard_map/ppermute | solution.py:277
  20.0 20.4 %collective-permute-start.1 = (bf16[4,128,256]{2,1,0:T(8,128)(2,1)S(1)}, bf16[4,128,256]{2,1,0:T(8,128)(2,1)S(1)}, u32[]{:S(2)}, u32[]{:S(2)}) collective-permute-start(bf16[4,128,256]{2,1,0:T(8,128)(2,1)S(1)} %copy-done.25), channel_id=1, source_target_pairs={{0,66},{2,64},{64,2},{66,0},{1,67},{3,65},{65,3},{67,1},{4,70},{6,... | collective-permute-start | bytes 786440 | tf_op jit(solution)/shard_map/ppermute | solution.py:274
  20.4 24.1 %collective-permute-start.2 = (bf16[4,128,256]{2,1,0:T(8,128)(2,1)S(1)}, bf16[4,128,256]{2,1,0:T(8,128)(2,1)S(1)}, u32[]{:S(2)}, u32[]{:S(2)}) collective-permute-start(bf16[4,128,256]{2,1,0:T(8,128)(2,1)S(1)} %copy-done.23), channel_id=1, source_target_pairs={{0,67},{1,66},{2,65},{3,64},{64,3},{65,2},{66,1},{67,0},{4,71},{5,... | collective-permute-start | bytes 786440 | tf_op jit(solution)/shard_map/ppermute | solution.py:275
  50.5 18.1 %collective-permute-start.6 = (bf16[256,1280]{1,0:T(8,128)(2,1)S(1)}, bf16[256,1280]{1,0:T(8,128)(2,1)S(1)}, u32[]{:S(2)}, u32[]{:S(2)}) collective-permute-start(bf16[256,1280]{1,0:T(8,128)(2,1)S(1)} %copy-done.17), channel_id=1, source_target_pairs={{0,66},{2,64},{64,2},{66,0},{1,67},{3,65},{65,3},{67,1},{4,70},{6,... | collective-permute-start | bytes 1966088 | tf_op jit(solution)/shard_map/ppermute | solution.py:305
  56.9 11.8 %collective-permute-start.7 = (bf16[128,1280]{1,0:T(8,128)(2,1)S(1)}, bf16[128,1280]{1,0:T(8,128)(2,1)S(1)}, u32[]{:S(2)}, u32[]{:S(2)}) collective-permute-start(bf16[128,1280]{1,0:T(8,128)(2,1)S(1)} %get-tuple-element.87), channel_id=1, source_target_pairs={{0,4},{4,8},{8,12},{12,0},{1,5},{5,9},{9,13},{13,1},{2,6},{6,10},{... | collective-permute-start | bytes 983048 | tf_op jit(solution)/shard_map/ppermute | solution.py:333
  68.7 16.9 %collective-permute-start.9 = (bf16[128,1280]{1,0:T(8,128)(2,1)}, bf16[128,1280]{1,0:T(8,128)(2,1)}, u32[]{:S(2)}, u32[]{:S(2)}) collective-permute-start(bf16[128,1280]{1,0:T(8,128)(2,1)} %get-tuple-element.93), channel_id=1, source_target_pairs={{0,8},{4,12},{8,0},{12,4},{1,9},{5,13},{9,1},{13,5},{2,10},{6,14},... | collective-permute-start | bytes 983048 | tf_op jit(solution)/shard_map/ppermute | solution.py:333
  71.8 16.5 %collective-permute-start.10 = (bf16[128,1280]{1,0:T(8,128)(2,1)}, bf16[128,1280]{1,0:T(8,128)(2,1)}, u32[]{:S(2)}, u32[]{:S(2)}) collective-permute-start(bf16[128,1280]{1,0:T(8,128)(2,1)} %get-tuple-element.94), channel_id=1, source_target_pairs={{0,12},{4,0},{8,4},{12,8},{1,13},{5,1},{9,5},{13,9},{2,14},{6,2},{... | collective-permute-start | bytes 983048 | tf_op jit(solution)/shard_map/ppermute | solution.py:333
  76.3 27.8 %collective-permute-start.13 = (bf16[128,1280]{1,0:T(8,128)(2,1)}, bf16[128,1280]{1,0:T(8,128)(2,1)S(1)}, u32[]{:S(2)}, u32[]{:S(2)}) collective-permute-start(bf16[128,1280]{1,0:T(8,128)(2,1)} %get-tuple-element.100), channel_id=1, source_target_pairs={{0,4},{4,8},{8,12},{12,0},{1,5},{5,9},{9,13},{13,1},{2,6},{6,10},{... | collective-permute-start | bytes 983048 | tf_op jit(solution)/shard_map/ppermute | solution.py:333
  77.2 26.9 %collective-permute-start.14 = (bf16[128,1280]{1,0:T(8,128)(2,1)}, bf16[128,1280]{1,0:T(8,128)(2,1)S(1)}, u32[]{:S(2)}, u32[]{:S(2)}) collective-permute-start(bf16[128,1280]{1,0:T(8,128)(2,1)} %get-tuple-element.101), channel_id=1, source_target_pairs={{0,8},{4,12},{8,0},{12,4},{1,9},{5,13},{9,1},{13,5},{2,10},{6,14},... | collective-permute-start | bytes 983048 | tf_op jit(solution)/shard_map/ppermute | solution.py:333
  78.4 25.8 %collective-permute-start.15 = (bf16[128,1280]{1,0:T(8,128)(2,1)}, bf16[128,1280]{1,0:T(8,128)(2,1)}, u32[]{:S(2)}, u32[]{:S(2)}) collective-permute-start(bf16[128,1280]{1,0:T(8,128)(2,1)} %get-tuple-element.102), channel_id=1, source_target_pairs={{0,12},{4,0},{8,4},{12,8},{1,13},{5,1},{9,5},{13,9},{2,14},{6,2},{... | collective-permute-start | bytes 983048 | tf_op jit(solution)/shard_map/ppermute | solution.py:333
  90.3 8.7 %collective-permute-start.11 = (bf16[128,640]{1,0:T(8,128)(2,1)S(1)}, bf16[128,640]{1,0:T(8,128)(2,1)S(1)}, u32[]{:S(2)}, u32[]{:S(2)}) collective-permute-start(bf16[128,640]{1,0:T(8,128)(2,1)S(1)} %get-tuple-element.95.refs_2_), channel_id=1, source_target_pairs={{0,32},{16,48},{32,0},{48,16},{1,33},{17,49},{33,1},{49,17},{2,34}... | collective-permute-start | bytes 491528 | tf_op jit(solution)/shard_map/ppermute | solution.py:366
  93.2 7.8 %collective-permute-start.12 = (bf16[128,640]{1,0:T(8,128)(2,1)S(1)}, bf16[128,640]{1,0:T(8,128)(2,1)S(1)}, u32[]{:S(2)}, u32[]{:S(2)}) collective-permute-start(bf16[128,640]{1,0:T(8,128)(2,1)S(1)} %get-tuple-element.97.refs_3_), channel_id=1, source_target_pairs={{0,16},{16,32},{32,48},{48,0},{1,17},{17,33},{33,49},{49,1},{2,18}... | collective-permute-start | bytes 491528 | tf_op jit(solution)/shard_map/ppermute | solution.py:366
  118.1 31.4 %collective-permute-start.23 = (bf16[128,2560]{1,0:T(8,128)(2,1)}, bf16[128,2560]{1,0:T(8,128)(2,1)}, u32[]{:S(2)}, u32[]{:S(2)}) collective-permute-start(bf16[128,2560]{1,0:T(8,128)(2,1)} %get-tuple-element.125), channel_id=1, source_target_pairs={{0,48},{16,0},{32,16},{48,32},{1,49},{17,1},{33,17},{49,33},{2,50}... | collective-permute-start | bytes 1966088 | tf_op jit(solution)/shard_map/ppermute | solution.py:393
  120.5 29.0 %collective-permute-start.24 = (bf16[128,2560]{1,0:T(8,128)(2,1)}, bf16[128,2560]{1,0:T(8,128)(2,1)}, u32[]{:S(2)}, u32[]{:S(2)}) collective-permute-start(bf16[128,2560]{1,0:T(8,128)(2,1)} %get-tuple-element.126), channel_id=1, source_target_pairs={{0,32},{16,48},{32,0},{48,16},{1,33},{17,49},{33,1},{49,17},{2,34}... | collective-permute-start | bytes 1966088 | tf_op jit(solution)/shard_map/ppermute | solution.py:393
  121.2 31.9 %collective-permute-start.25 = (bf16[128,2560]{1,0:T(8,128)(2,1)}, bf16[128,2560]{1,0:T(8,128)(2,1)}, u32[]{:S(2)}, u32[]{:S(2)}) collective-permute-start(bf16[128,2560]{1,0:T(8,128)(2,1)} %get-tuple-element.127), channel_id=1, source_target_pairs={{0,16},{16,32},{32,48},{48,0},{1,17},{17,33},{33,49},{49,1},{2,18}... | collective-permute-start | bytes 1966088 | tf_op jit(solution)/shard_map/ppermute | solution.py:393
  125.3 22.5 %collective-permute-start.22 = (bf16[2,160,640]{2,1,0:T(8,128)(2,1)}, bf16[2,160,640]{2,1,0:T(8,128)(2,1)}, u32[]{:S(2)}, u32[]{:S(2)}) collective-permute-start(bf16[2,160,640]{2,1,0:T(8,128)(2,1)} %get-tuple-element.122), channel_id=1, source_target_pairs={{0,4},{4,8},{8,12},{12,0},{1,5},{5,9},{9,13},{13,1},{2,6},{6,10},{... | collective-permute-start | bytes 1228808 | tf_op jit(solution)/shard_map/ppermute | solution.py:425
  145.1 18.5 %collective-permute-start.29 = (bf16[2,160,640]{2,1,0:T(8,128)(2,1)}, bf16[2,160,640]{2,1,0:T(8,128)(2,1)}, u32[]{:S(2)}, u32[]{:S(2)}) collective-permute-start(bf16[2,160,640]{2,1,0:T(8,128)(2,1)} %copy-done.20), channel_id=1, source_target_pairs={{0,8},{4,12},{8,0},{12,4},{1,9},{5,13},{9,1},{13,5},{2,10},{6,14},... | collective-permute-start | bytes 1228808 | tf_op jit(solution)/shard_map/ppermute | solution.py:425
  147.8 15.8 %collective-permute-start.30 = (bf16[2,160,640]{2,1,0:T(8,128)(2,1)}, bf16[2,160,640]{2,1,0:T(8,128)(2,1)}, u32[]{:S(2)}, u32[]{:S(2)}) collective-permute-start(bf16[2,160,640]{2,1,0:T(8,128)(2,1)} %copy-done.19), channel_id=1, source_target_pairs={{0,12},{4,0},{8,4},{12,8},{1,13},{5,1},{9,5},{13,9},{2,14},{6,2},{... | collective-permute-start | bytes 1228808 | tf_op jit(solution)/shard_map/ppermute | solution.py:425
  160.9 17.4 %collective-permute-start.35 = (bf16[128,1280]{1,0:T(8,128)(2,1)}, bf16[128,1280]{1,0:T(8,128)(2,1)}, u32[]{:S(2)}, u32[]{:S(2)}) collective-permute-start(bf16[128,1280]{1,0:T(8,128)(2,1)} %copy-done.21), channel_id=1, source_target_pairs={{0,64},{64,0},{1,65},{65,1},{2,66},{66,2},{3,67},{67,3},{4,68},{68... | collective-permute-start | bytes 983048 | tf_op jit(solution)/shard_map/ppermute | solution.py:441
  163.0 7.2 %collective-permute-start.36 = (f32[1,128]{1,0:T(1,128)S(1)}, f32[1,128]{1,0:T(1,128)S(1)}, u32[]{:S(2)}, u32[]{:S(2)}) collective-permute-start(f32[1,128]{1,0:T(1,128)S(1)} %bitcast.40), channel_id=1, source_target_pairs={{0,64},{64,0},{1,65},{65,1},{2,66},{66,2},{3,67},{67,3},{4,68},{68... | collective-permute-start | bytes 1544 | tf_op jit(solution)/shard_map/ppermute | solution.py:440
  165.6 7.9 %collective-permute-start.33 = (f32[21,128]{1,0:T(8,128)S(1)}, f32[21,128]{1,0:T(8,128)S(1)}, u32[]{:S(2)}, u32[]{:S(2)}) collective-permute-start(f32[21,128]{1,0:T(8,128)S(1)} %add_add_fusion), channel_id=1, source_target_pairs={{0,12},{4,0},{8,4},{12,8},{1,13},{5,1},{9,5},{13,9},{2,14},{6,2},{... | collective-permute-start | bytes 32264 | tf_op jit(solution)/shard_map/ppermute | solution.py:455
  170.2 7.3 %collective-permute-start.34 = (bf16[160,640]{1,0:T(8,128)(2,1)S(1)}, bf16[160,640]{1,0:T(8,128)(2,1)S(1)}, u32[]{:S(2)}, u32[]{:S(2)}) collective-permute-start(bf16[160,640]{1,0:T(8,128)(2,1)S(1)} %get-tuple-element.134), channel_id=1, source_target_pairs={{0,2},{2,0},{1,3},{3,1},{4,6},{6,4},{5,7},{7,5},{8,10},{10,8},{9,1... | collective-permute-start | bytes 614408 | tf_op jit(solution)/shard_map/ppermute | solution.py:454
  (46 other events, 276.2 us)
Sparse Core Ops, SparseCore 0:
  14.9 37.6 all-gather.1

commit v3 on v2

v3 whole, which is shorter than its diff:
```python
import math

import jax
import jax.numpy as jnp
from jax import lax
from jax.experimental import pallas as pl
from jax.experimental.pallas import tpu as pltpu
from jax.sharding import Mesh
from jax.sharding import PartitionSpec as P

D_T = 5120
D_S = 2560
HD = 128
HQ = 32
KVH = 4

BF = jnp.bfloat16
F32 = jnp.float32
NX = 4
NZ = 4
MP = ("x", "zh", "core")


def ring(n, k):
    return [(i, (i + k) % n) for i in range(n)]


WRAP = [(g * 2 + z, (1 - g) * 2 + (1 - z)) for g in range(2) for z in range(2)]
MIB = 32
COST = 1


def block_of(stage, core):
    return 2 + core if stage == 0 else 1 - core


def to_owner(stage, cross):
    return [
        (d * 2 + c, (d + block_of(stage, c)) % 4 * 2 + (1 - c if cross else c))
        for d in range(4)
        for c in range(2)
    ]


def whole(shape):
    return pl.BlockSpec(shape, lambda i, s: (0,) * len(shape))


def call(kernel, scalars, ins, outs, name, scratch=(), mib=MIB):
    outs = pl.pallas_call(
        kernel,
        out_shape=[jax.ShapeDtypeStruct(shape, t) for shape, t in outs],
        grid_spec=pltpu.PrefetchScalarGridSpec(
            num_scalar_prefetch=1,
            grid=(1,),
            in_specs=[spec for _, spec in ins],
            out_specs=[whole(shape) for shape, _ in outs],
            scratch_shapes=list(scratch),
        ),
        compiler_params=pltpu.CompilerParams(vmem_limit_bytes=mib * 1024 * 1024),
        cost_estimate=pl.CostEstimate(flops=COST, bytes_accessed=COST, transcendentals=0),
        name=name,
    )(scalars.value, *[a for a, _ in ins])
    scalars.after(outs[0])
    return outs


class Ordered:
    def __init__(self, value):
        self.value = value

    def after(self, array):
        self.value, _ = lax.optimization_barrier((self.value, array))


X, ZC, G, D, ZH, C, FIRST, LENGTHS = range(8)


def pick_kernel(s, q, w0, w1, w2, w3, res0, res1, q_out, w_out, res_out):
    q_out[...] = q[...]
    for i, w in enumerate((w0, w1, w2, w3)):
        w_out[:, i * 640 : i * 640 + 640] = w[...]
    res_out[:, :640] = res0[...]
    res_out[:, 640:] = res1[...]


def pick_weights_kernel(s, own0, own1, other, out0, out1):
    for i, (own, out) in enumerate(((own0, out0), (own1, out1))):
        out[:256] = own[...]
        out[256:] = other[:, i * 640 : i * 640 + 640]


def attend_kernel(s, q_ref, k_ref, v_ref, out_ref, vext):
    vext[:, :HD] = v_ref[...]
    vext[:, HD:] = jnp.ones((v_ref.shape[0], HD), BF)
    scale = HD ** (-0.5) * math.log2(math.e)
    rows = lax.broadcasted_iota(jnp.int32, (256, 512), 0) % 128
    cols = lax.broadcasted_iota(jnp.int32, (256, 512), 1)
    behind = cols - rows
    for part in range(NX):
        length = 512 * (part + 1)
        for block in range(2):
            q = q_ref[part, block]
            q = jnp.concatenate([q[:, :HD], q[:, HD:]], axis=0)
            scores = lax.dot_general(
                q, k_ref[:length, :], (((1,), (1,)), ((), ())), preferred_element_type=F32
            )
            allowed = behind <= (s[ZH] * 2 + block) * 128
            last = jnp.where(allowed, scores[:, length - 512 :], -1e30)
            if part:
                scores = jnp.concatenate([scores[:, : length - 512], last], axis=1)
            else:
                scores = last
            top = jnp.max(scores, axis=-1, keepdims=True)
            probs = jnp.exp2((scores - top) * scale).astype(BF)
            mixed = jnp.dot(probs, vext[:length, :], preferred_element_type=F32)
            mixed = (mixed[:, :HD] / mixed[:, HD:]).astype(BF)
            at = (block * NX + part) * 128
            out_ref[at : at + 128, :HD] = mixed[:128]
            out_ref[at : at + 128, HD:] = mixed[128:]


def project_kernel(s, ctx_a, ctx_ac, ctx_b, ctx_bc, w_a, w_ac, w_z, own, o1, o2, o3, total):
    def dot(a, b):
        return jnp.dot(a[...], b, preferred_element_type=F32)

    total[...] = (
        dot(ctx_a, w_a[...])
        + dot(ctx_ac, w_ac[...])
        + dot(ctx_b, w_z[:256])
        + dot(ctx_bc, w_z[256:])
    )
    for j, out in enumerate((own, o1, o2, o3)):
        for block in range(2):
            at = pl.multiple_of((block * NX + (s[X] + j) % NX) * 128, 128)
            out[block] = total[pl.ds(at, 128), :].astype(out.dtype)


def finish_kernel(s, own, r1, r2, r3, res, res_other, *refs):
    def rows(at):
        parts = own[at] + r1[at].astype(F32) + r2[at].astype(F32) + r3[at].astype(F32)
        return parts

    same, cross = refs[-2], refs[-1]
    same[...] = (res[...].astype(F32) + rows(s[C])).astype(BF)
    cross[...] = (res_other[...].astype(F32) + rows(1 - s[C])).astype(BF)


def assemble_kernel(s, same0, same1, got0, got1, target):
    for piece, stage, core in (
        (same0, 0, s[C]),
        (same1, 1, s[C]),
        (got0, 0, 1 - s[C]),
        (got1, 1, 1 - s[C]),
    ):
        at = pl.multiple_of(((s[D] + block_of(stage, core)) % 4) * 640, 128)
        target[:, pl.ds(at, 640)] = piece[...]


def three_parts(value):
    high = value.astype(BF)
    rest = value - high.astype(F32)
    middle = rest.astype(BF)
    low = rest - middle.astype(F32)
    lane = lax.broadcasted_iota(jnp.int32, (value.shape[0], 128), 1)
    wide = jnp.where(lane == 0, high.astype(F32), jnp.where(lane == 1, middle.astype(F32), 0.0))
    return jnp.where(lane == 2, low, wide).astype(BF)


def compare_kernel(s, pred, normed, proj, sm0, cr0, sm1, cr1, gp, gain, loss, *refs):
    first_of = refs[:3]
    last_of = refs[3:6]
    own_first, own_last, own_inner, grad, inner = refs[6:]
    square = jnp.zeros((1, 640), F32)
    for got, stage, core in (
        (sm0, 0, s[C]),
        (cr0, 0, 1 - s[C]),
        (sm1, 1, s[C]),
        (cr1, 1, 1 - s[C]),
    ):
        seq = (s[D] + 4 - block_of(stage, core)) % 4
        at = pl.multiple_of(seq * 128, 128)
        live = lax.broadcasted_iota(jnp.int32, (128, 640), 0) < s[LENGTHS + seq] - s[FIRST]
        here = pred[pl.ds(at, 128), :]
        diff = jnp.where(live, here - got[...].astype(F32), 0.0)
        square = square + jnp.sum(diff * diff, axis=0, keepdims=True)
        rounded = diff.astype(BF)
        gp[pl.ds(at, 128), :] = rounded
        inner[pl.ds(at, 128), :] = jnp.sum(rounded.astype(F32) * here, axis=-1, keepdims=True)
    loss[...] = square
    for far, outs, own in ((1, first_of, own_first), (0, last_of, own_last)):
        for part in range(2):
            half = s[G] if far == 0 else 1 - s[G]
            base = pl.multiple_of(half * 1280 + part * 640, 128)
            cols = slice(part * 640, part * 640 + 640)
            grad[...] = lax.dot_general(
                gp[...],
                proj[pl.ds(base, 640), :],
                (((1,), (1,)), ((), ())),
                preferred_element_type=F32,
            )
            gain[:, pl.ds(base, 640)] = jnp.sum(
                grad[...] * normed[:, pl.ds(base, 640)].astype(F32), axis=0, keepdims=True
            )
            for k in range(4):
                at = pl.multiple_of(((s[D] + 4 - k) % 4) * 128, 128)
                rows = grad[pl.ds(at, 128), :]
                if k == 0:
                    own[:, cols] = rows
                else:
                    outs[k - 1][:, cols] = rows.astype(BF)
    for k in range(4):
        at = pl.multiple_of(((s[D] + 4 - k) % 4) * 128, 128)
        if k == 0:
            own_inner[...] = inner[pl.ds(at, 128), :]
        else:
            first_of[k - 1][:, 1280:] = three_parts(inner[pl.ds(at, 128), :])


def added(own, parts, inner=None):
    total, inner_sum = own[...], None if inner is None else inner[...]
    for r in parts:
        total = total + r[:, :1280].astype(F32)
        if inner is not None:
            inner_sum = inner_sum + jnp.sum(r[:, 1280:].astype(F32), axis=-1, keepdims=True)
    return total, inner_sum


def combine_kernel(s, own, own_inner, r1, r2, r3, sent, inner):
    total, inner_sum = added(own, (r1, r2, r3), own_inner)
    sent[:, :1280] = total.astype(BF)
    sent[:, 1280:] = three_parts(inner_sum)
    inner[...] = inner_sum


def hidden_kernel(s, own, r1, r2, r3, inner, got, hidden, inverse_rms, gain, out):
    total, _ = added(own, (r1, r2, r3))
    inner_sum = inner[...] + jnp.sum(got[:, 1280:].astype(F32), axis=-1, keepdims=True)
    grad = total + got[:, :1280].astype(F32)
    scale = inverse_rms[...]
    unit = hidden[...].astype(F32) * scale
    out[...] = scale * (grad * gain[...] - unit * (inner_sum / D_S))


def gproj_kernel(s, normed, gp, sent, kept):
    first = s[C] == 0
    for part in range(NX):
        total = lax.dot_general(
            normed[:, part * 640 : part * 640 + 640],
            gp[...],
            (((0,), (0,)), ((), ())),
            preferred_element_type=F32,
        )
        for z in range(2):
            low = total[z * 320 : z * 320 + 160]
            high = total[z * 320 + 160 : z * 320 + 320]
            sent[part, z] = jnp.where(first, high, low).astype(BF)
            kept[part, z] = jnp.where(first, low, high)


def gproj_add_kernel(s, kept, recv, own, o1, o2, o3):
    for j, out in enumerate((own, o1, o2, o3)):
        at = (s[X] + j) % NX
        out[...] = (kept[at] + recv[at].astype(F32)).astype(out.dtype)


def gproj_sum_kernel(s, own, r1, r2, r3, sent, kept):
    z = s[ZH]

    def total(at):
        return own[at] + r1[at].astype(F32) + r2[at].astype(F32) + r3[at].astype(F32)

    sent[...] = total(1 - z).astype(BF)
    kept[...] = total(z)


def sum_over(array, axis, n):
    got = [lax.ppermute(array, axis, ring(n, j)) for j in range(1, n)]
    got = lax.optimization_barrier(got)
    return sum(got, array)


def body(
    queries, keys, values, out_weight, residual, student_hidden, norm_gain, projection, lengths
):
    g, d = lax.axis_index("grp"), lax.axis_index("dp")
    x, zh, c = lax.axis_index("x"), lax.axis_index("zh"), lax.axis_index("core")
    zc = zh * 2 + c
    m = x * 4 + zc
    half = D_T // 2
    blk = D_T // 8
    rows = D_S // 16
    width = D_S // 2
    barrier = lax.optimization_barrier
    scalars = Ordered(
        jnp.concatenate([jnp.stack([x, zc, g, d, zh, c, m * 128]).astype(jnp.int32), lengths])
    )
    swap = ring(2, 1)
    stages = (0, 1)

    def column(stage, near, mine, n):
        def index(i, s):
            core = s[C] if mine else 1 - s[C]
            side = s[G] if near else 1 - s[G]
            return (0, side * 4 + (s[D] + block_of(stage, core)) % 4)

        return pl.BlockSpec((n, blk), index)

    q5 = queries.reshape(NX, 4, 128, 256)
    q_block = (NX, 2, 128, 256)
    along_z, w_out, res_out = call(
        pick_kernel,
        scalars,
        [
            (q5, pl.BlockSpec(q_block, lambda i, s: (0, 1 - s[ZH], 0, 0))),
            *[(out_weight, column(st, near, False, 256)) for near in (False, True) for st in stages],
            *[(residual[0], column(st, True, False, 128)) for st in stages],
        ],
        [(q_block, BF), ((256, 4 * blk), BF), ((128, 2 * blk), BF)],
        "pick",
    )
    along_z = lax.ppermute(along_z, ("grp", "zh"), WRAP)
    w_other = lax.ppermute(w_out, "core", swap)
    res_other = lax.ppermute(res_out, "core", swap)

    hidden, _ = barrier((student_hidden[0], w_out))
    hidden = hidden.astype(F32)
    inverse_rms = lax.rsqrt(jnp.mean(hidden * hidden, axis=-1, keepdims=True) + 1e-06)
    normed = (hidden * inverse_rms * norm_gain).astype(BF)
    scalars.after(normed)
    normed = lax.all_gather(normed, "dp", axis=0, tiled=True)

    def attend(q, spec, name):
        return call(
            attend_kernel,
            scalars,
            [
                (q, spec),
                (keys[0], pl.BlockSpec((2048, HD), lambda i, s: (0, s[X]))),
                (values[0], pl.BlockSpec((2048, HD), lambda i, s: (0, s[X]))),
            ],
            [((1024, 256), BF)],
            name,
            scratch=[pltpu.VMEM((2048, 2 * HD), BF)],
            mib=40,
        )[0]

    ctx_a = attend(q5, pl.BlockSpec(q_block, lambda i, s: (0, s[ZH], 0, 0)), "attend_chip")
    w_z = call(
        pick_weights_kernel,
        scalars,
        [
            *[(out_weight, column(st, False, True, 256)) for st in stages],
            (w_other, pl.BlockSpec((256, 2 * blk), lambda i, s: (0, 0))),
        ],
        [((512, blk), BF)] * 2,
        "pick_weights",
    )
    w_z = [lax.ppermute(w, ("grp", "zh"), WRAP) for w in w_z]
    ctx_ac = lax.ppermute(ctx_a, "core", swap)
    along_z, _ = barrier((along_z, ctx_a))
    ctx_b = attend(along_z, whole(q_block), "attend_next")
    ctx_bc = lax.ppermute(ctx_b, "core", swap)

    projected = []
    for st in stages:
        own, *outs = call(
            project_kernel,
            scalars,
            [
                *[(ctx, whole((1024, 256))) for ctx in (ctx_a, ctx_ac, ctx_b, ctx_bc)],
                (out_weight, column(st, True, True, 256)),
                (w_other, pl.BlockSpec((256, blk), lambda i, s, st=st: (0, 2 + st))),
                (w_z[st], whole((512, blk))),
            ],
            [((2, 128, blk), F32)] + [((2, 128, blk), BF)] * 3,
            f"project_{st}",
            scratch=[pltpu.VMEM((1024, blk), F32)],
        )
        if st == 0:
            normed, _ = barrier((normed, own))
            predicted = jnp.dot(normed, projection, preferred_element_type=F32)
            scalars.after(predicted)
        projected.append((own, {j: lax.ppermute(outs[j - 1], "x", ring(NX, j)) for j in (2, 1, 3)}))

    compared, same, cross = [], [], []
    for st in stages:
        own, got = projected[st]
        done_same, done_cross = call(
            finish_kernel,
            scalars,
            [
                (own, whole((2, 128, blk))),
                *[(got[j], whole((2, 128, blk))) for j in (1, 2, 3)],
                (residual[0], column(st, True, True, 128)),
                (res_other, pl.BlockSpec((128, blk), lambda i, s, st=st: (0, st))),
            ],
            [((128, blk), BF)] * 2,
            f"finish_{st}",
        )
        same.append(done_same)
        cross.append(done_cross)
        compared.append(lax.ppermute(done_same, ("dp", "core"), to_owner(st, False)))
        compared.append(lax.ppermute(done_cross, ("dp", "core"), to_owner(st, True)))

    first_shape, last_shape = (128, width + 128), (128, width)
    gp, gain, loss, *backs, own_first, own_last, own_inner = call(
        compare_kernel,
        scalars,
        [
            (predicted, whole((512, blk))),
            (normed, whole((512, D_S))),
            (projection, whole((D_S, blk))),
            *[(a, whole((128, blk))) for a in compared],
        ],
        [((512, blk), BF), ((1, D_S), F32), ((1, blk), F32)]
        + [(first_shape, BF)] * 3
        + [(last_shape, BF)] * 3
        + [(last_shape, F32), (last_shape, F32), ((128, 1), F32)],
        "compare",
        scratch=[pltpu.VMEM((512, blk), F32), pltpu.VMEM((512, 1), F32)],
    )
    back_first = [lax.ppermute(backs[k - 1], "dp", ring(4, 4 - k)) for k in (1, 2, 3)]

    live_count = jnp.sum(lengths).astype(F32)
    part = (NX, 2, rows, blk)
    sent, kept = call(
        gproj_kernel,
        scalars,
        [(normed, whole((512, D_S))), (gp, whole((512, blk)))],
        [(part, BF), (part, F32)],
        "gproj",
    )
    recv = lax.ppermute(sent, "core", swap)
    small = jnp.concatenate([gain[0] / norm_gain, jnp.full((128,), jnp.sum(loss))]).reshape(-1, 128)
    small, _ = barrier((small, sent))
    small = sum_over(small, "dp", 4)
    own, *outs = call(
        gproj_add_kernel,
        scalars,
        [(kept, whole(part)), (recv, whole(part))],
        [(part[1:], F32)] + [(part[1:], BF)] * 3,
        "gproj_add",
    )
    got = {j: lax.ppermute(outs[j - 1], "x", ring(NX, j)) for j in (2, 1, 3)}
    *lasts, small = barrier((*backs[3:6], small))
    back_last = [lax.ppermute(lasts[k - 1], "dp", ring(4, 4 - k)) for k in (1, 2, 3)]
    small = small + lax.ppermute(small, "core", swap)
    small = sum_over(small, ("grp", "zh"), NZ)

    sent, inner = call(
        combine_kernel,
        scalars,
        [
            (own_first, whole(last_shape)),
            (own_inner, whole((128, 1))),
            *[(r, whole(first_shape)) for r in back_first],
        ],
        [(first_shape, BF), ((128, 1), F32)],
        "combine",
    )
    half_recv = lax.ppermute(sent, "grp", swap)
    cross = [lax.ppermute(a, "core", swap) for a in barrier((*cross, sent))[:2]]
    (target,) = call(
        assemble_kernel,
        scalars,
        [(a, whole((128, blk))) for a in (*same, *cross)],
        [((128, half), BF)],
        "assemble",
    )
    gsent, gkept = call(
        gproj_sum_kernel,
        scalars,
        [(own, whole(part[1:]))] + [(got[j], whole(part[1:])) for j in (1, 2, 3)],
        [((rows, blk), BF), ((rows, blk), F32)],
        "gproj_sum",
    )
    small, _ = barrier((small, gsent))
    gsent = lax.ppermute(gsent, "zh", swap)
    small = sum_over(small, "x", NX).reshape(-1)
    scalars.after(small)
    (grad_hidden,) = call(
        hidden_kernel,
        scalars,
        [
            (own_last, whole(last_shape)),
            *[(r, whole(last_shape)) for r in back_last],
            (inner, whole((128, 1))),
            (half_recv, whole(first_shape)),
            (student_hidden[0], pl.BlockSpec((128, width), lambda i, s: (0, s[G]))),
            (inverse_rms, whole((128, 1))),
            (norm_gain.reshape(1, D_S), pl.BlockSpec((1, width), lambda i, s: (0, s[G]))),
        ],
        [(last_shape, F32)],
        "hidden",
    )
    grad_proj = (gkept + gsent.astype(F32)) / live_count
    distill_loss = small[D_S] / (live_count * D_T)
    grad_gain = lax.dynamic_slice_in_dim(small, g * width, width, 0) / live_count
    return (target[None], distill_loss, grad_proj, grad_gain, grad_hidden[None])


def solution(mesh):
    fine = Mesh(mesh.devices.reshape(2, 4, 4, 2, 2), ("grp", "dp", "x", "zh", "core"))
    in_specs = (
        P("dp", None, MP),
        P("dp", None, None),
        P("dp", None, None),
        P(MP, None),
        P("dp", MP, None),
        P("dp", MP, None),
        P(),
        P(None, ("grp", "dp")),
        P(),
    )
    out_specs = (P("dp", MP, "grp"), P(), P(MP, ("grp", "dp")), P("grp"), P("dp", MP, "grp"))
    return jax.shard_map(body, mesh=fine, in_specs=in_specs, out_specs=out_specs, check_vma=False)
```

time: 190 us -> 182 us (0.958)
  waiting for transfers between devices: 59 us -> 41.1 us
  local copies, waits for them, and re-layouts: 10.4 us -> 19.7 us
  Pallas kernels: 37.4 us -> 40.8 us
  other arithmetic: 8.05 us -> 5.01 us
  starting transfers between devices: 50.2 us -> 52.9 us
    ppermute x24 -> x28, waiting for transfers between devices: 54.2 us -> 31.2 us  [the longest x9 12.1 us: sum_over(): got = [lax.ppermute(array, axis, ring(n, j)) for j in range(1, n)]]
    unnamed x64 -> x82, local copies, waits for them, and re-layouts: 9.1 us -> 17.7 us
    ppermute x6, waiting for transfers between devices: 2.7 us -> 7.74 us  [body(): lax.ppermute(outs[j - 1], 'x', ring(NX, j))]
    pallas_call x13 -> x15, Pallas kernels: 37.4 us -> 40.8 us  [call(): pl.pallas_call(kernel, out_shape=[jax.ShapeDtypeStruct(shape, t) for shap...]
    ppermute x3, starting transfers between devices: 4.87 us -> 7.52 us  [body(): got = {j: lax.ppermute(outs[j - 1], 'x', ring(NX, j)) for j in (2, 1, 3)}]
    mul x1 -> x0, other arithmetic: 2.15 us -> none  [body(): scaled_rows = unit_rows * norm_gain]
    broadcast_in_dim x1 -> x0, other arithmetic: 2.06 us -> none  [body(): return (target[None], distill_loss, grad_proj, grad_gain, grad_hidden[None])]
    ppermute x24 -> x28, starting transfers between devices: 31.8 us -> 33 us  [the longest x9 8.55 us: sum_over(): got = [lax.ppermute(array, axis, ring(n, j)) for j in range(1, n)]]
  transfers between devices with their start and end apart: 38 -> 42, of which waited for: 19 -> 15; matrix products, arithmetic and copies ran while one was open for 5% -> 5% of each run, Pallas kernels for 15% -> 17%
where the time goes in v3:
time: 182 us; the launch traced here: 181 us
  starting transfers between devices  52.9 us (29%)
  waiting for transfers between devices  41.1 us (23%)
  Pallas kernels  40.8 us (22%)
  local copies, waits for them, and re-layouts  19.7 us (11%)
  between operations  17 us (9%)
  matrix products  5.05 us (3%)
  other arithmetic  5.01 us (3%)
    pallas_call x15, Pallas kernels, call(): pl.pallas_call(kernel, out_shape=[jax.ShapeDtypeStruct(shape, t) for shap...  40.8 us
    unnamed x82, local copies, waits for them, and re-layouts  17.7 us
    ppermute x9, waiting for transfers between devices, sum_over(): got = [lax.ppermute(array, axis, ring(n, j)) for j in range(1, n)]  12.1 us
    ppermute x6, starting transfers between devices, body(): lax.ppermute(outs[j - 1], 'x', ring(NX, j))  9.72 us
    ppermute x9, starting transfers between devices, sum_over(): got = [lax.ppermute(array, axis, ring(n, j)) for j in range(1, n)]  8.55 us
    ppermute x2, waiting for transfers between devices, body(): w_z = [lax.ppermute(w, ('grp', 'zh'), WRAP) for w in w_z]  8.4 us
    ppermute x6, waiting for transfers between devices, body(): lax.ppermute(outs[j - 1], 'x', ring(NX, j))  7.74 us
    ppermute x3, starting transfers between devices, body(): got = {j: lax.ppermute(outs[j - 1], 'x', ring(NX, j)) for j in (2, 1, 3)}  7.52 us
  transfers between devices with their start and end apart: 42, of which 15 were waited for; matrix products, arithmetic and copies ran while one was open for 5% of the time, Pallas kernels for 17%

profile of v3, /device:TPU:0, one launch (start us, length us, event | category | flops | bytes accessed | tf_op | source)
XLA Modules:
  0.0 181.5 jit_solution(783683093738847027)
XLA Ops:
  15.8 4.2 %collective-permute-start.1 = (bf16[4,2,128,256]{3,2,1,0:T(8,128)(2,1)}, bf16[4,2,128,256]{3,2,1,0:T(8,128)(2,1)S(1)}, u32[]{:S(2)}, u32[]{:S(2)}) collective-permute-start(bf16[4,2,128,256]{3,2,1,0:T(8,128)(2,1)} %get-tuple-element.81), channel_id=1, source_target_pairs={{0,66},{2,64},{64,2},{66,0},{1,67},{3,65},{65,3},{67,1},{4,70},{6,... | collective-permute-start | bytes 1572872 | tf_op jit(solution)/shard_map/ppermute | solution.py:322
  24.4 5.0 %attend_chip.1.ctx_a = bf16[1024,256]{1,0:T(8,128)(2,1)S(1)} custom-call(s32[11]{0:T(128)S(1)} %concatenate.6.s, bf16[4,4,128,256]{3,2,1,0:T(8,128)(2,1)S(1)} %bitcast.35, bf16[2048,512]{1,0:T(8,128)(2,1)S(1)} %bitcast.27, bf16[2048,512]{1,0:T(8,128)(2,1)S(1)} %bitcast.29), custom_call_target="tpu_custom_call" | custom-call | flops 1 | bytes 1 | tf_op jit(solution)/shard_map/attend_chip/pallas_call | solution.py:50
  32.7 5.0 %attend_next.1.ctx_b = bf16[1024,256]{1,0:T(8,128)(2,1)S(1)} custom-call(s32[11]{0:T(128)S(1)} %concatenate.6.s, bf16[4,2,128,256]{3,2,1,0:T(8,128)(2,1)S(1)} %collective-permute-done.1.q_ref, bf16[2048,512]{1,0:T(8,128)(2,1)S(1)} %bitcast.28, bf16[2048,512]{1,0:T(8,128)(2,1)S(1)} %bitcast.30), custom_call_target="tpu_custom_call" | custom-call | flops 1 | bytes 1 | tf_op jit(solution)/shard_map/attend_next/pallas_call | solution.py:50
  37.8 3.4 %collective-permute-start.5 = (bf16[512,640]{1,0:T(8,128)(2,1)}, bf16[512,640]{1,0:T(8,128)(2,1)}, u32[]{:S(2)}, u32[]{:S(2)}) collective-permute-start(bf16[512,640]{1,0:T(8,128)(2,1)} %get-tuple-element.95), channel_id=1, source_target_pairs={{0,66},{2,64},{64,2},{66,0},{1,67},{3,65},{65,3},{67,1},{4,70},{6,... | collective-permute-start | bytes 1966088 | tf_op jit(solution)/shard_map/ppermute | solution.py:359
  41.4 8.4 %collective-permute-done.4.w_z = bf16[512,640]{1,0:T(8,128)(2,1)S(1)} collective-permute-done((bf16[512,640]{1,0:T(8,128)(2,1)S(1)}, bf16[512,640]{1,0:T(8,128)(2,1)S(1)}, u32[]{:S(2)}, u32[]{:S(2)}) %collective-permute-start.4) | collective-permute-done | bytes 655392 | tf_op jit(solution)/shard_map/ppermute | solution.py:359
  49.8 3.4 %project_0.1 = (f32[2,128,640]{2,1,0:T(8,128)S(1)}, bf16[2,128,640]{2,1,0:T(8,128)(2,1)}, bf16[2,128,640]{2,1,0:T(8,128)(2,1)}, bf16[2,128,640]{2,1,0:T(8,128)(2,1)}) custom-call(s32[11]{0:T(128)S(1)} %concatenate.6.s, bf16[1024,256]{1,0:T(8,128)(2,1)S(1)} %attend_chip.1.ctx_a, bf16[1024,256]{1,0:T(8,128)(2,1)S(1)} %collective-permute-done.2.ctx_ac, ...), custom_call_target="tpu_custom_call" | custom-call | flops 1 | bytes 1 | tf_op jit(solution)/shard_map/project_0/pallas_call | solution.py:50
  55.5 2.8 %collective-permute-start.7 = (bf16[2,128,640]{2,1,0:T(8,128)(2,1)}, bf16[2,128,640]{2,1,0:T(8,128)(2,1)}, u32[]{:S(2)}, u32[]{:S(2)}) collective-permute-start(bf16[2,128,640]{2,1,0:T(8,128)(2,1)} %get-tuple-element.99), channel_id=1, source_target_pairs={{0,8},{4,12},{8,0},{12,4},{1,9},{5,13},{9,1},{13,5},{2,10},{6,14},... | collective-permute-start | bytes 983048 | tf_op jit(solution)/shard_map/ppermute | solution.py:384
  59.8 5.1 %fusion.4.pred = f32[512,640]{1,0:T(8,128)S(1)} fusion(bf16[512,2560]{1,0:T(8,128)(2,1)} %all-gather.2.cloned.1.call-done.normed, bf16[2560,640]{1,0:T(8,128)(2,1)} %proj.1), kind=kOutput, calls=%fused_computation.13 | convolution fusion | flops 1677721600 | bytes 7208960 | tf_op jit(solution)/shard_map/dot_general | solution.py:382
  64.9 3.6 %project_1.1 = (f32[2,128,640]{2,1,0:T(8,128)S(1)}, bf16[2,128,640]{2,1,0:T(8,128)(2,1)S(1)}, bf16[2,128,640]{2,1,0:T(8,128)(2,1)S(1)}, bf16[2,128,640]{2,1,0:T(8,128)(2,1)S(1)}) custom-call(s32[11]{0:T(128)S(1)} %concatenate.6.s, bf16[1024,256]{1,0:T(8,128)(2,1)S(1)} %copy-done.11, bf16[1024,256]{1,0:T(8,128)(2,1)S(1)} %copy-done.20, ...), custom_call_target="tpu_custom_call" | custom-call | flops 1 | bytes 1 | tf_op jit(solution)/shard_map/project_1/pallas_call | solution.py:50
  74.8 3.2 %collective-permute-start.13 = (bf16[128,640]{1,0:T(8,128)(2,1)S(1)}, bf16[128,640]{1,0:T(8,128)(2,1)S(1)}, u32[]{:S(2)}, u32[]{:S(2)}) collective-permute-start(bf16[128,640]{1,0:T(8,128)(2,1)S(1)} %get-tuple-element.102.same0), channel_id=1, source_target_pairs={{0,32},{1,49},{16,48},{17,1},{32,0},{33,17},{48,16},{49,33},{2,34}... | collective-permute-start | bytes 491528 | tf_op jit(solution)/shard_map/ppermute | solution.py:403
  79.8 6.0 %collective-permute-done.11.r2 = bf16[2,128,640]{2,1,0:T(8,128)(2,1)S(1)} collective-permute-done((bf16[2,128,640]{2,1,0:T(8,128)(2,1)S(1)}, bf16[2,128,640]{2,1,0:T(8,128)(2,1)S(1)}, u32[]{:S(2)}, u32[]{:S(2)}) %collective-permute-start.11) | collective-permute-done | bytes 327712 | tf_op jit(solution)/shard_map/ppermute | solution.py:384
  87.6 3.7 %collective-permute-start.15 = (bf16[128,640]{1,0:T(8,128)(2,1)S(1)}, bf16[128,640]{1,0:T(8,128)(2,1)S(1)}, u32[]{:S(2)}, u32[]{:S(2)}) collective-permute-start(bf16[128,640]{1,0:T(8,128)(2,1)S(1)} %get-tuple-element.107.same1), channel_id=1, source_target_pairs={{0,16},{1,1},{16,32},{17,17},{32,48},{33,33},{48,0},{49,49},{2,18}... | collective-permute-start | bytes 491528 | tf_op jit(solution)/shard_map/ppermute | solution.py:403
  91.3 4.7 %collective-permute-done.15.sm1 = bf16[128,640]{1,0:T(8,128)(2,1)S(1)} collective-permute-done((bf16[128,640]{1,0:T(8,128)(2,1)S(1)}, bf16[128,640]{1,0:T(8,128)(2,1)S(1)}, u32[]{:S(2)}, u32[]{:S(2)}) %collective-permute-start.15) | collective-permute-done | bytes 163872 | tf_op jit(solution)/shard_map/ppermute | solution.py:403
  96.0 4.5 %compare.2 = (bf16[512,640]{1,0:T(8,128)(2,1)S(1)}, f32[1,2560]{1,0:T(1,128)S(1)}, f32[1,640]{1,0:T(1,128)S(1)}, bf16[128,1408]{1,0:T(8,128)(2,1)S(1)}, bf16[128...) custom-call(s32[11]{0:T(128)S(1)} %concatenate.6.s, ...), custom_call_target="tpu_custom_call" | custom-call | flops 1 | bytes 1 | tf_op jit(solution)/shard_map/compare/pallas_call | solution.py:50
  104.4 4.0 %gproj.1 = (bf16[4,2,160,640]{3,2,1,0:T(8,128)(2,1)}, f32[4,2,160,640]{3,2,1,0:T(8,128)S(1)}) custom-call(s32[11]{0:T(128)S(1)} %concatenate.6.s, bf16[512,2560]{1,0:T(8,128)(2,1)S(1)} %copy-done.6, bf16[512,640]{1,0:T(8,128)(2,1)S(1)} %get-tuple-element.111.gp), custom_call_target="tpu_custom_call" | custom-call | flops 1 | bytes 1 | tf_op jit(solution)/shard_map/gproj/pallas_call | solution.py:50
  125.9 3.2 %collective-permute-start.31 = (bf16[2,160,640]{2,1,0:T(8,128)(2,1)S(1)}, bf16[2,160,640]{2,1,0:T(8,128)(2,1)S(1)}, u32[]{:S(2)}, u32[]{:S(2)}) collective-permute-start(bf16[2,160,640]{2,1,0:T(8,128)(2,1)S(1)} %get-tuple-element.142), channel_id=1, source_target_pairs={{0,8},{4,12},{8,0},{12,4},{1,9},{5,13},{9,1},{13,5},{2,10},{6,14},... | collective-permute-start | bytes 1228808 | tf_op jit(solution)/shard_map/ppermute | solution.py:445
  129.2 3.5 %collective-permute-done.18.r1 = bf16[128,1408]{1,0:T(8,128)(2,1)S(1)} collective-permute-done((bf16[128,1408]{1,0:T(8,128)(2,1)}, bf16[128,1408]{1,0:T(8,128)(2,1)S(1)}, u32[]{:S(2)}, u32[]{:S(2)}) %collective-permute-start.18) | collective-permute-done | bytes 360480 | tf_op jit(solution)/shard_map/ppermute | solution.py:423
  132.7 3.3 %collective-permute-start.32 = (bf16[2,160,640]{2,1,0:T(8,128)(2,1)S(1)}, bf16[2,160,640]{2,1,0:T(8,128)(2,1)S(1)}, u32[]{:S(2)}, u32[]{:S(2)}) collective-permute-start(bf16[2,160,640]{2,1,0:T(8,128)(2,1)S(1)} %get-tuple-element.143), channel_id=1, source_target_pairs={{0,12},{4,0},{8,4},{12,8},{1,13},{5,1},{9,5},{13,9},{2,14},{6,2},{... | collective-permute-start | bytes 1228808 | tf_op jit(solution)/shard_map/ppermute | solution.py:445
  136.2 2.4 %collective-permute-start.27 = (f32[21,128]{1,0:T(8,128)S(1)}, f32[21,128]{1,0:T(8,128)S(1)}, u32[]{:S(2)}, u32[]{:S(2)}) collective-permute-start(f32[21,128]{1,0:T(8,128)S(1)} %add.67), channel_id=1, source_target_pairs={{0,2},{2,64},{64,66},{66,0},{1,3},{3,65},{65,67},{67,1},{4,6},{6,6... | collective-permute-start | bytes 32264 | tf_op jit(solution)/shard_map/ppermute | solution.py:278
  141.7 3.6 %collective-permute-start.37 = (bf16[128,1280]{1,0:T(8,128)(2,1)}, bf16[128,1280]{1,0:T(8,128)(2,1)S(1)}, u32[]{:S(2)}, u32[]{:S(2)}) collective-permute-start(bf16[128,1280]{1,0:T(8,128)(2,1)} %get-tuple-element.153), channel_id=1, source_target_pairs={{0,48},{16,0},{32,16},{48,32},{1,49},{17,1},{33,17},{49,33},{2,50}... | collective-permute-start | bytes 983048 | tf_op jit(solution)/shard_map/ppermute | solution.py:447
  151.2 2.9 %collective-permute-done.35 = f32[21,128]{1,0:T(8,128)S(1)} collective-permute-done((f32[21,128]{1,0:T(8,128)S(1)}, f32[21,128]{1,0:T(8,128)S(1)}, u32[]{:S(2)}, u32[]{:S(2)}) %collective-permute-start.35) | collective-permute-done | bytes 10784 | tf_op jit(solution)/shard_map/ppermute | solution.py:278
  154.4 4.9 %collective-permute-done.34 = f32[21,128]{1,0:T(8,128)S(1)} collective-permute-done((f32[21,128]{1,0:T(8,128)S(1)}, f32[21,128]{1,0:T(8,128)S(1)}, u32[]{:S(2)}, u32[]{:S(2)}) %collective-permute-start.34) | collective-permute-done | bytes 10784 | tf_op jit(solution)/shard_map/ppermute | solution.py:278
  160.7 3.5 %collective-permute-done.33 = f32[21,128]{1,0:T(8,128)S(1)} collective-permute-done((f32[21,128]{1,0:T(8,128)S(1)}, f32[21,128]{1,0:T(8,128)S(1)}, u32[]{:S(2)}, u32[]{:S(2)}) %collective-permute-start.33) | collective-permute-done | bytes 10784 | tf_op jit(solution)/shard_map/ppermute | solution.py:278
  166.5 2.9 %hidden.1 = f32[128,1280]{1,0:T(8,128)} custom-call(s32[11]{0:T(128)S(1)} %concatenate.6.s, f32[128,1280]{1,0:T(8,128)S(1)} %get-tuple-element.152.own, bf16[128,1280]{1,0:T(8,128)(2,1)S(1)} %collective-permute-done.37.r1, bf16[128,1280]{1,0:T(8,128)(2,1)} %collective-permute-done.38.r2, bf16[128,1280]{1,0:T(8,128)(2,1)} %collective-permute-done.39.r3, ...), custom_call_target="tpu_custom_call" | custom-call | flops 1 | bytes 1 | tf_op jit(solution)/shard_map/hidden/pallas_call | solution.py:50
  (177 shorter events, 67.4 us)
Async XLA Ops:
  7.2 52.6 %all-gather.2.cloned.1.call-start = ((), (), s32[]{:S(2)}) async-start(), calls=%async_computation | async-start | bytes 3276800 | tf_op jit(solution)/shard_map/all_gather | solution.py:331
  15.7 13.7 %collective-permute-start = (bf16[256,2560]{1,0:T(8,128)(2,1)}, bf16[256,2560]{1,0:T(8,128)(2,1)S(1)}, u32[]{:S(2)}, u32[]{:S(2)}) collective-permute-start(bf16[256,2560]{1,0:T(8,128)(2,1)} %get-tuple-element.83), channel_id=1, source_target_pairs={{0,1},{1,0},{2,3},{3,2},{4,5},{5,4},{6,7},{7,6},{8,9},{9,8},{10,11... | collective-permute-start | bytes 3932168 | tf_op jit(solution)/shard_map/ppermute | solution.py:323
  15.8 16.9 %collective-permute-start.1 = (bf16[4,2,128,256]{3,2,1,0:T(8,128)(2,1)}, bf16[4,2,128,256]{3,2,1,0:T(8,128)(2,1)S(1)}, u32[]{:S(2)}, u32[]{:S(2)}) collective-permute-start(bf16[4,2,128,256]{3,2,1,0:T(8,128)(2,1)} %get-tuple-element.81), channel_id=1, source_target_pairs={{0,66},{2,64},{64,2},{66,0},{1,67},{3,65},{65,3},{67,1},{4,70},{6,... | collective-permute-start | bytes 1572872 | tf_op jit(solution)/shard_map/ppermute | solution.py:322
  31.0 18.8 %collective-permute-start.4 = (bf16[512,640]{1,0:T(8,128)(2,1)S(1)}, bf16[512,640]{1,0:T(8,128)(2,1)S(1)}, u32[]{:S(2)}, u32[]{:S(2)}) collective-permute-start(bf16[512,640]{1,0:T(8,128)(2,1)S(1)} %get-tuple-element.87), channel_id=1, source_target_pairs={{0,66},{2,64},{64,2},{66,0},{1,67},{3,65},{65,3},{67,1},{4,70},{6,... | collective-permute-start | bytes 1966088 | tf_op jit(solution)/shard_map/ppermute | solution.py:359
  37.8 27.1 %collective-permute-start.5 = (bf16[512,640]{1,0:T(8,128)(2,1)}, bf16[512,640]{1,0:T(8,128)(2,1)}, u32[]{:S(2)}, u32[]{:S(2)}) collective-permute-start(bf16[512,640]{1,0:T(8,128)(2,1)} %get-tuple-element.95), channel_id=1, source_target_pairs={{0,66},{2,64},{64,2},{66,0},{1,67},{3,65},{65,3},{67,1},{4,70},{6,... | collective-permute-start | bytes 1966088 | tf_op jit(solution)/shard_map/ppermute | solution.py:359
  41.2 28.0 %collective-permute-start.9 = (bf16[128,1280]{1,0:T(8,128)(2,1)}, bf16[128,1280]{1,0:T(8,128)(2,1)}, u32[]{:S(2)}, u32[]{:S(2)}) collective-permute-start(bf16[128,1280]{1,0:T(8,128)(2,1)} %get-tuple-element.101), channel_id=1, source_target_pairs={{0,1},{1,0},{2,3},{3,2},{4,5},{5,4},{6,7},{7,6},{8,9},{9,8},{10,11... | collective-permute-start | bytes 983048 | tf_op jit(solution)/shard_map/ppermute | solution.py:324
  54.0 17.1 %collective-permute-start.6 = (bf16[2,128,640]{2,1,0:T(8,128)(2,1)}, bf16[2,128,640]{2,1,0:T(8,128)(2,1)}, u32[]{:S(2)}, u32[]{:S(2)}) collective-permute-start(bf16[2,128,640]{2,1,0:T(8,128)(2,1)} %get-tuple-element.98), channel_id=1, source_target_pairs={{0,4},{4,8},{8,12},{12,0},{1,5},{5,9},{9,13},{13,1},{2,6},{6,10},{... | collective-permute-start | bytes 983048 | tf_op jit(solution)/shard_map/ppermute | solution.py:384
  55.5 17.0 %collective-permute-start.7 = (bf16[2,128,640]{2,1,0:T(8,128)(2,1)}, bf16[2,128,640]{2,1,0:T(8,128)(2,1)}, u32[]{:S(2)}, u32[]{:S(2)}) collective-permute-start(bf16[2,128,640]{2,1,0:T(8,128)(2,1)} %get-tuple-element.99), channel_id=1, source_target_pairs={{0,8},{4,12},{8,0},{12,4},{1,9},{5,13},{9,1},{13,5},{2,10},{6,14},... | collective-permute-start | bytes 983048 | tf_op jit(solution)/shard_map/ppermute | solution.py:384
  58.3 14.3 %collective-permute-start.8 = (bf16[2,128,640]{2,1,0:T(8,128)(2,1)}, bf16[2,128,640]{2,1,0:T(8,128)(2,1)}, u32[]{:S(2)}, u32[]{:S(2)}) collective-permute-start(bf16[2,128,640]{2,1,0:T(8,128)(2,1)} %get-tuple-element.100), channel_id=1, source_target_pairs={{0,12},{4,0},{8,4},{12,8},{1,13},{5,1},{9,5},{13,9},{2,14},{6,2},{... | collective-permute-start | bytes 983048 | tf_op jit(solution)/shard_map/ppermute | solution.py:384
  69.2 16.6 %collective-permute-start.11 = (bf16[2,128,640]{2,1,0:T(8,128)(2,1)S(1)}, bf16[2,128,640]{2,1,0:T(8,128)(2,1)S(1)}, u32[]{:S(2)}, u32[]{:S(2)}) collective-permute-start(bf16[2,128,640]{2,1,0:T(8,128)(2,1)S(1)} %get-tuple-element.105), channel_id=1, source_target_pairs={{0,8},{4,12},{8,0},{12,4},{1,9},{5,13},{9,1},{13,5},{2,10},{6,14},... | collective-permute-start | bytes 983048 | tf_op jit(solution)/shard_map/ppermute | solution.py:384
  71.2 14.6 %collective-permute-start.12 = (bf16[2,128,640]{2,1,0:T(8,128)(2,1)S(1)}, bf16[2,128,640]{2,1,0:T(8,128)(2,1)S(1)}, u32[]{:S(2)}, u32[]{:S(2)}) collective-permute-start(bf16[2,128,640]{2,1,0:T(8,128)(2,1)S(1)} %get-tuple-element.106), channel_id=1, source_target_pairs={{0,12},{4,0},{8,4},{12,8},{1,13},{5,1},{9,5},{13,9},{2,14},{6,2},{... | collective-permute-start | bytes 983048 | tf_op jit(solution)/shard_map/ppermute | solution.py:384
  74.8 16.5 %collective-permute-start.13 = (bf16[128,640]{1,0:T(8,128)(2,1)S(1)}, bf16[128,640]{1,0:T(8,128)(2,1)S(1)}, u32[]{:S(2)}, u32[]{:S(2)}) collective-permute-start(bf16[128,640]{1,0:T(8,128)(2,1)S(1)} %get-tuple-element.102.same0), channel_id=1, source_target_pairs={{0,32},{1,49},{16,48},{17,1},{32,0},{33,17},{48,16},{49,33},{2,34}... | collective-permute-start | bytes 491528 | tf_op jit(solution)/shard_map/ppermute | solution.py:403
  78.1 13.3 %collective-permute-start.14 = (bf16[128,640]{1,0:T(8,128)(2,1)S(1)}, bf16[128,640]{1,0:T(8,128)(2,1)S(1)}, u32[]{:S(2)}, u32[]{:S(2)}) collective-permute-start(bf16[128,640]{1,0:T(8,128)(2,1)S(1)} %get-tuple-element.125), channel_id=1, source_target_pairs={{0,33},{1,48},{16,49},{17,0},{32,1},{33,16},{48,17},{49,32},{2,35}... | collective-permute-start | bytes 491528 | tf_op jit(solution)/shard_map/ppermute | solution.py:404
  110.1 12.0 %collective-permute-start.17 = (bf16[4,2,160,640]{3,2,1,0:T(8,128)(2,1)}, bf16[4,2,160,640]{3,2,1,0:T(8,128)(2,1)S(1)}, u32[]{:S(2)}, u32[]{:S(2)}) collective-permute-start(bf16[4,2,160,640]{3,2,1,0:T(8,128)(2,1)} %get-tuple-element.113), channel_id=1, source_target_pairs={{0,1},{1,0},{2,3},{3,2},{4,5},{5,4},{6,7},{7,6},{8,9},{9,8},{10,11... | collective-permute-start | bytes 4915208 | tf_op jit(solution)/shard_map/ppermute | solution.py:434
  114.8 17.9 %collective-permute-start.18 = (bf16[128,1408]{1,0:T(8,128)(2,1)}, bf16[128,1408]{1,0:T(8,128)(2,1)S(1)}, u32[]{:S(2)}, u32[]{:S(2)}) collective-permute-start(bf16[128,1408]{1,0:T(8,128)(2,1)} %copy-done.31), channel_id=1, source_target_pairs={{0,48},{16,0},{32,16},{48,32},{1,49},{17,1},{33,17},{49,33},{2,50}... | collective-permute-start | bytes 1081352 | tf_op jit(solution)/shard_map/ppermute | solution.py:423
  117.1 18.9 %collective-permute-start.19 = (bf16[128,1408]{1,0:T(8,128)(2,1)}, bf16[128,1408]{1,0:T(8,128)(2,1)S(1)}, u32[]{:S(2)}, u32[]{:S(2)}) collective-permute-start(bf16[128,1408]{1,0:T(8,128)(2,1)} %copy-done.30), channel_id=1, source_target_pairs={{0,32},{16,48},{32,0},{48,16},{1,33},{17,49},{33,1},{49,17},{2,34}... | collective-permute-start | bytes 1081352 | tf_op jit(solution)/shard_map/ppermute | solution.py:423
  118.7 17.5 %collective-permute-start.20 = (bf16[128,1408]{1,0:T(8,128)(2,1)}, bf16[128,1408]{1,0:T(8,128)(2,1)S(1)}, u32[]{:S(2)}, u32[]{:S(2)}) collective-permute-start(bf16[128,1408]{1,0:T(8,128)(2,1)} %copy-done.29), channel_id=1, source_target_pairs={{0,16},{16,32},{32,48},{48,0},{1,17},{17,33},{33,49},{49,1},{2,18}... | collective-permute-start | bytes 1081352 | tf_op jit(solution)/shard_map/ppermute | solution.py:423
  124.9 20.4 %collective-permute-start.30 = (bf16[2,160,640]{2,1,0:T(8,128)(2,1)S(1)}, bf16[2,160,640]{2,1,0:T(8,128)(2,1)S(1)}, u32[]{:S(2)}, u32[]{:S(2)}) collective-permute-start(bf16[2,160,640]{2,1,0:T(8,128)(2,1)S(1)} %get-tuple-element.141), channel_id=1, source_target_pairs={{0,4},{4,8},{8,12},{12,0},{1,5},{5,9},{9,13},{13,1},{2,6},{6,10},{... | collective-permute-start | bytes 1228808 | tf_op jit(solution)/shard_map/ppermute | solution.py:445
  125.9 21.2 %collective-permute-start.31 = (bf16[2,160,640]{2,1,0:T(8,128)(2,1)S(1)}, bf16[2,160,640]{2,1,0:T(8,128)(2,1)S(1)}, u32[]{:S(2)}, u32[]{:S(2)}) collective-permute-start(bf16[2,160,640]{2,1,0:T(8,128)(2,1)S(1)} %get-tuple-element.142), channel_id=1, source_target_pairs={{0,8},{4,12},{8,0},{12,4},{1,9},{5,13},{9,1},{13,5},{2,10},{6,14},... | collective-permute-start | bytes 1228808 | tf_op jit(solution)/shard_map/ppermute | solution.py:445
  132.7 16.3 %collective-permute-start.32 = (bf16[2,160,640]{2,1,0:T(8,128)(2,1)S(1)}, bf16[2,160,640]{2,1,0:T(8,128)(2,1)S(1)}, u32[]{:S(2)}, u32[]{:S(2)}) collective-permute-start(bf16[2,160,640]{2,1,0:T(8,128)(2,1)S(1)} %get-tuple-element.143), channel_id=1, source_target_pairs={{0,12},{4,0},{8,4},{12,8},{1,13},{5,1},{9,5},{13,9},{2,14},{6,2},{... | collective-permute-start | bytes 1228808 | tf_op jit(solution)/shard_map/ppermute | solution.py:445
  141.7 24.7 %collective-permute-start.37 = (bf16[128,1280]{1,0:T(8,128)(2,1)}, bf16[128,1280]{1,0:T(8,128)(2,1)S(1)}, u32[]{:S(2)}, u32[]{:S(2)}) collective-permute-start(bf16[128,1280]{1,0:T(8,128)(2,1)} %get-tuple-element.153), channel_id=1, source_target_pairs={{0,48},{16,0},{32,16},{48,32},{1,49},{17,1},{33,17},{49,33},{2,50}... | collective-permute-start | bytes 983048 | tf_op jit(solution)/shard_map/ppermute | solution.py:447
  145.3 21.1 %collective-permute-start.38 = (bf16[128,1280]{1,0:T(8,128)(2,1)S(1)}, bf16[128,1280]{1,0:T(8,128)(2,1)}, u32[]{:S(2)}, u32[]{:S(2)}) collective-permute-start(bf16[128,1280]{1,0:T(8,128)(2,1)S(1)} %copy-done.33), channel_id=1, source_target_pairs={{0,32},{16,48},{32,0},{48,16},{1,33},{17,49},{33,1},{49,17},{2,34}... | collective-permute-start | bytes 983048 | tf_op jit(solution)/shard_map/ppermute | solution.py:447
  145.3 21.1 %collective-permute-start.39 = (bf16[128,1280]{1,0:T(8,128)(2,1)S(1)}, bf16[128,1280]{1,0:T(8,128)(2,1)}, u32[]{:S(2)}, u32[]{:S(2)}) collective-permute-start(bf16[128,1280]{1,0:T(8,128)(2,1)S(1)} %get-tuple-element.155), channel_id=1, source_target_pairs={{0,16},{16,32},{32,48},{48,0},{1,17},{17,33},{33,49},{49,1},{2,18}... | collective-permute-start | bytes 983048 | tf_op jit(solution)/shard_map/ppermute | solution.py:447
  147.2 19.3 %collective-permute-start.40 = (bf16[128,1408]{1,0:T(8,128)(2,1)}, bf16[128,1408]{1,0:T(8,128)(2,1)S(1)}, u32[]{:S(2)}, u32[]{:S(2)}) collective-permute-start(bf16[128,1408]{1,0:T(8,128)(2,1)} %get-tuple-element.123), channel_id=1, source_target_pairs={{0,64},{64,0},{1,65},{65,1},{2,66},{66,2},{3,67},{67,3},{4,68},{68... | collective-permute-start | bytes 1081352 | tf_op jit(solution)/shard_map/ppermute | solution.py:462
  (59 other events, 426.8 us)
Sparse Core Ops, SparseCore 0:
  15.8 37.6 all-gather.1

commit v4 on v3

--- a/solution.py
+++ b/solution.py
@@ -46,21 +46,26 @@
     return pl.BlockSpec(shape, lambda i, s: (0,) * len(shape))
 
 
-def call(kernel, scalars, ins, outs, name, scratch=(), mib=MIB):
+def call(kernel, scalars, ins, outs, name, scratch=(), mib=MIB, pinned=(), steps=1):
     outs = pl.pallas_call(
         kernel,
-        out_shape=[jax.ShapeDtypeStruct(shape, t) for shape, t in outs],
+        out_shape=[
+            pltpu.HBM(o[0], o[1]) if len(o) == 3 else jax.ShapeDtypeStruct(*o) for o in outs
+        ],
         grid_spec=pltpu.PrefetchScalarGridSpec(
             num_scalar_prefetch=1,
-            grid=(1,),
+            grid=(steps,),
             in_specs=[spec for _, spec in ins],
-            out_specs=[whole(shape) for shape, _ in outs],
+            out_specs=[whole(o[0]) for o in outs],
             scratch_shapes=list(scratch),
         ),
         compiler_params=pltpu.CompilerParams(vmem_limit_bytes=mib * 1024 * 1024),
         cost_estimate=pl.CostEstimate(flops=COST, bytes_accessed=COST, transcendentals=0),
         name=name,
-    )(scalars.value, *[a for a, _ in ins])
+    )(scalars.value, *[
+            pltpu.with_memory_space_constraint(a, pltpu.HBM) if i in pinned else a
+            for i, (a, _) in enumerate(ins)
+        ])
     scalars.after(outs[0])
     return outs
 
@@ -74,6 +79,12 @@
 
 
 X, ZC, G, D, ZH, C, FIRST, LENGTHS = range(8)
+
+
+def column_block(s, stage, near, mine):
+    core = s[C] if mine else 1 - s[C]
+    side = s[G] if near else 1 - s[G]
+    return side * 4 + (s[D] + block_of(stage, core)) % 4
 
 
 def pick_kernel(s, q, w0, w1, w2, w3, res0, res1, q_out, w_out, res_out):
@@ -157,20 +168,7 @@
         target[:, pl.ds(at, 640)] = piece[...]
 
 
-def three_parts(value):
-    high = value.astype(BF)
-    rest = value - high.astype(F32)
-    middle = rest.astype(BF)
-    low = rest - middle.astype(F32)
-    lane = lax.broadcasted_iota(jnp.int32, (value.shape[0], 128), 1)
-    wide = jnp.where(lane == 0, high.astype(F32), jnp.where(lane == 1, middle.astype(F32), 0.0))
-    return jnp.where(lane == 2, low, wide).astype(BF)
-
-
-def compare_kernel(s, pred, normed, proj, sm0, cr0, sm1, cr1, gp, gain, loss, *refs):
-    first_of = refs[:3]
-    last_of = refs[3:6]
-    own_first, own_last, own_inner, grad, inner = refs[6:]
+def compare_kernel(s, pred, normed, proj, sm0, cr0, sm1, cr1, gp, back, small, inner):
     square = jnp.zeros((1, 640), F32)
     for got, stage, core in (
         (sm0, 0, s[C]),
@@ -187,59 +185,26 @@
         rounded = diff.astype(BF)
         gp[pl.ds(at, 128), :] = rounded
         inner[pl.ds(at, 128), :] = jnp.sum(rounded.astype(F32) * here, axis=-1, keepdims=True)
-    loss[...] = square
-    for far, outs, own in ((1, first_of, own_first), (0, last_of, own_last)):
-        for part in range(2):
-            half = s[G] if far == 0 else 1 - s[G]
-            base = pl.multiple_of(half * 1280 + part * 640, 128)
-            cols = slice(part * 640, part * 640 + 640)
-            grad[...] = lax.dot_general(
-                gp[...],
-                proj[pl.ds(base, 640), :],
-                (((1,), (1,)), ((), ())),
-                preferred_element_type=F32,
-            )
-            gain[:, pl.ds(base, 640)] = jnp.sum(
-                grad[...] * normed[:, pl.ds(base, 640)].astype(F32), axis=0, keepdims=True
-            )
-            for k in range(4):
-                at = pl.multiple_of(((s[D] + 4 - k) % 4) * 128, 128)
-                rows = grad[pl.ds(at, 128), :]
-                if k == 0:
-                    own[:, cols] = rows
-                else:
-                    outs[k - 1][:, cols] = rows.astype(BF)
-    for k in range(4):
-        at = pl.multiple_of(((s[D] + 4 - k) % 4) * 128, 128)
-        if k == 0:
-            own_inner[...] = inner[pl.ds(at, 128), :]
-        else:
-            first_of[k - 1][:, 1280:] = three_parts(inner[pl.ds(at, 128), :])
-
-
-def added(own, parts, inner=None):
-    total, inner_sum = own[...], None if inner is None else inner[...]
-    for r in parts:
-        total = total + r[:, :1280].astype(F32)
-        if inner is not None:
-            inner_sum = inner_sum + jnp.sum(r[:, 1280:].astype(F32), axis=-1, keepdims=True)
-    return total, inner_sum
-
-
-def combine_kernel(s, own, own_inner, r1, r2, r3, sent, inner):
-    total, inner_sum = added(own, (r1, r2, r3), own_inner)
-    sent[:, :1280] = total.astype(BF)
-    sent[:, 1280:] = three_parts(inner_sum)
-    inner[...] = inner_sum
-
-
-def hidden_kernel(s, own, r1, r2, r3, inner, got, hidden, inverse_rms, gain, out):
-    total, _ = added(own, (r1, r2, r3))
-    inner_sum = inner[...] + jnp.sum(got[:, 1280:].astype(F32), axis=-1, keepdims=True)
-    grad = total + got[:, :1280].astype(F32)
+    small[...] = jnp.zeros((32, 128), F32)
+    small[20:21, :] = jnp.broadcast_to(jnp.sum(square, axis=-1, keepdims=True), (1, 128))
+    turned = jnp.broadcast_to(inner[...], (512, 128)).T
+    for i in range(4):
+        small[21 + i : 22 + i, :] = turned[:1, i * 128 : i * 128 + 128]
+    for part in range(4):
+        cols = slice(part * 640, part * 640 + 640)
+        grad = lax.dot_general(
+            gp[...], proj[cols, :], (((1,), (1,)), ((), ())), preferred_element_type=F32
+        )
+        back[part // 2, :, (part % 2) * 640 : (part % 2) * 640 + 640] = grad.astype(BF)
+        gain = jnp.sum(grad * normed[:, cols].astype(F32), axis=0, keepdims=True)
+        for i in range(5):
+            small[part * 5 + i : part * 5 + i + 1, :] = gain[:, i * 128 : i * 128 + 128]
+
+
+def hidden_kernel(s, grad, inner, hidden, inverse_rms, norm_gain, out):
     scale = inverse_rms[...]
     unit = hidden[...].astype(F32) * scale
-    out[...] = scale * (grad * gain[...] - unit * (inner_sum / D_S))
+    out[...] = scale * (grad[...].astype(F32) * norm_gain[...] - unit * (inner[...] / D_S))
 
 
 def gproj_kernel(s, normed, gp, sent, kept):
@@ -300,9 +265,7 @@
 
     def column(stage, near, mine, n):
         def index(i, s):
-            core = s[C] if mine else 1 - s[C]
-            side = s[G] if near else 1 - s[G]
-            return (0, side * 4 + (s[D] + block_of(stage, core)) % 4)
+            return (0, column_block(s, stage, near, mine))
 
         return pl.BlockSpec((n, blk), index)
 
@@ -316,19 +279,13 @@
             *[(out_weight, column(st, near, False, 256)) for near in (False, True) for st in stages],
             *[(residual[0], column(st, True, False, 128)) for st in stages],
         ],
-        [(q_block, BF), ((256, 4 * blk), BF), ((128, 2 * blk), BF)],
+        [(q_block, BF, True), ((256, 4 * blk), BF, True), ((128, 2 * blk), BF, True)],
         "pick",
+        pinned=range(7),
     )
     along_z = lax.ppermute(along_z, ("grp", "zh"), WRAP)
     w_other = lax.ppermute(w_out, "core", swap)
     res_other = lax.ppermute(res_out, "core", swap)
-
-    hidden, _ = barrier((student_hidden[0], w_out))
-    hidden = hidden.astype(F32)
-    inverse_rms = lax.rsqrt(jnp.mean(hidden * hidden, axis=-1, keepdims=True) + 1e-06)
-    normed = (hidden * inverse_rms * norm_gain).astype(BF)
-    scalars.after(normed)
-    normed = lax.all_gather(normed, "dp", axis=0, tiled=True)
 
     def attend(q, spec, name):
         return call(
@@ -345,7 +302,13 @@
             mib=40,
         )[0]
 
-    ctx_a = attend(q5, pl.BlockSpec(q_block, lambda i, s: (0, s[ZH], 0, 0)), "attend_chip")
+    hidden, _ = barrier((student_hidden[0], w_out))
+    hidden = hidden.astype(F32)
+    inverse_rms = lax.rsqrt(jnp.mean(hidden * hidden, axis=-1, keepdims=True) + 1e-06)
+    normed = (hidden * inverse_rms * norm_gain).astype(BF)
+    scalars.after(normed)
+    normed = lax.all_gather(normed, "dp", axis=0, tiled=True)
+
     w_z = call(
         pick_weights_kernel,
         scalars,
@@ -353,9 +316,11 @@
             *[(out_weight, column(st, False, True, 256)) for st in stages],
             (w_other, pl.BlockSpec((256, 2 * blk), lambda i, s: (0, 0))),
         ],
-        [((512, blk), BF)] * 2,
+        [((512, blk), BF, True)] * 2,
         "pick_weights",
-    )
+        pinned=range(3),
+    )
+    ctx_a = attend(q5, pl.BlockSpec(q_block, lambda i, s: (0, s[ZH], 0, 0)), "attend_chip")
     w_z = [lax.ppermute(w, ("grp", "zh"), WRAP) for w in w_z]
     ctx_ac = lax.ppermute(ctx_a, "core", swap)
     along_z, _ = barrier((along_z, ctx_a))
@@ -373,7 +338,7 @@
                 (w_other, pl.BlockSpec((256, blk), lambda i, s, st=st: (0, 2 + st))),
                 (w_z[st], whole((512, blk))),
             ],
-            [((2, 128, blk), F32)] + [((2, 128, blk), BF)] * 3,
+            [((2, 128, blk), F32)] + [((2, 128, blk), BF, True)] * 3,
             f"project_{st}",
             scratch=[pltpu.VMEM((1024, blk), F32)],
         )
@@ -403,8 +368,8 @@
         compared.append(lax.ppermute(done_same, ("dp", "core"), to_owner(st, False)))
         compared.append(lax.ppermute(done_cross, ("dp", "core"), to_owner(st, True)))
 
-    first_shape, last_shape = (128, width + 128), (128, width)
-    gp, gain, loss, *backs, own_first, own_last, own_inner = call(
+    part = (NX, 2, rows, blk)
+    gp, back, small = call(
         compare_kernel,
         scalars,
         [
@@ -413,54 +378,37 @@
             (projection, whole((D_S, blk))),
             *[(a, whole((128, blk))) for a in compared],
         ],
-        [((512, blk), BF), ((1, D_S), F32), ((1, blk), F32)]
-        + [(first_shape, BF)] * 3
-        + [(last_shape, BF)] * 3
-        + [(last_shape, F32), (last_shape, F32), ((128, 1), F32)],
+        [((512, blk), BF, True), ((2, 512, width), BF, True), ((32, 128), F32, True)],
         "compare",
-        scratch=[pltpu.VMEM((512, blk), F32), pltpu.VMEM((512, 1), F32)],
-    )
-    back_first = [lax.ppermute(backs[k - 1], "dp", ring(4, 4 - k)) for k in (1, 2, 3)]
+        scratch=[pltpu.VMEM((512, 1), F32)],
+    )
+    back = back.reshape(1024, width)
+    summed = lax.psum_scatter(back, ("grp", "dp"), scatter_dimension=0, tiled=True)
 
     live_count = jnp.sum(lengths).astype(F32)
-    part = (NX, 2, rows, blk)
     sent, kept = call(
         gproj_kernel,
         scalars,
         [(normed, whole((512, D_S))), (gp, whole((512, blk)))],
-        [(part, BF), (part, F32)],
+        [(part, BF, True), (part, F32)],
         "gproj",
     )
     recv = lax.ppermute(sent, "core", swap)
-    small = jnp.concatenate([gain[0] / norm_gain, jnp.full((128,), jnp.sum(loss))]).reshape(-1, 128)
-    small, _ = barrier((small, sent))
-    small = sum_over(small, "dp", 4)
     own, *outs = call(
         gproj_add_kernel,
         scalars,
         [(kept, whole(part)), (recv, whole(part))],
-        [(part[1:], F32)] + [(part[1:], BF)] * 3,
+        [(part[1:], F32)] + [(part[1:], BF, True)] * 3,
         "gproj_add",
     )
     got = {j: lax.ppermute(outs[j - 1], "x", ring(NX, j)) for j in (2, 1, 3)}
-    *lasts, small = barrier((*backs[3:6], small))
-    back_last = [lax.ppermute(lasts[k - 1], "dp", ring(4, 4 - k)) for k in (1, 2, 3)]
-    small = small + lax.ppermute(small, "core", swap)
-    small = sum_over(small, ("grp", "zh"), NZ)
-
-    sent, inner = call(
-        combine_kernel,
-        scalars,
-        [
-            (own_first, whole(last_shape)),
-            (own_inner, whole((128, 1))),
-            *[(r, whole(first_shape)) for r in back_first],
-        ],
-        [(first_shape, BF), ((128, 1), F32)],
-        "combine",
-    )
-    half_recv = lax.ppermute(sent, "grp", swap)
-    cross = [lax.ppermute(a, "core", swap) for a in barrier((*cross, sent))[:2]]
+
+    small, _ = barrier((small, own))
+    cross = [lax.ppermute(a, "core", swap) for a in barrier((*cross, own))[:2]]
+    small = sum_over(small, "dp", 4)
+    small = sum_over(small, "grp", 2)
+    inner = lax.dynamic_slice_in_dim(small, 21 + d, 1, 0)
+    small = sum_over(small, "zh", 2)
     (target,) = call(
         assemble_kernel,
         scalars,
@@ -468,35 +416,39 @@
         [((128, half), BF)],
         "assemble",
     )
+    scalars.after(small)
     gsent, gkept = call(
         gproj_sum_kernel,
         scalars,
         [(own, whole(part[1:]))] + [(got[j], whole(part[1:])) for j in (1, 2, 3)],
-        [((rows, blk), BF), ((rows, blk), F32)],
+        [((rows, blk), BF, True), ((rows, blk), F32)],
         "gproj_sum",
     )
-    small, _ = barrier((small, gsent))
     gsent = lax.ppermute(gsent, "zh", swap)
-    small = sum_over(small, "x", NX).reshape(-1)
-    scalars.after(small)
+    small, _ = barrier((small, gkept))
+    small = sum_over(small, "core", 2)
+    small = sum_over(small, "x", NX)
+    grad_proj = (gkept + gsent.astype(F32)) / live_count
+    small = small.reshape(-1)
+    distill_loss = small[20 * 128] / (live_count * D_T)
+    gain_half = lax.dynamic_slice_in_dim(norm_gain, g * width, width, 0)
+    grad_gain = lax.dynamic_slice_in_dim(small, g * width, width, 0) / (gain_half * live_count)
+
+    half_shape = (128, width)
     (grad_hidden,) = call(
         hidden_kernel,
         scalars,
         [
-            (own_last, whole(last_shape)),
-            *[(r, whole(last_shape)) for r in back_last],
-            (inner, whole((128, 1))),
-            (half_recv, whole(first_shape)),
+            (summed, whole(half_shape)),
+            (inner.reshape(128, 1), whole((128, 1))),
             (student_hidden[0], pl.BlockSpec((128, width), lambda i, s: (0, s[G]))),
             (inverse_rms, whole((128, 1))),
             (norm_gain.reshape(1, D_S), pl.BlockSpec((1, width), lambda i, s: (0, s[G]))),
         ],
-        [(last_shape, F32)],
+        [(half_shape, F32)],
         "hidden",
-    )
-    grad_proj = (gkept + gsent.astype(F32)) / live_count
-    distill_loss = small[D_S] / (live_count * D_T)
-    grad_gain = lax.dynamic_slice_in_dim(small, g * width, width, 0) / live_count
+        pinned=range(1),
+    )
     return (target[None], distill_loss, grad_proj, grad_gain, grad_hidden[None])
 
 

time: 182 us -> 163 us (0.90)
  local copies, waits for them, and re-layouts: 19.7 us -> 5.27 us
  starting transfers between devices: 52.9 us -> 49 us
  Pallas kernels: 40.8 us -> 44.3 us
  waiting for transfers between devices: 41.1 us -> 38.7 us
    unnamed x82 -> x64, local copies, waits for them, and re-layouts: 17.7 us -> 3.78 us
    ppermute x10 -> x2, starting transfers between devices: 9.69 us -> 0.05 us  [body(): cross = [lax.ppermute(a, 'core', swap) for a in barrier((*cross, own))[:2]]]
    ppermute x9, starting transfers between devices: 8.55 us -> 12.9 us  [sum_over(): got = [lax.ppermute(array, axis, ring(n, j)) for j in range(1, n)]]
    ppermute x10 -> x2, waiting for transfers between devices: 5.57 us -> 1.34 us  [body(): cross = [lax.ppermute(a, 'core', swap) for a in barrier((*cross, own))[:2]]]
    pallas_call x15 -> x14, Pallas kernels: 40.8 us -> 44.3 us  [call(): pl.pallas_call(kernel, out_shape=[pltpu.HBM(o[0], o[1]) if len(o) == 3 el...]
    ppermute x1, waiting for transfers between devices: 0.58 us -> 4 us  [body(): gsent = lax.ppermute(gsent, 'zh', swap)]
    ppermute x1, waiting for transfers between devices: 0.01 us -> 3.34 us  [body(): recv = lax.ppermute(sent, 'core', swap)]
    ppermute x2, waiting for transfers between devices: 8.4 us -> 5.16 us  [body(): w_z = [lax.ppermute(w, ('grp', 'zh'), WRAP) for w in w_z]]
  transfers between devices with their start and end apart: 42 -> 35, of which waited for: 15 -> 13; matrix products, arithmetic and copies ran while one was open for 5% -> 5% of each run, Pallas kernels for 17% -> 21%
where the time goes in v4:
time: 163 us
  starting transfers between devices  49 us (30%)
  Pallas kernels  44.3 us (27%)
  waiting for transfers between devices  38.7 us (24%)
  between operations  16.9 us (10%)
  local copies, waits for them, and re-layouts  5.27 us (3%)
  matrix products  5.05 us (3%)
  other arithmetic  3.44 us (2%)
    pallas_call x14, Pallas kernels, call(): pl.pallas_call(kernel, out_shape=[pltpu.HBM(o[0], o[1]) if len(o) == 3 el...  44.3 us
    ppermute x9, starting transfers between devices, sum_over(): got = [lax.ppermute(array, axis, ring(n, j)) for j in range(1, n)]  12.9 us
    ppermute x6, starting transfers between devices, body(): lax.ppermute(outs[j - 1], 'x', ring(NX, j))  10 us
    ppermute x9, waiting for transfers between devices, sum_over(): got = [lax.ppermute(array, axis, ring(n, j)) for j in range(1, n)]  9.73 us
    ppermute x6, waiting for transfers between devices, body(): lax.ppermute(outs[j - 1], 'x', ring(NX, j))  7.65 us
    ppermute x2, starting transfers between devices, body(): lax.ppermute(done_same, ('dp', 'core'), to_owner(st, False))  6.74 us
    ppermute x2, starting transfers between devices, body(): w_z = [lax.ppermute(w, ('grp', 'zh'), WRAP) for w in w_z]  6.08 us
    ppermute x3, starting transfers between devices, body(): got = {j: lax.ppermute(outs[j - 1], 'x', ring(NX, j)) for j in (2, 1, 3)}  5.29 us
  transfers between devices with their start and end apart: 35, of which 13 were waited for; matrix products, arithmetic and copies ran while one was open for 5% of the time, Pallas kernels for 21%

profile of v4, /device:TPU:0, one launch (start us, length us, event | category | flops | bytes accessed | tf_op | source)
XLA Modules:
  0.0 162.6 jit_solution(17169734348229802035)
XLA Ops:
  8.0 3.5 %pick.1 = (bf16[4,2,128,256]{3,2,1,0:T(8,128)(2,1)}, bf16[256,2560]{1,0:T(8,128)(2,1)}, bf16[128,1280]{1,0:T(8,128)(2,1)}) custom-call(s32[11]{0:T(128)S(1)} %concatenate.3.s, bf16[4,4,128,256]{3,2,1,0:T(8,128)(2,1)} %bitcast.35, bf16[256,5120]{1,0:T(8,128)(2,1)} %w_a.3, bf16[256,5120]{1,0:T(8,128)(2,1)} %w_a.3, bf16[256,5120]{1,0:T(8,128)(2,1)} %w_a.3, ...), custom_call_target="tpu_custom_call" | custom-call | flops 1 | bytes 1 | tf_op jit(solution)/shard_map/pick/pallas_call | solution.py:50
  13.0 4.2 %collective-permute-start.1 = (bf16[4,2,128,256]{3,2,1,0:T(8,128)(2,1)}, bf16[4,2,128,256]{3,2,1,0:T(8,128)(2,1)S(1)}, u32[]{:S(2)}, u32[]{:S(2)}) collective-permute-start(bf16[4,2,128,256]{3,2,1,0:T(8,128)(2,1)} %get-tuple-element.62), channel_id=1, source_target_pairs={{0,66},{2,64},{64,2},{66,0},{1,67},{3,65},{65,3},{67,1},{4,70},{6,... | collective-permute-start | bytes 1572872 | tf_op jit(solution)/shard_map/ppermute | solution.py:286
  18.3 2.9 %pick_weights.1 = (bf16[512,640]{1,0:T(8,128)(2,1)}, bf16[512,640]{1,0:T(8,128)(2,1)}) custom-call(s32[11]{0:T(128)S(1)} %concatenate.3.s, bf16[256,5120]{1,0:T(8,128)(2,1)} %w_a.3, bf16[256,5120]{1,0:T(8,128)(2,1)} %w_a.3, bf16[256,2560]{1,0:T(8,128)(2,1)} %copy-done.2), custom_call_target="tpu_custom_call" | custom-call | flops 1 | bytes 1 | tf_op jit(solution)/shard_map/pick_weights/pallas_call | solution.py:50
  21.2 2.9 %collective-permute-start.4 = (bf16[512,640]{1,0:T(8,128)(2,1)}, bf16[512,640]{1,0:T(8,128)(2,1)S(1)}, u32[]{:S(2)}, u32[]{:S(2)}) collective-permute-start(bf16[512,640]{1,0:T(8,128)(2,1)} %get-tuple-element.67), channel_id=1, source_target_pairs={{0,66},{2,64},{64,2},{66,0},{1,67},{3,65},{65,3},{67,1},{4,70},{6,... | collective-permute-start | bytes 1966088 | tf_op jit(solution)/shard_map/ppermute | solution.py:324
  24.1 5.0 %attend_chip.1.ctx_a = bf16[1024,256]{1,0:T(8,128)(2,1)S(1)} custom-call(s32[11]{0:T(128)S(1)} %concatenate.3.s, bf16[4,4,128,256]{3,2,1,0:T(8,128)(2,1)S(1)} %bitcast.36, bf16[2048,512]{1,0:T(8,128)(2,1)S(1)} %bitcast.28, bf16[2048,512]{1,0:T(8,128)(2,1)S(1)} %bitcast.30), custom_call_target="tpu_custom_call" | custom-call | flops 1 | bytes 1 | tf_op jit(solution)/shard_map/attend_chip/pallas_call | solution.py:50
  30.2 5.0 %attend_next.1.ctx_b = bf16[1024,256]{1,0:T(8,128)(2,1)S(1)} custom-call(s32[11]{0:T(128)S(1)} %concatenate.3.s, bf16[4,2,128,256]{3,2,1,0:T(8,128)(2,1)S(1)} %collective-permute-done.1.q_ref, bf16[2048,512]{1,0:T(8,128)(2,1)S(1)} %bitcast.29, bf16[2048,512]{1,0:T(8,128)(2,1)S(1)} %bitcast.31), custom_call_target="tpu_custom_call" | custom-call | flops 1 | bytes 1 | tf_op jit(solution)/shard_map/attend_next/pallas_call | solution.py:50
  35.8 3.2 %collective-permute-start.5 = (bf16[512,640]{1,0:T(8,128)(2,1)}, bf16[512,640]{1,0:T(8,128)(2,1)}, u32[]{:S(2)}, u32[]{:S(2)}) collective-permute-start(bf16[512,640]{1,0:T(8,128)(2,1)} %get-tuple-element.76), channel_id=1, source_target_pairs={{0,66},{2,64},{64,2},{66,0},{1,67},{3,65},{65,3},{67,1},{4,70},{6,... | collective-permute-start | bytes 1966088 | tf_op jit(solution)/shard_map/ppermute | solution.py:324
  39.1 5.2 %collective-permute-done.4.w_z = bf16[512,640]{1,0:T(8,128)(2,1)S(1)} collective-permute-done((bf16[512,640]{1,0:T(8,128)(2,1)}, bf16[512,640]{1,0:T(8,128)(2,1)S(1)}, u32[]{:S(2)}, u32[]{:S(2)}) %collective-permute-start.4) | collective-permute-done | bytes 655392 | tf_op jit(solution)/shard_map/ppermute | solution.py:324
  44.2 3.5 %project_0.1 = (f32[2,128,640]{2,1,0:T(8,128)S(1)}, bf16[2,128,640]{2,1,0:T(8,128)(2,1)}, bf16[2,128,640]{2,1,0:T(8,128)(2,1)}, bf16[2,128,640]{2,1,0:T(8,128)(2,1)}) custom-call(s32[11]{0:T(128)S(1)} %concatenate.3.s, bf16[1024,256]{1,0:T(8,128)(2,1)S(1)} %attend_chip.1.ctx_a, bf16[1024,256]{1,0:T(8,128)(2,1)S(1)} %collective-permute-done.2.ctx_ac, ...), custom_call_target="tpu_custom_call" | custom-call | flops 1 | bytes 1 | tf_op jit(solution)/shard_map/project_0/pallas_call | solution.py:50
  50.1 2.7 %collective-permute-start.7 = (bf16[2,128,640]{2,1,0:T(8,128)(2,1)}, bf16[2,128,640]{2,1,0:T(8,128)(2,1)}, u32[]{:S(2)}, u32[]{:S(2)}) collective-permute-start(bf16[2,128,640]{2,1,0:T(8,128)(2,1)} %get-tuple-element.80), channel_id=1, source_target_pairs={{0,8},{4,12},{8,0},{12,4},{1,9},{5,13},{9,1},{13,5},{2,10},{6,14},... | collective-permute-start | bytes 983048 | tf_op jit(solution)/shard_map/ppermute | solution.py:349
  54.3 5.1 %fusion.4.pred = f32[512,640]{1,0:T(8,128)S(1)} fusion(bf16[512,2560]{1,0:T(8,128)(2,1)} %all-gather.2.cloned.1.call-done.normed, bf16[2560,640]{1,0:T(8,128)(2,1)} %proj.1), kind=kOutput, calls=%fused_computation.12 | convolution fusion | flops 1677721600 | bytes 7208960 | tf_op jit(solution)/shard_map/dot_general | solution.py:347
  59.4 4.5 %project_1.1 = (f32[2,128,640]{2,1,0:T(8,128)S(1)}, bf16[2,128,640]{2,1,0:T(8,128)(2,1)}, bf16[2,128,640]{2,1,0:T(8,128)(2,1)}, bf16[2,128,640]{2,1,0:T(8,128)(2,1)}) custom-call(s32[11]{0:T(128)S(1)} %concatenate.3.s, bf16[1024,256]{1,0:T(8,128)(2,1)S(1)} %copy-done.10, bf16[1024,256]{1,0:T(8,128)(2,1)S(1)} %copy-done.18, bf16[1024,256]{1,0:T(8,128)(2,1)S(1)} %copy-done.12, ...), custom_call_target="tpu_custom_call" | custom-call | flops 1 | bytes 1 | tf_op jit(solution)/shard_map/project_1/pallas_call | solution.py:50
  70.5 3.3 %collective-permute-start.13 = (bf16[128,640]{1,0:T(8,128)(2,1)S(1)}, bf16[128,640]{1,0:T(8,128)(2,1)S(1)}, u32[]{:S(2)}, u32[]{:S(2)}) collective-permute-start(bf16[128,640]{1,0:T(8,128)(2,1)S(1)} %get-tuple-element.83.same0), channel_id=1, source_target_pairs={{0,32},{1,49},{16,48},{17,1},{32,0},{33,17},{48,16},{49,33},{2,34}... | collective-permute-start | bytes 491528 | tf_op jit(solution)/shard_map/ppermute | solution.py:368
  75.3 6.2 %collective-permute-done.11.r2 = bf16[2,128,640]{2,1,0:T(8,128)(2,1)S(1)} collective-permute-done((bf16[2,128,640]{2,1,0:T(8,128)(2,1)}, bf16[2,128,640]{2,1,0:T(8,128)(2,1)S(1)}, u32[]{:S(2)}, u32[]{:S(2)}) %collective-permute-start.11) | collective-permute-done | bytes 327712 | tf_op jit(solution)/shard_map/ppermute | solution.py:349
  83.1 3.5 %collective-permute-start.15 = (bf16[128,640]{1,0:T(8,128)(2,1)S(1)}, bf16[128,640]{1,0:T(8,128)(2,1)S(1)}, u32[]{:S(2)}, u32[]{:S(2)}) collective-permute-start(bf16[128,640]{1,0:T(8,128)(2,1)S(1)} %get-tuple-element.88.same1), channel_id=1, source_target_pairs={{0,16},{1,1},{16,32},{17,17},{32,48},{33,33},{48,0},{49,49},{2,18}... | collective-permute-start | bytes 491528 | tf_op jit(solution)/shard_map/ppermute | solution.py:368
  87.3 4.3 %collective-permute-done.15.sm1 = bf16[128,640]{1,0:T(8,128)(2,1)S(1)} collective-permute-done((bf16[128,640]{1,0:T(8,128)(2,1)S(1)}, bf16[128,640]{1,0:T(8,128)(2,1)S(1)}, u32[]{:S(2)}, u32[]{:S(2)}) %collective-permute-start.15) | collective-permute-done | bytes 163872 | tf_op jit(solution)/shard_map/ppermute | solution.py:368
  91.6 4.9 %compare.1 = (bf16[512,640]{1,0:T(8,128)(2,1)}, bf16[2,512,1280]{2,1,0:T(8,128)(2,1)}, f32[32,128]{1,0:T(8,128)}) custom-call(s32[11]{0:T(128)S(1)} %concatenate.3.s, f32[512,640]{1,0:T(8,128)S(1)} %fusion.4.pred, bf16[512,2560]{1,0:T(8,128)(2,1)S(1)} %copy-done.5, bf16[2560,640]{1,0:T(8,128)(2,1)S(1)} %copy-done.14, ...), custom_call_target="tpu_custom_call" | custom-call | flops 1 | bytes 1 | tf_op jit(solution)/shard_map/compare/pallas_call | solution.py:50
  97.6 3.9 %gproj.1 = (bf16[4,2,160,640]{3,2,1,0:T(8,128)(2,1)}, f32[4,2,160,640]{3,2,1,0:T(8,128)S(1)}) custom-call(s32[11]{0:T(128)S(1)} %concatenate.3.s, bf16[512,2560]{1,0:T(8,128)(2,1)S(1)} %copy-done.5, bf16[512,640]{1,0:T(8,128)(2,1)S(1)} %copy-done.21), custom_call_target="tpu_custom_call" | custom-call | flops 1 | bytes 1 | tf_op jit(solution)/shard_map/gproj/pallas_call | solution.py:50
  103.1 3.3 %collective-permute-done.17.recv = bf16[4,2,160,640]{3,2,1,0:T(8,128)(2,1)S(1)} collective-permute-done((bf16[4,2,160,640]{3,2,1,0:T(8,128)(2,1)}, bf16[4,2,160,640]{3,2,1,0:T(8,128)(2,1)S(1)}, u32[]{:S(2)}, u32[]{:S(2)}) %collective-permute-start.17) | collective-permute-done | bytes 1638432 | tf_op jit(solution)/shard_map/ppermute | solution.py:396
  108.6 2.9 %collective-permute-start.21 = (f32[32,128]{1,0:T(8,128)S(1)}, f32[32,128]{1,0:T(8,128)S(1)}, u32[]{:S(2)}, u32[]{:S(2)}) collective-permute-start(f32[32,128]{1,0:T(8,128)S(1)} %copy-done.29), channel_id=1, source_target_pairs={{0,32},{16,48},{32,0},{48,16},{1,33},{17,49},{33,1},{49,17},{2,34}... | collective-permute-start | bytes 49160 | tf_op jit(solution)/shard_map/ppermute | solution.py:243
  118.3 4.0 %collective-permute-done.23 = f32[32,128]{1,0:T(8,128)S(1)} collective-permute-done((f32[32,128]{1,0:T(8,128)S(1)}, f32[32,128]{1,0:T(8,128)S(1)}, u32[]{:S(2)}, u32[]{:S(2)}) %collective-permute-start.23) | collective-permute-done | bytes 16416 | tf_op jit(solution)/shard_map/ppermute | solution.py:243
  122.3 2.8 %collective-permute-start.24 = (f32[32,128]{1,0:T(8,128)S(1)}, f32[32,128]{1,0:T(8,128)S(1)}, u32[]{:S(2)}, u32[]{:S(2)}) collective-permute-start(f32[32,128]{1,0:T(8,128)S(1)} %add.72), channel_id=1, source_target_pairs={{0,2},{2,0},{1,3},{3,1},{4,6},{6,4},{5,7},{7,5},{8,10},{10,8},{9,1... | collective-permute-start | bytes 49160 | tf_op jit(solution)/shard_map/ppermute | solution.py:243
  125.1 4.6 %collective-permute-done.24 = f32[32,128]{1,0:T(8,128)S(1)} collective-permute-done((f32[32,128]{1,0:T(8,128)S(1)}, f32[32,128]{1,0:T(8,128)S(1)}, u32[]{:S(2)}, u32[]{:S(2)}) %collective-permute-start.24) | collective-permute-done | bytes 16416 | tf_op jit(solution)/shard_map/ppermute | solution.py:243
  147.3 4.0 %collective-permute-done.32 = bf16[160,640]{1,0:T(8,128)(2,1)S(1)} collective-permute-done((bf16[160,640]{1,0:T(8,128)(2,1)}, bf16[160,640]{1,0:T(8,128)(2,1)S(1)}, u32[]{:S(2)}, u32[]{:S(2)}) %collective-permute-start.32) | collective-permute-done | bytes 204832 | tf_op jit(solution)/shard_map/ppermute | solution.py:427
  (144 shorter events, 50.4 us)
Async XLA Ops:
  7.2 47.1 %all-gather.2.cloned.1.call-start = ((), (), s32[]{:S(2)}) async-start(), calls=%async_computation.1 | async-start | bytes 3276800 | tf_op jit(solution)/shard_map/all_gather | solution.py:310
  12.8 139.3 %reduce-scatter.2.cloned.1.call-start = ((), (), s32[]{:S(2)}) async-start(), calls=%async_computation.2 | async-start | bytes 2949120 | tf_op jit(solution)/shard_map/reduce_scatter | solution.py:386
  13.0 17.2 %collective-permute-start.1 = (bf16[4,2,128,256]{3,2,1,0:T(8,128)(2,1)}, bf16[4,2,128,256]{3,2,1,0:T(8,128)(2,1)S(1)}, u32[]{:S(2)}, u32[]{:S(2)}) collective-permute-start(bf16[4,2,128,256]{3,2,1,0:T(8,128)(2,1)} %get-tuple-element.62), channel_id=1, source_target_pairs={{0,66},{2,64},{64,2},{66,0},{1,67},{3,65},{65,3},{67,1},{4,70},{6,... | collective-permute-start | bytes 1572872 | tf_op jit(solution)/shard_map/ppermute | solution.py:286
  21.2 23.0 %collective-permute-start.4 = (bf16[512,640]{1,0:T(8,128)(2,1)}, bf16[512,640]{1,0:T(8,128)(2,1)S(1)}, u32[]{:S(2)}, u32[]{:S(2)}) collective-permute-start(bf16[512,640]{1,0:T(8,128)(2,1)} %get-tuple-element.67), channel_id=1, source_target_pairs={{0,66},{2,64},{64,2},{66,0},{1,67},{3,65},{65,3},{67,1},{4,70},{6,... | collective-permute-start | bytes 1966088 | tf_op jit(solution)/shard_map/ppermute | solution.py:324
  35.8 23.5 %collective-permute-start.5 = (bf16[512,640]{1,0:T(8,128)(2,1)}, bf16[512,640]{1,0:T(8,128)(2,1)}, u32[]{:S(2)}, u32[]{:S(2)}) collective-permute-start(bf16[512,640]{1,0:T(8,128)(2,1)} %get-tuple-element.76), channel_id=1, source_target_pairs={{0,66},{2,64},{64,2},{66,0},{1,67},{3,65},{65,3},{67,1},{4,70},{6,... | collective-permute-start | bytes 1966088 | tf_op jit(solution)/shard_map/ppermute | solution.py:324
  39.0 25.5 %collective-permute-start.9 = (bf16[128,1280]{1,0:T(8,128)(2,1)}, bf16[128,1280]{1,0:T(8,128)(2,1)}, u32[]{:S(2)}, u32[]{:S(2)}) collective-permute-start(bf16[128,1280]{1,0:T(8,128)(2,1)} %get-tuple-element.82), channel_id=1, source_target_pairs={{0,1},{1,0},{2,3},{3,2},{4,5},{5,4},{6,7},{7,6},{8,9},{9,8},{10,11... | collective-permute-start | bytes 983048 | tf_op jit(solution)/shard_map/ppermute | solution.py:288
  48.6 18.2 %collective-permute-start.6 = (bf16[2,128,640]{2,1,0:T(8,128)(2,1)}, bf16[2,128,640]{2,1,0:T(8,128)(2,1)}, u32[]{:S(2)}, u32[]{:S(2)}) collective-permute-start(bf16[2,128,640]{2,1,0:T(8,128)(2,1)} %get-tuple-element.79), channel_id=1, source_target_pairs={{0,4},{4,8},{8,12},{12,0},{1,5},{5,9},{9,13},{13,1},{2,6},{6,10},{... | collective-permute-start | bytes 983048 | tf_op jit(solution)/shard_map/ppermute | solution.py:349
  50.1 18.2 %collective-permute-start.7 = (bf16[2,128,640]{2,1,0:T(8,128)(2,1)}, bf16[2,128,640]{2,1,0:T(8,128)(2,1)}, u32[]{:S(2)}, u32[]{:S(2)}) collective-permute-start(bf16[2,128,640]{2,1,0:T(8,128)(2,1)} %get-tuple-element.80), channel_id=1, source_target_pairs={{0,8},{4,12},{8,0},{12,4},{1,9},{5,13},{9,1},{13,5},{2,10},{6,14},... | collective-permute-start | bytes 983048 | tf_op jit(solution)/shard_map/ppermute | solution.py:349
  52.8 15.5 %collective-permute-start.8 = (bf16[2,128,640]{2,1,0:T(8,128)(2,1)}, bf16[2,128,640]{2,1,0:T(8,128)(2,1)}, u32[]{:S(2)}, u32[]{:S(2)}) collective-permute-start(bf16[2,128,640]{2,1,0:T(8,128)(2,1)} %get-tuple-element.81), channel_id=1, source_target_pairs={{0,12},{4,0},{8,4},{12,8},{1,13},{5,1},{9,5},{13,9},{2,14},{6,2},{... | collective-permute-start | bytes 983048 | tf_op jit(solution)/shard_map/ppermute | solution.py:349
  63.9 11.4 %collective-permute-start.10 = (bf16[2,128,640]{2,1,0:T(8,128)(2,1)}, bf16[2,128,640]{2,1,0:T(8,128)(2,1)S(1)}, u32[]{:S(2)}, u32[]{:S(2)}) collective-permute-start(bf16[2,128,640]{2,1,0:T(8,128)(2,1)} %get-tuple-element.85), channel_id=1, source_target_pairs={{0,4},{4,8},{8,12},{12,0},{1,5},{5,9},{9,13},{13,1},{2,6},{6,10},{... | collective-permute-start | bytes 983048 | tf_op jit(solution)/shard_map/ppermute | solution.py:349
  64.5 17.0 %collective-permute-start.11 = (bf16[2,128,640]{2,1,0:T(8,128)(2,1)}, bf16[2,128,640]{2,1,0:T(8,128)(2,1)S(1)}, u32[]{:S(2)}, u32[]{:S(2)}) collective-permute-start(bf16[2,128,640]{2,1,0:T(8,128)(2,1)} %get-tuple-element.86), channel_id=1, source_target_pairs={{0,8},{4,12},{8,0},{12,4},{1,9},{5,13},{9,1},{13,5},{2,10},{6,14},... | collective-permute-start | bytes 983048 | tf_op jit(solution)/shard_map/ppermute | solution.py:349
  66.8 14.6 %collective-permute-start.12 = (bf16[2,128,640]{2,1,0:T(8,128)(2,1)}, bf16[2,128,640]{2,1,0:T(8,128)(2,1)S(1)}, u32[]{:S(2)}, u32[]{:S(2)}) collective-permute-start(bf16[2,128,640]{2,1,0:T(8,128)(2,1)} %get-tuple-element.87), channel_id=1, source_target_pairs={{0,12},{4,0},{8,4},{12,8},{1,13},{5,1},{9,5},{13,9},{2,14},{6,2},{... | collective-permute-start | bytes 983048 | tf_op jit(solution)/shard_map/ppermute | solution.py:349
  70.5 16.8 %collective-permute-start.13 = (bf16[128,640]{1,0:T(8,128)(2,1)S(1)}, bf16[128,640]{1,0:T(8,128)(2,1)S(1)}, u32[]{:S(2)}, u32[]{:S(2)}) collective-permute-start(bf16[128,640]{1,0:T(8,128)(2,1)S(1)} %get-tuple-element.83.same0), channel_id=1, source_target_pairs={{0,32},{1,49},{16,48},{17,1},{32,0},{33,17},{48,16},{49,33},{2,34}... | collective-permute-start | bytes 491528 | tf_op jit(solution)/shard_map/ppermute | solution.py:368
  73.8 13.5 %collective-permute-start.14 = (bf16[128,640]{1,0:T(8,128)(2,1)S(1)}, bf16[128,640]{1,0:T(8,128)(2,1)S(1)}, u32[]{:S(2)}, u32[]{:S(2)}) collective-permute-start(bf16[128,640]{1,0:T(8,128)(2,1)S(1)} %get-tuple-element.99), channel_id=1, source_target_pairs={{0,33},{1,48},{16,49},{17,0},{32,1},{33,16},{48,17},{49,32},{2,35}... | collective-permute-start | bytes 491528 | tf_op jit(solution)/shard_map/ppermute | solution.py:369
  83.1 8.4 %collective-permute-start.15 = (bf16[128,640]{1,0:T(8,128)(2,1)S(1)}, bf16[128,640]{1,0:T(8,128)(2,1)S(1)}, u32[]{:S(2)}, u32[]{:S(2)}) collective-permute-start(bf16[128,640]{1,0:T(8,128)(2,1)S(1)} %get-tuple-element.88.same1), channel_id=1, source_target_pairs={{0,16},{1,1},{16,32},{17,17},{32,48},{33,33},{48,0},{49,49},{2,18}... | collective-permute-start | bytes 491528 | tf_op jit(solution)/shard_map/ppermute | solution.py:368
  108.2 8.5 %collective-permute-start.20 = (f32[32,128]{1,0:T(8,128)S(1)}, f32[32,128]{1,0:T(8,128)S(1)}, u32[]{:S(2)}, u32[]{:S(2)}) collective-permute-start(f32[32,128]{1,0:T(8,128)S(1)} %copy-done.29), channel_id=1, source_target_pairs={{0,16},{16,32},{32,48},{48,0},{1,17},{17,33},{33,49},{49,1},{2,18}... | collective-permute-start | bytes 49160 | tf_op jit(solution)/shard_map/ppermute | solution.py:243
  108.6 9.5 %collective-permute-start.21 = (f32[32,128]{1,0:T(8,128)S(1)}, f32[32,128]{1,0:T(8,128)S(1)}, u32[]{:S(2)}, u32[]{:S(2)}) collective-permute-start(f32[32,128]{1,0:T(8,128)S(1)} %copy-done.29), channel_id=1, source_target_pairs={{0,32},{16,48},{32,0},{48,16},{1,33},{17,49},{33,1},{49,17},{2,34}... | collective-permute-start | bytes 49160 | tf_op jit(solution)/shard_map/ppermute | solution.py:243
  111.5 6.7 %collective-permute-start.22 = (f32[32,128]{1,0:T(8,128)S(1)}, f32[32,128]{1,0:T(8,128)S(1)}, u32[]{:S(2)}, u32[]{:S(2)}) collective-permute-start(f32[32,128]{1,0:T(8,128)S(1)} %copy-done.29), channel_id=1, source_target_pairs={{0,48},{16,0},{32,16},{48,32},{1,49},{17,1},{33,17},{49,33},{2,50}... | collective-permute-start | bytes 49160 | tf_op jit(solution)/shard_map/ppermute | solution.py:243
  112.9 19.7 %collective-permute-start.25 = (bf16[2,160,640]{2,1,0:T(8,128)(2,1)}, bf16[2,160,640]{2,1,0:T(8,128)(2,1)S(1)}, u32[]{:S(2)}, u32[]{:S(2)}) collective-permute-start(bf16[2,160,640]{2,1,0:T(8,128)(2,1)} %get-tuple-element.108), channel_id=1, source_target_pairs={{0,4},{4,8},{8,12},{12,0},{1,5},{5,9},{9,13},{13,1},{2,6},{6,10},{... | collective-permute-start | bytes 1228808 | tf_op jit(solution)/shard_map/ppermute | solution.py:404
  114.4 20.2 %collective-permute-start.26 = (bf16[2,160,640]{2,1,0:T(8,128)(2,1)}, bf16[2,160,640]{2,1,0:T(8,128)(2,1)S(1)}, u32[]{:S(2)}, u32[]{:S(2)}) collective-permute-start(bf16[2,160,640]{2,1,0:T(8,128)(2,1)} %get-tuple-element.109), channel_id=1, source_target_pairs={{0,8},{4,12},{8,0},{12,4},{1,9},{5,13},{9,1},{13,5},{2,10},{6,14},... | collective-permute-start | bytes 1228808 | tf_op jit(solution)/shard_map/ppermute | solution.py:404
  116.8 17.9 %collective-permute-start.27 = (bf16[2,160,640]{2,1,0:T(8,128)(2,1)}, bf16[2,160,640]{2,1,0:T(8,128)(2,1)S(1)}, u32[]{:S(2)}, u32[]{:S(2)}) collective-permute-start(bf16[2,160,640]{2,1,0:T(8,128)(2,1)} %get-tuple-element.110), channel_id=1, source_target_pairs={{0,12},{4,0},{8,4},{12,8},{1,13},{5,1},{9,5},{13,9},{2,14},{6,2},{... | collective-permute-start | bytes 1228808 | tf_op jit(solution)/shard_map/ppermute | solution.py:404
  122.3 7.4 %collective-permute-start.24 = (f32[32,128]{1,0:T(8,128)S(1)}, f32[32,128]{1,0:T(8,128)S(1)}, u32[]{:S(2)}, u32[]{:S(2)}) collective-permute-start(f32[32,128]{1,0:T(8,128)S(1)} %add.72), channel_id=1, source_target_pairs={{0,2},{2,0},{1,3},{3,1},{4,6},{6,4},{5,7},{7,5},{8,10},{10,8},{9,1... | collective-permute-start | bytes 49160 | tf_op jit(solution)/shard_map/ppermute | solution.py:243
  137.4 6.8 %collective-permute-start.29 = (f32[32,128]{1,0:T(8,128)S(1)}, f32[32,128]{1,0:T(8,128)S(1)}, u32[]{:S(2)}, u32[]{:S(2)}) collective-permute-start(f32[32,128]{1,0:T(8,128)S(1)} %add.74), channel_id=1, source_target_pairs={{0,4},{4,8},{8,12},{12,0},{1,5},{5,9},{9,13},{13,1},{2,6},{6,10},{... | collective-permute-start | bytes 49160 | tf_op jit(solution)/shard_map/ppermute | solution.py:243
  142.9 8.4 %collective-permute-start.32 = (bf16[160,640]{1,0:T(8,128)(2,1)}, bf16[160,640]{1,0:T(8,128)(2,1)S(1)}, u32[]{:S(2)}, u32[]{:S(2)}) collective-permute-start(bf16[160,640]{1,0:T(8,128)(2,1)} %get-tuple-element.116), channel_id=1, source_target_pairs={{0,2},{2,0},{1,3},{3,1},{4,6},{6,4},{5,7},{7,5},{8,10},{10,8},{9,1... | collective-permute-start | bytes 614408 | tf_op jit(solution)/shard_map/ppermute | solution.py:427
  (43 other events, 347.6 us)
Sparse Core Ops, SparseCore 0:
  12.9 37.6 all-gather.1
  96.6 46.0 reduce-scatter.1

commit v5 on v4

--- a/solution.py
+++ b/solution.py
@@ -46,7 +46,7 @@
     return pl.BlockSpec(shape, lambda i, s: (0,) * len(shape))
 
 
-def call(kernel, scalars, ins, outs, name, scratch=(), mib=MIB, pinned=(), steps=1):
+def call(kernel, scalars, ins, outs, name, scratch=(), mib=MIB, pinned=(), steps=1, blocked=None):
     outs = pl.pallas_call(
         kernel,
         out_shape=[
@@ -56,7 +56,7 @@
             num_scalar_prefetch=1,
             grid=(steps,),
             in_specs=[spec for _, spec in ins],
-            out_specs=[whole(o[0]) for o in outs],
+            out_specs=[(blocked or {}).get(i, whole(o[0])) for i, o in enumerate(outs)],
             scratch_shapes=list(scratch),
         ),
         compiler_params=pltpu.CompilerParams(vmem_limit_bytes=mib * 1024 * 1024),
@@ -169,6 +169,25 @@
 
 
 def compare_kernel(s, pred, normed, proj, sm0, cr0, sm1, cr1, gp, back, small, inner):
+    step = pl.program_id(0)
+
+    @pl.when(step == 0)
+    def _():
+        differences(s, pred, (sm0, cr0, sm1, cr1), gp, small, inner)
+
+    for part in range(2):
+        base = pl.multiple_of((step * 2 + part) * 640, 128)
+        grad = lax.dot_general(
+            gp[...], proj[pl.ds(base, 640), :], (((1,), (1,)), ((), ())), preferred_element_type=F32
+        )
+        back[0, :, part * 640 : part * 640 + 640] = grad.astype(BF)
+        gain = jnp.sum(grad * normed[:, pl.ds(base, 640)].astype(F32), axis=0, keepdims=True)
+        for i in range(5):
+            small[pl.ds((step * 2 + part) * 5 + i, 1), :] = gain[:, i * 128 : i * 128 + 128]
+
+
+def differences(s, pred, gots, gp, small, inner):
+    sm0, cr0, sm1, cr1 = gots
     square = jnp.zeros((1, 640), F32)
     for got, stage, core in (
         (sm0, 0, s[C]),
@@ -190,15 +209,6 @@
     turned = jnp.broadcast_to(inner[...], (512, 128)).T
     for i in range(4):
         small[21 + i : 22 + i, :] = turned[:1, i * 128 : i * 128 + 128]
-    for part in range(4):
-        cols = slice(part * 640, part * 640 + 640)
-        grad = lax.dot_general(
-            gp[...], proj[cols, :], (((1,), (1,)), ((), ())), preferred_element_type=F32
-        )
-        back[part // 2, :, (part % 2) * 640 : (part % 2) * 640 + 640] = grad.astype(BF)
-        gain = jnp.sum(grad * normed[:, cols].astype(F32), axis=0, keepdims=True)
-        for i in range(5):
-            small[part * 5 + i : part * 5 + i + 1, :] = gain[:, i * 128 : i * 128 + 128]
 
 
 def hidden_kernel(s, grad, inner, hidden, inverse_rms, norm_gain, out):
@@ -381,6 +391,8 @@
         [((512, blk), BF, True), ((2, 512, width), BF, True), ((32, 128), F32, True)],
         "compare",
         scratch=[pltpu.VMEM((512, 1), F32)],
+        steps=2,
+        blocked={1: pl.BlockSpec((1, 512, width), lambda i, s: (i, 0, 0))},
     )
     back = back.reshape(1024, width)
     summed = lax.psum_scatter(back, ("grp", "dp"), scatter_dimension=0, tiled=True)
@@ -394,6 +406,10 @@
         "gproj",
     )
     recv = lax.ppermute(sent, "core", swap)
+    inner = small[21:25]
+    small = sum_over(small[:21], "x", NX)
+    small, _ = barrier((jnp.concatenate([small, inner]), sent))
+    recv, small = barrier((recv, small))
     own, *outs = call(
         gproj_add_kernel,
         scalars,
@@ -403,12 +419,12 @@
     )
     got = {j: lax.ppermute(outs[j - 1], "x", ring(NX, j)) for j in (2, 1, 3)}
 
+    cross = [lax.ppermute(a, "core", swap) for a in barrier((*cross, own))[:2]]
     small, _ = barrier((small, own))
-    cross = [lax.ppermute(a, "core", swap) for a in barrier((*cross, own))[:2]]
     small = sum_over(small, "dp", 4)
     small = sum_over(small, "grp", 2)
     inner = lax.dynamic_slice_in_dim(small, 21 + d, 1, 0)
-    small = sum_over(small, "zh", 2)
+    small = sum_over(small[:21], "zh", 2)
     (target,) = call(
         assemble_kernel,
         scalars,
@@ -427,8 +443,6 @@
     gsent = lax.ppermute(gsent, "zh", swap)
     small, _ = barrier((small, gkept))
     small = sum_over(small, "core", 2)
-    small = sum_over(small, "x", NX)
-    grad_proj = (gkept + gsent.astype(F32)) / live_count
     small = small.reshape(-1)
     distill_loss = small[20 * 128] / (live_count * D_T)
     gain_half = lax.dynamic_slice_in_dim(norm_gain, g * width, width, 0)
@@ -449,6 +463,8 @@
         "hidden",
         pinned=range(1),
     )
+    gsent, grad_hidden = barrier((gsent, grad_hidden))
+    grad_proj = (gkept + gsent.astype(F32)) / live_count
     return (target[None], distill_loss, grad_proj, grad_gain, grad_hidden[None])
 
 

time: 163 us -> 159 us (0.975)
  waiting for transfers between devices: 38.7 us -> 30.1 us
    ppermute x1, waiting for transfers between devices: 3.34 us -> 0.01 us  [body(): recv = lax.ppermute(sent, 'core', swap)]
    ppermute x9, starting transfers between devices: 12.9 us -> 14.7 us  [sum_over(): got = [lax.ppermute(array, axis, ring(n, j)) for j in range(1, n)]]
    ppermute x1, waiting for transfers between devices: 4 us -> 2.28 us  [body(): gsent = lax.ppermute(gsent, 'zh', swap)]
  transfers between devices with their start and end apart: 35 -> 35, of which waited for: 13 -> 13; matrix products, arithmetic and copies ran while one was open for 5% -> 5% of each run, Pallas kernels for 21% -> 23%
where the time goes in v5:
time: 159 us; the launch traced here: 157 us
  starting transfers between devices  50.2 us (32%)
  Pallas kernels  44.7 us (28%)
  waiting for transfers between devices  30.1 us (19%)
  between operations  16.9 us (11%)
  local copies, waits for them, and re-layouts  5.28 us (3%)
  matrix products  5.05 us (3%)
  other arithmetic  4.74 us (3%)
    pallas_call x14, Pallas kernels, call(): pl.pallas_call(kernel, out_shape=[pltpu.HBM(o[0], o[1]) if len(o) == 3 el...  44.7 us
    ppermute x9, starting transfers between devices, sum_over(): got = [lax.ppermute(array, axis, ring(n, j)) for j in range(1, n)]  14.7 us
    ppermute x6, starting transfers between devices, body(): lax.ppermute(outs[j - 1], 'x', ring(NX, j))  10 us
    ppermute x9, waiting for transfers between devices, sum_over(): got = [lax.ppermute(array, axis, ring(n, j)) for j in range(1, n)]  8.42 us
    ppermute x6, waiting for transfers between devices, body(): lax.ppermute(outs[j - 1], 'x', ring(NX, j))  7.65 us
    ppermute x2, starting transfers between devices, body(): lax.ppermute(done_same, ('dp', 'core'), to_owner(st, False))  6.75 us
    ppermute x2, starting transfers between devices, body(): w_z = [lax.ppermute(w, ('grp', 'zh'), WRAP) for w in w_z]  6.08 us
    ppermute x2, waiting for transfers between devices, body(): w_z = [lax.ppermute(w, ('grp', 'zh'), WRAP) for w in w_z]  5.13 us
  transfers between devices with their start and end apart: 35, of which 13 were waited for; matrix products, arithmetic and copies ran while one was open for 5% of the time, Pallas kernels for 23%

profile of v5, /device:TPU:0, one launch (start us, length us, event | category | flops | bytes accessed | tf_op | source)
XLA Modules:
  0.0 157.1 jit_solution(9032909103069415705)
XLA Ops:
  8.0 3.5 %pick.1 = (bf16[4,2,128,256]{3,2,1,0:T(8,128)(2,1)}, bf16[256,2560]{1,0:T(8,128)(2,1)}, bf16[128,1280]{1,0:T(8,128)(2,1)}) custom-call(s32[11]{0:T(128)S(1)} %concatenate.6.s, bf16[4,4,128,256]{3,2,1,0:T(8,128)(2,1)} %bitcast.35, bf16[256,5120]{1,0:T(8,128)(2,1)} %w_a.3, bf16[256,5120]{1,0:T(8,128)(2,1)} %w_a.3, bf16[256,5120]{1,0:T(8,128)(2,1)} %w_a.3, ...), custom_call_target="tpu_custom_call" | custom-call | flops 1 | bytes 1 | tf_op jit(solution)/shard_map/pick/pallas_call | solution.py:50
  13.0 4.2 %collective-permute-start.1 = (bf16[4,2,128,256]{3,2,1,0:T(8,128)(2,1)}, bf16[4,2,128,256]{3,2,1,0:T(8,128)(2,1)S(1)}, u32[]{:S(2)}, u32[]{:S(2)}) collective-permute-start(bf16[4,2,128,256]{3,2,1,0:T(8,128)(2,1)} %get-tuple-element.67), channel_id=1, source_target_pairs={{0,66},{2,64},{64,2},{66,0},{1,67},{3,65},{65,3},{67,1},{4,70},{6,... | collective-permute-start | bytes 1572872 | tf_op jit(solution)/shard_map/ppermute | solution.py:296
  18.3 2.9 %pick_weights.1 = (bf16[512,640]{1,0:T(8,128)(2,1)}, bf16[512,640]{1,0:T(8,128)(2,1)}) custom-call(s32[11]{0:T(128)S(1)} %concatenate.6.s, bf16[256,5120]{1,0:T(8,128)(2,1)} %w_a.3, bf16[256,5120]{1,0:T(8,128)(2,1)} %w_a.3, bf16[256,2560]{1,0:T(8,128)(2,1)} %copy-done.2), custom_call_target="tpu_custom_call" | custom-call | flops 1 | bytes 1 | tf_op jit(solution)/shard_map/pick_weights/pallas_call | solution.py:50
  21.2 2.9 %collective-permute-start.4 = (bf16[512,640]{1,0:T(8,128)(2,1)}, bf16[512,640]{1,0:T(8,128)(2,1)S(1)}, u32[]{:S(2)}, u32[]{:S(2)}) collective-permute-start(bf16[512,640]{1,0:T(8,128)(2,1)} %get-tuple-element.72), channel_id=1, source_target_pairs={{0,66},{2,64},{64,2},{66,0},{1,67},{3,65},{65,3},{67,1},{4,70},{6,... | collective-permute-start | bytes 1966088 | tf_op jit(solution)/shard_map/ppermute | solution.py:334
  24.1 5.1 %attend_chip.1.ctx_a = bf16[1024,256]{1,0:T(8,128)(2,1)S(1)} custom-call(s32[11]{0:T(128)S(1)} %concatenate.6.s, bf16[4,4,128,256]{3,2,1,0:T(8,128)(2,1)S(1)} %bitcast.36, bf16[2048,512]{1,0:T(8,128)(2,1)S(1)} %bitcast.28, bf16[2048,512]{1,0:T(8,128)(2,1)S(1)} %bitcast.30), custom_call_target="tpu_custom_call" | custom-call | flops 1 | bytes 1 | tf_op jit(solution)/shard_map/attend_chip/pallas_call | solution.py:50
  30.2 5.1 %attend_next.1.ctx_b = bf16[1024,256]{1,0:T(8,128)(2,1)S(1)} custom-call(s32[11]{0:T(128)S(1)} %concatenate.6.s, bf16[4,2,128,256]{3,2,1,0:T(8,128)(2,1)S(1)} %collective-permute-done.1.q_ref, bf16[2048,512]{1,0:T(8,128)(2,1)S(1)} %bitcast.29, bf16[2048,512]{1,0:T(8,128)(2,1)S(1)} %bitcast.31), custom_call_target="tpu_custom_call" | custom-call | flops 1 | bytes 1 | tf_op jit(solution)/shard_map/attend_next/pallas_call | solution.py:50
  35.9 3.2 %collective-permute-start.5 = (bf16[512,640]{1,0:T(8,128)(2,1)}, bf16[512,640]{1,0:T(8,128)(2,1)}, u32[]{:S(2)}, u32[]{:S(2)}) collective-permute-start(bf16[512,640]{1,0:T(8,128)(2,1)} %get-tuple-element.81), channel_id=1, source_target_pairs={{0,66},{2,64},{64,2},{66,0},{1,67},{3,65},{65,3},{67,1},{4,70},{6,... | collective-permute-start | bytes 1966088 | tf_op jit(solution)/shard_map/ppermute | solution.py:334
  39.1 5.1 %collective-permute-done.4.w_z = bf16[512,640]{1,0:T(8,128)(2,1)S(1)} collective-permute-done((bf16[512,640]{1,0:T(8,128)(2,1)}, bf16[512,640]{1,0:T(8,128)(2,1)S(1)}, u32[]{:S(2)}, u32[]{:S(2)}) %collective-permute-start.4) | collective-permute-done | bytes 655392 | tf_op jit(solution)/shard_map/ppermute | solution.py:334
  44.2 3.5 %project_0.1 = (f32[2,128,640]{2,1,0:T(8,128)S(1)}, bf16[2,128,640]{2,1,0:T(8,128)(2,1)}, bf16[2,128,640]{2,1,0:T(8,128)(2,1)}, bf16[2,128,640]{2,1,0:T(8,128)(2,1)}) custom-call(s32[11]{0:T(128)S(1)} %concatenate.6.s, bf16[1024,256]{1,0:T(8,128)(2,1)S(1)} %attend_chip.1.ctx_a, bf16[1024,256]{1,0:T(8,128)(2,1)S(1)} %collective-permute-done.2.ctx_ac, ...), custom_call_target="tpu_custom_call" | custom-call | flops 1 | bytes 1 | tf_op jit(solution)/shard_map/project_0/pallas_call | solution.py:50
  50.1 2.7 %collective-permute-start.7 = (bf16[2,128,640]{2,1,0:T(8,128)(2,1)}, bf16[2,128,640]{2,1,0:T(8,128)(2,1)}, u32[]{:S(2)}, u32[]{:S(2)}) collective-permute-start(bf16[2,128,640]{2,1,0:T(8,128)(2,1)} %get-tuple-element.85), channel_id=1, source_target_pairs={{0,8},{4,12},{8,0},{12,4},{1,9},{5,13},{9,1},{13,5},{2,10},{6,14},... | collective-permute-start | bytes 983048 | tf_op jit(solution)/shard_map/ppermute | solution.py:359
  54.3 5.1 %fusion.4.pred = f32[512,640]{1,0:T(8,128)S(1)} fusion(bf16[512,2560]{1,0:T(8,128)(2,1)} %all-gather.2.cloned.1.call-done.normed, bf16[2560,640]{1,0:T(8,128)(2,1)} %proj.1), kind=kOutput, calls=%fused_computation.15 | convolution fusion | flops 1677721600 | bytes 7208960 | tf_op jit(solution)/shard_map/dot_general | solution.py:357
  59.4 4.5 %project_1.1 = (f32[2,128,640]{2,1,0:T(8,128)S(1)}, bf16[2,128,640]{2,1,0:T(8,128)(2,1)}, bf16[2,128,640]{2,1,0:T(8,128)(2,1)}, bf16[2,128,640]{2,1,0:T(8,128)(2,1)}) custom-call(s32[11]{0:T(128)S(1)} %concatenate.6.s, bf16[1024,256]{1,0:T(8,128)(2,1)S(1)} %copy-done.10, bf16[1024,256]{1,0:T(8,128)(2,1)S(1)} %copy-done.18, bf16[1024,256]{1,0:T(8,128)(2,1)S(1)} %copy-done.12, ...), custom_call_target="tpu_custom_call" | custom-call | flops 1 | bytes 1 | tf_op jit(solution)/shard_map/project_1/pallas_call | solution.py:50
  70.6 3.3 %collective-permute-start.13 = (bf16[128,640]{1,0:T(8,128)(2,1)S(1)}, bf16[128,640]{1,0:T(8,128)(2,1)S(1)}, u32[]{:S(2)}, u32[]{:S(2)}) collective-permute-start(bf16[128,640]{1,0:T(8,128)(2,1)S(1)} %get-tuple-element.88.same0), channel_id=1, source_target_pairs={{0,32},{1,49},{16,48},{17,1},{32,0},{33,17},{48,16},{49,33},{2,34}... | collective-permute-start | bytes 491528 | tf_op jit(solution)/shard_map/ppermute | solution.py:378
  75.2 6.3 %collective-permute-done.11.r2 = bf16[2,128,640]{2,1,0:T(8,128)(2,1)S(1)} collective-permute-done((bf16[2,128,640]{2,1,0:T(8,128)(2,1)}, bf16[2,128,640]{2,1,0:T(8,128)(2,1)S(1)}, u32[]{:S(2)}, u32[]{:S(2)}) %collective-permute-start.11) | collective-permute-done | bytes 327712 | tf_op jit(solution)/shard_map/ppermute | solution.py:359
  83.2 3.5 %collective-permute-start.15 = (bf16[128,640]{1,0:T(8,128)(2,1)S(1)}, bf16[128,640]{1,0:T(8,128)(2,1)S(1)}, u32[]{:S(2)}, u32[]{:S(2)}) collective-permute-start(bf16[128,640]{1,0:T(8,128)(2,1)S(1)} %get-tuple-element.93.same1), channel_id=1, source_target_pairs={{0,16},{1,1},{16,32},{17,17},{32,48},{33,33},{48,0},{49,49},{2,18}... | collective-permute-start | bytes 491528 | tf_op jit(solution)/shard_map/ppermute | solution.py:378
  87.3 4.2 %collective-permute-done.15.sm1 = bf16[128,640]{1,0:T(8,128)(2,1)S(1)} collective-permute-done((bf16[128,640]{1,0:T(8,128)(2,1)S(1)}, bf16[128,640]{1,0:T(8,128)(2,1)S(1)}, u32[]{:S(2)}, u32[]{:S(2)}) %collective-permute-start.15) | collective-permute-done | bytes 163872 | tf_op jit(solution)/shard_map/ppermute | solution.py:378
  91.6 5.2 %compare.1 = (bf16[512,640]{1,0:T(8,128)(2,1)}, bf16[2,512,1280]{2,1,0:T(8,128)(2,1)}, f32[32,128]{1,0:T(8,128)}) custom-call(s32[11]{0:T(128)S(1)} %concatenate.6.s, f32[512,640]{1,0:T(8,128)S(1)} %fusion.4.pred, bf16[512,2560]{1,0:T(8,128)(2,1)S(1)} %copy-done.5, bf16[2560,640]{1,0:T(8,128)(2,1)S(1)} %copy-done.14, ...), custom_call_target="tpu_custom_call" | custom-call | flops 1 | bytes 1 | tf_op jit(solution)/shard_map/compare/pallas_call | solution.py:50
  97.9 4.0 %gproj.1 = (bf16[4,2,160,640]{3,2,1,0:T(8,128)(2,1)}, f32[4,2,160,640]{3,2,1,0:T(8,128)S(1)}) custom-call(s32[11]{0:T(128)S(1)} %concatenate.6.s, bf16[512,2560]{1,0:T(8,128)(2,1)S(1)} %copy-done.5, bf16[512,640]{1,0:T(8,128)(2,1)S(1)} %copy-done.21), custom_call_target="tpu_custom_call" | custom-call | flops 1 | bytes 1 | tf_op jit(solution)/shard_map/gproj/pallas_call | solution.py:50
  105.1 2.4 %collective-permute-start.19 = (f32[21,128]{1,0:T(8,128)S(1)}, f32[21,128]{1,0:T(8,128)S(1)}, u32[]{:S(2)}, u32[]{:S(2)}) collective-permute-start(f32[21,128]{1,0:T(8,128)S(1)} %slice.12), channel_id=1, source_target_pairs={{0,8},{4,12},{8,0},{12,4},{1,9},{5,13},{9,1},{13,5},{2,10},{6,14},... | collective-permute-start | bytes 32264 | tf_op jit(solution)/shard_map/ppermute | solution.py:253
  113.2 3.0 %collective-permute-start.24 = (f32[25,128]{1,0:T(8,128)S(1)}, f32[25,128]{1,0:T(8,128)S(1)}, u32[]{:S(2)}, u32[]{:S(2)}) collective-permute-start(f32[25,128]{1,0:T(8,128)S(1)} %pad_maximum_fusion), channel_id=1, source_target_pairs={{0,32},{16,48},{32,0},{48,16},{1,33},{17,49},{33,1},{49,17},{2,34}... | collective-permute-start | bytes 38408 | tf_op jit(solution)/shard_map/ppermute | solution.py:253
  117.8 3.7 %collective-permute-start.29 = (bf16[2,160,640]{2,1,0:T(8,128)(2,1)}, bf16[2,160,640]{2,1,0:T(8,128)(2,1)S(1)}, u32[]{:S(2)}, u32[]{:S(2)}) collective-permute-start(bf16[2,160,640]{2,1,0:T(8,128)(2,1)} %get-tuple-element.120), channel_id=1, source_target_pairs={{0,8},{4,12},{8,0},{12,4},{1,9},{5,13},{9,1},{13,5},{2,10},{6,14},... | collective-permute-start | bytes 1228808 | tf_op jit(solution)/shard_map/ppermute | solution.py:420
  121.7 4.5 %collective-permute-done.26 = f32[25,128]{1,0:T(8,128)S(1)} collective-permute-done((f32[25,128]{1,0:T(8,128)S(1)}, f32[25,128]{1,0:T(8,128)S(1)}, u32[]{:S(2)}, u32[]{:S(2)}) %collective-permute-start.26) | collective-permute-done | bytes 12832 | tf_op jit(solution)/shard_map/ppermute | solution.py:253
  126.3 4.9 %collective-permute-start.27 = (f32[21,128]{1,0:T(8,128)S(1)}, f32[21,128]{1,0:T(8,128)S(1)}, u32[]{:S(2)}, u32[]{:S(2)}) collective-permute-start(f32[21,128]{1,0:T(8,128)S(1)} %slice.16), channel_id=1, source_target_pairs={{0,2},{2,0},{1,3},{3,1},{4,6},{6,4},{5,7},{7,5},{8,10},{10,8},{9,1... | collective-permute-start | bytes 32264 | tf_op jit(solution)/shard_map/ppermute | solution.py:253
  143.5 2.5 %hidden.1 = f32[128,1280]{1,0:T(8,128)} custom-call(s32[11]{0:T(128)S(1)} %concatenate.6.s, bf16[128,1280]{1,0:T(8,128)(2,1)} %reduce-scatter.2.cloned.1.call-done.grad, f32[128,1]{1,0:T(8,128)S(1)} %copy.14.inner, bf16[128,2560]{1,0:T(8,128)(2,1)S(1)} %bitcast.34, f32[128,1]{1,0:T(8,128)S(1)} %copy.15.inverse_rms, f32[1,2560]{1,0:T(1,128)S(1)} %broadcast_in_dim.11.norm_gain), custom_call_target="tpu_custom_call" | custom-call | flops 1 | bytes 1 | tf_op jit(solution)/shard_map/hidden/pallas_call | solution.py:50
  (148 shorter events, 44.9 us)
Async XLA Ops:
  7.2 47.1 %all-gather.2.cloned.1.call-start = ((), (), s32[]{:S(2)}) async-start(), calls=%async_computation.1 | async-start | bytes 3276800 | tf_op jit(solution)/shard_map/all_gather | solution.py:320
  12.8 130.7 %reduce-scatter.2.cloned.1.call-start = ((), (), s32[]{:S(2)}) async-start(), calls=%async_computation.2 | async-start | bytes 2949120 | tf_op jit(solution)/shard_map/reduce_scatter | solution.py:398
  13.0 17.2 %collective-permute-start.1 = (bf16[4,2,128,256]{3,2,1,0:T(8,128)(2,1)}, bf16[4,2,128,256]{3,2,1,0:T(8,128)(2,1)S(1)}, u32[]{:S(2)}, u32[]{:S(2)}) collective-permute-start(bf16[4,2,128,256]{3,2,1,0:T(8,128)(2,1)} %get-tuple-element.67), channel_id=1, source_target_pairs={{0,66},{2,64},{64,2},{66,0},{1,67},{3,65},{65,3},{67,1},{4,70},{6,... | collective-permute-start | bytes 1572872 | tf_op jit(solution)/shard_map/ppermute | solution.py:296
  21.2 23.0 %collective-permute-start.4 = (bf16[512,640]{1,0:T(8,128)(2,1)}, bf16[512,640]{1,0:T(8,128)(2,1)S(1)}, u32[]{:S(2)}, u32[]{:S(2)}) collective-permute-start(bf16[512,640]{1,0:T(8,128)(2,1)} %get-tuple-element.72), channel_id=1, source_target_pairs={{0,66},{2,64},{64,2},{66,0},{1,67},{3,65},{65,3},{67,1},{4,70},{6,... | collective-permute-start | bytes 1966088 | tf_op jit(solution)/shard_map/ppermute | solution.py:334
  35.9 23.5 %collective-permute-start.5 = (bf16[512,640]{1,0:T(8,128)(2,1)}, bf16[512,640]{1,0:T(8,128)(2,1)}, u32[]{:S(2)}, u32[]{:S(2)}) collective-permute-start(bf16[512,640]{1,0:T(8,128)(2,1)} %get-tuple-element.81), channel_id=1, source_target_pairs={{0,66},{2,64},{64,2},{66,0},{1,67},{3,65},{65,3},{67,1},{4,70},{6,... | collective-permute-start | bytes 1966088 | tf_op jit(solution)/shard_map/ppermute | solution.py:334
  39.1 25.5 %collective-permute-start.9 = (bf16[128,1280]{1,0:T(8,128)(2,1)}, bf16[128,1280]{1,0:T(8,128)(2,1)}, u32[]{:S(2)}, u32[]{:S(2)}) collective-permute-start(bf16[128,1280]{1,0:T(8,128)(2,1)} %get-tuple-element.87), channel_id=1, source_target_pairs={{0,1},{1,0},{2,3},{3,2},{4,5},{5,4},{6,7},{7,6},{8,9},{9,8},{10,11... | collective-permute-start | bytes 983048 | tf_op jit(solution)/shard_map/ppermute | solution.py:298
  48.6 18.3 %collective-permute-start.6 = (bf16[2,128,640]{2,1,0:T(8,128)(2,1)}, bf16[2,128,640]{2,1,0:T(8,128)(2,1)}, u32[]{:S(2)}, u32[]{:S(2)}) collective-permute-start(bf16[2,128,640]{2,1,0:T(8,128)(2,1)} %get-tuple-element.84), channel_id=1, source_target_pairs={{0,4},{4,8},{8,12},{12,0},{1,5},{5,9},{9,13},{13,1},{2,6},{6,10},{... | collective-permute-start | bytes 983048 | tf_op jit(solution)/shard_map/ppermute | solution.py:359
  50.1 18.2 %collective-permute-start.7 = (bf16[2,128,640]{2,1,0:T(8,128)(2,1)}, bf16[2,128,640]{2,1,0:T(8,128)(2,1)}, u32[]{:S(2)}, u32[]{:S(2)}) collective-permute-start(bf16[2,128,640]{2,1,0:T(8,128)(2,1)} %get-tuple-element.85), channel_id=1, source_target_pairs={{0,8},{4,12},{8,0},{12,4},{1,9},{5,13},{9,1},{13,5},{2,10},{6,14},... | collective-permute-start | bytes 983048 | tf_op jit(solution)/shard_map/ppermute | solution.py:359
  52.8 15.5 %collective-permute-start.8 = (bf16[2,128,640]{2,1,0:T(8,128)(2,1)}, bf16[2,128,640]{2,1,0:T(8,128)(2,1)}, u32[]{:S(2)}, u32[]{:S(2)}) collective-permute-start(bf16[2,128,640]{2,1,0:T(8,128)(2,1)} %get-tuple-element.86), channel_id=1, source_target_pairs={{0,12},{4,0},{8,4},{12,8},{1,13},{5,1},{9,5},{13,9},{2,14},{6,2},{... | collective-permute-start | bytes 983048 | tf_op jit(solution)/shard_map/ppermute | solution.py:359
  63.9 11.3 %collective-permute-start.10 = (bf16[2,128,640]{2,1,0:T(8,128)(2,1)}, bf16[2,128,640]{2,1,0:T(8,128)(2,1)S(1)}, u32[]{:S(2)}, u32[]{:S(2)}) collective-permute-start(bf16[2,128,640]{2,1,0:T(8,128)(2,1)} %get-tuple-element.90), channel_id=1, source_target_pairs={{0,4},{4,8},{8,12},{12,0},{1,5},{5,9},{9,13},{13,1},{2,6},{6,10},{... | collective-permute-start | bytes 983048 | tf_op jit(solution)/shard_map/ppermute | solution.py:359
  64.5 16.9 %collective-permute-start.11 = (bf16[2,128,640]{2,1,0:T(8,128)(2,1)}, bf16[2,128,640]{2,1,0:T(8,128)(2,1)S(1)}, u32[]{:S(2)}, u32[]{:S(2)}) collective-permute-start(bf16[2,128,640]{2,1,0:T(8,128)(2,1)} %get-tuple-element.91), channel_id=1, source_target_pairs={{0,8},{4,12},{8,0},{12,4},{1,9},{5,13},{9,1},{13,5},{2,10},{6,14},... | collective-permute-start | bytes 983048 | tf_op jit(solution)/shard_map/ppermute | solution.py:359
  66.9 14.6 %collective-permute-start.12 = (bf16[2,128,640]{2,1,0:T(8,128)(2,1)}, bf16[2,128,640]{2,1,0:T(8,128)(2,1)S(1)}, u32[]{:S(2)}, u32[]{:S(2)}) collective-permute-start(bf16[2,128,640]{2,1,0:T(8,128)(2,1)} %get-tuple-element.92), channel_id=1, source_target_pairs={{0,12},{4,0},{8,4},{12,8},{1,13},{5,1},{9,5},{13,9},{2,14},{6,2},{... | collective-permute-start | bytes 983048 | tf_op jit(solution)/shard_map/ppermute | solution.py:359
  70.6 16.8 %collective-permute-start.13 = (bf16[128,640]{1,0:T(8,128)(2,1)S(1)}, bf16[128,640]{1,0:T(8,128)(2,1)S(1)}, u32[]{:S(2)}, u32[]{:S(2)}) collective-permute-start(bf16[128,640]{1,0:T(8,128)(2,1)S(1)} %get-tuple-element.88.same0), channel_id=1, source_target_pairs={{0,32},{1,49},{16,48},{17,1},{32,0},{33,17},{48,16},{49,33},{2,34}... | collective-permute-start | bytes 491528 | tf_op jit(solution)/shard_map/ppermute | solution.py:378
  73.8 13.5 %collective-permute-start.14 = (bf16[128,640]{1,0:T(8,128)(2,1)S(1)}, bf16[128,640]{1,0:T(8,128)(2,1)S(1)}, u32[]{:S(2)}, u32[]{:S(2)}) collective-permute-start(bf16[128,640]{1,0:T(8,128)(2,1)S(1)} %get-tuple-element.110), channel_id=1, source_target_pairs={{0,33},{1,48},{16,49},{17,0},{32,1},{33,16},{48,17},{49,32},{2,35}... | collective-permute-start | bytes 491528 | tf_op jit(solution)/shard_map/ppermute | solution.py:379
  83.2 8.4 %collective-permute-start.15 = (bf16[128,640]{1,0:T(8,128)(2,1)S(1)}, bf16[128,640]{1,0:T(8,128)(2,1)S(1)}, u32[]{:S(2)}, u32[]{:S(2)}) collective-permute-start(bf16[128,640]{1,0:T(8,128)(2,1)S(1)} %get-tuple-element.93.same1), channel_id=1, source_target_pairs={{0,16},{1,1},{16,32},{17,17},{32,48},{33,33},{48,0},{49,49},{2,18}... | collective-permute-start | bytes 491528 | tf_op jit(solution)/shard_map/ppermute | solution.py:378
  101.9 9.3 %collective-permute-start.17 = (bf16[4,2,160,640]{3,2,1,0:T(8,128)(2,1)}, bf16[4,2,160,640]{3,2,1,0:T(8,128)(2,1)S(1)}, u32[]{:S(2)}, u32[]{:S(2)}) collective-permute-start(bf16[4,2,160,640]{3,2,1,0:T(8,128)(2,1)} %get-tuple-element.99), channel_id=1, source_target_pairs={{0,1},{1,0},{2,3},{3,2},{4,5},{5,4},{6,7},{7,6},{8,9},{9,8},{10,11... | collective-permute-start | bytes 4915208 | tf_op jit(solution)/shard_map/ppermute | solution.py:408
  113.0 8.6 %collective-permute-start.23 = (f32[25,128]{1,0:T(8,128)S(1)}, f32[25,128]{1,0:T(8,128)S(1)}, u32[]{:S(2)}, u32[]{:S(2)}) collective-permute-start(f32[25,128]{1,0:T(8,128)S(1)} %pad_maximum_fusion), channel_id=1, source_target_pairs={{0,16},{16,32},{32,48},{48,0},{1,17},{17,33},{33,49},{49,1},{2,18}... | collective-permute-start | bytes 38408 | tf_op jit(solution)/shard_map/ppermute | solution.py:253
  113.2 8.4 %collective-permute-start.24 = (f32[25,128]{1,0:T(8,128)S(1)}, f32[25,128]{1,0:T(8,128)S(1)}, u32[]{:S(2)}, u32[]{:S(2)}) collective-permute-start(f32[25,128]{1,0:T(8,128)S(1)} %pad_maximum_fusion), channel_id=1, source_target_pairs={{0,32},{16,48},{32,0},{48,16},{1,33},{17,49},{33,1},{49,17},{2,34}... | collective-permute-start | bytes 38408 | tf_op jit(solution)/shard_map/ppermute | solution.py:253
  116.2 5.4 %collective-permute-start.25 = (f32[25,128]{1,0:T(8,128)S(1)}, f32[25,128]{1,0:T(8,128)S(1)}, u32[]{:S(2)}, u32[]{:S(2)}) collective-permute-start(f32[25,128]{1,0:T(8,128)S(1)} %pad_maximum_fusion), channel_id=1, source_target_pairs={{0,48},{16,0},{32,16},{48,32},{1,49},{17,1},{33,17},{49,33},{2,50}... | collective-permute-start | bytes 38408 | tf_op jit(solution)/shard_map/ppermute | solution.py:253
  117.5 19.5 %collective-permute-start.28 = (bf16[2,160,640]{2,1,0:T(8,128)(2,1)}, bf16[2,160,640]{2,1,0:T(8,128)(2,1)S(1)}, u32[]{:S(2)}, u32[]{:S(2)}) collective-permute-start(bf16[2,160,640]{2,1,0:T(8,128)(2,1)} %get-tuple-element.119), channel_id=1, source_target_pairs={{0,4},{4,8},{8,12},{12,0},{1,5},{5,9},{9,13},{13,1},{2,6},{6,10},{... | collective-permute-start | bytes 1228808 | tf_op jit(solution)/shard_map/ppermute | solution.py:420
  117.8 19.6 %collective-permute-start.29 = (bf16[2,160,640]{2,1,0:T(8,128)(2,1)}, bf16[2,160,640]{2,1,0:T(8,128)(2,1)S(1)}, u32[]{:S(2)}, u32[]{:S(2)}) collective-permute-start(bf16[2,160,640]{2,1,0:T(8,128)(2,1)} %get-tuple-element.120), channel_id=1, source_target_pairs={{0,8},{4,12},{8,0},{12,4},{1,9},{5,13},{9,1},{13,5},{2,10},{6,14},... | collective-permute-start | bytes 1228808 | tf_op jit(solution)/shard_map/ppermute | solution.py:420
  121.5 16.1 %collective-permute-start.30 = (bf16[2,160,640]{2,1,0:T(8,128)(2,1)}, bf16[2,160,640]{2,1,0:T(8,128)(2,1)S(1)}, u32[]{:S(2)}, u32[]{:S(2)}) collective-permute-start(bf16[2,160,640]{2,1,0:T(8,128)(2,1)} %get-tuple-element.121), channel_id=1, source_target_pairs={{0,12},{4,0},{8,4},{12,8},{1,13},{5,1},{9,5},{13,9},{2,14},{6,2},{... | collective-permute-start | bytes 1228808 | tf_op jit(solution)/shard_map/ppermute | solution.py:420
  126.3 7.9 %collective-permute-start.27 = (f32[21,128]{1,0:T(8,128)S(1)}, f32[21,128]{1,0:T(8,128)S(1)}, u32[]{:S(2)}, u32[]{:S(2)}) collective-permute-start(f32[21,128]{1,0:T(8,128)S(1)} %slice.16), channel_id=1, source_target_pairs={{0,2},{2,0},{1,3},{3,1},{4,6},{6,4},{5,7},{7,5},{8,10},{10,8},{9,1... | collective-permute-start | bytes 32264 | tf_op jit(solution)/shard_map/ppermute | solution.py:253
  139.1 9.3 %collective-permute-start.32 = (bf16[160,640]{1,0:T(8,128)(2,1)}, bf16[160,640]{1,0:T(8,128)(2,1)S(1)}, u32[]{:S(2)}, u32[]{:S(2)}) collective-permute-start(bf16[160,640]{1,0:T(8,128)(2,1)} %get-tuple-element.124), channel_id=1, source_target_pairs={{0,2},{2,0},{1,3},{3,1},{4,6},{6,4},{5,7},{7,5},{8,10},{10,8},{9,1... | collective-permute-start | bytes 614408 | tf_op jit(solution)/shard_map/ppermute | solution.py:443
  (43 other events, 366.2 us)
Sparse Core Ops, SparseCore 0:
  12.9 37.6 all-gather.1
  96.9 45.1 reduce-scatter.1

commit v6 on v5

--- a/solution.py
+++ b/solution.py
@@ -1,3 +1,4 @@
+import functools
 import math
 
 import jax
@@ -28,6 +29,7 @@
 WRAP = [(g * 2 + z, (1 - g) * 2 + (1 - z)) for g in range(2) for z in range(2)]
 MIB = 32
 COST = 1
+IN_HBM = pl.BlockSpec(memory_space=pltpu.HBM)
 
 
 def block_of(stage, core):
@@ -46,7 +48,7 @@
     return pl.BlockSpec(shape, lambda i, s: (0,) * len(shape))
 
 
-def call(kernel, scalars, ins, outs, name, scratch=(), mib=MIB, pinned=(), steps=1, blocked=None):
+def call(kernel, scalars, ins, outs, name, scratch=(), mib=MIB, pinned=(), steps=1, blocked=None, aliases=None):
     outs = pl.pallas_call(
         kernel,
         out_shape=[
@@ -61,6 +63,7 @@
         ),
         compiler_params=pltpu.CompilerParams(vmem_limit_bytes=mib * 1024 * 1024),
         cost_estimate=pl.CostEstimate(flops=COST, bytes_accessed=COST, transcendentals=0),
+        input_output_aliases=aliases or {},
         name=name,
     )(scalars.value, *[
             pltpu.with_memory_space_constraint(a, pltpu.HBM) if i in pinned else a
@@ -168,47 +171,57 @@
         target[:, pl.ds(at, 640)] = piece[...]
 
 
-def compare_kernel(s, pred, normed, proj, sm0, cr0, sm1, cr1, gp, back, small, inner):
-    step = pl.program_id(0)
-
-    @pl.when(step == 0)
-    def _():
-        differences(s, pred, (sm0, cr0, sm1, cr1), gp, small, inner)
-
-    for part in range(2):
-        base = pl.multiple_of((step * 2 + part) * 640, 128)
-        grad = lax.dot_general(
-            gp[...], proj[pl.ds(base, 640), :], (((1,), (1,)), ((), ())), preferred_element_type=F32
-        )
-        back[0, :, part * 640 : part * 640 + 640] = grad.astype(BF)
-        gain = jnp.sum(grad * normed[:, pl.ds(base, 640)].astype(F32), axis=0, keepdims=True)
-        for i in range(5):
-            small[pl.ds((step * 2 + part) * 5 + i, 1), :] = gain[:, i * 128 : i * 128 + 128]
-
-
-def differences(s, pred, gots, gp, small, inner):
-    sm0, cr0, sm1, cr1 = gots
+def compare_kernel(stage, s, pred, normed, proj, got_same, got_cross, *refs):
+    before, (gp_out, back_out, small, gp, back, sems) = refs[:-6], refs[-6:]
+    if stage == 0:
+        small[...] = jnp.zeros((32, 128), F32)
+    else:
+        small[...] = before[2][...]
     square = jnp.zeros((1, 640), F32)
-    for got, stage, core in (
-        (sm0, 0, s[C]),
-        (cr0, 0, 1 - s[C]),
-        (sm1, 1, s[C]),
-        (cr1, 1, 1 - s[C]),
-    ):
+    inner, starts, copies = [], [], []
+    for i, (got, core) in enumerate(((got_same, s[C]), (got_cross, 1 - s[C]))):
         seq = (s[D] + 4 - block_of(stage, core)) % 4
         at = pl.multiple_of(seq * 128, 128)
+        starts.append((seq, at))
         live = lax.broadcasted_iota(jnp.int32, (128, 640), 0) < s[LENGTHS + seq] - s[FIRST]
         here = pred[pl.ds(at, 128), :]
         diff = jnp.where(live, here - got[...].astype(F32), 0.0)
         square = square + jnp.sum(diff * diff, axis=0, keepdims=True)
         rounded = diff.astype(BF)
-        gp[pl.ds(at, 128), :] = rounded
-        inner[pl.ds(at, 128), :] = jnp.sum(rounded.astype(F32) * here, axis=-1, keepdims=True)
-    small[...] = jnp.zeros((32, 128), F32)
-    small[20:21, :] = jnp.broadcast_to(jnp.sum(square, axis=-1, keepdims=True), (1, 128))
-    turned = jnp.broadcast_to(inner[...], (512, 128)).T
-    for i in range(4):
-        small[21 + i : 22 + i, :] = turned[:1, i * 128 : i * 128 + 128]
+        gp[i * 128 : i * 128 + 128] = rounded
+        inner.append(jnp.sum(rounded.astype(F32) * here, axis=-1, keepdims=True))
+        copies.append(
+            pltpu.make_async_copy(gp.at[pl.ds(i * 128, 128)], gp_out.at[pl.ds(at, 128)], sems.at[i])
+        )
+        copies[-1].start()
+    small[20:21, :] = small[20:21, :] + jnp.sum(square, axis=-1, keepdims=True)
+    turned = jnp.broadcast_to(jnp.concatenate(inner, axis=0), (256, 128)).T
+    for i, (seq, _) in enumerate(starts):
+        small[pl.ds(21 + seq, 1), :] = turned[:1, i * 128 : i * 128 + 128]
+    for half in range(2):
+        for part in range(2):
+            base = half * 1280 + part * 640
+            grad = lax.dot_general(
+                gp[...], proj[base : base + 640, :], (((1,), (1,)), ((), ())), preferred_element_type=F32
+            )
+            total = jnp.zeros((128, 640), F32)
+            for i, (_, at) in enumerate(starts):
+                rows = grad[i * 128 : i * 128 + 128]
+                back[half, i, :, part * 640 : part * 640 + 640] = rows.astype(BF)
+                total = total + rows * normed[pl.ds(at, 128), base : base + 640].astype(F32)
+            gain = jnp.sum(total, axis=0, keepdims=True)
+            for i in range(5):
+                row = base // 128 + i
+                small[row : row + 1, :] = small[row : row + 1, :] + gain[:, i * 128 : i * 128 + 128]
+        for i, (_, at) in enumerate(starts):
+            copies.append(
+                pltpu.make_async_copy(
+                    back.at[half, i], back_out.at[half, pl.ds(at, 128)], sems.at[2 + half * 2 + i]
+                )
+            )
+            copies[-1].start()
+    for copy in copies:
+        copy.wait()
 
 
 def hidden_kernel(s, grad, inner, hidden, inverse_rms, norm_gain, out):
@@ -358,7 +371,7 @@
             scalars.after(predicted)
         projected.append((own, {j: lax.ppermute(outs[j - 1], "x", ring(NX, j)) for j in (2, 1, 3)}))
 
-    compared, same, cross = [], [], []
+    same, cross, arrived, written = [], [], [], ()
     for st in stages:
         own, got = projected[st]
         done_same, done_cross = call(
@@ -375,25 +388,37 @@
         )
         same.append(done_same)
         cross.append(done_cross)
-        compared.append(lax.ppermute(done_same, ("dp", "core"), to_owner(st, False)))
-        compared.append(lax.ppermute(done_cross, ("dp", "core"), to_owner(st, True)))
-
+        arrived.append(
+            (
+                lax.ppermute(done_same, ("dp", "core"), to_owner(st, False)),
+                lax.ppermute(done_cross, ("dp", "core"), to_owner(st, True)),
+            )
+        )
+    for st in stages:
+        specs = (IN_HBM, IN_HBM, whole((32, 128)))
+        written = call(
+            functools.partial(compare_kernel, st),
+            scalars,
+            [
+                (predicted, whole((512, blk))),
+                (normed, whole((512, D_S))),
+                (projection, whole((D_S, blk))),
+                *[(a, whole((128, blk))) for a in arrived[st]],
+                *zip(written, specs),
+            ],
+            [((512, blk), BF, True), ((2, 512, width), BF, True), ((32, 128), F32)],
+            f"compare_{st}",
+            scratch=[
+                pltpu.VMEM((256, blk), BF),
+                pltpu.VMEM((2, 2, 128, width), BF),
+                pltpu.SemaphoreType.DMA((6,)),
+            ],
+            pinned=(5, 6) if st else (),
+            blocked={0: IN_HBM, 1: IN_HBM},
+            aliases={6: 0, 7: 1} if st else {},
+        )
+    gp, back, small = written
     part = (NX, 2, rows, blk)
-    gp, back, small = call(
-        compare_kernel,
-        scalars,
-        [
-            (predicted, whole((512, blk))),
-            (normed, whole((512, D_S))),
-            (projection, whole((D_S, blk))),
-            *[(a, whole((128, blk))) for a in compared],
-        ],
-        [((512, blk), BF, True), ((2, 512, width), BF, True), ((32, 128), F32, True)],
-        "compare",
-        scratch=[pltpu.VMEM((512, 1), F32)],
-        steps=2,
-        blocked={1: pl.BlockSpec((1, 512, width), lambda i, s: (i, 0, 0))},
-    )
     back = back.reshape(1024, width)
     summed = lax.psum_scatter(back, ("grp", "dp"), scatter_dimension=0, tiled=True)
 
@@ -409,7 +434,6 @@
     inner = small[21:25]
     small = sum_over(small[:21], "x", NX)
     small, _ = barrier((jnp.concatenate([small, inner]), sent))
-    recv, small = barrier((recv, small))
     own, *outs = call(
         gproj_add_kernel,
         scalars,
@@ -422,9 +446,9 @@
     cross = [lax.ppermute(a, "core", swap) for a in barrier((*cross, own))[:2]]
     small, _ = barrier((small, own))
     small = sum_over(small, "dp", 4)
-    small = sum_over(small, "grp", 2)
-    inner = lax.dynamic_slice_in_dim(small, 21 + d, 1, 0)
-    small = sum_over(small[:21], "zh", 2)
+    along = barrier([lax.ppermute(small, ("grp", "zh"), ring(NZ, j)) for j in (1, 2, 3)])
+    inner = lax.dynamic_slice_in_dim(small + along[1], 21 + d, 1, 0)
+    small = sum(along, small)[:21]
     (target,) = call(
         assemble_kernel,
         scalars,

time: 159 us -> 157 us (0.987)
  waiting for transfers between devices: 30.1 us -> 24.8 us
  starting transfers between devices: 50.2 us -> 53 us
    ppermute x0 -> x3, starting transfers between devices: none -> 7.84 us  [body(): lax.ppermute(small, ('grp', 'zh'), ring(NZ, j))]
    ppermute x9 -> x7, waiting for transfers between devices: 8.42 us -> 2.43 us  [sum_over(): got = [lax.ppermute(array, axis, ring(n, j)) for j in range(1, n)]]
    ppermute x9 -> x7, starting transfers between devices: 14.7 us -> 9.81 us  [sum_over(): got = [lax.ppermute(array, axis, ring(n, j)) for j in range(1, n)]]
    ppermute x2, waiting for transfers between devices: 4.25 us -> 1.44 us  [body(): lax.ppermute(done_same, ('dp', 'core'), to_owner(st, False))]
    ppermute x0 -> x3, waiting for transfers between devices: none -> 2.25 us  [body(): lax.ppermute(small, ('grp', 'zh'), ring(NZ, j))]
    pallas_call x14 -> x15, Pallas kernels: 44.7 us -> 45.7 us  [call(): pl.pallas_call(kernel, out_shape=[pltpu.HBM(o[0], o[1]) if len(o) == 3 el...]
    unnamed x64 -> x60, local copies, waits for them, and re-layouts: 3.78 us -> 3.12 us
  transfers between devices with their start and end apart: 35 -> 36, of which waited for: 13 -> 14; matrix products, arithmetic and copies ran while one was open for 5% -> 6% of each run, Pallas kernels for 23% -> 25%
where the time goes in v6:
time: 157 us; the launch traced here: 156 us
  starting transfers between devices  53 us (34%)
  Pallas kernels  45.7 us (29%)
  waiting for transfers between devices  24.8 us (16%)
  between operations  17 us (11%)
  other arithmetic  5.44 us (3%)
  matrix products  5.05 us (3%)
  local copies, waits for them, and re-layouts  4.61 us (3%)
    pallas_call x15, Pallas kernels, call(): pl.pallas_call(kernel, out_shape=[pltpu.HBM(o[0], o[1]) if len(o) == 3 el...  45.7 us
    ppermute x6, starting transfers between devices, body(): lax.ppermute(outs[j - 1], 'x', ring(NX, j))  10 us
    ppermute x7, starting transfers between devices, sum_over(): got = [lax.ppermute(array, axis, ring(n, j)) for j in range(1, n)]  9.81 us
    ppermute x3, starting transfers between devices, body(): lax.ppermute(small, ('grp', 'zh'), ring(NZ, j))  7.84 us
    ppermute x6, waiting for transfers between devices, body(): lax.ppermute(outs[j - 1], 'x', ring(NX, j))  7.64 us
    ppermute x2, starting transfers between devices, body(): lax.ppermute(done_same, ('dp', 'core'), to_owner(st, False))  6.75 us
    ppermute x2, starting transfers between devices, body(): w_z = [lax.ppermute(w, ('grp', 'zh'), WRAP) for w in w_z]  6.08 us
    ppermute x2, waiting for transfers between devices, body(): w_z = [lax.ppermute(w, ('grp', 'zh'), WRAP) for w in w_z]  5.13 us
  transfers between devices with their start and end apart: 36, of which 14 were waited for; matrix products, arithmetic and copies ran while one was open for 6% of the time, Pallas kernels for 25%

profile of v6, /device:TPU:0, one launch (start us, length us, event | category | flops | bytes accessed | tf_op | source)
XLA Modules:
  0.0 155.7 jit_solution(987955906000415806)
XLA Ops:
  8.0 3.5 %pick.1 = (bf16[4,2,128,256]{3,2,1,0:T(8,128)(2,1)}, bf16[256,2560]{1,0:T(8,128)(2,1)}, bf16[128,1280]{1,0:T(8,128)(2,1)}) custom-call(s32[11]{0:T(128)S(1)} %concatenate.6.s, bf16[4,4,128,256]{3,2,1,0:T(8,128)(2,1)} %bitcast.35, bf16[256,5120]{1,0:T(8,128)(2,1)} %w_a.3, bf16[256,5120]{1,0:T(8,128)(2,1)} %w_a.3, bf16[256,5120]{1,0:T(8,128)(2,1)} %w_a.3, ...), custom_call_target="tpu_custom_call" | custom-call | flops 1 | bytes 1 | tf_op jit(solution)/shard_map/pick/pallas_call | solution.py:52
  13.0 4.2 %collective-permute-start.1 = (bf16[4,2,128,256]{3,2,1,0:T(8,128)(2,1)}, bf16[4,2,128,256]{3,2,1,0:T(8,128)(2,1)S(1)}, u32[]{:S(2)}, u32[]{:S(2)}) collective-permute-start(bf16[4,2,128,256]{3,2,1,0:T(8,128)(2,1)} %get-tuple-element.72), channel_id=1, source_target_pairs={{0,66},{2,64},{64,2},{66,0},{1,67},{3,65},{65,3},{67,1},{4,70},{6,... | collective-permute-start | bytes 1572872 | tf_op jit(solution)/shard_map/ppermute | solution.py:309
  18.3 2.9 %pick_weights.1 = (bf16[512,640]{1,0:T(8,128)(2,1)}, bf16[512,640]{1,0:T(8,128)(2,1)}) custom-call(s32[11]{0:T(128)S(1)} %concatenate.6.s, bf16[256,5120]{1,0:T(8,128)(2,1)} %w_a.3, bf16[256,5120]{1,0:T(8,128)(2,1)} %w_a.3, bf16[256,2560]{1,0:T(8,128)(2,1)} %copy-done.4), custom_call_target="tpu_custom_call" | custom-call | flops 1 | bytes 1 | tf_op jit(solution)/shard_map/pick_weights/pallas_call | solution.py:52
  21.2 2.9 %collective-permute-start.4 = (bf16[512,640]{1,0:T(8,128)(2,1)}, bf16[512,640]{1,0:T(8,128)(2,1)S(1)}, u32[]{:S(2)}, u32[]{:S(2)}) collective-permute-start(bf16[512,640]{1,0:T(8,128)(2,1)} %get-tuple-element.77), channel_id=1, source_target_pairs={{0,66},{2,64},{64,2},{66,0},{1,67},{3,65},{65,3},{67,1},{4,70},{6,... | collective-permute-start | bytes 1966088 | tf_op jit(solution)/shard_map/ppermute | solution.py:347
  24.1 5.1 %attend_chip.1.ctx_a = bf16[1024,256]{1,0:T(8,128)(2,1)S(1)} custom-call(s32[11]{0:T(128)S(1)} %concatenate.6.s, bf16[4,4,128,256]{3,2,1,0:T(8,128)(2,1)S(1)} %bitcast.36, bf16[2048,512]{1,0:T(8,128)(2,1)S(1)} %bitcast.28, bf16[2048,512]{1,0:T(8,128)(2,1)S(1)} %bitcast.30), custom_call_target="tpu_custom_call" | custom-call | flops 1 | bytes 1 | tf_op jit(solution)/shard_map/attend_chip/pallas_call | solution.py:52
  30.2 5.1 %attend_next.1.ctx_b = bf16[1024,256]{1,0:T(8,128)(2,1)S(1)} custom-call(s32[11]{0:T(128)S(1)} %concatenate.6.s, bf16[4,2,128,256]{3,2,1,0:T(8,128)(2,1)S(1)} %collective-permute-done.1.q_ref, bf16[2048,512]{1,0:T(8,128)(2,1)S(1)} %bitcast.29, bf16[2048,512]{1,0:T(8,128)(2,1)S(1)} %bitcast.31), custom_call_target="tpu_custom_call" | custom-call | flops 1 | bytes 1 | tf_op jit(solution)/shard_map/attend_next/pallas_call | solution.py:52
  35.9 3.2 %collective-permute-start.5 = (bf16[512,640]{1,0:T(8,128)(2,1)}, bf16[512,640]{1,0:T(8,128)(2,1)}, u32[]{:S(2)}, u32[]{:S(2)}) collective-permute-start(bf16[512,640]{1,0:T(8,128)(2,1)} %get-tuple-element.86), channel_id=1, source_target_pairs={{0,66},{2,64},{64,2},{66,0},{1,67},{3,65},{65,3},{67,1},{4,70},{6,... | collective-permute-start | bytes 1966088 | tf_op jit(solution)/shard_map/ppermute | solution.py:347
  39.1 5.1 %collective-permute-done.4.w_z = bf16[512,640]{1,0:T(8,128)(2,1)S(1)} collective-permute-done((bf16[512,640]{1,0:T(8,128)(2,1)}, bf16[512,640]{1,0:T(8,128)(2,1)S(1)}, u32[]{:S(2)}, u32[]{:S(2)}) %collective-permute-start.4) | collective-permute-done | bytes 655392 | tf_op jit(solution)/shard_map/ppermute | solution.py:347
  44.2 3.5 %project_0.1 = (f32[2,128,640]{2,1,0:T(8,128)S(1)}, bf16[2,128,640]{2,1,0:T(8,128)(2,1)}, bf16[2,128,640]{2,1,0:T(8,128)(2,1)}, bf16[2,128,640]{2,1,0:T(8,128)(2,1)}) custom-call(s32[11]{0:T(128)S(1)} %concatenate.6.s, bf16[1024,256]{1,0:T(8,128)(2,1)S(1)} %attend_chip.1.ctx_a, bf16[1024,256]{1,0:T(8,128)(2,1)S(1)} %collective-permute-done.2.ctx_ac, ...), custom_call_target="tpu_custom_call" | custom-call | flops 1 | bytes 1 | tf_op jit(solution)/shard_map/project_0/pallas_call | solution.py:52
  50.1 2.7 %collective-permute-start.7 = (bf16[2,128,640]{2,1,0:T(8,128)(2,1)}, bf16[2,128,640]{2,1,0:T(8,128)(2,1)}, u32[]{:S(2)}, u32[]{:S(2)}) collective-permute-start(bf16[2,128,640]{2,1,0:T(8,128)(2,1)} %get-tuple-element.90), channel_id=1, source_target_pairs={{0,8},{4,12},{8,0},{12,4},{1,9},{5,13},{9,1},{13,5},{2,10},{6,14},... | collective-permute-start | bytes 983048 | tf_op jit(solution)/shard_map/ppermute | solution.py:372
  54.3 5.1 %fusion.5.pred = f32[512,640]{1,0:T(8,128)S(1)} fusion(bf16[512,2560]{1,0:T(8,128)(2,1)} %all-gather.2.cloned.1.call-done.normed, bf16[2560,640]{1,0:T(8,128)(2,1)} %proj.3), kind=kOutput, calls=%fused_computation.18 | convolution fusion | flops 1677721600 | bytes 7208960 | tf_op jit(solution)/shard_map/dot_general | solution.py:370
  59.4 4.5 %project_1.1 = (f32[2,128,640]{2,1,0:T(8,128)S(1)}, bf16[2,128,640]{2,1,0:T(8,128)(2,1)}, bf16[2,128,640]{2,1,0:T(8,128)(2,1)}, bf16[2,128,640]{2,1,0:T(8,128)(2,1)}) custom-call(s32[11]{0:T(128)S(1)} %concatenate.6.s, bf16[1024,256]{1,0:T(8,128)(2,1)S(1)} %copy-done.11, bf16[1024,256]{1,0:T(8,128)(2,1)S(1)} %copy-done.19, bf16[1024,256]{1,0:T(8,128)(2,1)S(1)} %copy-done.13, ...), custom_call_target="tpu_custom_call" | custom-call | flops 1 | bytes 1 | tf_op jit(solution)/shard_map/project_1/pallas_call | solution.py:52
  70.6 3.3 %collective-permute-start.13 = (bf16[128,640]{1,0:T(8,128)(2,1)S(1)}, bf16[128,640]{1,0:T(8,128)(2,1)S(1)}, u32[]{:S(2)}, u32[]{:S(2)}) collective-permute-start(bf16[128,640]{1,0:T(8,128)(2,1)S(1)} %get-tuple-element.93.same0), channel_id=1, source_target_pairs={{0,32},{1,49},{16,48},{17,1},{32,0},{33,17},{48,16},{49,33},{2,34}... | collective-permute-start | bytes 491528 | tf_op jit(solution)/shard_map/ppermute | solution.py:393
  75.2 6.3 %collective-permute-done.11.r2 = bf16[2,128,640]{2,1,0:T(8,128)(2,1)S(1)} collective-permute-done((bf16[2,128,640]{2,1,0:T(8,128)(2,1)}, bf16[2,128,640]{2,1,0:T(8,128)(2,1)S(1)}, u32[]{:S(2)}, u32[]{:S(2)}) %collective-permute-start.11) | collective-permute-done | bytes 327712 | tf_op jit(solution)/shard_map/ppermute | solution.py:372
  83.2 3.5 %collective-permute-start.15 = (bf16[128,640]{1,0:T(8,128)(2,1)S(1)}, bf16[128,640]{1,0:T(8,128)(2,1)S(1)}, u32[]{:S(2)}, u32[]{:S(2)}) collective-permute-start(bf16[128,640]{1,0:T(8,128)(2,1)S(1)} %get-tuple-element.98.same1), channel_id=1, source_target_pairs={{0,16},{1,1},{16,32},{17,17},{32,48},{33,33},{48,0},{49,49},{2,18}... | collective-permute-start | bytes 491528 | tf_op jit(solution)/shard_map/ppermute | solution.py:393
  87.0 3.1 %compare_0.1 = (bf16[512,640]{1,0:T(8,128)(2,1)}, bf16[2,512,1280]{2,1,0:T(8,128)(2,1)}, f32[32,128]{1,0:T(8,128)S(1)}) custom-call(s32[11]{0:T(128)S(1)} %concatenate.6.s, f32[512,640]{1,0:T(8,128)S(1)} %fusion.5.pred, bf16[512,2560]{1,0:T(8,128)(2,1)S(1)} %copy-done.1, bf16[2560,640]{1,0:T(8,128)(2,1)S(1)} %copy-done.3, ...), custom_call_target="tpu_custom_call" | custom-call | flops 1 | bytes 1 | tf_op jit(solution)/shard_map/compare_0/pallas_call | solution.py:52
  91.6 3.1 %compare_1.1 = (bf16[512,640]{1,0:T(8,128)(2,1)}, bf16[2,512,1280]{2,1,0:T(8,128)(2,1)}, f32[32,128]{1,0:T(8,128)S(1)}) custom-call(s32[11]{0:T(128)S(1)} %concatenate.6.s, f32[512,640]{1,0:T(8,128)S(1)} %fusion.5.pred, bf16[512,2560]{1,0:T(8,128)(2,1)S(1)} %copy-done.1, ...), custom_call_target="tpu_custom_call", output_to_operand_aliasing={{0}: (6, {}), {1}: (7, {})} | custom-call | flops 1 | bytes 1 | tf_op jit(solution)/shard_map/compare_1/pallas_call | solution.py:52
  95.8 4.0 %gproj.1 = (bf16[4,2,160,640]{3,2,1,0:T(8,128)(2,1)}, f32[4,2,160,640]{3,2,1,0:T(8,128)S(1)}) custom-call(s32[11]{0:T(128)S(1)} %concatenate.6.s, bf16[512,2560]{1,0:T(8,128)(2,1)S(1)} %copy-done.1, bf16[512,640]{1,0:T(8,128)(2,1)S(1)} %copy-done.15), custom_call_target="tpu_custom_call" | custom-call | flops 1 | bytes 1 | tf_op jit(solution)/shard_map/gproj/pallas_call | solution.py:52
  103.0 2.4 %collective-permute-start.21 = (f32[21,128]{1,0:T(8,128)S(1)}, f32[21,128]{1,0:T(8,128)S(1)}, u32[]{:S(2)}, u32[]{:S(2)}) collective-permute-start(f32[21,128]{1,0:T(8,128)S(1)} %slice.12), channel_id=1, source_target_pairs={{0,8},{4,12},{8,0},{12,4},{1,9},{5,13},{9,1},{13,5},{2,10},{6,14},... | collective-permute-start | bytes 32264 | tf_op jit(solution)/shard_map/ppermute | solution.py:266
  111.1 3.0 %collective-permute-start.24 = (f32[25,128]{1,0:T(8,128)S(1)}, f32[25,128]{1,0:T(8,128)S(1)}, u32[]{:S(2)}, u32[]{:S(2)}) collective-permute-start(f32[25,128]{1,0:T(8,128)S(1)} %pad_maximum_fusion), channel_id=1, source_target_pairs={{0,32},{16,48},{32,0},{48,16},{1,33},{17,49},{33,1},{49,17},{2,34}... | collective-permute-start | bytes 38408 | tf_op jit(solution)/shard_map/ppermute | solution.py:266
  115.7 3.7 %collective-permute-start.30 = (bf16[2,160,640]{2,1,0:T(8,128)(2,1)}, bf16[2,160,640]{2,1,0:T(8,128)(2,1)S(1)}, u32[]{:S(2)}, u32[]{:S(2)}) collective-permute-start(bf16[2,160,640]{2,1,0:T(8,128)(2,1)} %get-tuple-element.130), channel_id=1, source_target_pairs={{0,8},{4,12},{8,0},{12,4},{1,9},{5,13},{9,1},{13,5},{2,10},{6,14},... | collective-permute-start | bytes 1228808 | tf_op jit(solution)/shard_map/ppermute | solution.py:444
  124.6 4.2 %collective-permute-start.28 = (f32[25,128]{1,0:T(8,128)S(1)}, f32[25,128]{1,0:T(8,128)S(1)}, u32[]{:S(2)}, u32[]{:S(2)}) collective-permute-start(f32[25,128]{1,0:T(8,128)S(1)} %add_add_fusion), channel_id=1, source_target_pairs={{0,66},{2,0},{64,2},{66,64},{1,67},{3,1},{65,3},{67,65},{4,70},{6,... | collective-permute-start | bytes 38408 | tf_op jit(solution)/shard_map/ppermute | solution.py:449
  141.6 2.5 %hidden.1 = f32[128,1280]{1,0:T(8,128)} custom-call(s32[11]{0:T(128)S(1)} %concatenate.6.s, bf16[128,1280]{1,0:T(8,128)(2,1)} %reduce-scatter.2.cloned.1.call-done.grad, f32[128,1]{1,0:T(8,128)S(1)} %copy.16.inner, bf16[128,2560]{1,0:T(8,128)(2,1)S(1)} %bitcast.34, f32[128,1]{1,0:T(8,128)S(1)} %copy.17.inverse_rms, f32[1,2560]{1,0:T(1,128)S(1)} %broadcast_in_dim.11.norm_gain), custom_call_target="tpu_custom_call" | custom-call | flops 1 | bytes 1 | tf_op jit(solution)/shard_map/hidden/pallas_call | solution.py:52
  144.1 2.7 %collective-permute-done.33 = bf16[160,640]{1,0:T(8,128)(2,1)S(1)} collective-permute-done((bf16[160,640]{1,0:T(8,128)(2,1)}, bf16[160,640]{1,0:T(8,128)(2,1)S(1)}, u32[]{:S(2)}, u32[]{:S(2)}) %collective-permute-start.33) | collective-permute-done | bytes 204832 | tf_op jit(solution)/shard_map/ppermute | solution.py:467
  (145 shorter events, 49.0 us)
Async XLA Ops:
  7.2 47.1 %all-gather.2.cloned.1.call-start = ((), (), s32[]{:S(2)}) async-start(), calls=%async_computation.1 | async-start | bytes 3276800 | tf_op jit(solution)/shard_map/all_gather | solution.py:333
  12.8 128.8 %reduce-scatter.2.cloned.1.call-start = ((), (), s32[]{:S(2)}) async-start(), calls=%async_computation.2 | async-start | bytes 2949120 | tf_op jit(solution)/shard_map/reduce_scatter | solution.py:423
  13.0 17.2 %collective-permute-start.1 = (bf16[4,2,128,256]{3,2,1,0:T(8,128)(2,1)}, bf16[4,2,128,256]{3,2,1,0:T(8,128)(2,1)S(1)}, u32[]{:S(2)}, u32[]{:S(2)}) collective-permute-start(bf16[4,2,128,256]{3,2,1,0:T(8,128)(2,1)} %get-tuple-element.72), channel_id=1, source_target_pairs={{0,66},{2,64},{64,2},{66,0},{1,67},{3,65},{65,3},{67,1},{4,70},{6,... | collective-permute-start | bytes 1572872 | tf_op jit(solution)/shard_map/ppermute | solution.py:309
  21.2 23.0 %collective-permute-start.4 = (bf16[512,640]{1,0:T(8,128)(2,1)}, bf16[512,640]{1,0:T(8,128)(2,1)S(1)}, u32[]{:S(2)}, u32[]{:S(2)}) collective-permute-start(bf16[512,640]{1,0:T(8,128)(2,1)} %get-tuple-element.77), channel_id=1, source_target_pairs={{0,66},{2,64},{64,2},{66,0},{1,67},{3,65},{65,3},{67,1},{4,70},{6,... | collective-permute-start | bytes 1966088 | tf_op jit(solution)/shard_map/ppermute | solution.py:347
  35.9 23.5 %collective-permute-start.5 = (bf16[512,640]{1,0:T(8,128)(2,1)}, bf16[512,640]{1,0:T(8,128)(2,1)}, u32[]{:S(2)}, u32[]{:S(2)}) collective-permute-start(bf16[512,640]{1,0:T(8,128)(2,1)} %get-tuple-element.86), channel_id=1, source_target_pairs={{0,66},{2,64},{64,2},{66,0},{1,67},{3,65},{65,3},{67,1},{4,70},{6,... | collective-permute-start | bytes 1966088 | tf_op jit(solution)/shard_map/ppermute | solution.py:347
  39.1 25.5 %collective-permute-start.9 = (bf16[128,1280]{1,0:T(8,128)(2,1)}, bf16[128,1280]{1,0:T(8,128)(2,1)}, u32[]{:S(2)}, u32[]{:S(2)}) collective-permute-start(bf16[128,1280]{1,0:T(8,128)(2,1)} %get-tuple-element.92), channel_id=1, source_target_pairs={{0,1},{1,0},{2,3},{3,2},{4,5},{5,4},{6,7},{7,6},{8,9},{9,8},{10,11... | collective-permute-start | bytes 983048 | tf_op jit(solution)/shard_map/ppermute | solution.py:311
  48.6 18.3 %collective-permute-start.6 = (bf16[2,128,640]{2,1,0:T(8,128)(2,1)}, bf16[2,128,640]{2,1,0:T(8,128)(2,1)}, u32[]{:S(2)}, u32[]{:S(2)}) collective-permute-start(bf16[2,128,640]{2,1,0:T(8,128)(2,1)} %get-tuple-element.89), channel_id=1, source_target_pairs={{0,4},{4,8},{8,12},{12,0},{1,5},{5,9},{9,13},{13,1},{2,6},{6,10},{... | collective-permute-start | bytes 983048 | tf_op jit(solution)/shard_map/ppermute | solution.py:372
  50.1 18.2 %collective-permute-start.7 = (bf16[2,128,640]{2,1,0:T(8,128)(2,1)}, bf16[2,128,640]{2,1,0:T(8,128)(2,1)}, u32[]{:S(2)}, u32[]{:S(2)}) collective-permute-start(bf16[2,128,640]{2,1,0:T(8,128)(2,1)} %get-tuple-element.90), channel_id=1, source_target_pairs={{0,8},{4,12},{8,0},{12,4},{1,9},{5,13},{9,1},{13,5},{2,10},{6,14},... | collective-permute-start | bytes 983048 | tf_op jit(solution)/shard_map/ppermute | solution.py:372
  52.8 15.5 %collective-permute-start.8 = (bf16[2,128,640]{2,1,0:T(8,128)(2,1)}, bf16[2,128,640]{2,1,0:T(8,128)(2,1)}, u32[]{:S(2)}, u32[]{:S(2)}) collective-permute-start(bf16[2,128,640]{2,1,0:T(8,128)(2,1)} %get-tuple-element.91), channel_id=1, source_target_pairs={{0,12},{4,0},{8,4},{12,8},{1,13},{5,1},{9,5},{13,9},{2,14},{6,2},{... | collective-permute-start | bytes 983048 | tf_op jit(solution)/shard_map/ppermute | solution.py:372
  63.9 11.3 %collective-permute-start.10 = (bf16[2,128,640]{2,1,0:T(8,128)(2,1)}, bf16[2,128,640]{2,1,0:T(8,128)(2,1)S(1)}, u32[]{:S(2)}, u32[]{:S(2)}) collective-permute-start(bf16[2,128,640]{2,1,0:T(8,128)(2,1)} %get-tuple-element.95), channel_id=1, source_target_pairs={{0,4},{4,8},{8,12},{12,0},{1,5},{5,9},{9,13},{13,1},{2,6},{6,10},{... | collective-permute-start | bytes 983048 | tf_op jit(solution)/shard_map/ppermute | solution.py:372
  64.5 16.9 %collective-permute-start.11 = (bf16[2,128,640]{2,1,0:T(8,128)(2,1)}, bf16[2,128,640]{2,1,0:T(8,128)(2,1)S(1)}, u32[]{:S(2)}, u32[]{:S(2)}) collective-permute-start(bf16[2,128,640]{2,1,0:T(8,128)(2,1)} %get-tuple-element.96), channel_id=1, source_target_pairs={{0,8},{4,12},{8,0},{12,4},{1,9},{5,13},{9,1},{13,5},{2,10},{6,14},... | collective-permute-start | bytes 983048 | tf_op jit(solution)/shard_map/ppermute | solution.py:372
  66.9 14.6 %collective-permute-start.12 = (bf16[2,128,640]{2,1,0:T(8,128)(2,1)}, bf16[2,128,640]{2,1,0:T(8,128)(2,1)S(1)}, u32[]{:S(2)}, u32[]{:S(2)}) collective-permute-start(bf16[2,128,640]{2,1,0:T(8,128)(2,1)} %get-tuple-element.97), channel_id=1, source_target_pairs={{0,12},{4,0},{8,4},{12,8},{1,13},{5,1},{9,5},{13,9},{2,14},{6,2},{... | collective-permute-start | bytes 983048 | tf_op jit(solution)/shard_map/ppermute | solution.py:372
  70.6 16.4 %collective-permute-start.13 = (bf16[128,640]{1,0:T(8,128)(2,1)S(1)}, bf16[128,640]{1,0:T(8,128)(2,1)S(1)}, u32[]{:S(2)}, u32[]{:S(2)}) collective-permute-start(bf16[128,640]{1,0:T(8,128)(2,1)S(1)} %get-tuple-element.93.same0), channel_id=1, source_target_pairs={{0,32},{1,49},{16,48},{17,1},{32,0},{33,17},{48,16},{49,33},{2,34}... | collective-permute-start | bytes 491528 | tf_op jit(solution)/shard_map/ppermute | solution.py:393
  73.8 13.1 %collective-permute-start.14 = (bf16[128,640]{1,0:T(8,128)(2,1)S(1)}, bf16[128,640]{1,0:T(8,128)(2,1)S(1)}, u32[]{:S(2)}, u32[]{:S(2)}) collective-permute-start(bf16[128,640]{1,0:T(8,128)(2,1)S(1)} %get-tuple-element.113), channel_id=1, source_target_pairs={{0,33},{1,48},{16,49},{17,0},{32,1},{33,16},{48,17},{49,32},{2,35}... | collective-permute-start | bytes 491528 | tf_op jit(solution)/shard_map/ppermute | solution.py:394
  83.2 8.4 %collective-permute-start.15 = (bf16[128,640]{1,0:T(8,128)(2,1)S(1)}, bf16[128,640]{1,0:T(8,128)(2,1)S(1)}, u32[]{:S(2)}, u32[]{:S(2)}) collective-permute-start(bf16[128,640]{1,0:T(8,128)(2,1)S(1)} %get-tuple-element.98.same1), channel_id=1, source_target_pairs={{0,16},{1,1},{16,32},{17,17},{32,48},{33,33},{48,0},{49,49},{2,18}... | collective-permute-start | bytes 491528 | tf_op jit(solution)/shard_map/ppermute | solution.py:393
  99.8 9.3 %collective-permute-start.17 = (bf16[4,2,160,640]{3,2,1,0:T(8,128)(2,1)}, bf16[4,2,160,640]{3,2,1,0:T(8,128)(2,1)S(1)}, u32[]{:S(2)}, u32[]{:S(2)}) collective-permute-start(bf16[4,2,160,640]{3,2,1,0:T(8,128)(2,1)} %get-tuple-element.108), channel_id=1, source_target_pairs={{0,1},{1,0},{2,3},{3,2},{4,5},{5,4},{6,7},{7,6},{8,9},{9,8},{10,11... | collective-permute-start | bytes 4915208 | tf_op jit(solution)/shard_map/ppermute | solution.py:433
  110.9 8.6 %collective-permute-start.23 = (f32[25,128]{1,0:T(8,128)S(1)}, f32[25,128]{1,0:T(8,128)S(1)}, u32[]{:S(2)}, u32[]{:S(2)}) collective-permute-start(f32[25,128]{1,0:T(8,128)S(1)} %pad_maximum_fusion), channel_id=1, source_target_pairs={{0,16},{16,32},{32,48},{48,0},{1,17},{17,33},{33,49},{49,1},{2,18}... | collective-permute-start | bytes 38408 | tf_op jit(solution)/shard_map/ppermute | solution.py:266
  111.1 8.5 %collective-permute-start.24 = (f32[25,128]{1,0:T(8,128)S(1)}, f32[25,128]{1,0:T(8,128)S(1)}, u32[]{:S(2)}, u32[]{:S(2)}) collective-permute-start(f32[25,128]{1,0:T(8,128)S(1)} %pad_maximum_fusion), channel_id=1, source_target_pairs={{0,32},{16,48},{32,0},{48,16},{1,33},{17,49},{33,1},{49,17},{2,34}... | collective-permute-start | bytes 38408 | tf_op jit(solution)/shard_map/ppermute | solution.py:266
  115.4 18.9 %collective-permute-start.29 = (bf16[2,160,640]{2,1,0:T(8,128)(2,1)}, bf16[2,160,640]{2,1,0:T(8,128)(2,1)S(1)}, u32[]{:S(2)}, u32[]{:S(2)}) collective-permute-start(bf16[2,160,640]{2,1,0:T(8,128)(2,1)} %get-tuple-element.129), channel_id=1, source_target_pairs={{0,4},{4,8},{8,12},{12,0},{1,5},{5,9},{9,13},{13,1},{2,6},{6,10},{... | collective-permute-start | bytes 1228808 | tf_op jit(solution)/shard_map/ppermute | solution.py:444
  115.7 19.6 %collective-permute-start.30 = (bf16[2,160,640]{2,1,0:T(8,128)(2,1)}, bf16[2,160,640]{2,1,0:T(8,128)(2,1)S(1)}, u32[]{:S(2)}, u32[]{:S(2)}) collective-permute-start(bf16[2,160,640]{2,1,0:T(8,128)(2,1)} %get-tuple-element.130), channel_id=1, source_target_pairs={{0,8},{4,12},{8,0},{12,4},{1,9},{5,13},{9,1},{13,5},{2,10},{6,14},... | collective-permute-start | bytes 1228808 | tf_op jit(solution)/shard_map/ppermute | solution.py:444
  119.5 16.0 %collective-permute-start.31 = (bf16[2,160,640]{2,1,0:T(8,128)(2,1)}, bf16[2,160,640]{2,1,0:T(8,128)(2,1)S(1)}, u32[]{:S(2)}, u32[]{:S(2)}) collective-permute-start(bf16[2,160,640]{2,1,0:T(8,128)(2,1)} %get-tuple-element.131), channel_id=1, source_target_pairs={{0,12},{4,0},{8,4},{12,8},{1,13},{5,1},{9,5},{13,9},{2,14},{6,2},{... | collective-permute-start | bytes 1228808 | tf_op jit(solution)/shard_map/ppermute | solution.py:444
  121.1 9.2 %collective-permute-start.27 = (f32[25,128]{1,0:T(8,128)S(1)}, f32[25,128]{1,0:T(8,128)S(1)}, u32[]{:S(2)}, u32[]{:S(2)}) collective-permute-start(f32[25,128]{1,0:T(8,128)S(1)} %add_add_fusion), channel_id=1, source_target_pairs={{0,64},{2,66},{64,0},{66,2},{1,65},{3,67},{65,1},{67,3},{4,68},{6,... | collective-permute-start | bytes 38408 | tf_op jit(solution)/shard_map/ppermute | solution.py:449
  124.6 6.6 %collective-permute-start.28 = (f32[25,128]{1,0:T(8,128)S(1)}, f32[25,128]{1,0:T(8,128)S(1)}, u32[]{:S(2)}, u32[]{:S(2)}) collective-permute-start(f32[25,128]{1,0:T(8,128)S(1)} %add_add_fusion), channel_id=1, source_target_pairs={{0,66},{2,0},{64,2},{66,64},{1,67},{3,1},{65,3},{67,65},{4,70},{6,... | collective-permute-start | bytes 38408 | tf_op jit(solution)/shard_map/ppermute | solution.py:449
  137.6 9.3 %collective-permute-start.33 = (bf16[160,640]{1,0:T(8,128)(2,1)}, bf16[160,640]{1,0:T(8,128)(2,1)S(1)}, u32[]{:S(2)}, u32[]{:S(2)}) collective-permute-start(bf16[160,640]{1,0:T(8,128)(2,1)} %get-tuple-element.134), channel_id=1, source_target_pairs={{0,2},{2,0},{1,3},{3,1},{4,6},{6,4},{5,7},{7,5},{8,10},{10,8},{9,1... | collective-permute-start | bytes 614408 | tf_op jit(solution)/shard_map/ppermute | solution.py:467
  (42 other events, 327.7 us)
Sparse Core Ops, SparseCore 0:
  12.9 37.6 all-gather.1
  94.8 45.1 reduce-scatter.1

commit v7 on v6

--- a/solution.py
+++ b/solution.py
@@ -432,7 +432,7 @@
     )
     recv = lax.ppermute(sent, "core", swap)
     inner = small[21:25]
-    small = sum_over(small[:21], "x", NX)
+    small = sum_over(small[:21], "core", 2)
     small, _ = barrier((jnp.concatenate([small, inner]), sent))
     own, *outs = call(
         gproj_add_kernel,
@@ -446,9 +446,9 @@
     cross = [lax.ppermute(a, "core", swap) for a in barrier((*cross, own))[:2]]
     small, _ = barrier((small, own))
     small = sum_over(small, "dp", 4)
-    along = barrier([lax.ppermute(small, ("grp", "zh"), ring(NZ, j)) for j in (1, 2, 3)])
-    inner = lax.dynamic_slice_in_dim(small + along[1], 21 + d, 1, 0)
-    small = sum(along, small)[:21]
+    small = sum_over(small, "grp", 2)
+    inner = lax.dynamic_slice_in_dim(small, 21 + d, 1, 0)
+    small = sum_over(small[:21], "zh", 2)
     (target,) = call(
         assemble_kernel,
         scalars,
@@ -466,12 +466,7 @@
     )
     gsent = lax.ppermute(gsent, "zh", swap)
     small, _ = barrier((small, gkept))
-    small = sum_over(small, "core", 2)
-    small = small.reshape(-1)
-    distill_loss = small[20 * 128] / (live_count * D_T)
-    gain_half = lax.dynamic_slice_in_dim(norm_gain, g * width, width, 0)
-    grad_gain = lax.dynamic_slice_in_dim(small, g * width, width, 0) / (gain_half * live_count)
-
+    sums = [lax.ppermute(small, "x", ring(NX, j)) for j in (1, 2, 3)]
     half_shape = (128, width)
     (grad_hidden,) = call(
         hidden_kernel,
@@ -489,6 +484,12 @@
     )
     gsent, grad_hidden = barrier((gsent, grad_hidden))
     grad_proj = (gkept + gsent.astype(F32)) / live_count
+    *sums, grad_proj = barrier((*sums, grad_proj))
+    small = sum(sums, small)
+    small = small.reshape(-1)
+    distill_loss = small[20 * 128] / (live_count * D_T)
+    gain_half = lax.dynamic_slice_in_dim(norm_gain, g * width, width, 0)
+    grad_gain = lax.dynamic_slice_in_dim(small, g * width, width, 0) / (gain_half * live_count)
     return (target[None], distill_loss, grad_proj, grad_gain, grad_hidden[None])
 
 

time: 157 us -> 156 us (level)
  starting transfers between devices: 53 us -> 43.5 us
  waiting for transfers between devices: 24.8 us -> 34.2 us
  other arithmetic: 5.44 us -> 3.44 us
    ppermute x7 -> x6, waiting for transfers between devices: 2.43 us -> 14.2 us  [sum_over(): got = [lax.ppermute(array, axis, ring(n, j)) for j in range(1, n)]]
    ppermute x3, starting transfers between devices: 7.84 us -> 3.13 us  [body(): sums = [lax.ppermute(small, 'x', ring(NX, j)) for j in (1, 2, 3)]]
    ppermute x7 -> x6, starting transfers between devices: 9.81 us -> 5.51 us  [sum_over(): got = [lax.ppermute(array, axis, ring(n, j)) for j in range(1, n)]]
    ppermute x1, waiting for transfers between devices: 2.74 us -> 0.01 us  [body(): gsent = lax.ppermute(gsent, 'zh', swap)]
    ppermute x3, waiting for transfers between devices: 2.25 us -> 0.25 us  [body(): sums = [lax.ppermute(small, 'x', ring(NX, j)) for j in (1, 2, 3)]]
    ppermute x1, starting transfers between devices: 1.6 us -> 0.01 us  [body(): recv = lax.ppermute(sent, 'core', swap)]
  transfers between devices with their start and end apart: 36 -> 35, of which waited for: 14 -> 13; matrix products, arithmetic and copies ran while one was open for 6% -> 4% of each run, Pallas kernels for 25% -> 25%
where the time goes in v7:
time: 156 us; the launch traced here: 153 us
  Pallas kernels  45.6 us (29%)
  starting transfers between devices  43.5 us (28%)
  waiting for transfers between devices  34.2 us (22%)
  between operations  17 us (11%)
  matrix products  5.05 us (3%)
  local copies, waits for them, and re-layouts  4.62 us (3%)
  other arithmetic  3.44 us (2%)
    pallas_call x15, Pallas kernels, call(): pl.pallas_call(kernel, out_shape=[pltpu.HBM(o[0], o[1]) if len(o) == 3 el...  45.6 us
    ppermute x6, waiting for transfers between devices, sum_over(): got = [lax.ppermute(array, axis, ring(n, j)) for j in range(1, n)]  14.2 us
    ppermute x6, starting transfers between devices, body(): lax.ppermute(outs[j - 1], 'x', ring(NX, j))  10 us
    ppermute x6, waiting for transfers between devices, body(): lax.ppermute(outs[j - 1], 'x', ring(NX, j))  7.64 us
    ppermute x2, starting transfers between devices, body(): lax.ppermute(done_same, ('dp', 'core'), to_owner(st, False))  6.96 us
    ppermute x2, starting transfers between devices, body(): w_z = [lax.ppermute(w, ('grp', 'zh'), WRAP) for w in w_z]  6.08 us
    ppermute x6, starting transfers between devices, sum_over(): got = [lax.ppermute(array, axis, ring(n, j)) for j in range(1, n)]  5.51 us
    ppermute x3, starting transfers between devices, body(): got = {j: lax.ppermute(outs[j - 1], 'x', ring(NX, j)) for j in (2, 1, 3)}  5.3 us
  transfers between devices with their start and end apart: 35, of which 13 were waited for; matrix products, arithmetic and copies ran while one was open for 4% of the time, Pallas kernels for 25%

profile of v7, /device:TPU:0, one launch (start us, length us, event | category | flops | bytes accessed | tf_op | source)
XLA Modules:
  0.0 153.3 jit_solution(12792296844792063277)
XLA Ops:
  8.0 3.5 %pick.1 = (bf16[4,2,128,256]{3,2,1,0:T(8,128)(2,1)}, bf16[256,2560]{1,0:T(8,128)(2,1)}, bf16[128,1280]{1,0:T(8,128)(2,1)}) custom-call(s32[11]{0:T(128)S(1)} %concatenate.6.s, bf16[4,4,128,256]{3,2,1,0:T(8,128)(2,1)} %bitcast.35, bf16[256,5120]{1,0:T(8,128)(2,1)} %w_a.3, bf16[256,5120]{1,0:T(8,128)(2,1)} %w_a.3, bf16[256,5120]{1,0:T(8,128)(2,1)} %w_a.3, ...), custom_call_target="tpu_custom_call" | custom-call | flops 1 | bytes 1 | tf_op jit(solution)/shard_map/pick/pallas_call | solution.py:52
  13.0 4.2 %collective-permute-start.1 = (bf16[4,2,128,256]{3,2,1,0:T(8,128)(2,1)}, bf16[4,2,128,256]{3,2,1,0:T(8,128)(2,1)S(1)}, u32[]{:S(2)}, u32[]{:S(2)}) collective-permute-start(bf16[4,2,128,256]{3,2,1,0:T(8,128)(2,1)} %get-tuple-element.70), channel_id=1, source_target_pairs={{0,66},{2,64},{64,2},{66,0},{1,67},{3,65},{65,3},{67,1},{4,70},{6,... | collective-permute-start | bytes 1572872 | tf_op jit(solution)/shard_map/ppermute | solution.py:309
  18.3 2.9 %pick_weights.1 = (bf16[512,640]{1,0:T(8,128)(2,1)}, bf16[512,640]{1,0:T(8,128)(2,1)}) custom-call(s32[11]{0:T(128)S(1)} %concatenate.6.s, bf16[256,5120]{1,0:T(8,128)(2,1)} %w_a.3, bf16[256,5120]{1,0:T(8,128)(2,1)} %w_a.3, bf16[256,2560]{1,0:T(8,128)(2,1)} %copy-done.4), custom_call_target="tpu_custom_call" | custom-call | flops 1 | bytes 1 | tf_op jit(solution)/shard_map/pick_weights/pallas_call | solution.py:52
  21.2 2.9 %collective-permute-start.4 = (bf16[512,640]{1,0:T(8,128)(2,1)}, bf16[512,640]{1,0:T(8,128)(2,1)S(1)}, u32[]{:S(2)}, u32[]{:S(2)}) collective-permute-start(bf16[512,640]{1,0:T(8,128)(2,1)} %get-tuple-element.75), channel_id=1, source_target_pairs={{0,66},{2,64},{64,2},{66,0},{1,67},{3,65},{65,3},{67,1},{4,70},{6,... | collective-permute-start | bytes 1966088 | tf_op jit(solution)/shard_map/ppermute | solution.py:347
  24.1 5.0 %attend_chip.1.ctx_a = bf16[1024,256]{1,0:T(8,128)(2,1)S(1)} custom-call(s32[11]{0:T(128)S(1)} %concatenate.6.s, bf16[4,4,128,256]{3,2,1,0:T(8,128)(2,1)S(1)} %bitcast.36, bf16[2048,512]{1,0:T(8,128)(2,1)S(1)} %bitcast.28, bf16[2048,512]{1,0:T(8,128)(2,1)S(1)} %bitcast.30), custom_call_target="tpu_custom_call" | custom-call | flops 1 | bytes 1 | tf_op jit(solution)/shard_map/attend_chip/pallas_call | solution.py:52
  30.2 5.1 %attend_next.1.ctx_b = bf16[1024,256]{1,0:T(8,128)(2,1)S(1)} custom-call(s32[11]{0:T(128)S(1)} %concatenate.6.s, bf16[4,2,128,256]{3,2,1,0:T(8,128)(2,1)S(1)} %collective-permute-done.1.q_ref, bf16[2048,512]{1,0:T(8,128)(2,1)S(1)} %bitcast.29, bf16[2048,512]{1,0:T(8,128)(2,1)S(1)} %bitcast.31), custom_call_target="tpu_custom_call" | custom-call | flops 1 | bytes 1 | tf_op jit(solution)/shard_map/attend_next/pallas_call | solution.py:52
  35.8 3.2 %collective-permute-start.5 = (bf16[512,640]{1,0:T(8,128)(2,1)}, bf16[512,640]{1,0:T(8,128)(2,1)}, u32[]{:S(2)}, u32[]{:S(2)}) collective-permute-start(bf16[512,640]{1,0:T(8,128)(2,1)} %get-tuple-element.84), channel_id=1, source_target_pairs={{0,66},{2,64},{64,2},{66,0},{1,67},{3,65},{65,3},{67,1},{4,70},{6,... | collective-permute-start | bytes 1966088 | tf_op jit(solution)/shard_map/ppermute | solution.py:347
  39.1 5.1 %collective-permute-done.4.w_z = bf16[512,640]{1,0:T(8,128)(2,1)S(1)} collective-permute-done((bf16[512,640]{1,0:T(8,128)(2,1)}, bf16[512,640]{1,0:T(8,128)(2,1)S(1)}, u32[]{:S(2)}, u32[]{:S(2)}) %collective-permute-start.4) | collective-permute-done | bytes 655392 | tf_op jit(solution)/shard_map/ppermute | solution.py:347
  44.2 3.5 %project_0.1 = (f32[2,128,640]{2,1,0:T(8,128)S(1)}, bf16[2,128,640]{2,1,0:T(8,128)(2,1)}, bf16[2,128,640]{2,1,0:T(8,128)(2,1)}, bf16[2,128,640]{2,1,0:T(8,128)(2,1)}) custom-call(s32[11]{0:T(128)S(1)} %concatenate.6.s, bf16[1024,256]{1,0:T(8,128)(2,1)S(1)} %attend_chip.1.ctx_a, bf16[1024,256]{1,0:T(8,128)(2,1)S(1)} %collective-permute-done.2.ctx_ac, ...), custom_call_target="tpu_custom_call" | custom-call | flops 1 | bytes 1 | tf_op jit(solution)/shard_map/project_0/pallas_call | solution.py:52
  50.1 2.7 %collective-permute-start.7 = (bf16[2,128,640]{2,1,0:T(8,128)(2,1)}, bf16[2,128,640]{2,1,0:T(8,128)(2,1)}, u32[]{:S(2)}, u32[]{:S(2)}) collective-permute-start(bf16[2,128,640]{2,1,0:T(8,128)(2,1)} %get-tuple-element.88), channel_id=1, source_target_pairs={{0,8},{4,12},{8,0},{12,4},{1,9},{5,13},{9,1},{13,5},{2,10},{6,14},... | collective-permute-start | bytes 983048 | tf_op jit(solution)/shard_map/ppermute | solution.py:372
  54.2 5.1 %fusion.4.pred = f32[512,640]{1,0:T(8,128)S(1)} fusion(bf16[512,2560]{1,0:T(8,128)(2,1)} %all-gather.2.cloned.1.call-done.normed, bf16[2560,640]{1,0:T(8,128)(2,1)} %proj.3), kind=kOutput, calls=%fused_computation.15 | convolution fusion | flops 1677721600 | bytes 7208960 | tf_op jit(solution)/shard_map/dot_general | solution.py:370
  59.4 4.5 %project_1.1 = (f32[2,128,640]{2,1,0:T(8,128)S(1)}, bf16[2,128,640]{2,1,0:T(8,128)(2,1)}, bf16[2,128,640]{2,1,0:T(8,128)(2,1)}, bf16[2,128,640]{2,1,0:T(8,128)(2,1)}) custom-call(s32[11]{0:T(128)S(1)} %concatenate.6.s, bf16[1024,256]{1,0:T(8,128)(2,1)S(1)} %copy-done.11, bf16[1024,256]{1,0:T(8,128)(2,1)S(1)} %copy-done.19, bf16[1024,256]{1,0:T(8,128)(2,1)S(1)} %copy-done.13, ...), custom_call_target="tpu_custom_call" | custom-call | flops 1 | bytes 1 | tf_op jit(solution)/shard_map/project_1/pallas_call | solution.py:52
  64.5 2.3 %collective-permute-start.11 = (bf16[2,128,640]{2,1,0:T(8,128)(2,1)}, bf16[2,128,640]{2,1,0:T(8,128)(2,1)S(1)}, u32[]{:S(2)}, u32[]{:S(2)}) collective-permute-start(bf16[2,128,640]{2,1,0:T(8,128)(2,1)} %get-tuple-element.94), channel_id=1, source_target_pairs={{0,8},{4,12},{8,0},{12,4},{1,9},{5,13},{9,1},{13,5},{2,10},{6,14},... | collective-permute-start | bytes 983048 | tf_op jit(solution)/shard_map/ppermute | solution.py:372
  70.5 3.3 %collective-permute-start.13 = (bf16[128,640]{1,0:T(8,128)(2,1)S(1)}, bf16[128,640]{1,0:T(8,128)(2,1)S(1)}, u32[]{:S(2)}, u32[]{:S(2)}) collective-permute-start(bf16[128,640]{1,0:T(8,128)(2,1)S(1)} %get-tuple-element.91.same0), channel_id=1, source_target_pairs={{0,32},{1,49},{16,48},{17,1},{32,0},{33,17},{48,16},{49,33},{2,34}... | collective-permute-start | bytes 491528 | tf_op jit(solution)/shard_map/ppermute | solution.py:393
  75.2 6.2 %collective-permute-done.11.r2 = bf16[2,128,640]{2,1,0:T(8,128)(2,1)S(1)} collective-permute-done((bf16[2,128,640]{2,1,0:T(8,128)(2,1)}, bf16[2,128,640]{2,1,0:T(8,128)(2,1)S(1)}, u32[]{:S(2)}, u32[]{:S(2)}) %collective-permute-start.11) | collective-permute-done | bytes 327712 | tf_op jit(solution)/shard_map/ppermute | solution.py:372
  83.3 3.7 %collective-permute-start.15 = (bf16[128,640]{1,0:T(8,128)(2,1)S(1)}, bf16[128,640]{1,0:T(8,128)(2,1)S(1)}, u32[]{:S(2)}, u32[]{:S(2)}) collective-permute-start(bf16[128,640]{1,0:T(8,128)(2,1)S(1)} %get-tuple-element.96.same1), channel_id=1, source_target_pairs={{0,16},{1,1},{16,32},{17,17},{32,48},{33,33},{48,0},{49,49},{2,18}... | collective-permute-start | bytes 491528 | tf_op jit(solution)/shard_map/ppermute | solution.py:393
  87.1 3.1 %compare_0.1 = (bf16[512,640]{1,0:T(8,128)(2,1)}, bf16[2,512,1280]{2,1,0:T(8,128)(2,1)}, f32[32,128]{1,0:T(8,128)S(1)}) custom-call(s32[11]{0:T(128)S(1)} %concatenate.6.s, f32[512,640]{1,0:T(8,128)S(1)} %fusion.4.pred, bf16[512,2560]{1,0:T(8,128)(2,1)S(1)} %copy-done.1, bf16[2560,640]{1,0:T(8,128)(2,1)S(1)} %copy-done.3, ...), custom_call_target="tpu_custom_call" | custom-call | flops 1 | bytes 1 | tf_op jit(solution)/shard_map/compare_0/pallas_call | solution.py:52
  91.7 3.1 %compare_1.1 = (bf16[512,640]{1,0:T(8,128)(2,1)}, bf16[2,512,1280]{2,1,0:T(8,128)(2,1)}, f32[32,128]{1,0:T(8,128)S(1)}) custom-call(s32[11]{0:T(128)S(1)} %concatenate.6.s, f32[512,640]{1,0:T(8,128)S(1)} %fusion.4.pred, bf16[512,2560]{1,0:T(8,128)(2,1)S(1)} %copy-done.1, ...), custom_call_target="tpu_custom_call", output_to_operand_aliasing={{0}: (6, {}), {1}: (7, {})} | custom-call | flops 1 | bytes 1 | tf_op jit(solution)/shard_map/compare_1/pallas_call | solution.py:52
  95.9 3.9 %gproj.1 = (bf16[4,2,160,640]{3,2,1,0:T(8,128)(2,1)}, f32[4,2,160,640]{3,2,1,0:T(8,128)S(1)}) custom-call(s32[11]{0:T(128)S(1)} %concatenate.6.s, bf16[512,2560]{1,0:T(8,128)(2,1)S(1)} %copy-done.1, bf16[512,640]{1,0:T(8,128)(2,1)S(1)} %copy-done.15), custom_call_target="tpu_custom_call" | custom-call | flops 1 | bytes 1 | tf_op jit(solution)/shard_map/gproj/pallas_call | solution.py:52
  100.4 2.6 %collective-permute-done.20 = f32[21,128]{1,0:T(8,128)S(1)} collective-permute-done((f32[21,128]{1,0:T(8,128)S(1)}, f32[21,128]{1,0:T(8,128)S(1)}, u32[]{:S(2)}, u32[]{:S(2)}) %collective-permute-start.20) | collective-permute-done | bytes 10784 | tf_op jit(solution)/shard_map/ppermute | solution.py:266
  110.7 2.9 %collective-permute-start.27 = (bf16[2,160,640]{2,1,0:T(8,128)(2,1)}, bf16[2,160,640]{2,1,0:T(8,128)(2,1)S(1)}, u32[]{:S(2)}, u32[]{:S(2)}) collective-permute-start(bf16[2,160,640]{2,1,0:T(8,128)(2,1)} %get-tuple-element.122), channel_id=1, source_target_pairs={{0,8},{4,12},{8,0},{12,4},{1,9},{5,13},{9,1},{13,5},{2,10},{6,14},... | collective-permute-start | bytes 1228808 | tf_op jit(solution)/shard_map/ppermute | solution.py:444
  114.1 4.7 %collective-permute-done.24 = f32[25,128]{1,0:T(8,128)S(1)} collective-permute-done((f32[25,128]{1,0:T(8,128)S(1)}, f32[25,128]{1,0:T(8,128)S(1)}, u32[]{:S(2)}, u32[]{:S(2)}) %collective-permute-start.24) | collective-permute-done | bytes 12832 | tf_op jit(solution)/shard_map/ppermute | solution.py:266
  120.4 6.8 %collective-permute-done.25 = f32[21,128]{1,0:T(8,128)S(1)} collective-permute-done((f32[21,128]{1,0:T(8,128)S(1)}, f32[21,128]{1,0:T(8,128)S(1)}, u32[]{:S(2)}, u32[]{:S(2)}) %collective-permute-start.25) | collective-permute-done | bytes 10784 | tf_op jit(solution)/shard_map/ppermute | solution.py:266
  139.9 2.5 %hidden.1 = f32[128,1280]{1,0:T(8,128)} custom-call(s32[11]{0:T(128)S(1)} %concatenate.6.s, bf16[128,1280]{1,0:T(8,128)(2,1)} %reduce-scatter.2.cloned.1.call-done.grad, f32[128,1]{1,0:T(8,128)S(1)} %copy.16.inner, bf16[128,2560]{1,0:T(8,128)(2,1)S(1)} %bitcast.34, f32[128,1]{1,0:T(8,128)S(1)} %copy.17.inverse_rms, f32[1,2560]{1,0:T(1,128)S(1)} %broadcast_in_dim.11.norm_gain), custom_call_target="tpu_custom_call" | custom-call | flops 1 | bytes 1 | tf_op jit(solution)/shard_map/hidden/pallas_call | solution.py:52
  (147 shorter events, 43.5 us)
Async XLA Ops:
  7.2 47.1 %all-gather.2.cloned.1.call-start = ((), (), s32[]{:S(2)}) async-start(), calls=%async_computation.1 | async-start | bytes 3276800 | tf_op jit(solution)/shard_map/all_gather | solution.py:333
  12.8 127.1 %reduce-scatter.2.cloned.1.call-start = ((), (), s32[]{:S(2)}) async-start(), calls=%async_computation.2 | async-start | bytes 2949120 | tf_op jit(solution)/shard_map/reduce_scatter | solution.py:423
  13.0 17.2 %collective-permute-start.1 = (bf16[4,2,128,256]{3,2,1,0:T(8,128)(2,1)}, bf16[4,2,128,256]{3,2,1,0:T(8,128)(2,1)S(1)}, u32[]{:S(2)}, u32[]{:S(2)}) collective-permute-start(bf16[4,2,128,256]{3,2,1,0:T(8,128)(2,1)} %get-tuple-element.70), channel_id=1, source_target_pairs={{0,66},{2,64},{64,2},{66,0},{1,67},{3,65},{65,3},{67,1},{4,70},{6,... | collective-permute-start | bytes 1572872 | tf_op jit(solution)/shard_map/ppermute | solution.py:309
  21.2 23.0 %collective-permute-start.4 = (bf16[512,640]{1,0:T(8,128)(2,1)}, bf16[512,640]{1,0:T(8,128)(2,1)S(1)}, u32[]{:S(2)}, u32[]{:S(2)}) collective-permute-start(bf16[512,640]{1,0:T(8,128)(2,1)} %get-tuple-element.75), channel_id=1, source_target_pairs={{0,66},{2,64},{64,2},{66,0},{1,67},{3,65},{65,3},{67,1},{4,70},{6,... | collective-permute-start | bytes 1966088 | tf_op jit(solution)/shard_map/ppermute | solution.py:347
  35.8 23.5 %collective-permute-start.5 = (bf16[512,640]{1,0:T(8,128)(2,1)}, bf16[512,640]{1,0:T(8,128)(2,1)}, u32[]{:S(2)}, u32[]{:S(2)}) collective-permute-start(bf16[512,640]{1,0:T(8,128)(2,1)} %get-tuple-element.84), channel_id=1, source_target_pairs={{0,66},{2,64},{64,2},{66,0},{1,67},{3,65},{65,3},{67,1},{4,70},{6,... | collective-permute-start | bytes 1966088 | tf_op jit(solution)/shard_map/ppermute | solution.py:347
  39.0 25.4 %collective-permute-start.9 = (bf16[128,1280]{1,0:T(8,128)(2,1)}, bf16[128,1280]{1,0:T(8,128)(2,1)}, u32[]{:S(2)}, u32[]{:S(2)}) collective-permute-start(bf16[128,1280]{1,0:T(8,128)(2,1)} %get-tuple-element.90), channel_id=1, source_target_pairs={{0,1},{1,0},{2,3},{3,2},{4,5},{5,4},{6,7},{7,6},{8,9},{9,8},{10,11... | collective-permute-start | bytes 983048 | tf_op jit(solution)/shard_map/ppermute | solution.py:311
  48.6 18.3 %collective-permute-start.6 = (bf16[2,128,640]{2,1,0:T(8,128)(2,1)}, bf16[2,128,640]{2,1,0:T(8,128)(2,1)}, u32[]{:S(2)}, u32[]{:S(2)}) collective-permute-start(bf16[2,128,640]{2,1,0:T(8,128)(2,1)} %get-tuple-element.87), channel_id=1, source_target_pairs={{0,4},{4,8},{8,12},{12,0},{1,5},{5,9},{9,13},{13,1},{2,6},{6,10},{... | collective-permute-start | bytes 983048 | tf_op jit(solution)/shard_map/ppermute | solution.py:372
  50.1 18.2 %collective-permute-start.7 = (bf16[2,128,640]{2,1,0:T(8,128)(2,1)}, bf16[2,128,640]{2,1,0:T(8,128)(2,1)}, u32[]{:S(2)}, u32[]{:S(2)}) collective-permute-start(bf16[2,128,640]{2,1,0:T(8,128)(2,1)} %get-tuple-element.88), channel_id=1, source_target_pairs={{0,8},{4,12},{8,0},{12,4},{1,9},{5,13},{9,1},{13,5},{2,10},{6,14},... | collective-permute-start | bytes 983048 | tf_op jit(solution)/shard_map/ppermute | solution.py:372
  52.8 15.5 %collective-permute-start.8 = (bf16[2,128,640]{2,1,0:T(8,128)(2,1)}, bf16[2,128,640]{2,1,0:T(8,128)(2,1)}, u32[]{:S(2)}, u32[]{:S(2)}) collective-permute-start(bf16[2,128,640]{2,1,0:T(8,128)(2,1)} %get-tuple-element.89), channel_id=1, source_target_pairs={{0,12},{4,0},{8,4},{12,8},{1,13},{5,1},{9,5},{13,9},{2,14},{6,2},{... | collective-permute-start | bytes 983048 | tf_op jit(solution)/shard_map/ppermute | solution.py:372
  63.9 11.4 %collective-permute-start.10 = (bf16[2,128,640]{2,1,0:T(8,128)(2,1)}, bf16[2,128,640]{2,1,0:T(8,128)(2,1)S(1)}, u32[]{:S(2)}, u32[]{:S(2)}) collective-permute-start(bf16[2,128,640]{2,1,0:T(8,128)(2,1)} %get-tuple-element.93), channel_id=1, source_target_pairs={{0,4},{4,8},{8,12},{12,0},{1,5},{5,9},{9,13},{13,1},{2,6},{6,10},{... | collective-permute-start | bytes 983048 | tf_op jit(solution)/shard_map/ppermute | solution.py:372
  64.5 17.0 %collective-permute-start.11 = (bf16[2,128,640]{2,1,0:T(8,128)(2,1)}, bf16[2,128,640]{2,1,0:T(8,128)(2,1)S(1)}, u32[]{:S(2)}, u32[]{:S(2)}) collective-permute-start(bf16[2,128,640]{2,1,0:T(8,128)(2,1)} %get-tuple-element.94), channel_id=1, source_target_pairs={{0,8},{4,12},{8,0},{12,4},{1,9},{5,13},{9,1},{13,5},{2,10},{6,14},... | collective-permute-start | bytes 983048 | tf_op jit(solution)/shard_map/ppermute | solution.py:372
  66.8 14.6 %collective-permute-start.12 = (bf16[2,128,640]{2,1,0:T(8,128)(2,1)}, bf16[2,128,640]{2,1,0:T(8,128)(2,1)S(1)}, u32[]{:S(2)}, u32[]{:S(2)}) collective-permute-start(bf16[2,128,640]{2,1,0:T(8,128)(2,1)} %get-tuple-element.95), channel_id=1, source_target_pairs={{0,12},{4,0},{8,4},{12,8},{1,13},{5,1},{9,5},{13,9},{2,14},{6,2},{... | collective-permute-start | bytes 983048 | tf_op jit(solution)/shard_map/ppermute | solution.py:372
  70.5 16.5 %collective-permute-start.13 = (bf16[128,640]{1,0:T(8,128)(2,1)S(1)}, bf16[128,640]{1,0:T(8,128)(2,1)S(1)}, u32[]{:S(2)}, u32[]{:S(2)}) collective-permute-start(bf16[128,640]{1,0:T(8,128)(2,1)S(1)} %get-tuple-element.91.same0), channel_id=1, source_target_pairs={{0,32},{1,49},{16,48},{17,1},{32,0},{33,17},{48,16},{49,33},{2,34}... | collective-permute-start | bytes 491528 | tf_op jit(solution)/shard_map/ppermute | solution.py:393
  73.8 13.2 %collective-permute-start.14 = (bf16[128,640]{1,0:T(8,128)(2,1)S(1)}, bf16[128,640]{1,0:T(8,128)(2,1)S(1)}, u32[]{:S(2)}, u32[]{:S(2)}) collective-permute-start(bf16[128,640]{1,0:T(8,128)(2,1)S(1)} %get-tuple-element.111), channel_id=1, source_target_pairs={{0,33},{1,48},{16,49},{17,0},{32,1},{33,16},{48,17},{49,32},{2,35}... | collective-permute-start | bytes 491528 | tf_op jit(solution)/shard_map/ppermute | solution.py:394
  83.1 7.1 %collective-permute-start.16 = (bf16[128,640]{1,0:T(8,128)(2,1)S(1)}, bf16[128,640]{1,0:T(8,128)(2,1)S(1)}, u32[]{:S(2)}, u32[]{:S(2)}) collective-permute-start(bf16[128,640]{1,0:T(8,128)(2,1)S(1)} %get-tuple-element.112), channel_id=1, source_target_pairs={{0,17},{1,0},{16,33},{17,16},{32,49},{33,32},{48,1},{49,48},{2,19}... | collective-permute-start | bytes 491528 | tf_op jit(solution)/shard_map/ppermute | solution.py:394
  83.3 8.4 %collective-permute-start.15 = (bf16[128,640]{1,0:T(8,128)(2,1)S(1)}, bf16[128,640]{1,0:T(8,128)(2,1)S(1)}, u32[]{:S(2)}, u32[]{:S(2)}) collective-permute-start(bf16[128,640]{1,0:T(8,128)(2,1)S(1)} %get-tuple-element.96.same1), channel_id=1, source_target_pairs={{0,16},{1,1},{16,32},{17,17},{32,48},{33,33},{48,0},{49,49},{2,18}... | collective-permute-start | bytes 491528 | tf_op jit(solution)/shard_map/ppermute | solution.py:393
  105.4 8.2 %collective-permute-start.23 = (f32[25,128]{1,0:T(8,128)S(1)}, f32[25,128]{1,0:T(8,128)S(1)}, u32[]{:S(2)}, u32[]{:S(2)}) collective-permute-start(f32[25,128]{1,0:T(8,128)S(1)} %pad_maximum_fusion), channel_id=1, source_target_pairs={{0,48},{16,0},{32,16},{48,32},{1,49},{17,1},{33,17},{49,33},{2,50}... | collective-permute-start | bytes 38408 | tf_op jit(solution)/shard_map/ppermute | solution.py:266
  107.1 6.9 %collective-permute-start.22 = (f32[25,128]{1,0:T(8,128)S(1)}, f32[25,128]{1,0:T(8,128)S(1)}, u32[]{:S(2)}, u32[]{:S(2)}) collective-permute-start(f32[25,128]{1,0:T(8,128)S(1)} %pad_maximum_fusion), channel_id=1, source_target_pairs={{0,32},{16,48},{32,0},{48,16},{1,33},{17,49},{33,1},{49,17},{2,34}... | collective-permute-start | bytes 38408 | tf_op jit(solution)/shard_map/ppermute | solution.py:266
  108.7 21.4 %collective-permute-start.26 = (bf16[2,160,640]{2,1,0:T(8,128)(2,1)}, bf16[2,160,640]{2,1,0:T(8,128)(2,1)S(1)}, u32[]{:S(2)}, u32[]{:S(2)}) collective-permute-start(bf16[2,160,640]{2,1,0:T(8,128)(2,1)} %get-tuple-element.121), channel_id=1, source_target_pairs={{0,4},{4,8},{8,12},{12,0},{1,5},{5,9},{9,13},{13,1},{2,6},{6,10},{... | collective-permute-start | bytes 1228808 | tf_op jit(solution)/shard_map/ppermute | solution.py:444
  110.7 20.5 %collective-permute-start.27 = (bf16[2,160,640]{2,1,0:T(8,128)(2,1)}, bf16[2,160,640]{2,1,0:T(8,128)(2,1)S(1)}, u32[]{:S(2)}, u32[]{:S(2)}) collective-permute-start(bf16[2,160,640]{2,1,0:T(8,128)(2,1)} %get-tuple-element.122), channel_id=1, source_target_pairs={{0,8},{4,12},{8,0},{12,4},{1,9},{5,13},{9,1},{13,5},{2,10},{6,14},... | collective-permute-start | bytes 1228808 | tf_op jit(solution)/shard_map/ppermute | solution.py:444
  113.6 17.6 %collective-permute-start.28 = (bf16[2,160,640]{2,1,0:T(8,128)(2,1)}, bf16[2,160,640]{2,1,0:T(8,128)(2,1)S(1)}, u32[]{:S(2)}, u32[]{:S(2)}) collective-permute-start(bf16[2,160,640]{2,1,0:T(8,128)(2,1)} %get-tuple-element.123), channel_id=1, source_target_pairs={{0,12},{4,0},{8,4},{12,8},{1,13},{5,1},{9,5},{13,9},{2,14},{6,2},{... | collective-permute-start | bytes 1228808 | tf_op jit(solution)/shard_map/ppermute | solution.py:444
  118.8 8.4 %collective-permute-start.25 = (f32[21,128]{1,0:T(8,128)S(1)}, f32[21,128]{1,0:T(8,128)S(1)}, u32[]{:S(2)}, u32[]{:S(2)}) collective-permute-start(f32[21,128]{1,0:T(8,128)S(1)} %slice.16), channel_id=1, source_target_pairs={{0,2},{2,0},{1,3},{3,1},{4,6},{6,4},{5,7},{7,5},{8,10},{10,8},{9,1... | collective-permute-start | bytes 32264 | tf_op jit(solution)/shard_map/ppermute | solution.py:266
  132.6 9.9 %collective-permute-start.32 = (bf16[160,640]{1,0:T(8,128)(2,1)}, bf16[160,640]{1,0:T(8,128)(2,1)S(1)}, u32[]{:S(2)}, u32[]{:S(2)}) collective-permute-start(bf16[160,640]{1,0:T(8,128)(2,1)} %get-tuple-element.126), channel_id=1, source_target_pairs={{0,2},{2,0},{1,3},{3,1},{4,6},{6,4},{5,7},{7,5},{8,10},{10,8},{9,1... | collective-permute-start | bytes 614408 | tf_op jit(solution)/shard_map/ppermute | solution.py:467
  135.4 7.8 %collective-permute-start.31 = (f32[21,128]{1,0:T(8,128)S(1)}, f32[21,128]{1,0:T(8,128)S(1)}, u32[]{:S(2)}, u32[]{:S(2)}) collective-permute-start(f32[21,128]{1,0:T(8,128)S(1)} %slice_add_fusion), channel_id=1, source_target_pairs={{0,12},{4,0},{8,4},{12,8},{1,13},{5,1},{9,5},{13,9},{2,14},{6,2},{... | collective-permute-start | bytes 32264 | tf_op jit(solution)/shard_map/ppermute | solution.py:469
  (42 other events, 375.4 us)
Sparse Core Ops, SparseCore 0:
  12.9 37.6 all-gather.1
  94.9 44.8 reduce-scatter.1

commit v8 on v7

--- a/solution.py
+++ b/solution.py
@@ -227,7 +227,8 @@
 def hidden_kernel(s, grad, inner, hidden, inverse_rms, norm_gain, out):
     scale = inverse_rms[...]
     unit = hidden[...].astype(F32) * scale
-    out[...] = scale * (grad[...].astype(F32) * norm_gain[...] - unit * (inner[...] / D_S))
+    mean_term = jnp.broadcast_to(inner[...], (128, 128)).T[:, :1] / D_S
+    out[...] = scale * (grad[...].astype(F32) * norm_gain[...] - unit * mean_term)
 
 
 def gproj_kernel(s, normed, gp, sent, kept):
@@ -473,7 +474,7 @@
         scalars,
         [
             (summed, whole(half_shape)),
-            (inner.reshape(128, 1), whole((128, 1))),
+            (inner, whole((1, 128))),
             (student_hidden[0], pl.BlockSpec((128, width), lambda i, s: (0, s[G]))),
             (inverse_rms, whole((128, 1))),
             (norm_gain.reshape(1, D_S), pl.BlockSpec((1, width), lambda i, s: (0, s[G]))),
@@ -486,10 +487,10 @@
     grad_proj = (gkept + gsent.astype(F32)) / live_count
     *sums, grad_proj = barrier((*sums, grad_proj))
     small = sum(sums, small)
-    small = small.reshape(-1)
-    distill_loss = small[20 * 128] / (live_count * D_T)
-    gain_half = lax.dynamic_slice_in_dim(norm_gain, g * width, width, 0)
-    grad_gain = lax.dynamic_slice_in_dim(small, g * width, width, 0) / (gain_half * live_count)
+    distill_loss = small[20, 0] / (live_count * D_T)
+    gain_rows = lax.dynamic_slice_in_dim(norm_gain.reshape(20, 128), g * 10, 10, 0)
+    gain_sums = lax.dynamic_slice_in_dim(small, g * 10, 10, 0)
+    grad_gain = (gain_sums / (gain_rows * live_count)).reshape(width)
     return (target[None], distill_loss, grad_proj, grad_gain, grad_hidden[None])
 
 

time: 156 us -> 156 us (level)
  transfers between devices with their start and end apart: 35 -> 35, of which waited for: 13 -> 13; matrix products, arithmetic and copies ran while one was open for 4% -> 4% of each run, Pallas kernels for 25% -> 26%
where the time goes in v8:
time: 156 us; the launch traced here: 153 us
  Pallas kernels  45.7 us (29%)
  starting transfers between devices  43.5 us (28%)
  waiting for transfers between devices  34.1 us (22%)
  between operations  16.9 us (11%)
  matrix products  5.05 us (3%)
  local copies, waits for them, and re-layouts  4.51 us (3%)
  other arithmetic  3.37 us (2%)
    pallas_call x15, Pallas kernels, call(): pl.pallas_call(kernel, out_shape=[pltpu.HBM(o[0], o[1]) if len(o) == 3 el...  45.7 us
    ppermute x6, waiting for transfers between devices, sum_over(): got = [lax.ppermute(array, axis, ring(n, j)) for j in range(1, n)]  14.2 us
    ppermute x6, starting transfers between devices, body(): lax.ppermute(outs[j - 1], 'x', ring(NX, j))  10 us
    ppermute x6, waiting for transfers between devices, body(): lax.ppermute(outs[j - 1], 'x', ring(NX, j))  7.64 us
    ppermute x2, starting transfers between devices, body(): lax.ppermute(done_same, ('dp', 'core'), to_owner(st, False))  6.96 us
    ppermute x2, starting transfers between devices, body(): w_z = [lax.ppermute(w, ('grp', 'zh'), WRAP) for w in w_z]  6.08 us
    ppermute x6, starting transfers between devices, sum_over(): got = [lax.ppermute(array, axis, ring(n, j)) for j in range(1, n)]  5.51 us
    ppermute x3, starting transfers between devices, body(): got = {j: lax.ppermute(outs[j - 1], 'x', ring(NX, j)) for j in (2, 1, 3)}  5.3 us
  transfers between devices with their start and end apart: 35, of which 13 were waited for; matrix products, arithmetic and copies ran while one was open for 4% of the time, Pallas kernels for 26%

profile of v8, /device:TPU:0, one launch (start us, length us, event | category | flops | bytes accessed | tf_op | source)
XLA Modules:
  0.0 153.1 jit_solution(15148661849735881763)
XLA Ops:
  8.0 3.5 %pick.1 = (bf16[4,2,128,256]{3,2,1,0:T(8,128)(2,1)}, bf16[256,2560]{1,0:T(8,128)(2,1)}, bf16[128,1280]{1,0:T(8,128)(2,1)}) custom-call(s32[11]{0:T(128)S(1)} %concatenate.6.s, bf16[4,4,128,256]{3,2,1,0:T(8,128)(2,1)} %bitcast.34, bf16[256,5120]{1,0:T(8,128)(2,1)} %w_a.3, bf16[256,5120]{1,0:T(8,128)(2,1)} %w_a.3, bf16[256,5120]{1,0:T(8,128)(2,1)} %w_a.3, ...), custom_call_target="tpu_custom_call" | custom-call | flops 1 | bytes 1 | tf_op jit(solution)/shard_map/pick/pallas_call | solution.py:52
  13.0 4.2 %collective-permute-start.1 = (bf16[4,2,128,256]{3,2,1,0:T(8,128)(2,1)}, bf16[4,2,128,256]{3,2,1,0:T(8,128)(2,1)S(1)}, u32[]{:S(2)}, u32[]{:S(2)}) collective-permute-start(bf16[4,2,128,256]{3,2,1,0:T(8,128)(2,1)} %get-tuple-element.70), channel_id=1, source_target_pairs={{0,66},{2,64},{64,2},{66,0},{1,67},{3,65},{65,3},{67,1},{4,70},{6,... | collective-permute-start | bytes 1572872 | tf_op jit(solution)/shard_map/ppermute | solution.py:310
  18.3 2.9 %pick_weights.1 = (bf16[512,640]{1,0:T(8,128)(2,1)}, bf16[512,640]{1,0:T(8,128)(2,1)}) custom-call(s32[11]{0:T(128)S(1)} %concatenate.6.s, bf16[256,5120]{1,0:T(8,128)(2,1)} %w_a.3, bf16[256,5120]{1,0:T(8,128)(2,1)} %w_a.3, bf16[256,2560]{1,0:T(8,128)(2,1)} %copy-done.4), custom_call_target="tpu_custom_call" | custom-call | flops 1 | bytes 1 | tf_op jit(solution)/shard_map/pick_weights/pallas_call | solution.py:52
  21.2 2.9 %collective-permute-start.4 = (bf16[512,640]{1,0:T(8,128)(2,1)}, bf16[512,640]{1,0:T(8,128)(2,1)S(1)}, u32[]{:S(2)}, u32[]{:S(2)}) collective-permute-start(bf16[512,640]{1,0:T(8,128)(2,1)} %get-tuple-element.75), channel_id=1, source_target_pairs={{0,66},{2,64},{64,2},{66,0},{1,67},{3,65},{65,3},{67,1},{4,70},{6,... | collective-permute-start | bytes 1966088 | tf_op jit(solution)/shard_map/ppermute | solution.py:348
  24.1 5.0 %attend_chip.1.ctx_a = bf16[1024,256]{1,0:T(8,128)(2,1)S(1)} custom-call(s32[11]{0:T(128)S(1)} %concatenate.6.s, bf16[4,4,128,256]{3,2,1,0:T(8,128)(2,1)S(1)} %bitcast.35, bf16[2048,512]{1,0:T(8,128)(2,1)S(1)} %bitcast.27, bf16[2048,512]{1,0:T(8,128)(2,1)S(1)} %bitcast.29), custom_call_target="tpu_custom_call" | custom-call | flops 1 | bytes 1 | tf_op jit(solution)/shard_map/attend_chip/pallas_call | solution.py:52
  30.2 5.1 %attend_next.1.ctx_b = bf16[1024,256]{1,0:T(8,128)(2,1)S(1)} custom-call(s32[11]{0:T(128)S(1)} %concatenate.6.s, bf16[4,2,128,256]{3,2,1,0:T(8,128)(2,1)S(1)} %collective-permute-done.1.q_ref, bf16[2048,512]{1,0:T(8,128)(2,1)S(1)} %bitcast.28, bf16[2048,512]{1,0:T(8,128)(2,1)S(1)} %bitcast.30), custom_call_target="tpu_custom_call" | custom-call | flops 1 | bytes 1 | tf_op jit(solution)/shard_map/attend_next/pallas_call | solution.py:52
  35.8 3.2 %collective-permute-start.5 = (bf16[512,640]{1,0:T(8,128)(2,1)}, bf16[512,640]{1,0:T(8,128)(2,1)}, u32[]{:S(2)}, u32[]{:S(2)}) collective-permute-start(bf16[512,640]{1,0:T(8,128)(2,1)} %get-tuple-element.84), channel_id=1, source_target_pairs={{0,66},{2,64},{64,2},{66,0},{1,67},{3,65},{65,3},{67,1},{4,70},{6,... | collective-permute-start | bytes 1966088 | tf_op jit(solution)/shard_map/ppermute | solution.py:348
  39.1 5.1 %collective-permute-done.4.w_z = bf16[512,640]{1,0:T(8,128)(2,1)S(1)} collective-permute-done((bf16[512,640]{1,0:T(8,128)(2,1)}, bf16[512,640]{1,0:T(8,128)(2,1)S(1)}, u32[]{:S(2)}, u32[]{:S(2)}) %collective-permute-start.4) | collective-permute-done | bytes 655392 | tf_op jit(solution)/shard_map/ppermute | solution.py:348
  44.2 3.5 %project_0.1 = (f32[2,128,640]{2,1,0:T(8,128)S(1)}, bf16[2,128,640]{2,1,0:T(8,128)(2,1)}, bf16[2,128,640]{2,1,0:T(8,128)(2,1)}, bf16[2,128,640]{2,1,0:T(8,128)(2,1)}) custom-call(s32[11]{0:T(128)S(1)} %concatenate.6.s, bf16[1024,256]{1,0:T(8,128)(2,1)S(1)} %attend_chip.1.ctx_a, bf16[1024,256]{1,0:T(8,128)(2,1)S(1)} %collective-permute-done.2.ctx_ac, ...), custom_call_target="tpu_custom_call" | custom-call | flops 1 | bytes 1 | tf_op jit(solution)/shard_map/project_0/pallas_call | solution.py:52
  50.1 2.7 %collective-permute-start.7 = (bf16[2,128,640]{2,1,0:T(8,128)(2,1)}, bf16[2,128,640]{2,1,0:T(8,128)(2,1)}, u32[]{:S(2)}, u32[]{:S(2)}) collective-permute-start(bf16[2,128,640]{2,1,0:T(8,128)(2,1)} %get-tuple-element.88), channel_id=1, source_target_pairs={{0,8},{4,12},{8,0},{12,4},{1,9},{5,13},{9,1},{13,5},{2,10},{6,14},... | collective-permute-start | bytes 983048 | tf_op jit(solution)/shard_map/ppermute | solution.py:373
  54.2 5.1 %fusion.4.pred = f32[512,640]{1,0:T(8,128)S(1)} fusion(bf16[512,2560]{1,0:T(8,128)(2,1)} %all-gather.2.cloned.1.call-done.normed, bf16[2560,640]{1,0:T(8,128)(2,1)} %proj.3), kind=kOutput, calls=%fused_computation.15 | convolution fusion | flops 1677721600 | bytes 7208960 | tf_op jit(solution)/shard_map/dot_general | solution.py:371
  59.4 4.5 %project_1.1 = (f32[2,128,640]{2,1,0:T(8,128)S(1)}, bf16[2,128,640]{2,1,0:T(8,128)(2,1)}, bf16[2,128,640]{2,1,0:T(8,128)(2,1)}, bf16[2,128,640]{2,1,0:T(8,128)(2,1)}) custom-call(s32[11]{0:T(128)S(1)} %concatenate.6.s, bf16[1024,256]{1,0:T(8,128)(2,1)S(1)} %copy-done.11, bf16[1024,256]{1,0:T(8,128)(2,1)S(1)} %copy-done.19, bf16[1024,256]{1,0:T(8,128)(2,1)S(1)} %copy-done.13, ...), custom_call_target="tpu_custom_call" | custom-call | flops 1 | bytes 1 | tf_op jit(solution)/shard_map/project_1/pallas_call | solution.py:52
  64.5 2.3 %collective-permute-start.11 = (bf16[2,128,640]{2,1,0:T(8,128)(2,1)}, bf16[2,128,640]{2,1,0:T(8,128)(2,1)S(1)}, u32[]{:S(2)}, u32[]{:S(2)}) collective-permute-start(bf16[2,128,640]{2,1,0:T(8,128)(2,1)} %get-tuple-element.94), channel_id=1, source_target_pairs={{0,8},{4,12},{8,0},{12,4},{1,9},{5,13},{9,1},{13,5},{2,10},{6,14},... | collective-permute-start | bytes 983048 | tf_op jit(solution)/shard_map/ppermute | solution.py:373
  70.5 3.3 %collective-permute-start.13 = (bf16[128,640]{1,0:T(8,128)(2,1)S(1)}, bf16[128,640]{1,0:T(8,128)(2,1)S(1)}, u32[]{:S(2)}, u32[]{:S(2)}) collective-permute-start(bf16[128,640]{1,0:T(8,128)(2,1)S(1)} %get-tuple-element.91.same0), channel_id=1, source_target_pairs={{0,32},{1,49},{16,48},{17,1},{32,0},{33,17},{48,16},{49,33},{2,34}... | collective-permute-start | bytes 491528 | tf_op jit(solution)/shard_map/ppermute | solution.py:394
  75.2 6.2 %collective-permute-done.11.r2 = bf16[2,128,640]{2,1,0:T(8,128)(2,1)S(1)} collective-permute-done((bf16[2,128,640]{2,1,0:T(8,128)(2,1)}, bf16[2,128,640]{2,1,0:T(8,128)(2,1)S(1)}, u32[]{:S(2)}, u32[]{:S(2)}) %collective-permute-start.11) | collective-permute-done | bytes 327712 | tf_op jit(solution)/shard_map/ppermute | solution.py:373
  83.3 3.7 %collective-permute-start.15 = (bf16[128,640]{1,0:T(8,128)(2,1)S(1)}, bf16[128,640]{1,0:T(8,128)(2,1)S(1)}, u32[]{:S(2)}, u32[]{:S(2)}) collective-permute-start(bf16[128,640]{1,0:T(8,128)(2,1)S(1)} %get-tuple-element.96.same1), channel_id=1, source_target_pairs={{0,16},{1,1},{16,32},{17,17},{32,48},{33,33},{48,0},{49,49},{2,18}... | collective-permute-start | bytes 491528 | tf_op jit(solution)/shard_map/ppermute | solution.py:394
  87.1 3.1 %compare_0.1 = (bf16[512,640]{1,0:T(8,128)(2,1)}, bf16[2,512,1280]{2,1,0:T(8,128)(2,1)}, f32[32,128]{1,0:T(8,128)S(1)}) custom-call(s32[11]{0:T(128)S(1)} %concatenate.6.s, f32[512,640]{1,0:T(8,128)S(1)} %fusion.4.pred, bf16[512,2560]{1,0:T(8,128)(2,1)S(1)} %copy-done.1, bf16[2560,640]{1,0:T(8,128)(2,1)S(1)} %copy-done.3, ...), custom_call_target="tpu_custom_call" | custom-call | flops 1 | bytes 1 | tf_op jit(solution)/shard_map/compare_0/pallas_call | solution.py:52
  91.7 3.1 %compare_1.1 = (bf16[512,640]{1,0:T(8,128)(2,1)}, bf16[2,512,1280]{2,1,0:T(8,128)(2,1)}, f32[32,128]{1,0:T(8,128)S(1)}) custom-call(s32[11]{0:T(128)S(1)} %concatenate.6.s, f32[512,640]{1,0:T(8,128)S(1)} %fusion.4.pred, bf16[512,2560]{1,0:T(8,128)(2,1)S(1)} %copy-done.1, ...), custom_call_target="tpu_custom_call", output_to_operand_aliasing={{0}: (6, {}), {1}: (7, {})} | custom-call | flops 1 | bytes 1 | tf_op jit(solution)/shard_map/compare_1/pallas_call | solution.py:52
  95.9 3.9 %gproj.1 = (bf16[4,2,160,640]{3,2,1,0:T(8,128)(2,1)}, f32[4,2,160,640]{3,2,1,0:T(8,128)S(1)}) custom-call(s32[11]{0:T(128)S(1)} %concatenate.6.s, bf16[512,2560]{1,0:T(8,128)(2,1)S(1)} %copy-done.1, bf16[512,640]{1,0:T(8,128)(2,1)S(1)} %copy-done.15), custom_call_target="tpu_custom_call" | custom-call | flops 1 | bytes 1 | tf_op jit(solution)/shard_map/gproj/pallas_call | solution.py:52
  100.4 2.6 %collective-permute-done.20 = f32[21,128]{1,0:T(8,128)S(1)} collective-permute-done((f32[21,128]{1,0:T(8,128)S(1)}, f32[21,128]{1,0:T(8,128)S(1)}, u32[]{:S(2)}, u32[]{:S(2)}) %collective-permute-start.20) | collective-permute-done | bytes 10784 | tf_op jit(solution)/shard_map/ppermute | solution.py:267
  110.7 2.9 %collective-permute-start.27 = (bf16[2,160,640]{2,1,0:T(8,128)(2,1)}, bf16[2,160,640]{2,1,0:T(8,128)(2,1)S(1)}, u32[]{:S(2)}, u32[]{:S(2)}) collective-permute-start(bf16[2,160,640]{2,1,0:T(8,128)(2,1)} %get-tuple-element.122), channel_id=1, source_target_pairs={{0,8},{4,12},{8,0},{12,4},{1,9},{5,13},{9,1},{13,5},{2,10},{6,14},... | collective-permute-start | bytes 1228808 | tf_op jit(solution)/shard_map/ppermute | solution.py:445
  114.1 4.7 %collective-permute-done.24 = f32[25,128]{1,0:T(8,128)S(1)} collective-permute-done((f32[25,128]{1,0:T(8,128)S(1)}, f32[25,128]{1,0:T(8,128)S(1)}, u32[]{:S(2)}, u32[]{:S(2)}) %collective-permute-start.24) | collective-permute-done | bytes 12832 | tf_op jit(solution)/shard_map/ppermute | solution.py:267
  120.4 6.8 %collective-permute-done.25 = f32[21,128]{1,0:T(8,128)S(1)} collective-permute-done((f32[21,128]{1,0:T(8,128)S(1)}, f32[21,128]{1,0:T(8,128)S(1)}, u32[]{:S(2)}, u32[]{:S(2)}) %collective-permute-start.25) | collective-permute-done | bytes 10784 | tf_op jit(solution)/shard_map/ppermute | solution.py:267
  139.9 2.6 %hidden.1 = f32[128,1280]{1,0:T(8,128)} custom-call(s32[11]{0:T(128)S(1)} %concatenate.6.s, bf16[128,1280]{1,0:T(8,128)(2,1)} %reduce-scatter.2.cloned.1.call-done.grad, f32[1,128]{1,0:T(1,128)S(1)} %constant_dynamic-slice_fusion.inner, bf16[128,2560]{1,0:T(8,128)(2,1)S(1)} %bitcast.33, f32[128,1]{1,0:T(8,128)S(1)} %copy.16.inverse_rms, ...), custom_call_target="tpu_custom_call" | custom-call | flops 1 | bytes 1 | tf_op jit(solution)/shard_map/hidden/pallas_call | solution.py:52
  (146 shorter events, 43.3 us)
Async XLA Ops:
  7.2 47.1 %all-gather.2.cloned.1.call-start = ((), (), s32[]{:S(2)}) async-start(), calls=%async_computation.1 | async-start | bytes 3276800 | tf_op jit(solution)/shard_map/all_gather | solution.py:334
  12.8 127.1 %reduce-scatter.2.cloned.1.call-start = ((), (), s32[]{:S(2)}) async-start(), calls=%async_computation.2 | async-start | bytes 2949120 | tf_op jit(solution)/shard_map/reduce_scatter | solution.py:424
  13.0 17.2 %collective-permute-start.1 = (bf16[4,2,128,256]{3,2,1,0:T(8,128)(2,1)}, bf16[4,2,128,256]{3,2,1,0:T(8,128)(2,1)S(1)}, u32[]{:S(2)}, u32[]{:S(2)}) collective-permute-start(bf16[4,2,128,256]{3,2,1,0:T(8,128)(2,1)} %get-tuple-element.70), channel_id=1, source_target_pairs={{0,66},{2,64},{64,2},{66,0},{1,67},{3,65},{65,3},{67,1},{4,70},{6,... | collective-permute-start | bytes 1572872 | tf_op jit(solution)/shard_map/ppermute | solution.py:310
  21.2 23.0 %collective-permute-start.4 = (bf16[512,640]{1,0:T(8,128)(2,1)}, bf16[512,640]{1,0:T(8,128)(2,1)S(1)}, u32[]{:S(2)}, u32[]{:S(2)}) collective-permute-start(bf16[512,640]{1,0:T(8,128)(2,1)} %get-tuple-element.75), channel_id=1, source_target_pairs={{0,66},{2,64},{64,2},{66,0},{1,67},{3,65},{65,3},{67,1},{4,70},{6,... | collective-permute-start | bytes 1966088 | tf_op jit(solution)/shard_map/ppermute | solution.py:348
  35.8 23.5 %collective-permute-start.5 = (bf16[512,640]{1,0:T(8,128)(2,1)}, bf16[512,640]{1,0:T(8,128)(2,1)}, u32[]{:S(2)}, u32[]{:S(2)}) collective-permute-start(bf16[512,640]{1,0:T(8,128)(2,1)} %get-tuple-element.84), channel_id=1, source_target_pairs={{0,66},{2,64},{64,2},{66,0},{1,67},{3,65},{65,3},{67,1},{4,70},{6,... | collective-permute-start | bytes 1966088 | tf_op jit(solution)/shard_map/ppermute | solution.py:348
  39.0 25.4 %collective-permute-start.9 = (bf16[128,1280]{1,0:T(8,128)(2,1)}, bf16[128,1280]{1,0:T(8,128)(2,1)}, u32[]{:S(2)}, u32[]{:S(2)}) collective-permute-start(bf16[128,1280]{1,0:T(8,128)(2,1)} %get-tuple-element.90), channel_id=1, source_target_pairs={{0,1},{1,0},{2,3},{3,2},{4,5},{5,4},{6,7},{7,6},{8,9},{9,8},{10,11... | collective-permute-start | bytes 983048 | tf_op jit(solution)/shard_map/ppermute | solution.py:312
  48.6 18.3 %collective-permute-start.6 = (bf16[2,128,640]{2,1,0:T(8,128)(2,1)}, bf16[2,128,640]{2,1,0:T(8,128)(2,1)}, u32[]{:S(2)}, u32[]{:S(2)}) collective-permute-start(bf16[2,128,640]{2,1,0:T(8,128)(2,1)} %get-tuple-element.87), channel_id=1, source_target_pairs={{0,4},{4,8},{8,12},{12,0},{1,5},{5,9},{9,13},{13,1},{2,6},{6,10},{... | collective-permute-start | bytes 983048 | tf_op jit(solution)/shard_map/ppermute | solution.py:373
  50.1 18.2 %collective-permute-start.7 = (bf16[2,128,640]{2,1,0:T(8,128)(2,1)}, bf16[2,128,640]{2,1,0:T(8,128)(2,1)}, u32[]{:S(2)}, u32[]{:S(2)}) collective-permute-start(bf16[2,128,640]{2,1,0:T(8,128)(2,1)} %get-tuple-element.88), channel_id=1, source_target_pairs={{0,8},{4,12},{8,0},{12,4},{1,9},{5,13},{9,1},{13,5},{2,10},{6,14},... | collective-permute-start | bytes 983048 | tf_op jit(solution)/shard_map/ppermute | solution.py:373
  52.8 15.5 %collective-permute-start.8 = (bf16[2,128,640]{2,1,0:T(8,128)(2,1)}, bf16[2,128,640]{2,1,0:T(8,128)(2,1)}, u32[]{:S(2)}, u32[]{:S(2)}) collective-permute-start(bf16[2,128,640]{2,1,0:T(8,128)(2,1)} %get-tuple-element.89), channel_id=1, source_target_pairs={{0,12},{4,0},{8,4},{12,8},{1,13},{5,1},{9,5},{13,9},{2,14},{6,2},{... | collective-permute-start | bytes 983048 | tf_op jit(solution)/shard_map/ppermute | solution.py:373
  63.9 11.4 %collective-permute-start.10 = (bf16[2,128,640]{2,1,0:T(8,128)(2,1)}, bf16[2,128,640]{2,1,0:T(8,128)(2,1)S(1)}, u32[]{:S(2)}, u32[]{:S(2)}) collective-permute-start(bf16[2,128,640]{2,1,0:T(8,128)(2,1)} %get-tuple-element.93), channel_id=1, source_target_pairs={{0,4},{4,8},{8,12},{12,0},{1,5},{5,9},{9,13},{13,1},{2,6},{6,10},{... | collective-permute-start | bytes 983048 | tf_op jit(solution)/shard_map/ppermute | solution.py:373
  64.5 17.0 %collective-permute-start.11 = (bf16[2,128,640]{2,1,0:T(8,128)(2,1)}, bf16[2,128,640]{2,1,0:T(8,128)(2,1)S(1)}, u32[]{:S(2)}, u32[]{:S(2)}) collective-permute-start(bf16[2,128,640]{2,1,0:T(8,128)(2,1)} %get-tuple-element.94), channel_id=1, source_target_pairs={{0,8},{4,12},{8,0},{12,4},{1,9},{5,13},{9,1},{13,5},{2,10},{6,14},... | collective-permute-start | bytes 983048 | tf_op jit(solution)/shard_map/ppermute | solution.py:373
  66.8 14.6 %collective-permute-start.12 = (bf16[2,128,640]{2,1,0:T(8,128)(2,1)}, bf16[2,128,640]{2,1,0:T(8,128)(2,1)S(1)}, u32[]{:S(2)}, u32[]{:S(2)}) collective-permute-start(bf16[2,128,640]{2,1,0:T(8,128)(2,1)} %get-tuple-element.95), channel_id=1, source_target_pairs={{0,12},{4,0},{8,4},{12,8},{1,13},{5,1},{9,5},{13,9},{2,14},{6,2},{... | collective-permute-start | bytes 983048 | tf_op jit(solution)/shard_map/ppermute | solution.py:373
  70.5 16.5 %collective-permute-start.13 = (bf16[128,640]{1,0:T(8,128)(2,1)S(1)}, bf16[128,640]{1,0:T(8,128)(2,1)S(1)}, u32[]{:S(2)}, u32[]{:S(2)}) collective-permute-start(bf16[128,640]{1,0:T(8,128)(2,1)S(1)} %get-tuple-element.91.same0), channel_id=1, source_target_pairs={{0,32},{1,49},{16,48},{17,1},{32,0},{33,17},{48,16},{49,33},{2,34}... | collective-permute-start | bytes 491528 | tf_op jit(solution)/shard_map/ppermute | solution.py:394
  73.8 13.2 %collective-permute-start.14 = (bf16[128,640]{1,0:T(8,128)(2,1)S(1)}, bf16[128,640]{1,0:T(8,128)(2,1)S(1)}, u32[]{:S(2)}, u32[]{:S(2)}) collective-permute-start(bf16[128,640]{1,0:T(8,128)(2,1)S(1)} %get-tuple-element.111), channel_id=1, source_target_pairs={{0,33},{1,48},{16,49},{17,0},{32,1},{33,16},{48,17},{49,32},{2,35}... | collective-permute-start | bytes 491528 | tf_op jit(solution)/shard_map/ppermute | solution.py:395
  83.1 7.1 %collective-permute-start.16 = (bf16[128,640]{1,0:T(8,128)(2,1)S(1)}, bf16[128,640]{1,0:T(8,128)(2,1)S(1)}, u32[]{:S(2)}, u32[]{:S(2)}) collective-permute-start(bf16[128,640]{1,0:T(8,128)(2,1)S(1)} %get-tuple-element.112), channel_id=1, source_target_pairs={{0,17},{1,0},{16,33},{17,16},{32,49},{33,32},{48,1},{49,48},{2,19}... | collective-permute-start | bytes 491528 | tf_op jit(solution)/shard_map/ppermute | solution.py:395
  83.3 8.4 %collective-permute-start.15 = (bf16[128,640]{1,0:T(8,128)(2,1)S(1)}, bf16[128,640]{1,0:T(8,128)(2,1)S(1)}, u32[]{:S(2)}, u32[]{:S(2)}) collective-permute-start(bf16[128,640]{1,0:T(8,128)(2,1)S(1)} %get-tuple-element.96.same1), channel_id=1, source_target_pairs={{0,16},{1,1},{16,32},{17,17},{32,48},{33,33},{48,0},{49,49},{2,18}... | collective-permute-start | bytes 491528 | tf_op jit(solution)/shard_map/ppermute | solution.py:394
  105.4 8.2 %collective-permute-start.23 = (f32[25,128]{1,0:T(8,128)S(1)}, f32[25,128]{1,0:T(8,128)S(1)}, u32[]{:S(2)}, u32[]{:S(2)}) collective-permute-start(f32[25,128]{1,0:T(8,128)S(1)} %pad_maximum_fusion), channel_id=1, source_target_pairs={{0,48},{16,0},{32,16},{48,32},{1,49},{17,1},{33,17},{49,33},{2,50}... | collective-permute-start | bytes 38408 | tf_op jit(solution)/shard_map/ppermute | solution.py:267
  107.1 6.9 %collective-permute-start.22 = (f32[25,128]{1,0:T(8,128)S(1)}, f32[25,128]{1,0:T(8,128)S(1)}, u32[]{:S(2)}, u32[]{:S(2)}) collective-permute-start(f32[25,128]{1,0:T(8,128)S(1)} %pad_maximum_fusion), channel_id=1, source_target_pairs={{0,32},{16,48},{32,0},{48,16},{1,33},{17,49},{33,1},{49,17},{2,34}... | collective-permute-start | bytes 38408 | tf_op jit(solution)/shard_map/ppermute | solution.py:267
  108.7 21.4 %collective-permute-start.26 = (bf16[2,160,640]{2,1,0:T(8,128)(2,1)}, bf16[2,160,640]{2,1,0:T(8,128)(2,1)S(1)}, u32[]{:S(2)}, u32[]{:S(2)}) collective-permute-start(bf16[2,160,640]{2,1,0:T(8,128)(2,1)} %get-tuple-element.121), channel_id=1, source_target_pairs={{0,4},{4,8},{8,12},{12,0},{1,5},{5,9},{9,13},{13,1},{2,6},{6,10},{... | collective-permute-start | bytes 1228808 | tf_op jit(solution)/shard_map/ppermute | solution.py:445
  110.7 20.5 %collective-permute-start.27 = (bf16[2,160,640]{2,1,0:T(8,128)(2,1)}, bf16[2,160,640]{2,1,0:T(8,128)(2,1)S(1)}, u32[]{:S(2)}, u32[]{:S(2)}) collective-permute-start(bf16[2,160,640]{2,1,0:T(8,128)(2,1)} %get-tuple-element.122), channel_id=1, source_target_pairs={{0,8},{4,12},{8,0},{12,4},{1,9},{5,13},{9,1},{13,5},{2,10},{6,14},... | collective-permute-start | bytes 1228808 | tf_op jit(solution)/shard_map/ppermute | solution.py:445
  113.6 17.6 %collective-permute-start.28 = (bf16[2,160,640]{2,1,0:T(8,128)(2,1)}, bf16[2,160,640]{2,1,0:T(8,128)(2,1)S(1)}, u32[]{:S(2)}, u32[]{:S(2)}) collective-permute-start(bf16[2,160,640]{2,1,0:T(8,128)(2,1)} %get-tuple-element.123), channel_id=1, source_target_pairs={{0,12},{4,0},{8,4},{12,8},{1,13},{5,1},{9,5},{13,9},{2,14},{6,2},{... | collective-permute-start | bytes 1228808 | tf_op jit(solution)/shard_map/ppermute | solution.py:445
  118.8 8.4 %collective-permute-start.25 = (f32[21,128]{1,0:T(8,128)S(1)}, f32[21,128]{1,0:T(8,128)S(1)}, u32[]{:S(2)}, u32[]{:S(2)}) collective-permute-start(f32[21,128]{1,0:T(8,128)S(1)} %slice.16), channel_id=1, source_target_pairs={{0,2},{2,0},{1,3},{3,1},{4,6},{6,4},{5,7},{7,5},{8,10},{10,8},{9,1... | collective-permute-start | bytes 32264 | tf_op jit(solution)/shard_map/ppermute | solution.py:267
  132.6 9.9 %collective-permute-start.32 = (bf16[160,640]{1,0:T(8,128)(2,1)}, bf16[160,640]{1,0:T(8,128)(2,1)S(1)}, u32[]{:S(2)}, u32[]{:S(2)}) collective-permute-start(bf16[160,640]{1,0:T(8,128)(2,1)} %get-tuple-element.126), channel_id=1, source_target_pairs={{0,2},{2,0},{1,3},{3,1},{4,6},{6,4},{5,7},{7,5},{8,10},{10,8},{9,1... | collective-permute-start | bytes 614408 | tf_op jit(solution)/shard_map/ppermute | solution.py:468
  135.3 8.0 %collective-permute-start.31 = (f32[21,128]{1,0:T(8,128)S(1)}, f32[21,128]{1,0:T(8,128)S(1)}, u32[]{:S(2)}, u32[]{:S(2)}) collective-permute-start(f32[21,128]{1,0:T(8,128)S(1)} %slice_add_fusion), channel_id=1, source_target_pairs={{0,12},{4,0},{8,4},{12,8},{1,13},{5,1},{9,5},{13,9},{2,14},{6,2},{... | collective-permute-start | bytes 32264 | tf_op jit(solution)/shard_map/ppermute | solution.py:470
  (42 other events, 375.5 us)
Sparse Core Ops, SparseCore 0:
  12.9 37.6 all-gather.1
  94.9 44.8 reduce-scatter.1

commit v9 on v8

--- a/solution.py
+++ b/solution.py
@@ -27,7 +27,7 @@
 
 
 WRAP = [(g * 2 + z, (1 - g) * 2 + (1 - z)) for g in range(2) for z in range(2)]
-MIB = 32
+MIB = 28
 COST = 1
 IN_HBM = pl.BlockSpec(memory_space=pltpu.HBM)
 
@@ -323,7 +323,7 @@
             [((1024, 256), BF)],
             name,
             scratch=[pltpu.VMEM((2048, 2 * HD), BF)],
-            mib=40,
+            mib=32,
         )[0]
 
     hidden, _ = barrier((student_hidden[0], w_out))

time: 156 us -> 156 us (level)
  no operation moved by 1% of the time
where the time goes in v9:
time: 156 us; the launch traced here: 153 us
  Pallas kernels  45.7 us (29%)
  starting transfers between devices  43.5 us (28%)
  waiting for transfers between devices  34.1 us (22%)
  between operations  16.9 us (11%)
  matrix products  5.05 us (3%)
  local copies, waits for them, and re-layouts  4.51 us (3%)
  other arithmetic  3.37 us (2%)
    pallas_call x15, Pallas kernels, call(): pl.pallas_call(kernel, out_shape=[pltpu.HBM(o[0], o[1]) if len(o) == 3 el...  45.7 us
    ppermute x6, waiting for transfers between devices, sum_over(): got = [lax.ppermute(array, axis, ring(n, j)) for j in range(1, n)]  14.2 us
    ppermute x6, starting transfers between devices, body(): lax.ppermute(outs[j - 1], 'x', ring(NX, j))  10 us
    ppermute x6, waiting for transfers between devices, body(): lax.ppermute(outs[j - 1], 'x', ring(NX, j))  7.64 us
    ppermute x2, starting transfers between devices, body(): lax.ppermute(done_same, ('dp', 'core'), to_owner(st, False))  6.96 us
    ppermute x2, starting transfers between devices, body(): w_z = [lax.ppermute(w, ('grp', 'zh'), WRAP) for w in w_z]  6.08 us
    ppermute x6, starting transfers between devices, sum_over(): got = [lax.ppermute(array, axis, ring(n, j)) for j in range(1, n)]  5.51 us
    ppermute x3, starting transfers between devices, body(): got = {j: lax.ppermute(outs[j - 1], 'x', ring(NX, j)) for j in (2, 1, 3)}  5.3 us
  transfers between devices with their start and end apart: 35, of which 13 were waited for; matrix products, arithmetic and copies ran while one was open for 4% of the time, Pallas kernels for 26%

profile of v9, /device:TPU:0, one launch (start us, length us, event | category | flops | bytes accessed | tf_op | source)
XLA Modules:
  0.0 153.1 jit_solution(7196813082437555211)
XLA Ops:
  8.0 3.5 %pick.1 = (bf16[4,2,128,256]{3,2,1,0:T(8,128)(2,1)}, bf16[256,2560]{1,0:T(8,128)(2,1)}, bf16[128,1280]{1,0:T(8,128)(2,1)}) custom-call(s32[11]{0:T(128)S(1)} %concatenate.6.s, bf16[4,4,128,256]{3,2,1,0:T(8,128)(2,1)} %bitcast.34, bf16[256,5120]{1,0:T(8,128)(2,1)} %w_a.3, bf16[256,5120]{1,0:T(8,128)(2,1)} %w_a.3, bf16[256,5120]{1,0:T(8,128)(2,1)} %w_a.3, ...), custom_call_target="tpu_custom_call" | custom-call | flops 1 | bytes 1 | tf_op jit(solution)/shard_map/pick/pallas_call | solution.py:52
  13.0 4.2 %collective-permute-start.1 = (bf16[4,2,128,256]{3,2,1,0:T(8,128)(2,1)}, bf16[4,2,128,256]{3,2,1,0:T(8,128)(2,1)S(1)}, u32[]{:S(2)}, u32[]{:S(2)}) collective-permute-start(bf16[4,2,128,256]{3,2,1,0:T(8,128)(2,1)} %get-tuple-element.70), channel_id=1, source_target_pairs={{0,66},{2,64},{64,2},{66,0},{1,67},{3,65},{65,3},{67,1},{4,70},{6,... | collective-permute-start | bytes 1572872 | tf_op jit(solution)/shard_map/ppermute | solution.py:310
  18.3 2.9 %pick_weights.1 = (bf16[512,640]{1,0:T(8,128)(2,1)}, bf16[512,640]{1,0:T(8,128)(2,1)}) custom-call(s32[11]{0:T(128)S(1)} %concatenate.6.s, bf16[256,5120]{1,0:T(8,128)(2,1)} %w_a.3, bf16[256,5120]{1,0:T(8,128)(2,1)} %w_a.3, bf16[256,2560]{1,0:T(8,128)(2,1)} %copy-done.4), custom_call_target="tpu_custom_call" | custom-call | flops 1 | bytes 1 | tf_op jit(solution)/shard_map/pick_weights/pallas_call | solution.py:52
  21.2 2.9 %collective-permute-start.4 = (bf16[512,640]{1,0:T(8,128)(2,1)}, bf16[512,640]{1,0:T(8,128)(2,1)S(1)}, u32[]{:S(2)}, u32[]{:S(2)}) collective-permute-start(bf16[512,640]{1,0:T(8,128)(2,1)} %get-tuple-element.75), channel_id=1, source_target_pairs={{0,66},{2,64},{64,2},{66,0},{1,67},{3,65},{65,3},{67,1},{4,70},{6,... | collective-permute-start | bytes 1966088 | tf_op jit(solution)/shard_map/ppermute | solution.py:348
  24.1 5.0 %attend_chip.1.ctx_a = bf16[1024,256]{1,0:T(8,128)(2,1)S(1)} custom-call(s32[11]{0:T(128)S(1)} %concatenate.6.s, bf16[4,4,128,256]{3,2,1,0:T(8,128)(2,1)S(1)} %bitcast.35, bf16[2048,512]{1,0:T(8,128)(2,1)S(1)} %bitcast.27, bf16[2048,512]{1,0:T(8,128)(2,1)S(1)} %bitcast.29), custom_call_target="tpu_custom_call" | custom-call | flops 1 | bytes 1 | tf_op jit(solution)/shard_map/attend_chip/pallas_call | solution.py:52
  30.2 5.1 %attend_next.1.ctx_b = bf16[1024,256]{1,0:T(8,128)(2,1)S(1)} custom-call(s32[11]{0:T(128)S(1)} %concatenate.6.s, bf16[4,2,128,256]{3,2,1,0:T(8,128)(2,1)S(1)} %collective-permute-done.1.q_ref, bf16[2048,512]{1,0:T(8,128)(2,1)S(1)} %bitcast.28, bf16[2048,512]{1,0:T(8,128)(2,1)S(1)} %bitcast.30), custom_call_target="tpu_custom_call" | custom-call | flops 1 | bytes 1 | tf_op jit(solution)/shard_map/attend_next/pallas_call | solution.py:52
  35.8 3.2 %collective-permute-start.5 = (bf16[512,640]{1,0:T(8,128)(2,1)}, bf16[512,640]{1,0:T(8,128)(2,1)}, u32[]{:S(2)}, u32[]{:S(2)}) collective-permute-start(bf16[512,640]{1,0:T(8,128)(2,1)} %get-tuple-element.84), channel_id=1, source_target_pairs={{0,66},{2,64},{64,2},{66,0},{1,67},{3,65},{65,3},{67,1},{4,70},{6,... | collective-permute-start | bytes 1966088 | tf_op jit(solution)/shard_map/ppermute | solution.py:348
  39.1 5.1 %collective-permute-done.4.w_z = bf16[512,640]{1,0:T(8,128)(2,1)S(1)} collective-permute-done((bf16[512,640]{1,0:T(8,128)(2,1)}, bf16[512,640]{1,0:T(8,128)(2,1)S(1)}, u32[]{:S(2)}, u32[]{:S(2)}) %collective-permute-start.4) | collective-permute-done | bytes 655392 | tf_op jit(solution)/shard_map/ppermute | solution.py:348
  44.2 3.5 %project_0.1 = (f32[2,128,640]{2,1,0:T(8,128)S(1)}, bf16[2,128,640]{2,1,0:T(8,128)(2,1)}, bf16[2,128,640]{2,1,0:T(8,128)(2,1)}, bf16[2,128,640]{2,1,0:T(8,128)(2,1)}) custom-call(s32[11]{0:T(128)S(1)} %concatenate.6.s, bf16[1024,256]{1,0:T(8,128)(2,1)S(1)} %attend_chip.1.ctx_a, bf16[1024,256]{1,0:T(8,128)(2,1)S(1)} %collective-permute-done.2.ctx_ac, ...), custom_call_target="tpu_custom_call" | custom-call | flops 1 | bytes 1 | tf_op jit(solution)/shard_map/project_0/pallas_call | solution.py:52
  50.1 2.7 %collective-permute-start.7 = (bf16[2,128,640]{2,1,0:T(8,128)(2,1)}, bf16[2,128,640]{2,1,0:T(8,128)(2,1)}, u32[]{:S(2)}, u32[]{:S(2)}) collective-permute-start(bf16[2,128,640]{2,1,0:T(8,128)(2,1)} %get-tuple-element.88), channel_id=1, source_target_pairs={{0,8},{4,12},{8,0},{12,4},{1,9},{5,13},{9,1},{13,5},{2,10},{6,14},... | collective-permute-start | bytes 983048 | tf_op jit(solution)/shard_map/ppermute | solution.py:373
  54.2 5.1 %fusion.4.pred = f32[512,640]{1,0:T(8,128)S(1)} fusion(bf16[512,2560]{1,0:T(8,128)(2,1)} %all-gather.2.cloned.1.call-done.normed, bf16[2560,640]{1,0:T(8,128)(2,1)} %proj.3), kind=kOutput, calls=%fused_computation.15 | convolution fusion | flops 1677721600 | bytes 7208960 | tf_op jit(solution)/shard_map/dot_general | solution.py:371
  59.4 4.5 %project_1.1 = (f32[2,128,640]{2,1,0:T(8,128)S(1)}, bf16[2,128,640]{2,1,0:T(8,128)(2,1)}, bf16[2,128,640]{2,1,0:T(8,128)(2,1)}, bf16[2,128,640]{2,1,0:T(8,128)(2,1)}) custom-call(s32[11]{0:T(128)S(1)} %concatenate.6.s, bf16[1024,256]{1,0:T(8,128)(2,1)S(1)} %copy-done.11, bf16[1024,256]{1,0:T(8,128)(2,1)S(1)} %copy-done.19, bf16[1024,256]{1,0:T(8,128)(2,1)S(1)} %copy-done.13, ...), custom_call_target="tpu_custom_call" | custom-call | flops 1 | bytes 1 | tf_op jit(solution)/shard_map/project_1/pallas_call | solution.py:52
  64.5 2.3 %collective-permute-start.11 = (bf16[2,128,640]{2,1,0:T(8,128)(2,1)}, bf16[2,128,640]{2,1,0:T(8,128)(2,1)S(1)}, u32[]{:S(2)}, u32[]{:S(2)}) collective-permute-start(bf16[2,128,640]{2,1,0:T(8,128)(2,1)} %get-tuple-element.94), channel_id=1, source_target_pairs={{0,8},{4,12},{8,0},{12,4},{1,9},{5,13},{9,1},{13,5},{2,10},{6,14},... | collective-permute-start | bytes 983048 | tf_op jit(solution)/shard_map/ppermute | solution.py:373
  70.5 3.3 %collective-permute-start.13 = (bf16[128,640]{1,0:T(8,128)(2,1)S(1)}, bf16[128,640]{1,0:T(8,128)(2,1)S(1)}, u32[]{:S(2)}, u32[]{:S(2)}) collective-permute-start(bf16[128,640]{1,0:T(8,128)(2,1)S(1)} %get-tuple-element.91.same0), channel_id=1, source_target_pairs={{0,32},{1,49},{16,48},{17,1},{32,0},{33,17},{48,16},{49,33},{2,34}... | collective-permute-start | bytes 491528 | tf_op jit(solution)/shard_map/ppermute | solution.py:394
  75.2 6.2 %collective-permute-done.11.r2 = bf16[2,128,640]{2,1,0:T(8,128)(2,1)S(1)} collective-permute-done((bf16[2,128,640]{2,1,0:T(8,128)(2,1)}, bf16[2,128,640]{2,1,0:T(8,128)(2,1)S(1)}, u32[]{:S(2)}, u32[]{:S(2)}) %collective-permute-start.11) | collective-permute-done | bytes 327712 | tf_op jit(solution)/shard_map/ppermute | solution.py:373
  83.3 3.7 %collective-permute-start.15 = (bf16[128,640]{1,0:T(8,128)(2,1)S(1)}, bf16[128,640]{1,0:T(8,128)(2,1)S(1)}, u32[]{:S(2)}, u32[]{:S(2)}) collective-permute-start(bf16[128,640]{1,0:T(8,128)(2,1)S(1)} %get-tuple-element.96.same1), channel_id=1, source_target_pairs={{0,16},{1,1},{16,32},{17,17},{32,48},{33,33},{48,0},{49,49},{2,18}... | collective-permute-start | bytes 491528 | tf_op jit(solution)/shard_map/ppermute | solution.py:394
  87.1 3.1 %compare_0.1 = (bf16[512,640]{1,0:T(8,128)(2,1)}, bf16[2,512,1280]{2,1,0:T(8,128)(2,1)}, f32[32,128]{1,0:T(8,128)S(1)}) custom-call(s32[11]{0:T(128)S(1)} %concatenate.6.s, f32[512,640]{1,0:T(8,128)S(1)} %fusion.4.pred, bf16[512,2560]{1,0:T(8,128)(2,1)S(1)} %copy-done.1, bf16[2560,640]{1,0:T(8,128)(2,1)S(1)} %copy-done.3, ...), custom_call_target="tpu_custom_call" | custom-call | flops 1 | bytes 1 | tf_op jit(solution)/shard_map/compare_0/pallas_call | solution.py:52
  91.7 3.1 %compare_1.1 = (bf16[512,640]{1,0:T(8,128)(2,1)}, bf16[2,512,1280]{2,1,0:T(8,128)(2,1)}, f32[32,128]{1,0:T(8,128)S(1)}) custom-call(s32[11]{0:T(128)S(1)} %concatenate.6.s, f32[512,640]{1,0:T(8,128)S(1)} %fusion.4.pred, bf16[512,2560]{1,0:T(8,128)(2,1)S(1)} %copy-done.1, ...), custom_call_target="tpu_custom_call", output_to_operand_aliasing={{0}: (6, {}), {1}: (7, {})} | custom-call | flops 1 | bytes 1 | tf_op jit(solution)/shard_map/compare_1/pallas_call | solution.py:52
  95.9 3.9 %gproj.1 = (bf16[4,2,160,640]{3,2,1,0:T(8,128)(2,1)}, f32[4,2,160,640]{3,2,1,0:T(8,128)S(1)}) custom-call(s32[11]{0:T(128)S(1)} %concatenate.6.s, bf16[512,2560]{1,0:T(8,128)(2,1)S(1)} %copy-done.1, bf16[512,640]{1,0:T(8,128)(2,1)S(1)} %copy-done.15), custom_call_target="tpu_custom_call" | custom-call | flops 1 | bytes 1 | tf_op jit(solution)/shard_map/gproj/pallas_call | solution.py:52
  100.4 2.6 %collective-permute-done.20 = f32[21,128]{1,0:T(8,128)S(1)} collective-permute-done((f32[21,128]{1,0:T(8,128)S(1)}, f32[21,128]{1,0:T(8,128)S(1)}, u32[]{:S(2)}, u32[]{:S(2)}) %collective-permute-start.20) | collective-permute-done | bytes 10784 | tf_op jit(solution)/shard_map/ppermute | solution.py:267
  110.7 2.9 %collective-permute-start.27 = (bf16[2,160,640]{2,1,0:T(8,128)(2,1)}, bf16[2,160,640]{2,1,0:T(8,128)(2,1)S(1)}, u32[]{:S(2)}, u32[]{:S(2)}) collective-permute-start(bf16[2,160,640]{2,1,0:T(8,128)(2,1)} %get-tuple-element.122), channel_id=1, source_target_pairs={{0,8},{4,12},{8,0},{12,4},{1,9},{5,13},{9,1},{13,5},{2,10},{6,14},... | collective-permute-start | bytes 1228808 | tf_op jit(solution)/shard_map/ppermute | solution.py:445
  114.1 4.7 %collective-permute-done.24 = f32[25,128]{1,0:T(8,128)S(1)} collective-permute-done((f32[25,128]{1,0:T(8,128)S(1)}, f32[25,128]{1,0:T(8,128)S(1)}, u32[]{:S(2)}, u32[]{:S(2)}) %collective-permute-start.24) | collective-permute-done | bytes 12832 | tf_op jit(solution)/shard_map/ppermute | solution.py:267
  120.4 6.8 %collective-permute-done.25 = f32[21,128]{1,0:T(8,128)S(1)} collective-permute-done((f32[21,128]{1,0:T(8,128)S(1)}, f32[21,128]{1,0:T(8,128)S(1)}, u32[]{:S(2)}, u32[]{:S(2)}) %collective-permute-start.25) | collective-permute-done | bytes 10784 | tf_op jit(solution)/shard_map/ppermute | solution.py:267
  139.9 2.6 %hidden.1 = f32[128,1280]{1,0:T(8,128)} custom-call(s32[11]{0:T(128)S(1)} %concatenate.6.s, bf16[128,1280]{1,0:T(8,128)(2,1)} %reduce-scatter.2.cloned.1.call-done.grad, f32[1,128]{1,0:T(1,128)S(1)} %constant_dynamic-slice_fusion.inner, bf16[128,2560]{1,0:T(8,128)(2,1)S(1)} %bitcast.33, f32[128,1]{1,0:T(8,128)S(1)} %copy.16.inverse_rms, ...), custom_call_target="tpu_custom_call" | custom-call | flops 1 | bytes 1 | tf_op jit(solution)/shard_map/hidden/pallas_call | solution.py:52
  (146 shorter events, 43.3 us)
Async XLA Ops:
  7.2 47.1 %all-gather.2.cloned.1.call-start = ((), (), s32[]{:S(2)}) async-start(), calls=%async_computation.1 | async-start | bytes 3276800 | tf_op jit(solution)/shard_map/all_gather | solution.py:334
  12.8 127.1 %reduce-scatter.2.cloned.1.call-start = ((), (), s32[]{:S(2)}) async-start(), calls=%async_computation.2 | async-start | bytes 2949120 | tf_op jit(solution)/shard_map/reduce_scatter | solution.py:424
  13.0 17.2 %collective-permute-start.1 = (bf16[4,2,128,256]{3,2,1,0:T(8,128)(2,1)}, bf16[4,2,128,256]{3,2,1,0:T(8,128)(2,1)S(1)}, u32[]{:S(2)}, u32[]{:S(2)}) collective-permute-start(bf16[4,2,128,256]{3,2,1,0:T(8,128)(2,1)} %get-tuple-element.70), channel_id=1, source_target_pairs={{0,66},{2,64},{64,2},{66,0},{1,67},{3,65},{65,3},{67,1},{4,70},{6,... | collective-permute-start | bytes 1572872 | tf_op jit(solution)/shard_map/ppermute | solution.py:310
  21.2 23.0 %collective-permute-start.4 = (bf16[512,640]{1,0:T(8,128)(2,1)}, bf16[512,640]{1,0:T(8,128)(2,1)S(1)}, u32[]{:S(2)}, u32[]{:S(2)}) collective-permute-start(bf16[512,640]{1,0:T(8,128)(2,1)} %get-tuple-element.75), channel_id=1, source_target_pairs={{0,66},{2,64},{64,2},{66,0},{1,67},{3,65},{65,3},{67,1},{4,70},{6,... | collective-permute-start | bytes 1966088 | tf_op jit(solution)/shard_map/ppermute | solution.py:348
  35.8 23.5 %collective-permute-start.5 = (bf16[512,640]{1,0:T(8,128)(2,1)}, bf16[512,640]{1,0:T(8,128)(2,1)}, u32[]{:S(2)}, u32[]{:S(2)}) collective-permute-start(bf16[512,640]{1,0:T(8,128)(2,1)} %get-tuple-element.84), channel_id=1, source_target_pairs={{0,66},{2,64},{64,2},{66,0},{1,67},{3,65},{65,3},{67,1},{4,70},{6,... | collective-permute-start | bytes 1966088 | tf_op jit(solution)/shard_map/ppermute | solution.py:348
  39.0 25.4 %collective-permute-start.9 = (bf16[128,1280]{1,0:T(8,128)(2,1)}, bf16[128,1280]{1,0:T(8,128)(2,1)}, u32[]{:S(2)}, u32[]{:S(2)}) collective-permute-start(bf16[128,1280]{1,0:T(8,128)(2,1)} %get-tuple-element.90), channel_id=1, source_target_pairs={{0,1},{1,0},{2,3},{3,2},{4,5},{5,4},{6,7},{7,6},{8,9},{9,8},{10,11... | collective-permute-start | bytes 983048 | tf_op jit(solution)/shard_map/ppermute | solution.py:312
  48.6 18.3 %collective-permute-start.6 = (bf16[2,128,640]{2,1,0:T(8,128)(2,1)}, bf16[2,128,640]{2,1,0:T(8,128)(2,1)}, u32[]{:S(2)}, u32[]{:S(2)}) collective-permute-start(bf16[2,128,640]{2,1,0:T(8,128)(2,1)} %get-tuple-element.87), channel_id=1, source_target_pairs={{0,4},{4,8},{8,12},{12,0},{1,5},{5,9},{9,13},{13,1},{2,6},{6,10},{... | collective-permute-start | bytes 983048 | tf_op jit(solution)/shard_map/ppermute | solution.py:373
  50.1 18.2 %collective-permute-start.7 = (bf16[2,128,640]{2,1,0:T(8,128)(2,1)}, bf16[2,128,640]{2,1,0:T(8,128)(2,1)}, u32[]{:S(2)}, u32[]{:S(2)}) collective-permute-start(bf16[2,128,640]{2,1,0:T(8,128)(2,1)} %get-tuple-element.88), channel_id=1, source_target_pairs={{0,8},{4,12},{8,0},{12,4},{1,9},{5,13},{9,1},{13,5},{2,10},{6,14},... | collective-permute-start | bytes 983048 | tf_op jit(solution)/shard_map/ppermute | solution.py:373
  52.8 15.5 %collective-permute-start.8 = (bf16[2,128,640]{2,1,0:T(8,128)(2,1)}, bf16[2,128,640]{2,1,0:T(8,128)(2,1)}, u32[]{:S(2)}, u32[]{:S(2)}) collective-permute-start(bf16[2,128,640]{2,1,0:T(8,128)(2,1)} %get-tuple-element.89), channel_id=1, source_target_pairs={{0,12},{4,0},{8,4},{12,8},{1,13},{5,1},{9,5},{13,9},{2,14},{6,2},{... | collective-permute-start | bytes 983048 | tf_op jit(solution)/shard_map/ppermute | solution.py:373
  63.9 11.4 %collective-permute-start.10 = (bf16[2,128,640]{2,1,0:T(8,128)(2,1)}, bf16[2,128,640]{2,1,0:T(8,128)(2,1)S(1)}, u32[]{:S(2)}, u32[]{:S(2)}) collective-permute-start(bf16[2,128,640]{2,1,0:T(8,128)(2,1)} %get-tuple-element.93), channel_id=1, source_target_pairs={{0,4},{4,8},{8,12},{12,0},{1,5},{5,9},{9,13},{13,1},{2,6},{6,10},{... | collective-permute-start | bytes 983048 | tf_op jit(solution)/shard_map/ppermute | solution.py:373
  64.5 17.0 %collective-permute-start.11 = (bf16[2,128,640]{2,1,0:T(8,128)(2,1)}, bf16[2,128,640]{2,1,0:T(8,128)(2,1)S(1)}, u32[]{:S(2)}, u32[]{:S(2)}) collective-permute-start(bf16[2,128,640]{2,1,0:T(8,128)(2,1)} %get-tuple-element.94), channel_id=1, source_target_pairs={{0,8},{4,12},{8,0},{12,4},{1,9},{5,13},{9,1},{13,5},{2,10},{6,14},... | collective-permute-start | bytes 983048 | tf_op jit(solution)/shard_map/ppermute | solution.py:373
  66.8 14.6 %collective-permute-start.12 = (bf16[2,128,640]{2,1,0:T(8,128)(2,1)}, bf16[2,128,640]{2,1,0:T(8,128)(2,1)S(1)}, u32[]{:S(2)}, u32[]{:S(2)}) collective-permute-start(bf16[2,128,640]{2,1,0:T(8,128)(2,1)} %get-tuple-element.95), channel_id=1, source_target_pairs={{0,12},{4,0},{8,4},{12,8},{1,13},{5,1},{9,5},{13,9},{2,14},{6,2},{... | collective-permute-start | bytes 983048 | tf_op jit(solution)/shard_map/ppermute | solution.py:373
  70.5 16.5 %collective-permute-start.13 = (bf16[128,640]{1,0:T(8,128)(2,1)S(1)}, bf16[128,640]{1,0:T(8,128)(2,1)S(1)}, u32[]{:S(2)}, u32[]{:S(2)}) collective-permute-start(bf16[128,640]{1,0:T(8,128)(2,1)S(1)} %get-tuple-element.91.same0), channel_id=1, source_target_pairs={{0,32},{1,49},{16,48},{17,1},{32,0},{33,17},{48,16},{49,33},{2,34}... | collective-permute-start | bytes 491528 | tf_op jit(solution)/shard_map/ppermute | solution.py:394
  73.8 13.2 %collective-permute-start.14 = (bf16[128,640]{1,0:T(8,128)(2,1)S(1)}, bf16[128,640]{1,0:T(8,128)(2,1)S(1)}, u32[]{:S(2)}, u32[]{:S(2)}) collective-permute-start(bf16[128,640]{1,0:T(8,128)(2,1)S(1)} %get-tuple-element.111), channel_id=1, source_target_pairs={{0,33},{1,48},{16,49},{17,0},{32,1},{33,16},{48,17},{49,32},{2,35}... | collective-permute-start | bytes 491528 | tf_op jit(solution)/shard_map/ppermute | solution.py:395
  83.1 7.1 %collective-permute-start.16 = (bf16[128,640]{1,0:T(8,128)(2,1)S(1)}, bf16[128,640]{1,0:T(8,128)(2,1)S(1)}, u32[]{:S(2)}, u32[]{:S(2)}) collective-permute-start(bf16[128,640]{1,0:T(8,128)(2,1)S(1)} %get-tuple-element.112), channel_id=1, source_target_pairs={{0,17},{1,0},{16,33},{17,16},{32,49},{33,32},{48,1},{49,48},{2,19}... | collective-permute-start | bytes 491528 | tf_op jit(solution)/shard_map/ppermute | solution.py:395
  83.3 8.4 %collective-permute-start.15 = (bf16[128,640]{1,0:T(8,128)(2,1)S(1)}, bf16[128,640]{1,0:T(8,128)(2,1)S(1)}, u32[]{:S(2)}, u32[]{:S(2)}) collective-permute-start(bf16[128,640]{1,0:T(8,128)(2,1)S(1)} %get-tuple-element.96.same1), channel_id=1, source_target_pairs={{0,16},{1,1},{16,32},{17,17},{32,48},{33,33},{48,0},{49,49},{2,18}... | collective-permute-start | bytes 491528 | tf_op jit(solution)/shard_map/ppermute | solution.py:394
  105.4 8.2 %collective-permute-start.23 = (f32[25,128]{1,0:T(8,128)S(1)}, f32[25,128]{1,0:T(8,128)S(1)}, u32[]{:S(2)}, u32[]{:S(2)}) collective-permute-start(f32[25,128]{1,0:T(8,128)S(1)} %pad_maximum_fusion), channel_id=1, source_target_pairs={{0,48},{16,0},{32,16},{48,32},{1,49},{17,1},{33,17},{49,33},{2,50}... | collective-permute-start | bytes 38408 | tf_op jit(solution)/shard_map/ppermute | solution.py:267
  107.1 6.9 %collective-permute-start.22 = (f32[25,128]{1,0:T(8,128)S(1)}, f32[25,128]{1,0:T(8,128)S(1)}, u32[]{:S(2)}, u32[]{:S(2)}) collective-permute-start(f32[25,128]{1,0:T(8,128)S(1)} %pad_maximum_fusion), channel_id=1, source_target_pairs={{0,32},{16,48},{32,0},{48,16},{1,33},{17,49},{33,1},{49,17},{2,34}... | collective-permute-start | bytes 38408 | tf_op jit(solution)/shard_map/ppermute | solution.py:267
  108.7 21.4 %collective-permute-start.26 = (bf16[2,160,640]{2,1,0:T(8,128)(2,1)}, bf16[2,160,640]{2,1,0:T(8,128)(2,1)S(1)}, u32[]{:S(2)}, u32[]{:S(2)}) collective-permute-start(bf16[2,160,640]{2,1,0:T(8,128)(2,1)} %get-tuple-element.121), channel_id=1, source_target_pairs={{0,4},{4,8},{8,12},{12,0},{1,5},{5,9},{9,13},{13,1},{2,6},{6,10},{... | collective-permute-start | bytes 1228808 | tf_op jit(solution)/shard_map/ppermute | solution.py:445
  110.7 20.5 %collective-permute-start.27 = (bf16[2,160,640]{2,1,0:T(8,128)(2,1)}, bf16[2,160,640]{2,1,0:T(8,128)(2,1)S(1)}, u32[]{:S(2)}, u32[]{:S(2)}) collective-permute-start(bf16[2,160,640]{2,1,0:T(8,128)(2,1)} %get-tuple-element.122), channel_id=1, source_target_pairs={{0,8},{4,12},{8,0},{12,4},{1,9},{5,13},{9,1},{13,5},{2,10},{6,14},... | collective-permute-start | bytes 1228808 | tf_op jit(solution)/shard_map/ppermute | solution.py:445
  113.6 17.6 %collective-permute-start.28 = (bf16[2,160,640]{2,1,0:T(8,128)(2,1)}, bf16[2,160,640]{2,1,0:T(8,128)(2,1)S(1)}, u32[]{:S(2)}, u32[]{:S(2)}) collective-permute-start(bf16[2,160,640]{2,1,0:T(8,128)(2,1)} %get-tuple-element.123), channel_id=1, source_target_pairs={{0,12},{4,0},{8,4},{12,8},{1,13},{5,1},{9,5},{13,9},{2,14},{6,2},{... | collective-permute-start | bytes 1228808 | tf_op jit(solution)/shard_map/ppermute | solution.py:445
  118.8 8.4 %collective-permute-start.25 = (f32[21,128]{1,0:T(8,128)S(1)}, f32[21,128]{1,0:T(8,128)S(1)}, u32[]{:S(2)}, u32[]{:S(2)}) collective-permute-start(f32[21,128]{1,0:T(8,128)S(1)} %slice.16), channel_id=1, source_target_pairs={{0,2},{2,0},{1,3},{3,1},{4,6},{6,4},{5,7},{7,5},{8,10},{10,8},{9,1... | collective-permute-start | bytes 32264 | tf_op jit(solution)/shard_map/ppermute | solution.py:267
  132.6 9.9 %collective-permute-start.32 = (bf16[160,640]{1,0:T(8,128)(2,1)}, bf16[160,640]{1,0:T(8,128)(2,1)S(1)}, u32[]{:S(2)}, u32[]{:S(2)}) collective-permute-start(bf16[160,640]{1,0:T(8,128)(2,1)} %get-tuple-element.126), channel_id=1, source_target_pairs={{0,2},{2,0},{1,3},{3,1},{4,6},{6,4},{5,7},{7,5},{8,10},{10,8},{9,1... | collective-permute-start | bytes 614408 | tf_op jit(solution)/shard_map/ppermute | solution.py:468
  135.3 8.0 %collective-permute-start.31 = (f32[21,128]{1,0:T(8,128)S(1)}, f32[21,128]{1,0:T(8,128)S(1)}, u32[]{:S(2)}, u32[]{:S(2)}) collective-permute-start(f32[21,128]{1,0:T(8,128)S(1)} %slice_add_fusion), channel_id=1, source_target_pairs={{0,12},{4,0},{8,4},{12,8},{1,13},{5,1},{9,5},{13,9},{2,14},{6,2},{... | collective-permute-start | bytes 32264 | tf_op jit(solution)/shard_map/ppermute | solution.py:470
  (42 other events, 375.5 us)
Sparse Core Ops, SparseCore 0:
  12.9 37.6 all-gather.1
  94.9 44.8 reduce-scatter.1
